TPU v7x, 32 devices: a whole 2x2x4 slice. The times are simulated.
32 devices in a mesh: blk: 8 (over z, y), head: 4 (over x, core).
Axes of the slice: x: 2, y: 2, z: 4, core: 2. Of those that a mesh axis runs over, the one named last changes fastest.
Arguments:
- encoder_input: bfloat16 [2, 16, 256, 768], P(None, 'blk', 'head'), may hold values from -6 to 6
- passage_lengths: int32 [2, 16], P(None, 'blk'), may hold values from 32 to 256, as said below
- decoder_input: bfloat16 [2, 20, 768], P(None, 'head'), may hold values from -6 to 6
- encoder_query: bfloat16 [768, 768], P('blk', 'head'), may hold values from -0.21875 to 0.21875
- encoder_key: bfloat16 [768, 768], P('blk', 'head'), may hold values from -0.21875 to 0.21875
- encoder_value: bfloat16 [768, 768], P('blk', 'head'), may hold values from -0.21875 to 0.21875
- encoder_output: bfloat16 [768, 768], P('head', 'blk'), may hold values from -1.75 to 1.75
- encoder_inner: bfloat16 [768, 3072], P('blk', 'head'), may hold values from -0.21875 to 0.21875
- encoder_outer: bfloat16 [3072, 768], P('head', 'blk'), may hold values from -0.109375 to 0.109375
- decoder_query: bfloat16 [768, 768], P('blk', 'head'), may hold values from -0.21875 to 0.21875
- decoder_key: bfloat16 [768, 768], P('blk', 'head'), may hold values from -0.21875 to 0.21875
- decoder_value: bfloat16 [768, 768], P('blk', 'head'), may hold values from -0.21875 to 0.21875
- decoder_output: bfloat16 [768, 768], P('head', 'blk'), may hold values from -0.625 to 0.625
- cross_query: bfloat16 [768, 768], P('blk', 'head'), may hold values from -0.21875 to 0.21875
- cross_key: bfloat16 [768, 768], P('blk', 'head'), may hold values from -0.21875 to 0.21875
- cross_value: bfloat16 [768, 768], P('blk', 'head'), may hold values from -0.21875 to 0.21875
- cross_output: bfloat16 [768, 768], P('head', 'blk'), may hold values from -4 to 4
- decoder_inner: bfloat16 [768, 3072], P('blk', 'head'), may hold values from -0.21875 to 0.21875
- decoder_outer: bfloat16 [3072, 768], P('head', 'blk'), may hold values from -0.109375 to 0.109375
- encoder_gains: float32 [2, 768], replicated, may hold values from 0.1 to 1.9
- decoder_gains: float32 [3, 768], replicated, may hold values from 0.1 to 1.9
- encoder_cotangent: bfloat16 [2, 16, 256, 768], P(None, 'blk', 'head'), may hold values from -6 to 6
- decoder_cotangent: bfloat16 [2, 20, 768], P(None, 'head'), may hold values from -6 to 6
Outputs:
- encoder_states: bfloat16 [2, 16, 256, 768], P(None, 'blk', 'head')
- decoder_states: bfloat16 [2, 20, 768], P(None, 'head')
- encoder_input_grad: float32 [2, 16, 256, 768], P(None, 'blk', 'head')
- decoder_input_grad: float32 [2, 20, 768], P(None, 'head')
- encoder_query_grad: float32 [768, 768], P('blk', 'head')
- encoder_key_grad: float32 [768, 768], P('blk', 'head')
- encoder_value_grad: float32 [768, 768], P('blk', 'head')
- encoder_output_grad: float32 [768, 768], P('head', 'blk')
- encoder_inner_grad: float32 [768, 3072], P('blk', 'head')
- encoder_outer_grad: float32 [3072, 768], P('head', 'blk')
- decoder_query_grad: float32 [768, 768], P('blk', 'head')
- decoder_key_grad: float32 [768, 768], P('blk', 'head')
- decoder_value_grad: float32 [768, 768], P('blk', 'head')
- decoder_output_grad: float32 [768, 768], P('head', 'blk')
- cross_query_grad: float32 [768, 768], P('blk', 'head')
- cross_key_grad: float32 [768, 768], P('blk', 'head')
- cross_value_grad: float32 [768, 768], P('blk', 'head')
- cross_output_grad: float32 [768, 768], P('head', 'blk')
- decoder_inner_grad: float32 [768, 3072], P('blk', 'head')
- decoder_outer_grad: float32 [3072, 768], P('head', 'blk')
- encoder_gains_grad: float32 [2, 768], replicated
- decoder_gains_grad: float32 [3, 768], replicated
Inputs may be any that keep to these rules, and one draw needn't show every extreme that they name: `passage_lengths`: used token slots of each passage; the first passage of every question fills all 256 slots.
All inputs are finite; a program needn't handle non-finite values.
Results may differ from a plain program's by a relative error of at most 0.029.
The roundings to bfloat16 on the way count: a program that leaves them out, or rounds other values in their place, can miss the bound.
Values may be sent and summed in bfloat16 or wider, within the bound.
No kernel may reach another device: no remote copies, remote signals or barrier semaphores. Data moves between devices by JAX's collectives and lax.ppermute only.
A program may use at most 128 MiB of HBM per device.

v0:
```python
import jax
import jax.numpy as jnp
from jax import lax
from jax.sharding import PartitionSpec as P

HDIM = 64


highest = lax.Precision.HIGHEST
masked_score = -1000000000.0


def joined(array, axis, combine):
    everything = jax.tree.map(lambda part: lax.all_gather(part, axis), array)
    initial = jax.tree.map(lambda part: part[0], everything)

    def turn(k, so_far):
        return combine(so_far, jax.tree.map(lambda part: part[k], everything))

    return lax.fori_loop(1, lax.axis_size(axis), turn, initial)


def norm_rows(values, gain):
    return values * lax.rsqrt(jnp.mean(values * values, axis=-1, keepdims=True) + 1e-06) * gain


def norm_back(values, gain, grad):
    pull = jax.vjp(norm_rows, values, gain)[1]
    return pull(grad)


def gelu_tanh(values):
    return jax.nn.gelu(values, approximate=True)


def gelu_back(values, grad):
    return jax.vjp(gelu_tanh, values)[1](grad)[0]


def project(left, weight):
    return jnp.einsum("...k,kn->...n", left, weight, preferred_element_type=jnp.float32)


def project_back(left, weight):
    return jnp.einsum("...n,kn->...k", left, weight, preferred_element_type=jnp.float32)


def weight_grad(left, right):
    flat_left = left.reshape(-1, left.shape[-1])
    flat_right = right.reshape(-1, right.shape[-1])
    return jnp.einsum("rk,rn->kn", flat_left, flat_right, preferred_element_type=jnp.float32)


def rows_in(values):
    return lax.all_gather(values, "head", axis=1, tiled=True)


def rows_out(values):
    return lax.psum_scatter(values, "head", scatter_dimension=1, tiled=True)


def ffn_in(values):
    return lax.all_gather(values, "head", axis=1, tiled=True)


def ffn_out(values):
    return lax.psum_scatter(values, "head", scatter_dimension=1, tiled=True)


def attend(query, keys, vals, allowed, scale):
    scores = jnp.einsum("bqhc,bkhc->bhqk", query, keys, preferred_element_type=jnp.float32) * scale
    scores = jnp.where(allowed, scores, masked_score)
    top = jnp.max(scores, axis=-1, keepdims=True)
    spread = jnp.exp(scores - top)
    total = jnp.sum(spread, axis=-1, keepdims=True)
    probs = (spread / total).astype(jnp.bfloat16)
    context = jnp.einsum("bhqk,bkhc->bqhc", probs, vals, preferred_element_type=jnp.float32).astype(
        jnp.bfloat16
    )
    return (context, top + jnp.log(total))


def attend_back(query, keys, vals, allowed, log_total, dcontext, scale):
    scores = jnp.einsum("bqhc,bkhc->bhqk", query, keys, preferred_element_type=jnp.float32) * scale
    scores = jnp.where(allowed, scores, masked_score)
    probs = jnp.exp(scores - log_total)
    dvals = jnp.einsum(
        "bhqk,bqhc->bkhc", probs.astype(jnp.bfloat16), dcontext, preferred_element_type=jnp.float32
    )
    dprobs = jnp.einsum("bqhc,bkhc->bhqk", dcontext, vals, preferred_element_type=jnp.float32)
    dscores = probs * (dprobs - jnp.sum(probs * dprobs, axis=-1, keepdims=True))
    dscores = dscores.astype(jnp.bfloat16)
    dquery = (
        jnp.einsum("bhqk,bkhc->bqhc", dscores, keys, preferred_element_type=jnp.float32) * scale
    )
    dkeys = (
        jnp.einsum("bhqk,bqhc->bkhc", dscores, query, preferred_element_type=jnp.float32) * scale
    )
    return (dquery.astype(jnp.bfloat16), dkeys.astype(jnp.bfloat16), dvals.astype(jnp.bfloat16))


def combine(earlier, later):
    top = jnp.maximum(earlier[0], later[0])
    weight_a = jnp.exp(earlier[0] - top)
    weight_b = jnp.exp(later[0] - top)
    return (
        top,
        earlier[1] * weight_a + later[1] * weight_b,
        earlier[2] * weight_a[..., None] + later[2] * weight_b[..., None],
    )


def shards(
    encoder_input,
    passage_lengths,
    decoder_input,
    encoder_query,
    encoder_key,
    encoder_value,
    encoder_output,
    encoder_inner,
    encoder_outer,
    decoder_query,
    decoder_key,
    decoder_value,
    decoder_output,
    cross_query,
    cross_key,
    cross_value,
    cross_output,
    decoder_inner,
    decoder_outer,
    encoder_gains,
    decoder_gains,
    encoder_cotangent,
    decoder_cotangent,
):
    fetched = (
        lax.all_gather(encoder_query, "blk", axis=0, tiled=True),
        lax.all_gather(encoder_key, "blk", axis=0, tiled=True),
        lax.all_gather(encoder_value, "blk", axis=0, tiled=True),
        lax.all_gather(encoder_inner, "blk", axis=0, tiled=True),
        lax.all_gather(decoder_query, "blk", axis=0, tiled=True),
        lax.all_gather(decoder_key, "blk", axis=0, tiled=True),
        lax.all_gather(decoder_value, "blk", axis=0, tiled=True),
        lax.all_gather(cross_query, "blk", axis=0, tiled=True),
        lax.all_gather(cross_key, "blk", axis=0, tiled=True),
        lax.all_gather(cross_value, "blk", axis=0, tiled=True),
        lax.all_gather(decoder_inner, "blk", axis=0, tiled=True),
        lax.all_gather(encoder_output, "blk", axis=1, tiled=True),
        lax.all_gather(encoder_outer, "blk", axis=1, tiled=True),
        lax.all_gather(decoder_output, "blk", axis=1, tiled=True),
        lax.all_gather(cross_output, "blk", axis=1, tiled=True),
        lax.all_gather(decoder_outer, "blk", axis=1, tiled=True),
    )
    (
        enc_wquery,
        enc_wkey,
        enc_wvalue,
        enc_winner,
        dec_wquery,
        dec_wkey,
        dec_wvalue,
        cross_wquery,
        cross_wkey,
        cross_wvalue,
        dec_winner,
        enc_woutput,
        enc_wouter,
        dec_woutput,
        cross_woutput,
        dec_wouter,
    ) = fetched
    scale = HDIM ** (-0.5)
    count_q, count_pass, part, width = encoder_input.shape
    slot = part * lax.axis_size("head")
    blocks = count_q * count_pass
    heads_dev = enc_wquery.shape[1] // HDIM

    def heads_of(values):
        return values.reshape(values.shape[0], values.shape[1], heads_dev, HDIM)

    x_rows = encoder_input.astype(jnp.float32).reshape(blocks, part, width)
    first_norm = rows_in(norm_rows(x_rows, encoder_gains[0]).astype(jnp.bfloat16))
    enc_queries = project(first_norm, enc_wquery).astype(jnp.bfloat16)
    enc_keys = project(first_norm, enc_wkey).astype(jnp.bfloat16)
    enc_values = project(first_norm, enc_wvalue).astype(jnp.bfloat16)
    valid = jnp.arange(slot)[None, :] < passage_lengths.reshape(blocks)[:, None]
    enc_allowed = valid[:, None, None, :]
    enc_context, enc_log_total = attend(
        heads_of(enc_queries), heads_of(enc_keys), heads_of(enc_values), enc_allowed, scale
    )
    enc_context = enc_context.reshape(blocks, slot, -1)
    hidden_rows = x_rows + rows_out(project(enc_context, enc_woutput))
    second_norm = ffn_in(norm_rows(hidden_rows, encoder_gains[1]).astype(jnp.bfloat16))
    enc_inner = project(second_norm, enc_winner)
    enc_active = gelu_tanh(enc_inner).astype(jnp.bfloat16)
    state_rows = hidden_rows + ffn_out(project(enc_active, enc_wouter))
    state_low = state_rows.astype(jnp.bfloat16)
    state_full = rows_in(state_low)
    cross_keys = (
        project(state_full, cross_wkey)
        .astype(jnp.bfloat16)
        .reshape(count_q, count_pass * slot, heads_dev, HDIM)
    )
    cross_vals = (
        project(state_full, cross_wvalue)
        .astype(jnp.bfloat16)
        .reshape(count_q, count_pass * slot, heads_dev, HDIM)
    )
    key_valid = valid.reshape(count_q, count_pass * slot)
    dec_part = decoder_input.shape[1]
    dec_rows = dec_part * lax.axis_size("head")
    z_rows = decoder_input.astype(jnp.float32)
    third_norm = rows_in(norm_rows(z_rows, decoder_gains[0]).astype(jnp.bfloat16))
    dec_queries = project(third_norm, dec_wquery).astype(jnp.bfloat16)
    dec_keys = project(third_norm, dec_wkey).astype(jnp.bfloat16)
    dec_values = project(third_norm, dec_wvalue).astype(jnp.bfloat16)
    causal = (jnp.arange(dec_rows)[:, None] >= jnp.arange(dec_rows)[None, :])[None, None]
    dec_context, dec_log_total = attend(
        heads_of(dec_queries), heads_of(dec_keys), heads_of(dec_values), causal, scale
    )
    dec_context = dec_context.reshape(count_q, dec_rows, -1)
    after_self = z_rows + rows_out(project(dec_context, dec_woutput))
    fourth_norm = rows_in(norm_rows(after_self, decoder_gains[1]).astype(jnp.bfloat16))
    cross_queries = heads_of(project(fourth_norm, cross_wquery).astype(jnp.bfloat16))
    cross_allowed = key_valid[:, None, None, :]
    cross_scores = (
        jnp.einsum("qihc,qthc->qhit", cross_queries, cross_keys, preferred_element_type=jnp.float32)
        * scale
    )
    cross_scores = jnp.where(cross_allowed, cross_scores, masked_score)
    local_top = jnp.max(cross_scores, axis=-1)
    local_exp = jnp.exp(cross_scores - local_top[..., None])
    local_total = jnp.sum(local_exp, axis=-1)
    local_sum = jnp.einsum(
        "qhit,qthc->qhic", local_exp, cross_vals.astype(jnp.float32), precision=highest
    )
    global_top, global_total, global_sum = joined(
        (local_top, local_total, local_sum), "blk", combine
    )
    cross_out = global_sum / global_total[..., None]
    cross_log_total = global_top + jnp.log(global_total)
    cross_context = (
        cross_out.astype(jnp.bfloat16).transpose(0, 2, 1, 3).reshape(count_q, dec_rows, -1)
    )
    after_cross = after_self + rows_out(project(cross_context, cross_woutput))
    fifth_norm = ffn_in(norm_rows(after_cross, decoder_gains[2]).astype(jnp.bfloat16))
    dec_inner = project(fifth_norm, dec_winner)
    dec_active = gelu_tanh(dec_inner).astype(jnp.bfloat16)
    out_rows = after_cross + ffn_out(project(dec_active, dec_wouter))
    grad_out = decoder_cotangent.astype(jnp.float32)
    dec_ffn_full = ffn_in(grad_out.astype(jnp.bfloat16))
    grad_dec_outer = weight_grad(dec_active, dec_ffn_full)
    dec_inner_grad = gelu_back(dec_inner, project_back(dec_ffn_full, dec_wouter)).astype(
        jnp.bfloat16
    )
    grad_dec_inner = weight_grad(fifth_norm, dec_inner_grad)
    norm_grad, gain_four = norm_back(
        after_cross, decoder_gains[2], ffn_out(project_back(dec_inner_grad, dec_winner))
    )
    grad_cross = grad_out + norm_grad
    cross_full = rows_in(grad_cross.astype(jnp.bfloat16))
    grad_cross_output = weight_grad(cross_context, cross_full)
    dcross_context = project_back(cross_full, cross_woutput).astype(jnp.bfloat16)
    dcross_context = dcross_context.reshape(count_q, dec_rows, heads_dev, HDIM).transpose(
        0, 2, 1, 3
    )
    cross_probs = jnp.exp(cross_scores - cross_log_total[..., None])
    dcross_vals = jnp.einsum(
        "qhit,qhic->qthc", cross_probs, dcross_context.astype(jnp.float32), precision=highest
    )
    dcross_probs = jnp.einsum(
        "qhic,qthc->qhit", dcross_context, cross_vals, preferred_element_type=jnp.float32
    )
    row_terms = jnp.sum(dcross_context.astype(jnp.float32) * cross_out, axis=-1)
    dcross_scores = cross_probs * (dcross_probs - row_terms[..., None])
    query_part = (
        jnp.einsum(
            "qhit,qthc->qihc", dcross_scores, cross_keys.astype(jnp.float32), precision=highest
        )
        * scale
    )
    dcross_keys = (
        jnp.einsum(
            "qhit,qihc->qthc", dcross_scores, cross_queries.astype(jnp.float32), precision=highest
        )
        * scale
    ).astype(jnp.bfloat16)
    dcross_vals = dcross_vals.astype(jnp.bfloat16)
    dcross_query = lax.psum(query_part, "blk").astype(jnp.bfloat16).reshape(count_q, dec_rows, -1)
    grad_cross_query = weight_grad(fourth_norm, dcross_query)
    norm_grad, gain_three = norm_back(
        after_self, decoder_gains[1], rows_out(project_back(dcross_query, cross_wquery))
    )
    grad_self = grad_cross + norm_grad
    self_full = rows_in(grad_self.astype(jnp.bfloat16))
    grad_dec_output = weight_grad(dec_context, self_full)
    dself_context = heads_of(project_back(self_full, dec_woutput).astype(jnp.bfloat16))
    dself_query, dself_key, dself_value = attend_back(
        heads_of(dec_queries),
        heads_of(dec_keys),
        heads_of(dec_values),
        causal,
        dec_log_total,
        dself_context,
        scale,
    )
    dself_query = dself_query.reshape(count_q, dec_rows, -1)
    dself_key = dself_key.reshape(count_q, dec_rows, -1)
    dself_value = dself_value.reshape(count_q, dec_rows, -1)
    grad_dec_query = weight_grad(third_norm, dself_query)
    grad_dec_key = weight_grad(third_norm, dself_key)
    grad_dec_value = weight_grad(third_norm, dself_value)
    third_grad = (
        project_back(dself_query, dec_wquery)
        + project_back(dself_key, dec_wkey)
        + project_back(dself_value, dec_wvalue)
    )
    norm_grad, gain_two = norm_back(z_rows, decoder_gains[0], rows_out(third_grad))
    decoder_input_grad = grad_self + norm_grad
    keys_flat = dcross_keys.reshape(blocks, slot, -1)
    vals_flat = dcross_vals.reshape(blocks, slot, -1)
    grad_cross_key = weight_grad(state_full, keys_flat)
    grad_cross_value = weight_grad(state_full, vals_flat)
    state_cross = rows_out(
        project_back(keys_flat, cross_wkey) + project_back(vals_flat, cross_wvalue)
    )
    grad_state = encoder_cotangent.astype(jnp.float32).reshape(blocks, part, width) + state_cross
    enc_ffn_full = ffn_in(grad_state.astype(jnp.bfloat16))
    grad_enc_outer = weight_grad(enc_active, enc_ffn_full)
    enc_inner_grad = gelu_back(enc_inner, project_back(enc_ffn_full, enc_wouter)).astype(
        jnp.bfloat16
    )
    grad_enc_inner = weight_grad(second_norm, enc_inner_grad)
    norm_grad, gain_one = norm_back(
        hidden_rows, encoder_gains[1], ffn_out(project_back(enc_inner_grad, enc_winner))
    )
    grad_hidden = grad_state + norm_grad
    attn_full = rows_in(grad_hidden.astype(jnp.bfloat16))
    grad_enc_output = weight_grad(enc_context, attn_full)
    denc_context = heads_of(project_back(attn_full, enc_woutput).astype(jnp.bfloat16))
    denc_query, denc_key, denc_value = attend_back(
        heads_of(enc_queries),
        heads_of(enc_keys),
        heads_of(enc_values),
        enc_allowed,
        enc_log_total,
        denc_context,
        scale,
    )
    denc_query = denc_query.reshape(blocks, slot, -1)
    denc_key = denc_key.reshape(blocks, slot, -1)
    denc_value = denc_value.reshape(blocks, slot, -1)
    grad_enc_query = weight_grad(first_norm, denc_query)
    grad_enc_key = weight_grad(first_norm, denc_key)
    grad_enc_value = weight_grad(first_norm, denc_value)
    first_grad = (
        project_back(denc_query, enc_wquery)
        + project_back(denc_key, enc_wkey)
        + project_back(denc_value, enc_wvalue)
    )
    norm_grad, gain_zero = norm_back(x_rows, encoder_gains[0], rows_out(first_grad))
    encoder_input_grad = (grad_hidden + norm_grad).reshape(encoder_input.shape)
    summed = (
        lax.psum_scatter(grad_enc_query, "blk", scatter_dimension=0, tiled=True),
        lax.psum_scatter(grad_enc_key, "blk", scatter_dimension=0, tiled=True),
        lax.psum_scatter(grad_enc_value, "blk", scatter_dimension=0, tiled=True),
        lax.psum_scatter(grad_enc_inner, "blk", scatter_dimension=0, tiled=True),
        lax.psum_scatter(grad_cross_key, "blk", scatter_dimension=0, tiled=True),
        lax.psum_scatter(grad_cross_value, "blk", scatter_dimension=0, tiled=True),
        lax.psum_scatter(grad_enc_output, "blk", scatter_dimension=1, tiled=True),
        lax.psum_scatter(grad_enc_outer, "blk", scatter_dimension=1, tiled=True),
    )
    position = lax.axis_index("blk")
    blk_count = lax.axis_size("blk")

    def own_slice(grad, dim):
        size = grad.shape[dim] // blk_count
        return lax.dynamic_slice_in_dim(grad, position * size, size, dim)

    leading = (position == 0).astype(jnp.float32)
    enc_gain_parts = jnp.stack([gain_zero, gain_one])
    dec_gain_parts = jnp.stack([gain_two * leading, gain_three * leading, gain_four * leading])
    enc_gain_total, dec_gain_total = lax.psum((enc_gain_parts, dec_gain_parts), ("blk", "head"))
    return (
        state_low.reshape(encoder_input.shape),
        out_rows.astype(jnp.bfloat16),
        encoder_input_grad,
        decoder_input_grad,
        summed[0],
        summed[1],
        summed[2],
        summed[6],
        summed[3],
        summed[7],
        own_slice(grad_dec_query, 0),
        own_slice(grad_dec_key, 0),
        own_slice(grad_dec_value, 0),
        own_slice(grad_dec_output, 1),
        own_slice(grad_cross_query, 0),
        summed[4],
        summed[5],
        own_slice(grad_cross_output, 1),
        own_slice(grad_dec_inner, 0),
        own_slice(grad_dec_outer, 1),
        enc_gain_total,
        dec_gain_total,
    )


def solution(mesh):
    placed = (
        P(None, "blk", "head", None),
        P(None, "blk"),
        P(None, "head", None),
        P("blk", "head"),
        P("blk", "head"),
        P("blk", "head"),
        P("head", "blk"),
        P("blk", "head"),
        P("head", "blk"),
        P("blk", "head"),
        P("blk", "head"),
        P("blk", "head"),
        P("head", "blk"),
        P("blk", "head"),
        P("blk", "head"),
        P("blk", "head"),
        P("head", "blk"),
        P("blk", "head"),
        P("head", "blk"),
        P(),
        P(),
        P(None, "blk", "head", None),
        P(None, "head", None),
    )
    return jax.shard_map(
        shards,
        mesh=mesh,
        in_specs=placed,
        out_specs=(
            P(None, "blk", "head", None),
            P(None, "head", None),
            P(None, "blk", "head", None),
            P(None, "head", None),
            P("blk", "head"),
            P("blk", "head"),
            P("blk", "head"),
            P("head", "blk"),
            P("blk", "head"),
            P("head", "blk"),
            P("blk", "head"),
            P("blk", "head"),
            P("blk", "head"),
            P("head", "blk"),
            P("blk", "head"),
            P("blk", "head"),
            P("blk", "head"),
            P("head", "blk"),
            P("blk", "head"),
            P("head", "blk"),
            P(),
            P(),
        ),
        check_vma=False,
    )
```

profile of v0, /device:TPU:0, one launch (start us, length us, event | category | flops | bytes accessed | tf_op | source)
XLA Modules:
  0.0 1669.2 jit_solution(3727587759226969671)
XLA Ops:
  14.3 34.9 %all_gather.103 = bf16[192,768]{0,1:T(8,128)(2,1)} all-gather(bf16[192,96]{0,1:T(8,128)(2,1)S(1)} %copy.271), channel_id=1, replica_groups=mesh['blk'=8,'head'=4] {'blk'}, dimensions={1}, use_global_device_ids=true | all-gather | bytes 331776 | tf_op jit(solution)/shard_map/all_gather | solution.py:150
  49.2 31.5 %all_gather.101 = bf16[768,192]{1,0:T(8,128)(2,1)S(1)} all-gather(bf16[96,192]{1,0:T(8,128)(2,1)} %param.28), channel_id=1, replica_groups=mesh['blk'=8,'head'=4] {'blk'}, dimensions={0}, use_global_device_ids=true | all-gather | bytes 331776 | tf_op jit(solution)/shard_map/all_gather | solution.py:139
  80.7 31.4 %all_gather.102 = bf16[768,192]{1,0:T(8,128)(2,1)S(1)} all-gather(bf16[96,192]{1,0:T(8,128)(2,1)} %param.29), channel_id=1, replica_groups=mesh['blk'=8,'head'=4] {'blk'}, dimensions={0}, use_global_device_ids=true | all-gather | bytes 331776 | tf_op jit(solution)/shard_map/all_gather | solution.py:140
  154.4 38.3 %reduce-scatter.16.cloned.1.call-done = f32[4,64,768]{2,1,0:T(8,128)} async-done(((f32[4,256,768]{2,1,0:T(8,128)}), f32[4,64,768]{2,1,0:T(8,128)}) %reduce-scatter.16.cloned.1.call-update) | async-done | bytes 786448 | tf_op jit(solution)/shard_map/reduce_scatter | solution.py:59
  223.8 39.1 %all-gather.19.cloned.1.call-done = bf16[768,768]{0,1:T(8,128)(2,1)} async-done(((bf16[768,96]{0,1:T(8,128)(2,1)}), bf16[768,768]{0,1:T(8,128)(2,1)}) %all-gather.19.cloned.1.call-update) | async-done | bytes 1179664 | tf_op jit(solution)/shard_map/all_gather | solution.py:151
  347.7 31.3 %all_gather.108 = bf16[768,192]{1,0:T(8,128)(2,1)S(1)} all-gather(bf16[96,192]{1,0:T(8,128)(2,1)} %param.36), channel_id=1, replica_groups=mesh['blk'=8,'head'=4] {'blk'}, dimensions={0}, use_global_device_ids=true | all-gather | bytes 331776 | tf_op jit(solution)/shard_map/all_gather | solution.py:145
  429.0 33.2 %all_gather.123 = bf16[192,768]{0,1:T(8,128)(2,1)} all-gather(bf16[192,96]{0,1:T(8,128)(2,1)} %copy.305), channel_id=1, replica_groups=mesh['blk'=8,'head'=4] {'blk'}, dimensions={1}, use_global_device_ids=true | all-gather | bytes 331776 | tf_op jit(solution)/shard_map/all_gather | solution.py:153
  462.2 33.4 %all_gather.113 = bf16[768,192]{1,0:T(8,128)(2,1)} all-gather(bf16[96,192]{1,0:T(8,128)(2,1)} %param.38), channel_id=1, replica_groups=mesh['blk'=8,'head'=4] {'blk'}, dimensions={0}, use_global_device_ids=true | all-gather | bytes 331776 | tf_op jit(solution)/shard_map/all_gather | solution.py:146
  495.6 33.2 %all_gather.115 = bf16[768,192]{1,0:T(8,128)(2,1)} all-gather(bf16[96,192]{1,0:T(8,128)(2,1)} %param.39), channel_id=1, replica_groups=mesh['blk'=8,'head'=4] {'blk'}, dimensions={0}, use_global_device_ids=true | all-gather | bytes 331776 | tf_op jit(solution)/shard_map/all_gather | solution.py:147
  528.8 33.2 %all_gather.120 = bf16[768,192]{1,0:T(8,128)(2,1)} all-gather(bf16[96,192]{1,0:T(8,128)(2,1)} %param.40), channel_id=1, replica_groups=mesh['blk'=8,'head'=4] {'blk'}, dimensions={0}, use_global_device_ids=true | all-gather | bytes 331776 | tf_op jit(solution)/shard_map/all_gather | solution.py:148
  651.5 31.3 %all-gather.2 = f32[16,3,20,64]{3,2,1,0:T(8,128)S(1)} all-gather(f32[2,3,20,64]{3,2,1,0:T(8,128)S(1)} %fusion.85), channel_id=4, replica_groups=mesh['blk'=8,'head'=4] {'blk'}, dimensions={0}, use_global_device_ids=true | all-gather | bytes 276480 | tf_op jit(solution)/shard_map/all_gather | solution.py:14
  756.7 40.0 %all-gather.25.cloned.1.call-done = bf16[768,768]{0,1:T(8,128)(2,1)} async-done(((bf16[768,96]{0,1:T(8,128)(2,1)}), bf16[768,768]{0,1:T(8,128)(2,1)}) %all-gather.25.cloned.1.call-update) | async-done | bytes 1179664 | tf_op jit(solution)/shard_map/all_gather | solution.py:154
  861.2 38.7 %reduce-scatter.20.cloned.1.call-done = f32[4,64,768]{2,1,0:T(8,128)} async-done(((f32[4,256,768]{2,1,0:T(8,128)}), f32[4,64,768]{2,1,0:T(8,128)}) %reduce-scatter.20.cloned.1.call-update) | async-done | bytes 786448 | tf_op jit(solution)/shard_map/reduce_scatter | solution.py:59
  904.2 38.7 %psum.21 = bf16[2,20,3,64]{3,0,2,1:T(2,128)(2,1)} all-reduce(f32[2,20,3,64]{3,0,2,1:T(2,128)} %bitcast.327), channel_id=1, replica_groups=mesh['blk'=8,'head'=4] {'blk'}, use_global_device_ids=true, to_apply=%region_27.28 | all-reduce | flops 7680 | bytes 46080 | tf_op jit(solution)/shard_map/psum | solution.py:291
  976.3 39.9 %reduce-scatter.22.cloned.1.call-done = f32[4,64,768]{2,1,0:T(8,128)} async-done(((f32[4,256,768]{2,1,0:T(8,128)}), f32[4,64,768]{2,1,0:T(8,128)}) %reduce-scatter.22.cloned.1.call-update) | async-done | bytes 786448 | tf_op jit(solution)/shard_map/reduce_scatter | solution.py:67
  1111.3 36.4 %reduce-scatter.40.cloned.1.call-done = f32[96,192]{1,0:T(8,128)} async-done(((f32[768,192]{1,0:T(8,128)}), f32[96,192]{1,0:T(8,128)}) %reduce-scatter.40.cloned.1.call-update) | async-done | bytes 73744
  1149.4 37.7 %reduce-scatter.24.cloned.1.call-done = f32[4,64,768]{2,1,0:T(8,128)} async-done(((f32[4,256,768]{2,1,0:T(8,128)}), f32[4,64,768]{2,1,0:T(8,128)}) %reduce-scatter.24.cloned.1.call-update) | async-done | bytes 786448 | tf_op jit(solution)/shard_map/reduce_scatter | solution.py:59
  1188.4 40.2 %all-reduce.6 = (f32[2,768]{1,0:T(2,128)}, f32[3,768]{1,0:T(4,128)}) all-reduce(f32[2,768]{1,0:T(2,128)S(1)} %pad_maximum_fusion.1, f32[3,768]{1,0:T(4,128)S(1)} %pad_maximum_fusion), channel_id=1, replica_groups=mesh['blk'=8,'head'=4] {'blk','head'}, use_global_device_ids=true, to_apply=%region_43.44 | all-reduce | flops 3840 | bytes 30720 | tf_op jit(solution)/shard_map/psum | solution.py:385
  1253.9 65.4 %reduce-scatter.38.cloned.1.call-done = f32[96,192]{1,0:T(8,128)} async-done(((f32[768,192]{1,0:T(8,128)}), f32[96,192]{1,0:T(8,128)}) %reduce-scatter.38.cloned.1.call-update) | async-done | bytes 73744 | tf_op jit(solution)/shard_map/reduce_scatter | solution.py:371
  1319.3 72.6 %reduce-scatter.34.cloned.1.call-done = f32[768,96]{0,1:T(8,128)} async-done(((f32[768,768]{0,1:T(8,128)}), f32[768,96]{0,1:T(8,128)}) %reduce-scatter.34.cloned.1.call-update) | async-done | bytes 294928 | tf_op jit(solution)/shard_map/reduce_scatter | solution.py:373
  1391.9 72.6 %reduce-scatter.32.cloned.1.call-done = f32[96,768]{1,0:T(8,128)} async-done(((f32[768,768]{1,0:T(8,128)}), f32[96,768]{1,0:T(8,128)}) %reduce-scatter.32.cloned.1.call-update) | async-done | bytes 294928 | tf_op jit(solution)/shard_map/reduce_scatter | solution.py:369
  1464.5 65.9 %reduce-scatter.30.cloned.1.call-done = f32[96,192]{1,0:T(8,128)} async-done(((f32[768,192]{1,0:T(8,128)}), f32[96,192]{1,0:T(8,128)}) %reduce-scatter.30.cloned.1.call-update) | async-done | bytes 73744 | tf_op jit(solution)/shard_map/reduce_scatter | solution.py:368
  1530.5 65.5 %reduce-scatter.28.cloned.1.call-done = f32[96,192]{1,0:T(8,128)} async-done(((f32[768,192]{1,0:T(8,128)}), f32[96,192]{1,0:T(8,128)}) %reduce-scatter.28.cloned.1.call-update) | async-done | bytes 73744 | tf_op jit(solution)/shard_map/reduce_scatter | solution.py:367
  1596.0 65.9 %reduce-scatter.26.cloned.1.call-done = f32[96,192]{1,0:T(8,128)} async-done(((f32[768,192]{1,0:T(8,128)}), f32[96,192]{1,0:T(8,128)}) %reduce-scatter.26.cloned.1.call-update) | async-done | bytes 73744 | tf_op jit(solution)/shard_map/reduce_scatter | solution.py:366
  (509 shorter events, 622.3 us)
Async XLA Ops:
  8.0 135.3 %all-gather.13.cloned.1.call-start = ((), (), s32[]{:S(2)}) async-start(), calls=%async_computation.13 | async-start | bytes 1966080 | tf_op jit(solution)/shard_map/all_gather | solution.py:55
  12.6 180.1 %reduce-scatter.16.cloned.1.call-start = ((), (), s32[]{:S(2)}) async-start(), calls=%async_computation.14 | async-start | bytes 3932160 | tf_op jit(solution)/shard_map/reduce_scatter | solution.py:59
  196.1 66.9 %all-gather.19.cloned.1.call-start = ((), (), s32[]{:S(2)}) async-start(), calls=%async_computation.17 | async-start | bytes 1327104 | tf_op jit(solution)/shard_map/all_gather | solution.py:151
  196.7 224.7 %reduce-scatter.18.cloned.1.call-start = ((), (), s32[]{:S(2)}) async-start(), calls=%async_computation.18 | async-start | bytes 3932160 | tf_op jit(solution)/shard_map/reduce_scatter | solution.py:67
  268.8 294.4 %all-reduce.14.cloned.1.call-start = ((), (), s32[]{:S(2)}) async-start(), calls=%async_computation.35 | async-start | bytes 245760
  421.3 153.5 %all-gather.21.cloned.1.call-start = ((), (), s32[]{:S(2)}) async-start(), calls=%async_computation.19 | async-start | bytes 1966080 | tf_op jit(solution)/shard_map/all_gather | solution.py:55
  423.6 317.1 %all-reduce.16.cloned.1.call-start = ((), (), s32[]{:S(2)}) async-start(), calls=%async_computation.36 | async-start | bytes 245760
  712.0 84.7 %all-gather.25.cloned.1.call-start = ((), (), s32[]{:S(2)}) async-start(), calls=%async_computation.21 | async-start | bytes 1327104 | tf_op jit(solution)/shard_map/all_gather | solution.py:154
  712.7 118.0 %all-reduce.18.cloned.1.call-start = ((), (), s32[]{:S(2)}) async-start(), calls=%async_computation.37 | async-start | bytes 245760
  801.5 98.5 %reduce-scatter.20.cloned.1.call-start = ((), (), s32[]{:S(2)}) async-start(), calls=%async_computation.22 | async-start | bytes 3932160 | tf_op jit(solution)/shard_map/reduce_scatter | solution.py:59
  861.2 87.1 %all-gather.27.cloned.1.call-start = ((), (), s32[]{:S(2)}) async-start(), calls=%async_computation.23 | async-start | bytes 1966080 | tf_op jit(solution)/shard_map/all_gather | solution.py:63
  902.0 72.9 %all-reduce.20.cloned.1.call-start = ((), (), s32[]{:S(2)}) async-start(), calls=%async_computation.38 | async-start | bytes 245760
  947.8 68.4 %reduce-scatter.22.cloned.1.call-start = ((), (), s32[]{:S(2)}) async-start(), calls=%async_computation.24 | async-start | bytes 3932160 | tf_op jit(solution)/shard_map/reduce_scatter | solution.py:67
  958.2 91.4 %all-gather.29.cloned.1.call-start = ((), (), s32[]{:S(2)}) async-start(), calls=%async_computation.25 | async-start | bytes 1966080 | tf_op jit(solution)/shard_map/all_gather | solution.py:55
  1022.1 82.2 %all-reduce.22.cloned.1.call-start = ((), (), s32[]{:S(2)}) async-start(), calls=%async_computation.39 | async-start | bytes 491520
  1049.5 98.2 %reduce-scatter.40.cloned.1.call-start = ((), (), s32[]{:S(2)}) async-start(), calls=%async_computation.34 | async-start | bytes 884736
  1059.4 127.6 %reduce-scatter.24.cloned.1.call-start = ((), (), s32[]{:S(2)}) async-start(), calls=%async_computation.26 | async-start | bytes 3932160 | tf_op jit(solution)/shard_map/reduce_scatter | solution.py:59
  1067.2 186.7 %reduce-scatter.36.cloned.1.call-start = ((), (), s32[]{:S(2)}) async-start(), calls=%async_computation.32 | async-start | bytes 884736 | tf_op jit(solution)/shard_map/reduce_scatter | solution.py:370
  1070.3 249.0 %reduce-scatter.38.cloned.1.call-start = ((), (), s32[]{:S(2)}) async-start(), calls=%async_computation.33 | async-start | bytes 884736 | tf_op jit(solution)/shard_map/reduce_scatter | solution.py:371
  1071.9 320.0 %reduce-scatter.34.cloned.1.call-start = ((), (), s32[]{:S(2)}) async-start(), calls=%async_computation.31 | async-start | bytes 2654208 | tf_op jit(solution)/shard_map/reduce_scatter | solution.py:373
  1077.7 386.8 %reduce-scatter.32.cloned.1.call-start = ((), (), s32[]{:S(2)}) async-start(), calls=%async_computation.30 | async-start | bytes 2654208 | tf_op jit(solution)/shard_map/reduce_scatter | solution.py:369
  1082.1 448.4 %reduce-scatter.30.cloned.1.call-start = ((), (), s32[]{:S(2)}) async-start(), calls=%async_computation.29 | async-start | bytes 884736 | tf_op jit(solution)/shard_map/reduce_scatter | solution.py:368
  1092.3 503.7 %reduce-scatter.28.cloned.1.call-start = ((), (), s32[]{:S(2)}) async-start(), calls=%async_computation.28 | async-start | bytes 884736 | tf_op jit(solution)/shard_map/reduce_scatter | solution.py:367
  1098.9 562.9 %reduce-scatter.26.cloned.1.call-start = ((), (), s32[]{:S(2)}) async-start(), calls=%async_computation.27 | async-start | bytes 884736 | tf_op jit(solution)/shard_map/reduce_scatter | solution.py:366
  (98 other events, 1288.0 us)
Sparse Core Ops, SparseCore 0:
  12.7 22.3 all-gather.12
  153.9 38.7 reduce-scatter.15
  421.4 29.0 all-reduce.13
  452.6 20.2 all-gather.20
  711.3 29.3 all-reduce.15
  801.6 29.0 all-reduce.17
  861.3 38.6 reduce-scatter.19
  947.9 26.9 all-reduce.19
  977.6 38.5 reduce-scatter.21
Sparse Core Ops, SparseCore 1:
  156.7 42.2 all-gather.16
  201.1 17.9 all-gather.14
  221.4 41.5 all-gather.18
  268.9 36.3 reduce-scatter.17
  714.2 40.2 all-gather.22
  756.7 40.0 all-gather.24
  902.1 19.5 all-gather.26
  1022.2 19.5 all-gather.28
  1049.6 31.2 all-reduce.21
  1084.5 63.2 reduce-scatter.39
  1150.2 36.8 reduce-scatter.23
  1191.3 62.6 reduce-scatter.35
  1257.7 61.6 reduce-scatter.37
  1323.8 68.0 reduce-scatter.33
  1396.4 68.1 reduce-scatter.31
  1468.8 61.6 reduce-scatter.29
  1534.3 61.6 reduce-scatter.27
  1600.3 61.5 reduce-scatter.25
where the time goes:
time: 1680 us; the launch traced here: 1670 us
  waiting for transfers between devices  790 us (47%)
  blocking collectives  592 us (35%)
  matrix products  114 us (7%)
  local copies, waits for them, and re-layouts  88.4 us (5%)
  other arithmetic  65.5 us (4%)
  between operations  17.7 us (1%)
    reduce_scatter x3, waiting for transfers between devices, rows_out(): return lax.psum_scatter(values, 'head', scatter_dimension=1, tiled=True)  115 us
    unnamed x33, waiting for transfers between devices  97.8 us
    all_gather x3, blocking collectives, joined(): everything = jax.tree.map(lambda part: lax.all_gather(part, axis), array)  92.1 us
    reduce_scatter x1, waiting for transfers between devices, shards(): lax.psum_scatter(grad_enc_inner, 'blk', scatter_dimension=0, tiled=True)  72.6 us
    reduce_scatter x1, waiting for transfers between devices, shards(): lax.psum_scatter(grad_enc_outer, 'blk', scatter_dimension=1, tiled=True)  72.6 us
    reduce_scatter x1, waiting for transfers between devices, shards(): lax.psum_scatter(grad_enc_value, 'blk', scatter_dimension=0, tiled=True)  65.9 us
    reduce_scatter x1, waiting for transfers between devices, shards(): lax.psum_scatter(grad_enc_query, 'blk', scatter_dimension=0, tiled=True)  65.9 us
    reduce_scatter x1, waiting for transfers between devices, shards(): lax.psum_scatter(grad_enc_key, 'blk', scatter_dimension=0, tiled=True)  65.5 us
  transfers between devices with their start and end apart: 27, of which 20 were waited for; matrix products, arithmetic and copies ran while one was open for 9% of the time, Pallas kernels for 0%

commit v1 on v0

v1 whole, which is shorter than its diff:
```python
import math

import jax
import jax.numpy as jnp
import numpy as np
from jax import lax
from jax.experimental import pallas as pl
from jax.experimental.pallas import tpu as pltpu
from jax.sharding import PartitionSpec as P

HDIM = 64
SCALE = HDIM ** (-0.5)
LANES = 128
EPS = 1e-06
masked_score = -1000000000.0
f32 = jnp.float32
bf16 = jnp.bfloat16

PLACES, HEAD, BLK, LENGTHS = 0, 8, 9, 10


def swap(value, axis, bits):
    size = lax.axis_size(axis)
    return lax.ppermute(value, axis, [(i, i ^ bits) for i in range(size)])


def spread(rows):
    across = swap(rows, "head", 2)
    beside = swap(rows, "head", 1)
    return [rows, beside, across, swap(across, "head", 1)]


def collect(keep, send_beside, keep_across, send_corner):
    corner = swap(send_corner, "head", 1)
    beside = swap(send_beside, "head", 1)
    across = swap((keep_across + corner.astype(f32)).astype(bf16), "head", 2)
    return [keep, beside, across]


def share(value):
    return [swap(value, "head", k) for k in (1, 2, 3)]


def tree_sum(value, axes):
    for axis in axes:
        bits = 1
        while bits < lax.axis_size(axis):
            value = value + swap(value, axis, bits)
            bits *= 2
    return value


def ring_order(count):
    return [*range(0, count, 2), *range(count - 1, 0, -2)]


OFFSETS = (0, -1, 1, -2, 2, -3, 3, -4)


def ring_steps(count):
    order = ring_order(count)
    forth = [(order[i], order[(i + 1) % count]) for i in range(count)]
    return forth, [(b, a) for a, b in forth]


def place_table(count):
    order = ring_order(count)
    at = {b: i for i, b in enumerate(order)}
    return np.array(
        [[order[(at[b] + o) % count] for o in OFFSETS] for b in range(count)], np.int32
    )


def fetch(own):
    count = lax.axis_size("blk")
    if count != 8:
        everything = lax.all_gather(own, "blk", axis=0, tiled=True)
        return jnp.split(everything, 8, axis=0)
    forth, back = ring_steps(count)
    left = right = own
    pieces = [own]
    for _ in range(3):
        left = lax.ppermute(left, "blk", forth)
        right = lax.ppermute(right, "blk", back)
        pieces += [left, right]
    return [*pieces, lax.ppermute(left, "blk", forth)]


def reduce_pieces(pieces):
    count = lax.axis_size("blk")
    if count != 8:
        everything = jnp.concatenate([p.astype(f32) for p in pieces], axis=0)
        return lax.psum_scatter(everything, "blk", scatter_dimension=0, tiled=True)
    forth, back = ring_steps(count)
    by = dict(zip(OFFSETS, pieces, strict=True))
    ahead, behind = by[-4], by[-3]

    def add(a, b):
        return (a.astype(f32) + b.astype(f32)).astype(bf16)

    for k in (3, 2, 1):
        ahead = add(lax.ppermute(ahead, "blk", forth), by[k])
        if k > 1:
            behind = add(lax.ppermute(behind, "blk", back), by[1 - k])
    ahead = lax.ppermute(ahead, "blk", forth)
    behind = lax.ppermute(behind, "blk", back)
    return by[0] + ahead.astype(f32) + behind.astype(f32)


def dot(left, right, over=(1, 0)):
    return lax.dot_general(
        left, right, (((over[0],), (over[1],)), ((), ())), preferred_element_type=f32
    )


def dot_t(left, right):
    return dot(left, right, (1, 1))


def t_dot(left, right):
    return dot(left, right, (0, 0))


def norm_rows(values, gain):
    return values * lax.rsqrt(jnp.mean(values * values, axis=-1, keepdims=True) + EPS) * gain


def norm_back(values, gain, grad):
    inverse = lax.rsqrt(jnp.mean(values * values, axis=-1, keepdims=True) + EPS)
    unit = values * inverse
    weighted = grad * gain
    along = jnp.mean(weighted * unit, axis=-1, keepdims=True)
    return inverse * (weighted - unit * along), grad * unit


def gelu_both(values):
    root = math.sqrt(2.0 / math.pi)
    square = values * values
    bent = jnp.tanh(root * values * (1.0 + 0.044715 * square))
    half = 0.5 * (1.0 + bent)
    slope = half + 0.5 * values * (1.0 - bent * bent) * root * (1.0 + 3 * 0.044715 * square)
    return values * half, slope


def heads_in(width):
    return [slice(at, at + HDIM) for at in range(0, width, HDIM)]


def assemble(info, pieces, targets):
    rows = pieces[0].shape[0]
    for t, piece in enumerate(pieces):
        at = pl.ds(pl.multiple_of(info[PLACES + t] * rows, 16), rows)
        column = 0
        for target in targets:
            target[at, :] = piece[:, column : column + target.shape[1]]
            column += target.shape[1]


def hand_out(info, sources, pieces):
    rows = pieces[0].shape[0]
    for t, piece in enumerate(pieces):
        at = pl.ds(pl.multiple_of(info[PLACES + t] * rows, 16), rows)
        column = 0
        for source in sources:
            piece[:, column : column + source.shape[1]] = source[at, :].astype(piece.dtype)
            column += source.shape[1]


def token_rows(refs):
    return jnp.concatenate([r[0] for r in refs], axis=0)


def emit(partial, outs):
    part = outs[0].shape[1]
    for r, out in enumerate(outs):
        out[0] = partial[r * part : (r + 1) * part].astype(out.dtype)


def slots_used(info, b, part, slot):
    column = lax.broadcasted_iota(jnp.int32, (1, slot), 1)
    position = (lax.div(column, part) ^ info[HEAD]) * part + lax.rem(column, part)
    return position < info[LENGTHS + b]


def call(body, info, stepped, fixed, out_stepped, out_fixed, scratch=(), flops=0, steps=1):
    def by_step(shape):
        return pl.BlockSpec((1, *shape[1:]), lambda b: (b,) + (0,) * (len(shape) - 1))

    def whole(shape):
        return pl.BlockSpec(shape, lambda b: (0,) * len(shape))

    counts = [len(stepped), len(fixed), len(out_stepped), len(out_fixed), len(scratch)]
    stops = np.cumsum(counts)

    def split(info_ref, *refs):
        body(info_ref, *(refs[e - c : e] for c, e in zip(counts, stops, strict=True)))

    arrays = [*stepped, *fixed, *out_stepped, *out_fixed]
    moved = sum(math.prod(a.shape) * a.dtype.itemsize for a in arrays)
    return pl.pallas_call(
        split,
        grid=(steps,),
        in_specs=[
            pl.BlockSpec(memory_space=pltpu.SMEM),
            *(by_step(a.shape) for a in stepped),
            *(whole(a.shape) for a in fixed),
        ],
        out_specs=[
            *(by_step(a.shape) for a in out_stepped),
            *(whole(a.shape) for a in out_fixed),
        ],
        out_shape=[*out_stepped, *out_fixed],
        scratch_shapes=list(scratch),
        compiler_params=pltpu.CompilerParams(
            dimension_semantics=("arbitrary",), vmem_limit_bytes=48 * 1024 * 1024
        ),
        cost_estimate=pl.CostEstimate(
            flops=int(flops), bytes_accessed=int(moved), transcendentals=0
        ),
    )(info, *stepped, *fixed)


def like(shape, dtype):
    return jax.ShapeDtypeStruct(tuple(shape), dtype)


def by_rows(fn, info, stepped, fixed, dtypes, gain=False):
    steps, _, width = stepped[0].shape

    def body(info_ref, ins, whole, outs, sums, _):
        results = fn(*(r[0].astype(f32) for r in ins), *(r[...] for r in whole))
        for out, value in zip(outs, results, strict=False):
            out[0] = value.astype(out.dtype)
        for total in sums:

            @pl.when(pl.program_id(0) == 0)
            def _():
                total[...] = jnp.zeros_like(total)

            total[...] += jnp.sum(results[-1], axis=0, keepdims=True)

    return call(
        body,
        info,
        stepped,
        fixed,
        [like(stepped[0].shape, d) for d in dtypes],
        [like((1, width), f32)] * gain,
        flops=10 * math.prod(stepped[0].shape),
        steps=steps,
    )


def partial_rows(blocks, part, width):
    return [like((blocks, part, width), d) for d in (f32, bf16, f32, bf16)]


def piece_shapes(rows, columns):
    return [like((rows, columns), f32), *[like((rows, columns), bf16)] * 7]


def encoder_attention(info, normed, pieces):
    blocks, part, width = normed[0].shape
    slot = part * len(normed)
    size = pieces[0].shape[1] // 4
    count = size // HDIM

    def body(info, rows, pieces, outs, weights, _):
        qkv, probs, context = outs[:3]
        w_in, w_out = weights
        b = pl.program_id(0)

        @pl.when(b == 0)
        def _():
            assemble(info, pieces, weights)

        qkv[0] = dot(token_rows(rows), w_in[...]).astype(bf16)
        allowed = slots_used(info, b, part, slot)
        for k, at in enumerate(heads_in(size)):
            query, keys, vals = (qkv[0, :, j * size + at.start : j * size + at.stop] for j in range(3))
            scores = jnp.where(allowed, dot_t(query, keys) * SCALE, masked_score)
            spread_out = jnp.exp(scores - jnp.max(scores, axis=-1, keepdims=True))
            weight = (spread_out / jnp.sum(spread_out, axis=-1, keepdims=True)).astype(bf16)
            probs[0, k] = weight
            context[0, :, at] = dot(weight, vals).astype(bf16)
        emit(dot_t(context[0], w_out[...]), outs[3:])

    return call(
        body,
        info,
        normed,
        pieces,
        [
            like((blocks, slot, 3 * size), bf16),
            like((blocks, count, slot, slot), bf16),
            like((blocks, slot, size), bf16),
            *partial_rows(blocks, part, width),
        ],
        [like((width, 3 * size), bf16), like((width, size), bf16)],
        flops=2 * blocks * slot * (width * size * 4 + 8 * slot * size),
        steps=blocks,
    )


def encoder_attention_back(info, grads, normed, qkv, probs, context, w_in, w_out, gains):
    blocks, part, width = normed[0].shape
    slot = part * len(normed)
    size = w_out.shape[1]

    def body(info, stepped, fixed, outs, ends, scratch):
        grad_refs, normed_refs = stepped[:4], stepped[4:8]
        qkv, probs, context = stepped[8:]
        w_in, w_out, gains = fixed
        pieces, gain_out = ends[:-1], ends[-1]
        total_in, total_out, moved = scratch
        b = pl.program_id(0)

        @pl.when(b == 0)
        def _():
            total_in[...] = jnp.zeros_like(total_in)
            total_out[...] = jnp.zeros_like(total_out)
            gain_out[...] = jnp.zeros_like(gain_out)

        grad = token_rows(grad_refs)
        rows = token_rows(normed_refs)
        dcontext = dot(grad, w_out[...]).astype(bf16)
        for k, at in enumerate(heads_in(size)):
            query, keys, vals = (qkv[0, :, j * size + at.start : j * size + at.stop] for j in range(3))
            weight = probs[0, k]
            dprobs = dot_t(dcontext[:, at], vals)
            wide = weight.astype(f32)
            dscores = wide * (dprobs - jnp.sum(wide * dprobs, axis=-1, keepdims=True))
            dscores = dscores.astype(bf16)
            terms = (
                dot(dscores, keys) * SCALE,
                t_dot(dscores, query) * SCALE,
                t_dot(weight, dcontext[:, at]),
            )
            for j, term in enumerate(terms):
                moved[:, j * size + at.start : j * size + at.stop] = term.astype(bf16)
        partial = dot_t(moved[...], w_in[...])
        emit(partial, outs)
        gain_out[...] += jnp.sum(partial * rows.astype(f32), axis=0, keepdims=True) / gains[0:1, :]
        total_in[...] += t_dot(rows, moved[...])
        total_out[...] += t_dot(grad, context[0])

        @pl.when(b == blocks - 1)
        def _():
            hand_out(info, (total_in, total_out), pieces)

    results = call(
        body,
        info,
        [*grads, *normed, qkv, probs, context],
        [w_in, w_out, gains],
        partial_rows(blocks, part, width),
        [*piece_shapes(width // 8, 4 * size), like((1, width), f32)],
        [
            pltpu.VMEM((width, 3 * size), f32),
            pltpu.VMEM((width, size), f32),
            pltpu.VMEM((slot, 3 * size), bf16),
        ],
        flops=2 * blocks * slot * (width * size * 8 + 20 * slot * size),
        steps=blocks,
    )
    return results[:4], results[4:12], results[12]


def encoder_ffn(info, normed, inner_pieces, outer_pieces):
    blocks, part, width = normed[0].shape
    slot = part * len(normed)
    hidden = inner_pieces[0].shape[1]

    def body(info, rows, pieces, outs, weights, _):
        active, slope = outs[:2]
        w_inner, w_outer = weights

        @pl.when(pl.program_id(0) == 0)
        def _():
            assemble(info, pieces[:8], (w_inner,))
            assemble(info, pieces[8:], (w_outer,))

        value, bend = gelu_both(dot(token_rows(rows), w_inner[...]))
        active[0] = value.astype(bf16)
        slope[0] = bend.astype(bf16)
        emit(dot_t(active[0], w_outer[...]), outs[2:])

    return call(
        body,
        info,
        normed,
        [*inner_pieces, *outer_pieces],
        [*[like((blocks, slot, hidden), bf16)] * 2, *partial_rows(blocks, part, width)],
        [like((width, hidden), bf16)] * 2,
        flops=4 * blocks * slot * width * hidden,
        steps=blocks,
    )


def encoder_ffn_back(info, grads, slope, w_inner, w_outer):
    blocks, part, width = grads[0].shape
    slot = part * len(grads)
    hidden = w_inner.shape[1]

    def body(info, stepped, weights, outs, ends, _):
        dinner = outs[0]
        w_inner, w_outer = weights
        back = dot(token_rows(stepped[:4]), w_outer[...])
        dinner[0] = (back * stepped[4][0].astype(f32)).astype(bf16)
        emit(dot_t(dinner[0], w_inner[...]), outs[1:])

    return call(
        body,
        info,
        [*grads, slope],
        [w_inner, w_outer],
        [like((blocks, slot, hidden), bf16), *partial_rows(blocks, part, width)],
        [],
        flops=4 * blocks * slot * width * hidden,
        steps=blocks,
    )


def weight_grads(info, left, right):
    blocks, part, width = left[0].shape
    columns = right.shape[2]

    def body(info, stepped, _, outs, pieces, scratch):
        total = scratch[0]
        b = pl.program_id(0)

        @pl.when(b == 0)
        def _():
            total[...] = jnp.zeros_like(total)

        total[...] += t_dot(token_rows(stepped[:4]), stepped[4][0])

        @pl.when(b == blocks - 1)
        def _():
            hand_out(info, (total,), pieces)

    return call(
        body,
        info,
        [*left, right],
        [],
        [],
        piece_shapes(width // 8, columns),
        [pltpu.VMEM((width, columns), f32)],
        flops=2 * blocks * part * 4 * width * columns,
        steps=blocks,
    )


def cross_forward(info, states, pieces, queries, own_question, count_pass):
    blocks, part, width = states[0].shape
    slot = part * len(states)
    size = queries.shape[1]
    rows_dec = queries.shape[0]

    def body(info, rows, fixed, outs, ends, scratch):
        pieces, queries, question = fixed[:8], fixed[8], fixed[9]
        stats, weight = ends
        held = scratch[0]
        b = pl.program_id(0)

        @pl.when(b == 0)
        def _():
            assemble(info, pieces, (weight,))

        made = dot(token_rows(rows), weight[...]).astype(bf16)
        outs[0][0] = made
        held[pl.ds(pl.multiple_of(b * slot, slot), slot), :] = made

        @pl.when(b == blocks - 1)
        def _():
            allowed = jnp.concatenate(
                [
                    slots_used(info, k, part, slot) & (question[...] == k // count_pass)
                    for k in range(blocks)
                ],
                axis=1,
            )
            lane = lax.broadcasted_iota(jnp.int32, (rows_dec, HDIM), 1)
            for k, at in enumerate(heads_in(size)):
                scores = dot_t(queries[:, at], held[:, at]) * SCALE
                scores = jnp.where(allowed, scores, masked_score)
                top = jnp.max(scores, axis=-1, keepdims=True)
                spread_out = jnp.exp(scores - top)
                total = jnp.sum(spread_out, axis=-1, keepdims=True)
                vals = held[:, size + at.start : size + at.stop]
                stats[:, k * LANES : k * LANES + HDIM] = dot(spread_out.astype(bf16), vals)
                stats[:, k * LANES + HDIM : (k + 1) * LANES] = jnp.where(lane == 0, top, total)

    return call(
        body,
        info,
        states,
        [*pieces, queries, own_question],
        [like((blocks, slot, 2 * size), bf16)],
        [like((rows_dec, size // HDIM * LANES), f32), like((width, 2 * size), bf16)],
        [pltpu.VMEM((blocks * slot, 2 * size), bf16)],
        flops=4 * blocks * slot * width * size,
        steps=blocks,
    )


def merge(info, own, other, bits):
    def body(info, _, ins, __, outs, ___):
        mine, yours = ins[0][...], ins[1][...]
        later = (info[BLK] & bits) != 0
        first, second = jnp.where(later, yours, mine), jnp.where(later, mine, yours)
        lane = lax.broadcasted_iota(jnp.int32, (first.shape[0], HDIM), 1)
        for at in range(0, first.shape[1], LANES):
            pairs = [(v[:, at + HDIM : at + HDIM + 1], v[:, at + HDIM + 1 : at + HDIM + 2]) for v in (first, second)]
            top = jnp.maximum(pairs[0][0], pairs[1][0])
            by_first, by_second = jnp.exp(pairs[0][0] - top), jnp.exp(pairs[1][0] - top)
            total = pairs[0][1] * by_first + pairs[1][1] * by_second
            outs[0][:, at : at + HDIM] = (
                first[:, at : at + HDIM] * by_first + second[:, at : at + HDIM] * by_second
            )
            outs[0][:, at + HDIM : at + LANES] = jnp.where(lane == 0, top, total)

    return call(body, info, [], [own, other], [], [like(own.shape, f32)])[0]


def cross_out(info, stats, w_output):
    rows, columns = stats.shape
    size = columns // LANES * HDIM
    width = w_output.shape[0]

    def body(info, _, ins, __, outs, scratch):
        stats, w_output = ins
        out, log_total, context, own, sent = outs
        log_total[...] = jnp.zeros_like(log_total)
        for k, at in enumerate(heads_in(size)):
            base = k * LANES
            top = stats[:, base + HDIM : base + HDIM + 1]
            total = stats[:, base + HDIM + 1 : base + HDIM + 2]
            out[:, at] = stats[:, base : base + HDIM] / total
            log_total[:, k : k + 1] = top + jnp.log(total)
        context[...] = out[...].astype(bf16)
        own[...] = dot_t(context[...], w_output[...])
        sent[...] = own[...].astype(bf16)

    return call(
        body,
        info,
        [],
        [stats, w_output],
        [],
        [
            like((rows, size), f32),
            like((rows, LANES), f32),
            like((rows, size), bf16),
            like((rows, width), f32),
            like((rows, width), bf16),
        ],
        flops=2 * rows * size * width,
    )


def cross_back(info, key_vals, inputs, own_question, count_pass, slot, part):
    cotangent, after_cross, terms, gains, w_output, out, log_total, queries, weight = inputs
    blocks = key_vals.shape[0]
    rows_dec, width = after_cross.shape
    size = queries.shape[1]

    def body(info, stepped, fixed, outs, ends, scratch):
        cotangent, after_cross, own, r1, r2, r3, gains, w_output, out, log_total, queries, weight, question = fixed
        key_vals = stepped[0]
        dkey_vals = outs[0]
        dcross, dcross_low, gain_out, dqueries = ends
        dcontext, row_terms = scratch
        b = pl.program_id(0)

        @pl.when(b == 0)
        def _():
            total = own[...] + r1[...].astype(f32) + r2[...].astype(f32) + r3[...].astype(f32)
            back, gain_rows = norm_back(after_cross[...], gains[2:3, :], total)
            dcross[...] = cotangent[...].astype(f32) + back
            dcross_low[...] = dcross[...].astype(bf16)
            gain_out[...] = gain_rows
            dcontext[...] = dot(dcross_low[...], w_output[...]).astype(bf16)
            for k, at in enumerate(heads_in(size)):
                row_terms[:, k : k + 1] = jnp.sum(
                    dcontext[:, at].astype(f32) * out[:, at], axis=-1, keepdims=True
                )
            dqueries[...] = jnp.zeros_like(dqueries)

        allowed = slots_used(info, b, part, slot) & (question[...] == lax.div(b, count_pass))
        for k, at in enumerate(heads_in(size)):
            keys, vals = key_vals[0, :, at], key_vals[0, :, size + at.start : size + at.stop]
            scores = dot_t(queries[:, at], keys) * SCALE
            scores = jnp.where(allowed, scores, masked_score)
            probs = jnp.exp(scores - log_total[:, k : k + 1])
            dprobs = dot_t(dcontext[:, at], vals)
            dscores = (probs * (dprobs - row_terms[:, k : k + 1])).astype(bf16)
            dqueries[:, at] += dot(dscores, keys) * SCALE
            dkey_vals[0, :, at] = (t_dot(dscores, queries[:, at]) * SCALE).astype(bf16)
            dkey_vals[0, :, size + at.start : size + at.stop] = t_dot(
                probs.astype(bf16), dcontext[:, at]
            ).astype(bf16)
        emit(dot_t(dkey_vals[0], weight[...]), outs[1:])

    return call(
        body,
        info,
        [key_vals],
        [cotangent, after_cross, *terms, gains, w_output, out, log_total, queries, weight, own_question],
        [like(key_vals.shape, bf16), *partial_rows(blocks, part, width)],
        [
            like((rows_dec, width), f32),
            like((rows_dec, width), bf16),
            like((rows_dec, width), f32),
            like((rows_dec, size), f32),
        ],
        [pltpu.VMEM((rows_dec, size), bf16), pltpu.VMEM((rows_dec, LANES), f32)],
        flops=4 * blocks * slot * width * size,
        steps=blocks,
    )


def summed(refs):
    total = refs[0][...]
    for ref in refs[1:]:
        total = total + ref[...].astype(f32)
    return total


def decoder_self(info, rows, gains, pieces, order):
    count, width = rows.shape
    size = pieces[0].shape[1] // 4

    def body(info, _, ins, __, outs, scratch):
        rows, gains, order_q, order_k = ins[:4]
        normed, qkv, probs, context, own, sent, w_in, w_out = outs
        assemble(info, ins[4:], (w_in, w_out))
        normed[...] = norm_rows(rows[...].astype(f32), gains[0:1, :]).astype(bf16)
        qkv[...] = dot(normed[...], w_in[...]).astype(bf16)
        query_at, key_at = order_q[...], order_k[...]
        same = lax.div(query_at, 1000) == lax.div(key_at, 1000)
        allowed = same & (key_at <= query_at) & (key_at >= 0) & (query_at >= 0)
        for k, at in enumerate(heads_in(size)):
            query, keys, vals = (qkv[:, j * size + at.start : j * size + at.stop] for j in range(3))
            scores = jnp.where(allowed, dot_t(query, keys) * SCALE, masked_score)
            spread_out = jnp.exp(scores - jnp.max(scores, axis=-1, keepdims=True))
            weight = spread_out / jnp.sum(spread_out, axis=-1, keepdims=True)
            weight = jnp.where(allowed, weight, 0.0)
            probs[k] = weight
            context[:, at] = dot(weight.astype(bf16), vals).astype(bf16)
        own[...] = dot_t(context[...], w_out[...])
        sent[...] = own[...].astype(bf16)

    return call(
        body,
        info,
        [],
        [rows, gains, *order, *pieces],
        [],
        [
            like((count, width), bf16),
            like((count, 3 * size), bf16),
            like((size // HDIM, count, count), f32),
            like((count, size), bf16),
            like((count, width), f32),
            like((count, width), bf16),
            like((width, 3 * size), bf16),
            like((width, size), bf16),
        ],
        flops=2 * count * width * size * 4,
    )


def decoder_queries(info, rows, terms, cotangent, gains, cross_pieces, inner_pieces, outer_pieces):
    count, width = rows.shape
    size = cross_pieces[0].shape[1] // 2
    hidden = inner_pieces[0].shape[1]

    def body(info, _, ins, __, outs, scratch):
        rows, own, r1, r2, r3, cotangent, gains = ins[:7]
        after_self, normed, queries, back, w_query, w_output, w_inner, w_outer = outs
        assemble(info, ins[7:15], (w_query, w_output))
        assemble(info, ins[15:23], (w_inner,))
        assemble(info, ins[23:31], (w_outer,))
        after_self[...] = rows[...].astype(f32) + summed((own, r1, r2, r3))
        normed[...] = norm_rows(after_self[...], gains[1:2, :]).astype(bf16)
        queries[...] = dot(normed[...], w_query[...]).astype(bf16)
        back[...] = dot(cotangent[...], w_outer[...])

    return call(
        body,
        info,
        [],
        [rows, *terms, cotangent, gains, *cross_pieces, *inner_pieces, *outer_pieces],
        [],
        [
            like((count, width), f32),
            like((count, width), bf16),
            like((count, size), bf16),
            like((count, hidden), f32),
            like((width, size), bf16),
            like((width, size), bf16),
            like((width, hidden), bf16),
            like((width, hidden), bf16),
        ],
        flops=2 * count * width * (size + hidden),
    )


def decoder_ffn(info, after_self, terms, back, gains, w_inner):
    count, width = after_self.shape
    hidden = w_inner.shape[1]

    def body(info, _, ins, __, outs, scratch):
        after_self, own, r1, r2, r3, back, gains, w_inner = ins
        after_cross, normed, active, dinner, own_back, sent_back = outs
        after_cross[...] = after_self[...] + summed((own, r1, r2, r3))
        normed[...] = norm_rows(after_cross[...], gains[2:3, :]).astype(bf16)
        value, slope = gelu_both(dot(normed[...], w_inner[...]))
        active[...] = value.astype(bf16)
        dinner[...] = (slope * back[...]).astype(bf16)
        own_back[...] = dot_t(dinner[...], w_inner[...])
        sent_back[...] = own_back[...].astype(bf16)

    return call(
        body,
        info,
        [],
        [after_self, *terms, back, gains, w_inner],
        [],
        [
            like((count, width), f32),
            like((count, width), bf16),
            like((count, hidden), bf16),
            like((count, hidden), bf16),
            like((count, width), f32),
            like((count, width), bf16),
        ],
        flops=4 * count * width * hidden,
    )


def project_rows(info, rows, weight):
    count, width = rows.shape[0], weight.shape[0]

    def body(info, _, ins, __, outs, scratch):
        outs[0][...] = dot_t(ins[0][...].astype(bf16), ins[1][...])
        outs[1][...] = outs[0][...].astype(bf16)

    return call(
        body,
        info,
        [],
        [rows, weight],
        [],
        [like((count, width), f32), like((count, width), bf16)],
        flops=2 * count * width * weight.shape[1],
    )


def decoder_self_back(info, dcross, after_self, terms, gains, w_out, w_in, qkv, probs):
    count, width = after_self.shape
    size = w_out.shape[1]

    def body(info, _, ins, __, outs, scratch):
        dcross, after_self, own, r1, r2, r3, gains, w_out, w_in, qkv, probs = ins
        dself, dself_low, gain_rows, moved, own_back, sent_back = outs
        back, gain_rows[...] = norm_back(after_self[...], gains[1:2, :], summed((own, r1, r2, r3)))
        dself[...] = dcross[...] + back
        dself_low[...] = dself[...].astype(bf16)
        dcontext = dot(dself_low[...], w_out[...]).astype(bf16)
        for k, at in enumerate(heads_in(size)):
            query, keys, vals = (qkv[:, j * size + at.start : j * size + at.stop] for j in range(3))
            weight = probs[k]
            dprobs = dot_t(dcontext[:, at], vals)
            dscores = weight * (dprobs - jnp.sum(weight * dprobs, axis=-1, keepdims=True))
            dscores = dscores.astype(bf16)
            found = (
                dot(dscores, keys) * SCALE,
                t_dot(dscores, query) * SCALE,
                t_dot(weight.astype(bf16), dcontext[:, at]),
            )
            for j, term in enumerate(found):
                moved[:, j * size + at.start : j * size + at.stop] = term.astype(bf16)
        own_back[...] = dot_t(moved[...], w_in[...])
        sent_back[...] = own_back[...].astype(bf16)

    return call(
        body,
        info,
        [],
        [dcross, after_self, *terms, gains, w_out, w_in, qkv, probs],
        [],
        [
            like((count, width), f32),
            like((count, width), bf16),
            like((count, width), f32),
            like((count, 3 * size), bf16),
            like((count, width), f32),
            like((count, width), bf16),
        ],
        flops=2 * count * width * size * 4,
    )


def decoder_ends(info, rows, dself, terms, gains, after_cross, out_terms):
    count, width = dself.shape

    def body(info, _, ins, __, outs, scratch):
        rows, dself, after_cross, gains = ins[:4]
        grad, gain_rows, states = outs
        back, gain_rows[...] = norm_back(rows[...].astype(f32), gains[0:1, :], summed(ins[4:8]))
        grad[...] = dself[...] + back
        states[...] = (after_cross[...] + summed(ins[8:12])).astype(bf16)

    return call(
        body,
        info,
        [],
        [rows, dself, after_cross, gains, *terms, *out_terms],
        [],
        [like((count, width), f32), like((count, width), f32), like((count, width), bf16)],
    )


def decoder_weight_grads(info, own, pairs_in, pairs_out):
    count, width = pairs_in[0][0].shape

    def body(info, _, ins, __, outs, scratch):
        row = lax.broadcasted_iota(jnp.int32, (own, width), 0) + info[BLK] * own
        column = lax.broadcasted_iota(jnp.int32, (own, width), 1)
        pick = jnp.where(row == column, 1.0, 0.0).astype(bf16)
        n = 2 * len(pairs_in)
        for k, out in enumerate(outs):
            left, right = ins[2 * k][...], ins[2 * k + 1][...]
            if 2 * k < n:
                out[...] = t_dot(dot_t(left, pick).astype(bf16), right)
            else:
                out[...] = t_dot(left, dot_t(right, pick).astype(bf16))

    outs = [like((own, r.shape[1]), f32) for _, r in pairs_in]
    outs += [like((l.shape[1], own), f32) for l, _ in pairs_out]
    flat = [a for pair in (*pairs_in, *pairs_out) for a in pair]
    return call(body, info, [], flat, [], outs, flops=2 * count * own * width * 10)


def shards(
    encoder_input,
    passage_lengths,
    decoder_input,
    encoder_query,
    encoder_key,
    encoder_value,
    encoder_output,
    encoder_inner,
    encoder_outer,
    decoder_query,
    decoder_key,
    decoder_value,
    decoder_output,
    cross_query,
    cross_key,
    cross_value,
    cross_output,
    decoder_inner,
    decoder_outer,
    encoder_gains,
    decoder_gains,
    encoder_cotangent,
    decoder_cotangent,
):
    head, blk = lax.axis_index("head"), lax.axis_index("blk")
    blk_count, head_count = lax.axis_size("blk"), lax.axis_size("head")
    count_q, count_pass, part, width = encoder_input.shape
    blocks = count_q * count_pass
    slot = part * head_count
    own = width // blk_count
    if blk_count == 8:
        places = jnp.asarray(place_table(8))[blk]
    else:
        places = jnp.arange(8, dtype=jnp.int32)
    info = jnp.concatenate(
        [places, jnp.stack([head, blk]).astype(jnp.int32), passage_lengths.reshape(blocks)]
    )

    attention_pieces = fetch(
        jnp.concatenate([encoder_query, encoder_key, encoder_value, encoder_output.T], axis=1)
    )
    inner_pieces = fetch(encoder_inner)
    outer_pieces = fetch(encoder_outer.T)
    self_pieces = fetch(
        jnp.concatenate([decoder_query, decoder_key, decoder_value, decoder_output.T], axis=1)
    )
    cross_kv_pieces = fetch(jnp.concatenate([cross_key, cross_value], axis=1))
    cross_qo_pieces = fetch(jnp.concatenate([cross_query, cross_output.T], axis=1))
    dec_inner_pieces = fetch(decoder_inner)
    dec_outer_pieces = fetch(decoder_outer.T)

    inputs = encoder_input.reshape(blocks, part, width)
    first = by_rows(
        lambda x, g: (norm_rows(x, g[0:1]),), info, [inputs], [encoder_gains], [bf16]
    )[0]
    first_all = spread(first)
    qkv, probs, context, *partial, w_in, w_out = encoder_attention(
        info, first_all, attention_pieces
    )

    def enter_ffn(x, a, b, c, g):
        hidden = x + a + b + c
        return hidden, norm_rows(hidden, g[1:2])

    hidden, second = by_rows(
        enter_ffn, info, [inputs, *collect(*partial)], [encoder_gains], [f32, bf16]
    )
    second_all = spread(second)
    active, slope, *partial, w_inner, w_outer = encoder_ffn(
        info, second_all, inner_pieces, outer_pieces
    )
    states = by_rows(
        lambda h, a, b, c: (h + a + b + c,), info, [hidden, *collect(*partial)], [], [bf16]
    )[0]
    states_all = spread(states)

    dec_part = decoder_input.shape[1]
    dec_own = count_q * dec_part
    dec_rows = dec_own * head_count
    filled = -(-dec_rows // 16) * 16
    pair = jnp.stack([decoder_input, decoder_cotangent]).reshape(2, dec_own, width)
    parts = jnp.stack([pair, *share(pair)])
    parts = jnp.where(head & 1, parts[jnp.array([1, 0, 3, 2])], parts)
    parts = jnp.where(head & 2, parts[jnp.array([2, 3, 0, 1])], parts)
    both = parts.transpose(1, 0, 2, 3).reshape(2, dec_rows, width)
    both = jnp.pad(both, ((0, 0), (0, filled - dec_rows), (0, 0)))
    dec_in, cotangent = both[0], both[1]
    index = np.arange(filled)
    question = (index % dec_own) // dec_part
    position = index // dec_own * dec_part + index % dec_part
    order = np.where(index < dec_rows, question * 1000 + position, -1).astype(np.int32)
    order = (jnp.asarray(order[:, None]), jnp.asarray(order[None, :]))
    question = jnp.asarray(question[:, None].astype(np.int32))

    third, dec_qkv, dec_probs, dec_context, mine, sent, dec_w_in, dec_w_out = decoder_self(
        info, dec_in, decoder_gains, self_pieces, order
    )
    (
        after_self,
        fourth,
        queries,
        outer_back,
        w_cross_query,
        w_cross_output,
        w_dec_inner,
        w_dec_outer,
    ) = decoder_queries(
        info,
        dec_in,
        [mine, *share(sent)],
        cotangent,
        decoder_gains,
        cross_qo_pieces,
        dec_inner_pieces,
        dec_outer_pieces,
    )

    key_vals, stats, w_cross = cross_forward(
        info, states_all, cross_kv_pieces, queries, question, count_pass
    )
    bits = 1
    while bits < blk_count:
        stats = merge(info, stats, swap(stats, "blk", bits), bits)
        bits *= 2
    out, log_total, cross_context, mine, sent = cross_out(info, stats, w_cross_output)
    after_cross, fifth, dec_active, dec_dinner, mine, sent = decoder_ffn(
        info, after_self, [mine, *share(sent)], outer_back, decoder_gains, w_dec_inner
    )
    dkey_vals, *rest = cross_back(
        info,
        key_vals,
        (
            cotangent,
            after_cross,
            [mine, *share(sent)],
            decoder_gains,
            w_cross_output,
            out,
            log_total,
            queries,
            w_cross,
        ),
        question,
        count_pass,
        slot,
        part,
    )
    partial, (dcross, dcross_low, gain_four, dqueries) = rest[:4], rest[4:]

    def enter_back(cot, a, b, c):
        grad = cot + a + b + c
        return grad, grad

    dstates, dstates_low = by_rows(
        enter_back,
        info,
        [encoder_cotangent.reshape(blocks, part, width), *collect(*partial)],
        [],
        [f32, bf16],
    )
    dstates_all = spread(dstates_low)
    grad_cross = reduce_pieces(weight_grads(info, states_all, dkey_vals))
    dinner, *partial = encoder_ffn_back(info, dstates_all, slope, w_inner, w_outer)

    def middle_back(dy, h, a, b, c, g):
        back, gain_rows = norm_back(h, g[1:2], a + b + c)
        grad = dy + back
        return grad, grad, gain_rows

    dhidden, dhidden_low, gain_one = by_rows(
        middle_back,
        info,
        [dstates, hidden, *collect(*partial)],
        [encoder_gains],
        [f32, bf16],
        gain=True,
    )
    dhidden_all = spread(dhidden_low)
    grad_outer = reduce_pieces(weight_grads(info, dstates_all, active))
    grad_inner = reduce_pieces(weight_grads(info, second_all, dinner))

    partial, pieces, gain_zero = encoder_attention_back(
        info, dhidden_all, first_all, qkv, probs, context, w_in, w_out, encoder_gains
    )

    def last_back(dh, x, a, b, c, g):
        return (dh + norm_back(x, g[0:1], a + b + c)[0],)

    input_grad = by_rows(
        last_back, info, [dhidden, inputs, *collect(*partial)], [encoder_gains], [f32]
    )[0]
    grad_attention = reduce_pieces(pieces)

    dqueries = tree_sum(dqueries, ("blk",)).astype(bf16)
    mine, sent = project_rows(info, dqueries, w_cross_query)
    dself, dself_low, gain_three, dself_qkv, own_back, sent_back = decoder_self_back(
        info,
        dcross,
        after_self,
        [mine, *share(sent)],
        decoder_gains,
        dec_w_out,
        dec_w_in,
        dec_qkv,
        dec_probs,
    )
    out_mine, out_sent = project_rows(info, dec_active, w_dec_outer)
    dec_grad, gain_two, dec_states = decoder_ends(
        info,
        dec_in,
        dself,
        [own_back, *share(sent_back)],
        decoder_gains,
        after_cross,
        [out_mine, *share(out_sent)],
    )
    (
        grad_dec_qkv,
        grad_cross_query,
        grad_dec_inner,
        grad_dec_output,
        grad_cross_output,
        grad_dec_outer,
    ) = decoder_weight_grads(
        info,
        own,
        [(third, dself_qkv), (fourth, dqueries), (fifth, dec_dinner)],
        [(dec_context, dself_low), (cross_context, dcross_low), (dec_active, cotangent)],
    )

    def own_rows(values):
        return lax.dynamic_slice_in_dim(values, head * dec_own, dec_own, 0)

    leading = (blk == 0).astype(f32)
    dec_gains = [
        jnp.sum(own_rows(g), axis=0, keepdims=True) * leading
        for g in (gain_two, gain_three, gain_four)
    ]
    gains = tree_sum(
        jnp.concatenate([gain_zero, gain_one, *dec_gains], axis=0), ("head", "blk")
    )

    def dec_shape(values):
        return own_rows(values).reshape(count_q, dec_part, width)

    size = encoder_query.shape[1]
    return (
        states.reshape(encoder_input.shape),
        dec_shape(dec_states),
        input_grad.reshape(encoder_input.shape),
        dec_shape(dec_grad),
        grad_attention[:, :size],
        grad_attention[:, size : 2 * size],
        grad_attention[:, 2 * size : 3 * size],
        grad_attention[:, 3 * size :].T,
        grad_inner,
        grad_outer.T,
        grad_dec_qkv[:, :size],
        grad_dec_qkv[:, size : 2 * size],
        grad_dec_qkv[:, 2 * size :],
        grad_dec_output,
        grad_cross_query,
        grad_cross[:, :size],
        grad_cross[:, size:],
        grad_cross_output,
        grad_dec_inner,
        grad_dec_outer,
        gains[:2],
        gains[2:],
    )


def solution(mesh):
    placed = (
        P(None, "blk", "head", None),
        P(None, "blk"),
        P(None, "head", None),
        P("blk", "head"),
        P("blk", "head"),
        P("blk", "head"),
        P("head", "blk"),
        P("blk", "head"),
        P("head", "blk"),
        P("blk", "head"),
        P("blk", "head"),
        P("blk", "head"),
        P("head", "blk"),
        P("blk", "head"),
        P("blk", "head"),
        P("blk", "head"),
        P("head", "blk"),
        P("blk", "head"),
        P("head", "blk"),
        P(),
        P(),
        P(None, "blk", "head", None),
        P(None, "head", None),
    )
    return jax.shard_map(
        shards,
        mesh=mesh,
        in_specs=placed,
        out_specs=(placed[0], placed[2], placed[0], placed[2], *placed[3:19], P(), P()),
        check_vma=False,
    )
```

time: 1680 us -> 421 us (0.25)
  waiting for transfers between devices: 790 us -> 119 us
  blocking collectives: 592 us -> 0 us
  starting transfers between devices: 1.95 us -> 126 us
  matrix products: 114 us -> 0 us
  Pallas kernels: 0 us -> 85.1 us
  other arithmetic: 65.5 us -> 21.1 us
  local copies, waits for them, and re-layouts: 88.4 us -> 64.4 us
    reduce_scatter x12 -> x0, waiting for transfers between devices: 585 us -> none  [the longest x3 115 us: rows_out(): return lax.psum_scatter(values, 'head', scatter_dimension=1, tiled=True)]
    all_gather x21 -> x0, blocking collectives: 513 us -> none  [the longest x3 92.1 us: joined(): everything = jax.tree.map(lambda part: lax.all_gather(part, axis), array)]
    ppermute x0 -> x146, starting transfers between devices: none -> 126 us  [the longest x62 36.4 us: swap(): return lax.ppermute(value, axis, [(i, i ^ bits) for i in range(size)])]
    ppermute x0 -> x146, waiting for transfers between devices: none -> 119 us  [the longest x62 72 us: swap(): return lax.ppermute(value, axis, [(i, i ^ bits) for i in range(size)])]
    dot_general x65 -> x0, matrix products: 112 us -> none  [the longest x16 34.5 us: project(): jnp.einsum('...k,kn->...n', left, weight, preferred_element_type=jnp.floa...]
    all_gather x9 -> x0, waiting for transfers between devices: 107 us -> none  [the longest x1 40 us: shards(): lax.all_gather(decoder_outer, 'blk', axis=1, tiled=True)]
    unnamed x33 -> x0, waiting for transfers between devices: 97.8 us -> none
    pallas_call x0 -> x27, Pallas kernels: none -> 85.1 us  [call(): pl.pallas_call(split, grid=(steps,), in_specs=[pl.BlockSpec(memory_space=...]
  transfers between devices with their start and end apart: 27 -> 146, of which waited for: 20 -> 51; matrix products, arithmetic and copies ran while one was open for 9% -> 9% of each run, Pallas kernels for 0% -> 12%
where the time goes in v1:
time: 421 us; the launch traced here: 419 us
  starting transfers between devices  126 us (30%)
  waiting for transfers between devices  119 us (28%)
  Pallas kernels  85.1 us (20%)
  local copies, waits for them, and re-layouts  64.4 us (15%)
  other arithmetic  21.1 us (5%)
    pallas_call x27, Pallas kernels, call(): pl.pallas_call(split, grid=(steps,), in_specs=[pl.BlockSpec(memory_space=...  85.1 us
    ppermute x62, waiting for transfers between devices, swap(): return lax.ppermute(value, axis, [(i, i ^ bits) for i in range(size)])  72 us
    unnamed x364, local copies, waits for them, and re-layouts  53.7 us
    ppermute x62, starting transfers between devices, swap(): return lax.ppermute(value, axis, [(i, i ^ bits) for i in range(size)])  36.4 us
    ppermute x24, starting transfers between devices, fetch(): right = lax.ppermute(right, 'blk', back)  28 us
    ppermute x24, starting transfers between devices, fetch(): left = lax.ppermute(left, 'blk', forth)  22.9 us
    ppermute x24, waiting for transfers between devices, fetch(): left = lax.ppermute(left, 'blk', forth)  14.3 us
    ppermute x8, starting transfers between devices, reduce_pieces(): behind = add(lax.ppermute(behind, 'blk', back), by[1 - k])  12.5 us
  transfers between devices with their start and end apart: 146, of which 51 were waited for; matrix products, arithmetic and copies ran while one was open for 9% of the time, Pallas kernels for 12%

profile of v1, /device:TPU:0, one launch (start us, length us, event | category | flops | bytes accessed | tf_op | source)
XLA Modules:
  0.0 418.7 jit_solution(4641266721667426608)
XLA Ops:
  5.0 3.0 collective-permute-start.1
  11.9 3.3 collective-permute-done.3.refs_5_
  30.6 7.5 %shard_map.445 = (bf16[4,256,576]{2,1,0:T(8,128)(2,1)}, bf16[4,3,256,256]{3,2,1,0:T(8,128)(2,1)}, bf16[4,256,192]{2,1,0:T(8,128)(2,1)S(1)}, f32[4,64,768]{2,1,0:...) custom-call(s32[14]{0:T(128)S(1)} %pad_add_fusion.info_ref, ...), custom_call_target="tpu_custom_call" | custom-call | flops 2013265920 | bytes 9437184 | tf_op jit(solution)/shard_map/pallas_call | solution.py:200
  42.0 10.0 %collective-permute-done.12.refs_3_ = bf16[4,64,768]{2,1,0:T(8,128)(2,1)S(1)} collective-permute-done((bf16[4,64,768]{2,1,0:T(8,128)(2,1)S(1)}, bf16[4,64,768]{2,1,0:T(8,128)(2,1)S(1)}, u32[]{:S(2)}, u32[]{:S(2)}) %collective-permute-start.12) | collective-permute-done | bytes 393248 | tf_op jit(solution)/shard_map/ppermute | solution.py:24
  96.6 7.8 %shard_map.447 = (bf16[4,256,768]{2,1,0:T(8,128)(2,1)}, bf16[4,256,768]{2,1,0:T(8,128)(2,1)}, f32[4,64,768]{2,1,0:T(8,128)S(1)}, bf16[4,64,768]{2,1,0:T(8,128)(2...) custom-call(s32[14]{0:T(128)S(1)} %pad_add_fusion.info_ref, ...), custom_call_target="tpu_custom_call" | custom-call | flops 2415919104 | bytes 11796480 | tf_op jit(solution)/shard_map/pallas_call | solution.py:200
  132.0 3.3 collective-permute-done.71.refs_25_
  192.6 3.8 shard_map.451
  199.5 3.0 collective-permute-done.77.refs_1_
  204.4 3.3 collective-permute-done.78.refs_1_
  209.8 4.9 %collective-permute-done.79.refs_1_ = f32[48,384]{1,0:T(8,128)S(1)} collective-permute-done((f32[48,384]{1,0:T(8,128)S(1)}, f32[48,384]{1,0:T(8,128)S(1)}, u32[]{:S(2)}, u32[]{:S(2)}) %collective-permute-start.79) | collective-permute-done | bytes 73760 | tf_op jit(solution)/shard_map/ppermute | solution.py:24
  239.0 7.6 %shard_map.457 = (bf16[4,256,384]{2,1,0:T(8,128)(2,1)S(1)}, f32[4,64,768]{2,1,0:T(8,128)S(1)}, bf16[4,64,768]{2,1,0:T(8,128)(2,1)}, f32[4,64,768]{2,1,0:T(8,128)...) custom-call(s32[14]{0:T(128)S(1)} %pad_add_fusion.info_ref, ...), custom_call_target="tpu_custom_call" | custom-call | flops 603979776 | bytes 5901504 | tf_op jit(solution)/shard_map/pallas_call | solution.py:200
  258.1 3.7 collective-permute-done.88
  279.1 7.9 %collective-permute-done.100.refs_3_ = bf16[4,64,768]{2,1,0:T(8,128)(2,1)} collective-permute-done((bf16[4,64,768]{2,1,0:T(8,128)(2,1)}, bf16[4,64,768]{2,1,0:T(8,128)(2,1)}, u32[]{:S(2)}, u32[]{:S(2)}) %collective-permute-start.100) | collective-permute-done | bytes 393248 | tf_op jit(solution)/shard_map/ppermute | solution.py:24
  287.1 3.2 shard_map.462
  298.2 6.5 %collective-permute-done.102.refs_2_ = bf16[4,64,768]{2,1,0:T(8,128)(2,1)S(1)} collective-permute-done((bf16[4,64,768]{2,1,0:T(8,128)(2,1)}, bf16[4,64,768]{2,1,0:T(8,128)(2,1)S(1)}, u32[]{:S(2)}, u32[]{:S(2)}) %collective-permute-start.102) | collective-permute-done | bytes 393248 | tf_op jit(solution)/shard_map/ppermute | solution.py:24
  311.0 3.8 shard_map.468
  315.2 5.9 %shard_map.463 = (bf16[4,256,768]{2,1,0:T(8,128)(2,1)}, f32[4,64,768]{2,1,0:T(8,128)S(1)}, bf16[4,64,768]{2,1,0:T(8,128)(2,1)S(1)}, f32[4,64,768]{2,1,0:T(8,128)S(1)}, bf16[4,64,768]{2,1,0:T(8,128)(2,1)S(1)}) custom-call(s32[14]{0:T(128)S(1)} %pad_add_fusion.info_ref, bf16[4,64,768]{2,1,0:T(8,128)(2,1)} %get-tuple-element.195.refs_0_, ...), custom_call_target="tpu_custom_call" | custom-call | flops 2415919104 | bytes 9437184 | tf_op jit(solution)/shard_map/pallas_call | solution.py:200
  325.2 3.0 shard_map.467
  336.6 5.6 %collective-permute-done.106.refs_4_ = bf16[4,64,768]{2,1,0:T(8,128)(2,1)S(1)} collective-permute-done((bf16[4,64,768]{2,1,0:T(8,128)(2,1)S(1)}, bf16[4,64,768]{2,1,0:T(8,128)(2,1)S(1)}, u32[]{:S(2)}, u32[]{:S(2)}) %collective-permute-start.106) | collective-permute-done | bytes 393248 | tf_op jit(solution)/shard_map/ppermute | solution.py:24
  348.4 5.8 %collective-permute-done.108.refs_2_ = bf16[4,64,768]{2,1,0:T(8,128)(2,1)S(1)} collective-permute-done((bf16[4,64,768]{2,1,0:T(8,128)(2,1)S(1)}, bf16[4,64,768]{2,1,0:T(8,128)(2,1)S(1)}, u32[]{:S(2)}, u32[]{:S(2)}) %collective-permute-start.108) | collective-permute-done | bytes 393248 | tf_op jit(solution)/shard_map/ppermute | solution.py:24
  357.7 12.9 %shard_map.465 = (f32[4,64,768]{2,1,0:T(8,128)}, bf16[4,64,768]{2,1,0:T(8,128)(2,1)}, f32[4,64,768]{2,1,0:T(8,128)}, bf16[4,64,768]{2,1,0:T(8,128)(2,1)S(1)}, f3...) custom-call(s32[14]{0:T(128)S(1)} %pad_add_fusion.info_ref, ...), custom_call_target="tpu_custom_call" | custom-call | flops 4429185024 | bytes 11166720 | tf_op jit(solution)/shard_map/pallas_call | solution.py:200
  395.6 2.9 collective-permute-done.114
  401.2 3.5 collective-permute-done.115
  411.5 4.6 %collective-permute-done.112.refs_4_ = bf16[4,64,768]{2,1,0:T(8,128)(2,1)S(1)} collective-permute-done((bf16[4,64,768]{2,1,0:T(8,128)(2,1)}, bf16[4,64,768]{2,1,0:T(8,128)(2,1)S(1)}, u32[]{:S(2)}, u32[]{:S(2)}) %collective-permute-start.112) | collective-permute-done | bytes 393248 | tf_op jit(solution)/shard_map/ppermute | solution.py:24
  (736 shorter events, 289.4 us)
Async XLA Ops:
  53.2 15.1 %collective-permute-start.14 = (bf16[4,64,768]{2,1,0:T(8,128)(2,1)S(1)}, bf16[4,64,768]{2,1,0:T(8,128)(2,1)S(1)}, u32[]{:S(2)}, u32[]{:S(2)}) collective-permute-start(bf16[4,64,768]{2,1,0:T(8,128)(2,1)S(1)} %get-tuple-element.151.refs_0_), channel_id=1, source_target_pairs={{0,2},{1,3},{2,0},{3,1},{4,6},{5,7},{6,4},{7,5},{8,10},{9,11},{10,... | collective-permute-start | bytes 1179656 | tf_op jit(solution)/shard_map/ppermute | solution.py:24
  68.4 18.2 %collective-permute-start.13 = (bf16[4,64,768]{2,1,0:T(8,128)(2,1)S(1)}, bf16[4,64,768]{2,1,0:T(8,128)(2,1)S(1)}, u32[]{:S(2)}, u32[]{:S(2)}) collective-permute-start(bf16[4,64,768]{2,1,0:T(8,128)(2,1)S(1)} %get-tuple-element.151.refs_0_), channel_id=1, source_target_pairs={{0,1},{1,0},{2,3},{3,2},{4,5},{5,4},{6,7},{7,6},{8,9},{9,8},{10,11... | collective-permute-start | bytes 1179656 | tf_op jit(solution)/shard_map/ppermute | solution.py:24
  68.4 18.2 %collective-permute-start.15 = (bf16[4,64,768]{2,1,0:T(8,128)(2,1)S(1)}, bf16[4,64,768]{2,1,0:T(8,128)(2,1)S(1)}, u32[]{:S(2)}, u32[]{:S(2)}) collective-permute-start(bf16[4,64,768]{2,1,0:T(8,128)(2,1)S(1)} %collective-permute-done.14.refs_2_), channel_id=1, source_target_pairs={{0,1},{1,0},{2,3},{3,2},{4,5},{5,4},{6,7},{7,6},{8,9},{9,8},{10,11... | collective-permute-start | bytes 1179656 | tf_op jit(solution)/shard_map/ppermute | solution.py:24
  106.7 17.4 %collective-permute-start.31 = (bf16[4,64,768]{2,1,0:T(8,128)(2,1)}, bf16[4,64,768]{2,1,0:T(8,128)(2,1)}, u32[]{:S(2)}, u32[]{:S(2)}) collective-permute-start(bf16[4,64,768]{2,1,0:T(8,128)(2,1)} %get-tuple-element.155), channel_id=1, source_target_pairs={{0,1},{1,0},{2,3},{3,2},{4,5},{5,4},{6,7},{7,6},{8,9},{9,8},{10,11... | collective-permute-start | bytes 1179656 | tf_op jit(solution)/shard_map/ppermute | solution.py:24
  127.4 17.8 %collective-permute-start.30 = (bf16[4,64,768]{2,1,0:T(8,128)(2,1)S(1)}, bf16[4,64,768]{2,1,0:T(8,128)(2,1)S(1)}, u32[]{:S(2)}, u32[]{:S(2)}) collective-permute-start(bf16[4,64,768]{2,1,0:T(8,128)(2,1)S(1)} %copy-done.119), channel_id=1, source_target_pairs={{0,1},{1,0},{2,3},{3,2},{4,5},{5,4},{6,7},{7,6},{8,9},{9,8},{10,11... | collective-permute-start | bytes 1179656 | tf_op jit(solution)/shard_map/ppermute | solution.py:24
  127.4 18.5 %collective-permute-start.32 = (bf16[4,64,768]{2,1,0:T(8,128)(2,1)S(1)}, bf16[4,64,768]{2,1,0:T(8,128)(2,1)S(1)}, u32[]{:S(2)}, u32[]{:S(2)}) collective-permute-start(bf16[4,64,768]{2,1,0:T(8,128)(2,1)S(1)} %add_convert_fusion.3), channel_id=1, source_target_pairs={{0,2},{1,3},{2,0},{3,1},{4,6},{5,7},{6,4},{7,5},{8,10},{9,11},{10,... | collective-permute-start | bytes 1179656 | tf_op jit(solution)/shard_map/ppermute | solution.py:24
  156.1 15.0 %collective-permute-start.37 = (bf16[4,64,768]{2,1,0:T(8,128)(2,1)}, bf16[4,64,768]{2,1,0:T(8,128)(2,1)S(1)}, u32[]{:S(2)}, u32[]{:S(2)}) collective-permute-start(bf16[4,64,768]{2,1,0:T(8,128)(2,1)} %shard_map.448.refs_0_), channel_id=1, source_target_pairs={{0,2},{1,3},{2,0},{3,1},{4,6},{5,7},{6,4},{7,5},{8,10},{9,11},{10,... | collective-permute-start | bytes 1179656 | tf_op jit(solution)/shard_map/ppermute | solution.py:24
  171.1 21.5 %collective-permute-start.36 = (bf16[4,64,768]{2,1,0:T(8,128)(2,1)S(1)}, bf16[4,64,768]{2,1,0:T(8,128)(2,1)S(1)}, u32[]{:S(2)}, u32[]{:S(2)}) collective-permute-start(bf16[4,64,768]{2,1,0:T(8,128)(2,1)S(1)} %copy-done.2), channel_id=1, source_target_pairs={{0,1},{1,0},{2,3},{3,2},{4,5},{5,4},{6,7},{7,6},{8,9},{9,8},{10,11... | collective-permute-start | bytes 1179656 | tf_op jit(solution)/shard_map/ppermute | solution.py:24
  171.1 21.5 %collective-permute-start.38 = (bf16[4,64,768]{2,1,0:T(8,128)(2,1)S(1)}, bf16[4,64,768]{2,1,0:T(8,128)(2,1)S(1)}, u32[]{:S(2)}, u32[]{:S(2)}) collective-permute-start(bf16[4,64,768]{2,1,0:T(8,128)(2,1)S(1)} %collective-permute-done.37.refs_2_), channel_id=1, source_target_pairs={{0,1},{1,0},{2,3},{3,2},{4,5},{5,4},{6,7},{7,6},{8,9},{9,8},{10,11... | collective-permute-start | bytes 1179656 | tf_op jit(solution)/shard_map/ppermute | solution.py:24
  232.7 58.5 %collective-permute-start.97 = (bf16[48,768]{1,0:T(8,128)(2,1)}, bf16[48,768]{1,0:T(8,128)(2,1)}, u32[]{:S(2)}, u32[]{:S(2)}) collective-permute-start(bf16[48,768]{1,0:T(8,128)(2,1)} %get-tuple-element.188), channel_id=1, source_target_pairs={{0,3},{1,2},{2,1},{3,0},{4,7},{5,6},{6,5},{7,4},{8,11},{9,10},{10,... | collective-permute-start | bytes 221192 | tf_op jit(solution)/shard_map/ppermute | solution.py:24
  251.6 22.1 %collective-permute-start.99 = (bf16[4,64,768]{2,1,0:T(8,128)(2,1)S(1)}, bf16[4,64,768]{2,1,0:T(8,128)(2,1)S(1)}, u32[]{:S(2)}, u32[]{:S(2)}) collective-permute-start(bf16[4,64,768]{2,1,0:T(8,128)(2,1)S(1)} %get-tuple-element.193), channel_id=1, source_target_pairs={{0,1},{1,0},{2,3},{3,2},{4,5},{5,4},{6,7},{7,6},{8,9},{9,8},{10,11... | collective-permute-start | bytes 1179656 | tf_op jit(solution)/shard_map/ppermute | solution.py:24
  267.2 25.1 %collective-permute-start.96 = (bf16[48,768]{1,0:T(8,128)(2,1)}, bf16[48,768]{1,0:T(8,128)(2,1)}, u32[]{:S(2)}, u32[]{:S(2)}) collective-permute-start(bf16[48,768]{1,0:T(8,128)(2,1)} %get-tuple-element.188), channel_id=1, source_target_pairs={{0,2},{1,3},{2,0},{3,1},{4,6},{5,7},{6,4},{7,5},{8,10},{9,11},{10,... | collective-permute-start | bytes 221192 | tf_op jit(solution)/shard_map/ppermute | solution.py:24
  268.5 24.5 %collective-permute-start.136 = (bf16[96,384]{1,0:T(8,128)(2,1)}, bf16[96,384]{1,0:T(8,128)(2,1)}, u32[]{:S(2)}, u32[]{:S(2)}) collective-permute-start(bf16[96,384]{1,0:T(8,128)(2,1)} %add_convert_fusion.23), channel_id=1, source_target_pairs={{0,8},{8,16},{16,24},{24,28},{28,20},{20,12},{12,4},{4,0},{1,9},{9... | collective-permute-start | bytes 221192 | tf_op jit(solution)/shard_map/ppermute | solution.py:102
  278.9 15.9 %collective-permute-start.95 = (bf16[48,768]{1,0:T(8,128)(2,1)}, bf16[48,768]{1,0:T(8,128)(2,1)S(1)}, u32[]{:S(2)}, u32[]{:S(2)}) collective-permute-start(bf16[48,768]{1,0:T(8,128)(2,1)} %get-tuple-element.188), channel_id=1, source_target_pairs={{0,1},{1,0},{2,3},{3,2},{4,5},{5,4},{6,7},{7,6},{8,9},{9,8},{10,11... | collective-permute-start | bytes 221192 | tf_op jit(solution)/shard_map/ppermute | solution.py:24
  314.8 15.5 %collective-permute-start.127 = (bf16[96,768]{1,0:T(8,128)(2,1)S(1)}, bf16[96,768]{1,0:T(8,128)(2,1)S(1)}, u32[]{:S(2)}, u32[]{:S(2)}) collective-permute-start(bf16[96,768]{1,0:T(8,128)(2,1)S(1)} %get-tuple-element.234), channel_id=1, source_target_pairs={{0,8},{8,16},{16,24},{24,28},{28,20},{20,12},{12,4},{4,0},{1,9},{9... | collective-permute-start | bytes 442376 | tf_op jit(solution)/shard_map/ppermute | solution.py:102
  328.6 16.4 %collective-permute-start.124 = (bf16[96,768]{1,0:T(8,128)(2,1)S(1)}, bf16[96,768]{1,0:T(8,128)(2,1)S(1)}, u32[]{:S(2)}, u32[]{:S(2)}) collective-permute-start(bf16[96,768]{1,0:T(8,128)(2,1)S(1)} %get-tuple-element.229), channel_id=1, source_target_pairs={{8,0},{16,8},{24,16},{28,24},{20,28},{12,20},{4,12},{0,4},{9,1},{1... | collective-permute-start | bytes 442376 | tf_op jit(solution)/shard_map/ppermute | solution.py:104
  330.4 17.0 %collective-permute-start.128 = (bf16[96,768]{1,0:T(8,128)(2,1)S(1)}, bf16[96,768]{1,0:T(8,128)(2,1)S(1)}, u32[]{:S(2)}, u32[]{:S(2)}) collective-permute-start(bf16[96,768]{1,0:T(8,128)(2,1)S(1)} %add_convert_fusion.9), channel_id=1, source_target_pairs={{0,8},{8,16},{16,24},{24,28},{28,20},{20,12},{12,4},{4,0},{1,9},{9... | collective-permute-start | bytes 442376 | tf_op jit(solution)/shard_map/ppermute | solution.py:102
  336.2 18.7 %collective-permute-start.121 = (bf16[96,768]{1,0:T(8,128)(2,1)S(1)}, bf16[96,768]{1,0:T(8,128)(2,1)S(1)}, u32[]{:S(2)}, u32[]{:S(2)}) collective-permute-start(bf16[96,768]{1,0:T(8,128)(2,1)S(1)} %add_convert_fusion.14), channel_id=1, source_target_pairs={{0,8},{8,16},{16,24},{24,28},{28,20},{20,12},{12,4},{4,0},{1,9},{9... | collective-permute-start | bytes 442376 | tf_op jit(solution)/shard_map/ppermute | solution.py:102
  345.7 26.5 %collective-permute-start.125 = (bf16[96,768]{1,0:T(8,128)(2,1)}, bf16[96,768]{1,0:T(8,128)(2,1)}, u32[]{:S(2)}, u32[]{:S(2)}) collective-permute-start(bf16[96,768]{1,0:T(8,128)(2,1)} %add_convert_fusion.11), channel_id=1, source_target_pairs={{8,0},{16,8},{24,16},{28,24},{20,28},{12,20},{4,12},{0,4},{9,1},{1... | collective-permute-start | bytes 442376 | tf_op jit(solution)/shard_map/ppermute | solution.py:104
  348.1 28.1 %collective-permute-start.129 = (bf16[96,768]{1,0:T(8,128)(2,1)}, bf16[96,768]{1,0:T(8,128)(2,1)}, u32[]{:S(2)}, u32[]{:S(2)}) collective-permute-start(bf16[96,768]{1,0:T(8,128)(2,1)} %add_convert_fusion.8), channel_id=1, source_target_pairs={{0,8},{8,16},{16,24},{24,28},{28,20},{20,12},{12,4},{4,0},{1,9},{9... | collective-permute-start | bytes 442376 | tf_op jit(solution)/shard_map/ppermute | solution.py:102
  354.9 29.0 %collective-permute-start.133 = (bf16[96,768]{1,0:T(8,128)(2,1)}, bf16[96,768]{1,0:T(8,128)(2,1)}, u32[]{:S(2)}, u32[]{:S(2)}) collective-permute-start(bf16[96,768]{1,0:T(8,128)(2,1)} %add_convert_fusion.5), channel_id=1, source_target_pairs={{8,0},{16,8},{24,16},{28,24},{20,28},{12,20},{4,12},{0,4},{9,1},{1... | collective-permute-start | bytes 442376 | tf_op jit(solution)/shard_map/ppermute | solution.py:106
  357.4 23.2 %collective-permute-start.122 = (bf16[96,768]{1,0:T(8,128)(2,1)}, bf16[96,768]{1,0:T(8,128)(2,1)}, u32[]{:S(2)}, u32[]{:S(2)}) collective-permute-start(bf16[96,768]{1,0:T(8,128)(2,1)} %add_convert_fusion.13), channel_id=1, source_target_pairs={{0,8},{8,16},{16,24},{24,28},{28,20},{20,12},{12,4},{4,0},{1,9},{9... | collective-permute-start | bytes 442376 | tf_op jit(solution)/shard_map/ppermute | solution.py:102
  390.4 21.1 %collective-permute-start.110 = (bf16[4,64,768]{2,1,0:T(8,128)(2,1)}, bf16[4,64,768]{2,1,0:T(8,128)(2,1)S(1)}, u32[]{:S(2)}, u32[]{:S(2)}) collective-permute-start(bf16[4,64,768]{2,1,0:T(8,128)(2,1)} %get-tuple-element.211), channel_id=1, source_target_pairs={{0,1},{1,0},{2,3},{3,2},{4,5},{5,4},{6,7},{7,6},{8,9},{9,8},{10,11... | collective-permute-start | bytes 1179656 | tf_op jit(solution)/shard_map/ppermute | solution.py:24
  390.4 16.9 %collective-permute-start.111 = (bf16[4,64,768]{2,1,0:T(8,128)(2,1)S(1)}, bf16[4,64,768]{2,1,0:T(8,128)(2,1)S(1)}, u32[]{:S(2)}, u32[]{:S(2)}) collective-permute-start(bf16[4,64,768]{2,1,0:T(8,128)(2,1)S(1)} %copy-done.117), channel_id=1, source_target_pairs={{0,1},{1,0},{2,3},{3,2},{4,5},{5,4},{6,7},{7,6},{8,9},{9,8},{10,11... | collective-permute-start | bytes 1179656 | tf_op jit(solution)/shard_map/ppermute | solution.py:24
  (299 other events, 2566.0 us)

commit v2 on v1

--- a/solution.py
+++ b/solution.py
@@ -12,6 +12,8 @@
 SCALE = HDIM ** (-0.5)
 LANES = 128
 EPS = 1e-06
+VMEM_LIMIT = 40 * 1024 * 1024
+LARGE = 1 << 18
 masked_score = -1000000000.0
 f32 = jnp.float32
 bf16 = jnp.bfloat16
@@ -24,30 +26,12 @@
     return lax.ppermute(value, axis, [(i, i ^ bits) for i in range(size)])
 
 
-def spread(rows):
-    across = swap(rows, "head", 2)
-    beside = swap(rows, "head", 1)
-    return [rows, beside, across, swap(across, "head", 1)]
-
-
-def collect(keep, send_beside, keep_across, send_corner):
-    corner = swap(send_corner, "head", 1)
-    beside = swap(send_beside, "head", 1)
-    across = swap((keep_across + corner.astype(f32)).astype(bf16), "head", 2)
-    return [keep, beside, across]
+def sync(*values):
+    return lax.optimization_barrier(values)
 
 
 def share(value):
     return [swap(value, "head", k) for k in (1, 2, 3)]
-
-
-def tree_sum(value, axes):
-    for axis in axes:
-        bits = 1
-        while bits < lax.axis_size(axis):
-            value = value + swap(value, axis, bits)
-            bits *= 2
-    return value
 
 
 def ring_order(count):
@@ -71,40 +55,56 @@
     )
 
 
-def fetch(own):
+def gather_rows(own):
+    return lax.all_gather(own, "blk", axis=0, tiled=True)
+
+
+def fetch_start(own):
+    if lax.axis_size("blk") == 8:
+        return {0: own}
+    return dict(zip(OFFSETS, jnp.split(gather_rows(own), 8, axis=0), strict=True))
+
+
+def fetch_step(pieces, *offsets):
     count = lax.axis_size("blk")
     if count != 8:
-        everything = lax.all_gather(own, "blk", axis=0, tiled=True)
-        return jnp.split(everything, 8, axis=0)
+        return pieces
     forth, back = ring_steps(count)
-    left = right = own
-    pieces = [own]
-    for _ in range(3):
-        left = lax.ppermute(left, "blk", forth)
-        right = lax.ppermute(right, "blk", back)
-        pieces += [left, right]
-    return [*pieces, lax.ppermute(left, "blk", forth)]
-
-
-def reduce_pieces(pieces):
+    more = {
+        k: lax.ppermute(pieces[k + 1 if k < 0 else k - 1], "blk", forth if k < 0 else back)
+        for k in offsets
+    }
+    return {**pieces, **more}
+
+
+def in_turn(pieces):
+    return [pieces[k] if k in pieces else pieces[-k] for k in OFFSETS]
+
+
+def add_low(a, b):
+    return (a.astype(f32) + b.astype(f32)).astype(bf16)
+
+
+def reduce_step(pieces, moving, step):
     count = lax.axis_size("blk")
     if count != 8:
-        everything = jnp.concatenate([p.astype(f32) for p in pieces], axis=0)
-        return lax.psum_scatter(everything, "blk", scatter_dimension=0, tiled=True)
+        return []
     forth, back = ring_steps(count)
     by = dict(zip(OFFSETS, pieces, strict=True))
-    ahead, behind = by[-4], by[-3]
-
-    def add(a, b):
-        return (a.astype(f32) + b.astype(f32)).astype(bf16)
-
-    for k in (3, 2, 1):
-        ahead = add(lax.ppermute(ahead, "blk", forth), by[k])
-        if k > 1:
-            behind = add(lax.ppermute(behind, "blk", back), by[1 - k])
+    if step == 1:
+        ahead, behind = by[-4], by[-3]
+    else:
+        ahead = add_low(moving[0], by[5 - step])
+        behind = add_low(moving[1], by[step - 4]) if step < 4 else None
     ahead = lax.ppermute(ahead, "blk", forth)
-    behind = lax.ppermute(behind, "blk", back)
-    return by[0] + ahead.astype(f32) + behind.astype(f32)
+    return [ahead, moving[1] if behind is None else lax.ppermute(behind, "blk", back)]
+
+
+def reduce_terms(pieces, moving):
+    if lax.axis_size("blk") != 8:
+        everything = jnp.concatenate([p.astype(f32) for p in pieces], axis=0)
+        return [lax.psum_scatter(everything, "blk", scatter_dimension=0, tiled=True)]
+    return [pieces[0], *moving]
 
 
 def dot(left, right, over=(1, 0)):
@@ -146,14 +146,24 @@
     return [slice(at, at + HDIM) for at in range(0, width, HDIM)]
 
 
-def assemble(info, pieces, targets):
+def assemble(info, pieces, targets, signals):
     rows = pieces[0].shape[0]
+    copies = []
     for t, piece in enumerate(pieces):
         at = pl.ds(pl.multiple_of(info[PLACES + t] * rows, 16), rows)
         column = 0
-        for target in targets:
-            target[at, :] = piece[:, column : column + target.shape[1]]
-            column += target.shape[1]
+        for k, target in enumerate(targets):
+            wide = target.shape[1]
+            copies.append(
+                pltpu.make_async_copy(
+                    piece.at[:, column : column + wide], target.at[at, :], signals.at[k, t]
+                )
+            )
+            column += wide
+    for copy in copies:
+        copy.start()
+    for copy in copies:
+        copy.wait()
 
 
 def hand_out(info, sources, pieces):
@@ -182,18 +192,33 @@
     return position < info[LENGTHS + b]
 
 
-def call(body, info, stepped, fixed, out_stepped, out_fixed, scratch=(), flops=0, steps=1):
+def call(
+    body, info, stepped, fixed, out_stepped, out_fixed, scratch=(), flops=0, steps=1, near=False
+):
     def by_step(shape):
         return pl.BlockSpec((1, *shape[1:]), lambda b: (b,) + (0,) * (len(shape) - 1))
 
-    def whole(shape):
-        return pl.BlockSpec(shape, lambda b: (0,) * len(shape))
+    def whole(a):
+        if isinstance(a, Far):
+            return pl.BlockSpec(memory_space=pltpu.HBM)
+        index = (0, a.index) if type(a) is Columns else (0,) * len(a.shape)
+        return pl.BlockSpec(a.shape, lambda b: index)
 
     counts = [len(stepped), len(fixed), len(out_stepped), len(out_fixed), len(scratch)]
     stops = np.cumsum(counts)
 
     def split(info_ref, *refs):
         body(info_ref, *(refs[e - c : e] for c, e in zip(counts, stops, strict=True)))
+
+    def large(a):
+        return not near and math.prod(a.shape) * a.dtype.itemsize >= LARGE
+
+    def given(a):
+        array = a.array if isinstance(a, (Columns, Far)) else a
+        return pltpu.with_memory_space_constraint(array, pltpu.HBM) if large(a) else array
+
+    def made(a):
+        return a.array if isinstance(a, Near) else pltpu.HBM(a.shape, a.dtype) if large(a) else a
 
     arrays = [*stepped, *fixed, *out_stepped, *out_fixed]
     moved = sum(math.prod(a.shape) * a.dtype.itemsize for a in arrays)
@@ -203,21 +228,37 @@
         in_specs=[
             pl.BlockSpec(memory_space=pltpu.SMEM),
             *(by_step(a.shape) for a in stepped),
-            *(whole(a.shape) for a in fixed),
+            *(whole(a) for a in fixed),
         ],
         out_specs=[
             *(by_step(a.shape) for a in out_stepped),
-            *(whole(a.shape) for a in out_fixed),
+            *(whole(a) for a in out_fixed),
         ],
-        out_shape=[*out_stepped, *out_fixed],
+        out_shape=[made(a) for a in (*out_stepped, *out_fixed)],
         scratch_shapes=list(scratch),
         compiler_params=pltpu.CompilerParams(
-            dimension_semantics=("arbitrary",), vmem_limit_bytes=48 * 1024 * 1024
+            dimension_semantics=("arbitrary",), vmem_limit_bytes=VMEM_LIMIT
         ),
         cost_estimate=pl.CostEstimate(
             flops=int(flops), bytes_accessed=int(moved), transcendentals=0
         ),
-    )(info, *stepped, *fixed)
+    )(info, *(given(a) for a in (*stepped, *fixed)))
+
+
+class Columns:
+    def __init__(self, array, width, index):
+        self.array, self.index, self.dtype = array, index, array.dtype
+        self.shape = (array.shape[0], width)
+
+
+class Near(Columns):
+    def __init__(self, array):
+        self.array, self.shape, self.dtype = array, array.shape, array.dtype
+
+
+class Far:
+    def __init__(self, array):
+        self.array, self.shape, self.dtype = array, array.shape, array.dtype
 
 
 def like(shape, dtype):
@@ -248,15 +289,16 @@
         [like((1, width), f32)] * gain,
         flops=10 * math.prod(stepped[0].shape),
         steps=steps,
+        near=True,
     )
 
 
 def partial_rows(blocks, part, width):
-    return [like((blocks, part, width), d) for d in (f32, bf16, f32, bf16)]
+    return [Near(like((blocks, part, width), d)) for d in (f32, bf16, f32, bf16)]
 
 
 def piece_shapes(rows, columns):
-    return [like((rows, columns), f32), *[like((rows, columns), bf16)] * 7]
+    return [like((rows, columns), f32), *[Near(like((rows, columns), bf16))] * 7]
 
 
 def encoder_attention(info, normed, pieces):
@@ -265,14 +307,17 @@
     size = pieces[0].shape[1] // 4
     count = size // HDIM
 
-    def body(info, rows, pieces, outs, weights, _):
+    def body(info, rows, pieces, outs, weights, scratch):
         qkv, probs, context = outs[:3]
         w_in, w_out = weights
+        together, signals = scratch
         b = pl.program_id(0)
 
         @pl.when(b == 0)
         def _():
-            assemble(info, pieces, weights)
+            assemble(info, pieces, (together,), signals)
+            w_in[...] = together[:, : 3 * size]
+            w_out[...] = together[:, 3 * size :]
 
         qkv[0] = dot(token_rows(rows), w_in[...]).astype(bf16)
         allowed = slots_used(info, b, part, slot)
@@ -289,7 +334,7 @@
         body,
         info,
         normed,
-        pieces,
+        [Far(p) for p in pieces],
         [
             like((blocks, slot, 3 * size), bf16),
             like((blocks, count, slot, slot), bf16),
@@ -297,6 +342,7 @@
             *partial_rows(blocks, part, width),
         ],
         [like((width, 3 * size), bf16), like((width, size), bf16)],
+        [pltpu.VMEM((width, 4 * size), bf16), pltpu.SemaphoreType.DMA((1, len(pieces)))],
         flops=2 * blocks * slot * (width * size * 4 + 8 * slot * size),
         steps=blocks,
     )
@@ -366,19 +412,18 @@
     return results[:4], results[4:12], results[12]
 
 
-def encoder_ffn(info, normed, inner_pieces, outer_pieces):
+def encoder_ffn(info, normed, pieces):
     blocks, part, width = normed[0].shape
     slot = part * len(normed)
-    hidden = inner_pieces[0].shape[1]
-
-    def body(info, rows, pieces, outs, weights, _):
+    hidden = pieces[0].shape[1] // 2
+
+    def body(info, rows, pieces, outs, weights, scratch):
         active, slope = outs[:2]
         w_inner, w_outer = weights
 
         @pl.when(pl.program_id(0) == 0)
         def _():
-            assemble(info, pieces[:8], (w_inner,))
-            assemble(info, pieces[8:], (w_outer,))
+            assemble(info, pieces, weights, scratch[0])
 
         value, bend = gelu_both(dot(token_rows(rows), w_inner[...]))
         active[0] = value.astype(bf16)
@@ -389,9 +434,10 @@
         body,
         info,
         normed,
-        [*inner_pieces, *outer_pieces],
+        [Far(p) for p in pieces],
         [*[like((blocks, slot, hidden), bf16)] * 2, *partial_rows(blocks, part, width)],
         [like((width, hidden), bf16)] * 2,
+        [pltpu.SemaphoreType.DMA((2, len(pieces)))],
         flops=4 * blocks * slot * width * hidden,
         steps=blocks,
     )
@@ -421,53 +467,73 @@
     )
 
 
-def weight_grads(info, left, right):
-    blocks, part, width = left[0].shape
-    columns = right.shape[2]
-
-    def body(info, stepped, _, outs, pieces, scratch):
-        total = scratch[0]
+def weight_grads(info, pairs, more=()):
+    blocks, part, width = pairs[0][0][0].shape
+    widths = [right.shape[2] for _, right in pairs]
+    total_width = sum(widths) + sum(m.shape[1] for m in more)
+
+    def body(info, stepped, more, _, ends, totals):
         b = pl.program_id(0)
-
-        @pl.when(b == 0)
-        def _():
-            total[...] = jnp.zeros_like(total)
-
-        total[...] += t_dot(token_rows(stepped[:4]), stepped[4][0])
-
-        @pl.when(b == blocks - 1)
-        def _():
-            hand_out(info, (total,), pieces)
-
-    return call(
-        body,
-        info,
-        [*left, right],
-        [],
-        [],
-        piece_shapes(width // 8, columns),
-        [pltpu.VMEM((width, columns), f32)],
-        flops=2 * blocks * part * 4 * width * columns,
+        totals = totals if more else ends
+        for k, total in enumerate(totals):
+            left, right = stepped[5 * k : 5 * k + 4], stepped[5 * k + 4]
+            found = t_dot(token_rows(left), right[0])
+
+            @pl.when(b == 0)
+            def _():
+                total[...] = found
+
+            @pl.when(b > 0)
+            def _():
+                total[...] += found
+
+        if more:
+
+            @pl.when(b == blocks - 1)
+            def _():
+                hand_out(info, (*more, *totals), ends)
+
+    return call(
+        body,
+        info,
+        [a for left, right in pairs for a in (*left, right)],
+        more,
+        [],
+        piece_shapes(width // 8, total_width)
+        if more
+        else [like((width, w), f32) for w in widths],
+        [pltpu.VMEM((width, w), f32) for w in widths] if more else [],
+        flops=2 * blocks * part * 4 * width * total_width,
         steps=blocks,
     )
 
 
-def cross_forward(info, states, pieces, queries, own_question, count_pass):
+def finish(info, terms, widths, turned):
+    rows = terms[0].shape[0]
+    shapes = [(w, rows) if t else (rows, w) for w, t in zip(widths, turned, strict=True)]
+
+    def body(info, _, ins, __, outs, ___):
+        total = summed(ins)
+        column = 0
+        for out, wide, turn in zip(outs, widths, turned, strict=True):
+            found = total[:, column : column + wide]
+            out[...] = found.T if turn else found
+            column += wide
+
+    return call(body, info, [], terms, [], [like(s, f32) for s in shapes])
+
+
+def cross_forward(info, states, weight, queries, own_question, count_pass):
     blocks, part, width = states[0].shape
     slot = part * len(states)
     size = queries.shape[1]
     rows_dec = queries.shape[0]
 
     def body(info, rows, fixed, outs, ends, scratch):
-        pieces, queries, question = fixed[:8], fixed[8], fixed[9]
-        stats, weight = ends
+        weight, queries, question = fixed
+        stats = ends[0]
         held = scratch[0]
         b = pl.program_id(0)
-
-        @pl.when(b == 0)
-        def _():
-            assemble(info, pieces, (weight,))
-
         made = dot(token_rows(rows), weight[...]).astype(bf16)
         outs[0][0] = made
         held[pl.ds(pl.multiple_of(b * slot, slot), slot), :] = made
@@ -496,9 +562,9 @@
         body,
         info,
         states,
-        [*pieces, queries, own_question],
+        [weight, queries, own_question],
         [like((blocks, slot, 2 * size), bf16)],
-        [like((rows_dec, size // HDIM * LANES), f32), like((width, 2 * size), bf16)],
+        [like((rows_dec, size // HDIM * LANES), f32)],
         [pltpu.VMEM((blocks * slot, 2 * size), bf16)],
         flops=4 * blocks * slot * width * size,
         steps=blocks,
@@ -628,16 +694,15 @@
     return total
 
 
-def decoder_self(info, rows, gains, pieces, order):
+def decoder_self(info, rows, gains, weight, order):
     count, width = rows.shape
-    size = pieces[0].shape[1] // 4
+    size = weight.shape[1] // 4
 
     def body(info, _, ins, __, outs, scratch):
-        rows, gains, order_q, order_k = ins[:4]
-        normed, qkv, probs, context, own, sent, w_in, w_out = outs
-        assemble(info, ins[4:], (w_in, w_out))
+        rows, gains, order_q, order_k, weight = ins
+        normed, qkv, probs, context, own, sent = outs
         normed[...] = norm_rows(rows[...].astype(f32), gains[0:1, :]).astype(bf16)
-        qkv[...] = dot(normed[...], w_in[...]).astype(bf16)
+        qkv[...] = dot(normed[...], weight[:, : 3 * size]).astype(bf16)
         query_at, key_at = order_q[...], order_k[...]
         same = lax.div(query_at, 1000) == lax.div(key_at, 1000)
         allowed = same & (key_at <= query_at) & (key_at >= 0) & (query_at >= 0)
@@ -645,18 +710,18 @@
             query, keys, vals = (qkv[:, j * size + at.start : j * size + at.stop] for j in range(3))
             scores = jnp.where(allowed, dot_t(query, keys) * SCALE, masked_score)
             spread_out = jnp.exp(scores - jnp.max(scores, axis=-1, keepdims=True))
-            weight = spread_out / jnp.sum(spread_out, axis=-1, keepdims=True)
-            weight = jnp.where(allowed, weight, 0.0)
-            probs[k] = weight
-            context[:, at] = dot(weight.astype(bf16), vals).astype(bf16)
-        own[...] = dot_t(context[...], w_out[...])
+            share_out = spread_out / jnp.sum(spread_out, axis=-1, keepdims=True)
+            share_out = jnp.where(allowed, share_out, 0.0)
+            probs[k] = share_out
+            context[:, at] = dot(share_out.astype(bf16), vals).astype(bf16)
+        own[...] = dot_t(context[...], weight[:, 3 * size :])
         sent[...] = own[...].astype(bf16)
 
     return call(
         body,
         info,
         [],
-        [rows, gains, *order, *pieces],
+        [rows, gains, *order, weight],
         [],
         [
             like((count, width), bf16),
@@ -665,46 +730,59 @@
             like((count, size), bf16),
             like((count, width), f32),
             like((count, width), bf16),
-            like((width, 3 * size), bf16),
-            like((width, size), bf16),
         ],
         flops=2 * count * width * size * 4,
     )
 
 
-def decoder_queries(info, rows, terms, cotangent, gains, cross_pieces, inner_pieces, outer_pieces):
+def decoder_queries(info, rows, terms, gains, weight):
     count, width = rows.shape
-    size = cross_pieces[0].shape[1] // 2
-    hidden = inner_pieces[0].shape[1]
+    size = weight.shape[1] // 2
 
     def body(info, _, ins, __, outs, scratch):
-        rows, own, r1, r2, r3, cotangent, gains = ins[:7]
-        after_self, normed, queries, back, w_query, w_output, w_inner, w_outer = outs
-        assemble(info, ins[7:15], (w_query, w_output))
-        assemble(info, ins[15:23], (w_inner,))
-        assemble(info, ins[23:31], (w_outer,))
+        rows, own, r1, r2, r3, gains, weight = ins
+        after_self, normed, queries, w_query, w_output = outs
+        w_query[...] = weight[:, :size]
+        w_output[...] = weight[:, size:]
         after_self[...] = rows[...].astype(f32) + summed((own, r1, r2, r3))
         normed[...] = norm_rows(after_self[...], gains[1:2, :]).astype(bf16)
         queries[...] = dot(normed[...], w_query[...]).astype(bf16)
-        back[...] = dot(cotangent[...], w_outer[...])
-
-    return call(
-        body,
-        info,
-        [],
-        [rows, *terms, cotangent, gains, *cross_pieces, *inner_pieces, *outer_pieces],
+
+    return call(
+        body,
+        info,
+        [],
+        [rows, *terms, gains, weight],
         [],
         [
             like((count, width), f32),
             like((count, width), bf16),
             like((count, size), bf16),
-            like((count, hidden), f32),
             like((width, size), bf16),
             like((width, size), bf16),
-            like((width, hidden), bf16),
-            like((width, hidden), bf16),
         ],
-        flops=2 * count * width * (size + hidden),
+        flops=2 * count * width * size,
+    )
+
+
+def decoder_back(info, cotangent, pieces):
+    count, width = cotangent.shape
+    hidden = pieces[0].shape[1] // 2
+
+    def body(info, _, ins, __, outs, scratch):
+        w_inner, w_outer, back = outs
+        assemble(info, ins[1:], (w_inner, w_outer), scratch[0])
+        back[...] = dot(ins[0][...], w_outer[...])
+
+    return call(
+        body,
+        info,
+        [],
+        [cotangent, *(Far(p) for p in pieces)],
+        [],
+        [*[like((width, hidden), bf16)] * 2, like((count, hidden), f32)],
+        [pltpu.SemaphoreType.DMA((2, len(pieces)))],
+        flops=2 * count * width * hidden,
     )
 
 
@@ -759,66 +837,70 @@
     )
 
 
-def decoder_self_back(info, dcross, after_self, terms, gains, w_out, w_in, qkv, probs):
+def decoder_self_back(
+    info, dcross, after_self, terms, gains, weight, qkv, probs, active, w_outer
+):
     count, width = after_self.shape
-    size = w_out.shape[1]
+    size = weight.shape[1] // 4
 
     def body(info, _, ins, __, outs, scratch):
-        dcross, after_self, own, r1, r2, r3, gains, w_out, w_in, qkv, probs = ins
+        dcross, after_self, own, r1, r2, r3, gains, weight, qkv, probs, active, w_outer = ins
         dself, dself_low, gain_rows, moved, own_back, sent_back = outs
         back, gain_rows[...] = norm_back(after_self[...], gains[1:2, :], summed((own, r1, r2, r3)))
         dself[...] = dcross[...] + back
         dself_low[...] = dself[...].astype(bf16)
-        dcontext = dot(dself_low[...], w_out[...]).astype(bf16)
+        dcontext = dot(dself_low[...], weight[:, 3 * size :]).astype(bf16)
         for k, at in enumerate(heads_in(size)):
             query, keys, vals = (qkv[:, j * size + at.start : j * size + at.stop] for j in range(3))
-            weight = probs[k]
+            share_out = probs[k]
             dprobs = dot_t(dcontext[:, at], vals)
-            dscores = weight * (dprobs - jnp.sum(weight * dprobs, axis=-1, keepdims=True))
+            dscores = share_out * (dprobs - jnp.sum(share_out * dprobs, axis=-1, keepdims=True))
             dscores = dscores.astype(bf16)
             found = (
                 dot(dscores, keys) * SCALE,
                 t_dot(dscores, query) * SCALE,
-                t_dot(weight.astype(bf16), dcontext[:, at]),
+                t_dot(share_out.astype(bf16), dcontext[:, at]),
             )
             for j, term in enumerate(found):
                 moved[:, j * size + at.start : j * size + at.stop] = term.astype(bf16)
-        own_back[...] = dot_t(moved[...], w_in[...])
+        own_back[:count, :] = dot_t(moved[...], weight[:, : 3 * size])
+        own_back[count:, :] = dot_t(active[...], w_outer[...])
         sent_back[...] = own_back[...].astype(bf16)
 
     return call(
         body,
         info,
         [],
-        [dcross, after_self, *terms, gains, w_out, w_in, qkv, probs],
+        [dcross, after_self, *terms, gains, weight, qkv, probs, active, w_outer],
         [],
         [
             like((count, width), f32),
             like((count, width), bf16),
             like((count, width), f32),
             like((count, 3 * size), bf16),
-            like((count, width), f32),
-            like((count, width), bf16),
+            like((2 * count, width), f32),
+            like((2 * count, width), bf16),
         ],
-        flops=2 * count * width * size * 4,
-    )
-
-
-def decoder_ends(info, rows, dself, terms, gains, after_cross, out_terms):
+        flops=2 * count * width * size * 8,
+    )
+
+
+def decoder_ends(info, rows, dself, terms, gains, after_cross):
     count, width = dself.shape
 
     def body(info, _, ins, __, outs, scratch):
         rows, dself, after_cross, gains = ins[:4]
         grad, gain_rows, states = outs
-        back, gain_rows[...] = norm_back(rows[...].astype(f32), gains[0:1, :], summed(ins[4:8]))
+        total = summed(ins[4:8])
+        back, gain_rows[...] = norm_back(rows[...].astype(f32), gains[0:1, :], total[:count])
         grad[...] = dself[...] + back
-        states[...] = (after_cross[...] + summed(ins[8:12])).astype(bf16)
-
-    return call(
-        body,
-        info,
-        [],
-        [rows, dself, after_cross, gains, *terms, *out_terms],
+        states[...] = (after_cross[...] + total[count:]).astype(bf16)
+
+    return call(
+        body,
+        info,
+        [],
+        [rows, dself, after_cross, gains, *terms],
         [],
         [like((count, width), f32), like((count, width), f32), like((count, width), bf16)],
     )
@@ -884,55 +966,94 @@
         [places, jnp.stack([head, blk]).astype(jnp.int32), passage_lengths.reshape(blocks)]
     )
 
-    attention_pieces = fetch(
-        jnp.concatenate([encoder_query, encoder_key, encoder_value, encoder_output.T], axis=1)
-    )
-    inner_pieces = fetch(encoder_inner)
-    outer_pieces = fetch(encoder_outer.T)
-    self_pieces = fetch(
-        jnp.concatenate([decoder_query, decoder_key, decoder_value, decoder_output.T], axis=1)
-    )
-    cross_kv_pieces = fetch(jnp.concatenate([cross_key, cross_value], axis=1))
-    cross_qo_pieces = fetch(jnp.concatenate([cross_query, cross_output.T], axis=1))
-    dec_inner_pieces = fetch(decoder_inner)
-    dec_outer_pieces = fetch(decoder_outer.T)
-
+    size, units = encoder_query.shape[1], encoder_inner.shape[1]
     inputs = encoder_input.reshape(blocks, part, width)
-    first = by_rows(
-        lambda x, g: (norm_rows(x, g[0:1]),), info, [inputs], [encoder_gains], [bf16]
-    )[0]
-    first_all = spread(first)
-    qkv, probs, context, *partial, w_in, w_out = encoder_attention(
-        info, first_all, attention_pieces
-    )
-
-    def enter_ffn(x, a, b, c, g):
-        hidden = x + a + b + c
-        return hidden, norm_rows(hidden, g[1:2])
-
-    hidden, second = by_rows(
-        enter_ffn, info, [inputs, *collect(*partial)], [encoder_gains], [f32, bf16]
-    )
-    second_all = spread(second)
-    active, slope, *partial, w_inner, w_outer = encoder_ffn(
-        info, second_all, inner_pieces, outer_pieces
-    )
-    states = by_rows(
-        lambda h, a, b, c: (h + a + b + c,), info, [hidden, *collect(*partial)], [], [bf16]
-    )[0]
-    states_all = spread(states)
-
     dec_part = decoder_input.shape[1]
     dec_own = count_q * dec_part
     dec_rows = dec_own * head_count
     filled = -(-dec_rows // 16) * 16
+
+    attention = jnp.concatenate(
+        [encoder_query, encoder_key, encoder_value, encoder_output.T], axis=1
+    )
+    attention, inputs = sync(attention, inputs)
+    attention = fetch_step(fetch_start(attention), -1, 1)
+    first = by_rows(
+        lambda x, g: (norm_rows(x, g[0:1]),), info, [inputs], [encoder_gains], [bf16]
+    )[0]
+    cross_self = jnp.concatenate(
+        [
+            cross_key,
+            cross_value,
+            cross_query,
+            cross_output.T,
+            decoder_query,
+            decoder_key,
+            decoder_value,
+            decoder_output.T,
+        ],
+        axis=1,
+    )
+    attention, first, cross_self = sync(attention, first, cross_self)
+
+    cross_self = gather_rows(cross_self)
+    attention = fetch_step(attention, -2, 2)
+    first_all = [first, swap(first, "head", 1), swap(first, "head", 2)]
+    ffn = jnp.concatenate([encoder_inner, encoder_outer.T], axis=1)
+    attention, first_all, ffn = sync(attention, first_all, ffn)
+
+    attention = fetch_step(attention, -3, 3)
+    first_all.append(swap(first_all[2], "head", 1))
     pair = jnp.stack([decoder_input, decoder_cotangent]).reshape(2, dec_own, width)
-    parts = jnp.stack([pair, *share(pair)])
-    parts = jnp.where(head & 1, parts[jnp.array([1, 0, 3, 2])], parts)
-    parts = jnp.where(head & 2, parts[jnp.array([2, 3, 0, 1])], parts)
-    both = parts.transpose(1, 0, 2, 3).reshape(2, dec_rows, width)
+    both = lax.all_gather(pair, "head", axis=1, tiled=True)
     both = jnp.pad(both, ((0, 0), (0, filled - dec_rows), (0, 0)))
+    attention, first_all, ffn, both = sync(attention, first_all, ffn, both)
+
+    attention, ffn = fetch_step(attention, -4), fetch_step(fetch_start(ffn), 1)
+    dec_ffn = jnp.concatenate([decoder_inner, decoder_outer.T], axis=1)
+    attention, ffn, first_all, dec_ffn = sync(attention, ffn, first_all, dec_ffn)
+
+    qkv, probs, context, *partial, w_in, w_out = encoder_attention(
+        info, first_all, in_turn(attention)
+    )
+    ffn = fetch_step(ffn, -1, 2)
+    partial, ffn = sync(partial, ffn)
+
+    def to_core(partial):
+        return [swap(partial[1], "head", 1), swap(partial[3], "head", 1)]
+
+    def to_chip(partial, beside):
+        return swap((partial[2] + beside[1].astype(f32)).astype(bf16), "head", 2)
+
+    beside = to_core(partial)
+    partial, beside, ffn = sync(partial, beside, ffn)
+    across = to_chip(partial, beside)
+    ffn = fetch_step(ffn, -2, 3)
+    partial, beside, across, ffn = sync(partial, beside, across, ffn)
+
+    def enter_ffn(x, a, b, c, g):
+        hidden = x + a + b + c
+        return hidden, norm_rows(hidden, g[1:2])
+
+    hidden, second = by_rows(
+        enter_ffn, info, [inputs, partial[0], beside[0], across], [encoder_gains], [f32, bf16]
+    )
+    second, ffn = sync(second, ffn)
+    ffn = fetch_step(ffn, -3, 4)
+    second_all = [second, swap(second, "head", 1), swap(second, "head", 2)]
+    second_all, ffn, dec_ffn = sync(second_all, ffn, dec_ffn)
+    second_all.append(swap(second_all[2], "head", 1))
+    second_all, dec_ffn = sync(second_all, dec_ffn)
+
+    dec_ffn = fetch_step(fetch_start(dec_ffn), -1, 1)
+    active, slope, *partial, w_inner, w_outer = encoder_ffn(info, second_all, in_turn(ffn))
+    partial, dec_ffn = sync(partial, dec_ffn)
+    beside = to_core(partial)
+    partial, beside, cross_self, both, dec_ffn = sync(partial, beside, cross_self, both, dec_ffn)
     dec_in, cotangent = both[0], both[1]
+    w_cross, w_cross_qo = (Columns(cross_self, 2 * size, k) for k in (0, 1))
+    w_self = Columns(cross_self, 4 * size, 1)
+
     index = np.arange(filled)
     question = (index % dec_own) // dec_part
     position = index // dec_own * dec_part + index % dec_part
@@ -940,36 +1061,41 @@
     order = (jnp.asarray(order[:, None]), jnp.asarray(order[None, :]))
     question = jnp.asarray(question[:, None].astype(np.int32))
 
-    third, dec_qkv, dec_probs, dec_context, mine, sent, dec_w_in, dec_w_out = decoder_self(
-        info, dec_in, decoder_gains, self_pieces, order
-    )
-    (
-        after_self,
-        fourth,
-        queries,
-        outer_back,
-        w_cross_query,
-        w_cross_output,
-        w_dec_inner,
-        w_dec_outer,
-    ) = decoder_queries(
-        info,
-        dec_in,
-        [mine, *share(sent)],
-        cotangent,
-        decoder_gains,
-        cross_qo_pieces,
-        dec_inner_pieces,
-        dec_outer_pieces,
-    )
-
-    key_vals, stats, w_cross = cross_forward(
-        info, states_all, cross_kv_pieces, queries, question, count_pass
-    )
-    bits = 1
-    while bits < blk_count:
-        stats = merge(info, stats, swap(stats, "blk", bits), bits)
-        bits *= 2
+    across = to_chip(partial, beside)
+    third, dec_qkv, dec_probs, dec_context, mine, sent = decoder_self(
+        info, dec_in, decoder_gains, w_self, order
+    )
+    dec_ffn = fetch_step(dec_ffn, -2, 2)
+    partial, beside, across, mine, sent, dec_ffn = sync(
+        partial, beside, across, mine, sent, dec_ffn
+    )
+    states = by_rows(
+        lambda h, a, b, c: (h + a + b + c,),
+        info,
+        [hidden, partial[0], beside[0], across],
+        [],
+        [bf16],
+    )[0]
+    states, sent, dec_ffn = sync(states, sent, dec_ffn)
+    states_all = [states, swap(states, "head", 1), swap(states, "head", 2)]
+    terms = [mine, *share(sent)]
+    dec_ffn = fetch_step(dec_ffn, -3, 3)
+    states_all, terms, dec_ffn = sync(states_all, terms, dec_ffn)
+    states_all.append(swap(states_all[2], "head", 1))
+    after_self, fourth, queries, w_cross_query, w_cross_output = decoder_queries(
+        info, dec_in, terms, decoder_gains, w_cross_qo
+    )
+    states_all, queries, dec_ffn = sync(states_all, queries, dec_ffn)
+
+    key_vals, stats = cross_forward(info, states_all, w_cross, queries, question, count_pass)
+    dec_ffn = fetch_step(dec_ffn, -4)
+    bits = [1 << k for k in range((blk_count - 1).bit_length())]
+    stats, dec_ffn = sync(stats, dec_ffn)
+    w_dec_inner, w_dec_outer, outer_back = decoder_back(info, cotangent, in_turn(dec_ffn))
+    for k in bits:
+        stats = merge(info, stats, swap(stats, "blk", k), k)
+        if k == bits[0]:
+            stats, outer_back = sync(stats, outer_back)
     out, log_total, cross_context, mine, sent = cross_out(info, stats, w_cross_output)
     after_cross, fifth, dec_active, dec_dinner, mine, sent = decoder_ffn(
         info, after_self, [mine, *share(sent)], outer_back, decoder_gains, w_dec_inner
@@ -995,6 +1121,21 @@
     )
     partial, (dcross, dcross_low, gain_four, dqueries) = rest[:4], rest[4:]
 
+    def some(value, which):
+        for k in which:
+            value = value + swap(value, "blk", k)
+        return value
+
+    partial, dqueries, dkey_vals = sync(partial, dqueries, dkey_vals)
+    beside = to_core(partial)
+    partial, beside, dkey_vals, dqueries = sync(partial, beside, dkey_vals, dqueries)
+    across = to_chip(partial, beside)
+    dqueries = some(dqueries, bits[:1])
+    cross_sum = weight_grads(info, [(states_all, dkey_vals)])[0]
+    partial, beside, across, cross_sum, dqueries = sync(
+        partial, beside, across, cross_sum, dqueries
+    )
+
     def enter_back(cot, a, b, c):
         grad = cot + a + b + c
         return grad, grad
@@ -1002,13 +1143,27 @@
     dstates, dstates_low = by_rows(
         enter_back,
         info,
-        [encoder_cotangent.reshape(blocks, part, width), *collect(*partial)],
+        [encoder_cotangent.reshape(blocks, part, width), partial[0], beside[0], across],
         [],
         [f32, bf16],
     )
-    dstates_all = spread(dstates_low)
-    grad_cross = reduce_pieces(weight_grads(info, states_all, dkey_vals))
+    dstates_low, dqueries = sync(dstates_low, dqueries)
+    dstates_all = [dstates_low, swap(dstates_low, "head", 1), swap(dstates_low, "head", 2)]
+    dqueries = some(dqueries, bits[1:]).astype(bf16)
+    dstates_all, dqueries = sync(dstates_all, dqueries)
+    dstates_all.append(swap(dstates_all[2], "head", 1))
+    mine, sent = project_rows(info, dqueries, w_cross_query)
+    dstates_all, sent = sync(dstates_all, sent)
     dinner, *partial = encoder_ffn_back(info, dstates_all, slope, w_inner, w_outer)
+    terms = [mine, *share(sent)]
+    partial, dinner, terms = sync(partial, dinner, terms)
+    beside = to_core(partial)
+    partial, beside, dinner = sync(partial, beside, dinner)
+    across = to_chip(partial, beside)
+    ffn_sums = weight_grads(
+        info, [(second_all, dinner), (dstates_all, active)], [cross_sum]
+    )
+    partial, beside, across, ffn_sums, terms = sync(partial, beside, across, ffn_sums, terms)
 
     def middle_back(dy, h, a, b, c, g):
         back, gain_rows = norm_back(h, g[1:2], a + b + c)
@@ -1018,50 +1173,59 @@
     dhidden, dhidden_low, gain_one = by_rows(
         middle_back,
         info,
-        [dstates, hidden, *collect(*partial)],
+        [dstates, hidden, partial[0], beside[0], across],
         [encoder_gains],
         [f32, bf16],
         gain=True,
     )
-    dhidden_all = spread(dhidden_low)
-    grad_outer = reduce_pieces(weight_grads(info, dstates_all, active))
-    grad_inner = reduce_pieces(weight_grads(info, second_all, dinner))
-
-    partial, pieces, gain_zero = encoder_attention_back(
-        info, dhidden_all, first_all, qkv, probs, context, w_in, w_out, encoder_gains
-    )
-
-    def last_back(dh, x, a, b, c, g):
-        return (dh + norm_back(x, g[0:1], a + b + c)[0],)
-
-    input_grad = by_rows(
-        last_back, info, [dhidden, inputs, *collect(*partial)], [encoder_gains], [f32]
-    )[0]
-    grad_attention = reduce_pieces(pieces)
-
-    dqueries = tree_sum(dqueries, ("blk",)).astype(bf16)
-    mine, sent = project_rows(info, dqueries, w_cross_query)
+    dhidden_low, ffn_sums, terms = sync(dhidden_low, ffn_sums, terms)
+    dhidden_all = [dhidden_low, swap(dhidden_low, "head", 1), swap(dhidden_low, "head", 2)]
+    ffn_moving = reduce_step(ffn_sums, None, 1)
     dself, dself_low, gain_three, dself_qkv, own_back, sent_back = decoder_self_back(
         info,
         dcross,
         after_self,
-        [mine, *share(sent)],
+        terms,
         decoder_gains,
-        dec_w_out,
-        dec_w_in,
+        w_self,
         dec_qkv,
         dec_probs,
-    )
-    out_mine, out_sent = project_rows(info, dec_active, w_dec_outer)
+        dec_active,
+        w_dec_outer,
+    )
+    dhidden_all, ffn_moving, sent_back = sync(dhidden_all, ffn_moving, sent_back)
+    dhidden_all.append(swap(dhidden_all[2], "head", 1))
+    dhidden_all, ffn_moving, sent_back = sync(dhidden_all, ffn_moving, sent_back)
+
+    partial, sums, gain_zero = encoder_attention_back(
+        info, dhidden_all, first_all, qkv, probs, context, w_in, w_out, encoder_gains
+    )
+    ffn_moving = reduce_step(ffn_sums, ffn_moving, 2)
+    terms = [own_back, *share(sent_back)]
+    partial, sums, ffn_moving, gain_zero, terms = sync(
+        partial, sums, ffn_moving, gain_zero, terms
+    )
+    moving = reduce_step(sums, None, 1)
+    beside = to_core(partial)
     dec_grad, gain_two, dec_states = decoder_ends(
-        info,
-        dec_in,
-        dself,
-        [own_back, *share(sent_back)],
-        decoder_gains,
-        after_cross,
-        [out_mine, *share(out_sent)],
-    )
+        info, dec_in, dself, terms, decoder_gains, after_cross
+    )
+
+    def own_rows(values):
+        return lax.dynamic_slice_in_dim(values, head * dec_own, dec_own, 0)
+
+    leading = (blk == 0).astype(f32)
+    dec_gains = [
+        jnp.sum(own_rows(g), axis=0, keepdims=True) * leading
+        for g in (gain_two, gain_three, gain_four)
+    ]
+    gains = jnp.concatenate([gain_zero, gain_one, *dec_gains], axis=0)
+    gains = gains + swap(gains, "head", 1)
+    partial, beside, moving, gains, ffn_moving = sync(partial, beside, moving, gains, ffn_moving)
+    across = to_chip(partial, beside)
+    moving = reduce_step(sums, moving, 2)
+    ffn_moving = reduce_step(ffn_sums, ffn_moving, 3)
+    gains = gains + swap(gains, "head", 2)
     (
         grad_dec_qkv,
         grad_cross_query,
@@ -1075,41 +1239,57 @@
         [(third, dself_qkv), (fourth, dqueries), (fifth, dec_dinner)],
         [(dec_context, dself_low), (cross_context, dcross_low), (dec_active, cotangent)],
     )
-
-    def own_rows(values):
-        return lax.dynamic_slice_in_dim(values, head * dec_own, dec_own, 0)
-
-    leading = (blk == 0).astype(f32)
-    dec_gains = [
-        jnp.sum(own_rows(g), axis=0, keepdims=True) * leading
-        for g in (gain_two, gain_three, gain_four)
-    ]
-    gains = tree_sum(
-        jnp.concatenate([gain_zero, gain_one, *dec_gains], axis=0), ("head", "blk")
+    partial, beside, across, moving, gains, ffn_moving = sync(
+        partial, beside, across, moving, gains, ffn_moving
+    )
+
+    def last_back(dh, x, a, b, c, g):
+        return (dh + norm_back(x, g[0:1], a + b + c)[0],)
+
+    moving = reduce_step(sums, moving, 3)
+    ffn_moving = reduce_step(ffn_sums, ffn_moving, 4)
+    gains = some(gains, bits[:1])
+    input_grad = by_rows(
+        last_back,
+        info,
+        [dhidden, inputs, partial[0], beside[0], across],
+        [encoder_gains],
+        [f32],
+    )[0]
+    moving, ffn_moving, gains = sync(moving, ffn_moving, gains)
+    moving = reduce_step(sums, moving, 4)
+    gains = some(gains, bits[1:])
+    grad_cross_key, grad_cross_value, grad_inner, grad_outer = finish(
+        info,
+        reduce_terms(ffn_sums, ffn_moving),
+        (size, size, units, units),
+        (False, False, False, True),
+    )
+    grad_query, grad_key, grad_value, grad_output = finish(
+        info, reduce_terms(sums, moving), (size,) * 4, (False, False, False, True)
     )
 
     def dec_shape(values):
         return own_rows(values).reshape(count_q, dec_part, width)
 
-    size = encoder_query.shape[1]
     return (
         states.reshape(encoder_input.shape),
         dec_shape(dec_states),
         input_grad.reshape(encoder_input.shape),
         dec_shape(dec_grad),
-        grad_attention[:, :size],
-        grad_attention[:, size : 2 * size],
-        grad_attention[:, 2 * size : 3 * size],
-        grad_attention[:, 3 * size :].T,
+        grad_query,
+        grad_key,
+        grad_value,
+        grad_output,
         grad_inner,
-        grad_outer.T,
+        grad_outer,
         grad_dec_qkv[:, :size],
         grad_dec_qkv[:, size : 2 * size],
         grad_dec_qkv[:, 2 * size :],
         grad_dec_output,
         grad_cross_query,
-        grad_cross[:, :size],
-        grad_cross[:, size:],
+        grad_cross_key,
+        grad_cross_value,
         grad_cross_output,
         grad_dec_inner,
         grad_dec_outer,

time: 421 us -> 359 us (0.85)
  starting transfers between devices: 126 us -> 72 us
  local copies, waits for them, and re-layouts: 64.4 us -> 26.4 us
  Pallas kernels: 85.1 us -> 105 us
  other arithmetic: 21.1 us -> 8.33 us
  between operations: 2.53 us -> 15.3 us
  waiting for transfers between devices: 119 us -> 125 us
  blocking collectives: 0 us -> 5.4 us
    ppermute x84 -> x35, starting transfers between devices: 90 us -> 37.7 us  [the longest x21 22.9 us: fetch_step(): lax.ppermute(pieces[k + 1 if k < 0 else k - 1], 'blk', forth if k < 0 els...]
    unnamed x364 -> x197, local copies, waits for them, and re-layouts: 53.7 us -> 16.8 us
    pallas_call x27 -> x28, Pallas kernels: 85.1 us -> 105 us  [call(): pl.pallas_call(split, grid=(steps,), in_specs=[pl.BlockSpec(memory_space=...]
    ppermute x84 -> x35, waiting for transfers between devices: 47.1 us -> 64.1 us  [the longest x21 50.6 us: fetch_step(): lax.ppermute(pieces[k + 1 if k < 0 else k - 1], 'blk', forth if k < 0 els...]
    ppermute x62 -> x56, waiting for transfers between devices: 72 us -> 60.9 us  [swap(): return lax.ppermute(value, axis, [(i, i ^ bits) for i in range(size)])]
    all_gather x0 -> x1, blocking collectives: none -> 5.4 us  [shards(): both = lax.all_gather(pair, 'head', axis=1, tiled=True)]
    convert_element_type x26 -> x16, other arithmetic: 11.3 us -> 7.14 us  [the longest x10 4.62 us: add_low(): return (a.astype(f32) + b.astype(f32)).astype(bf16)]
    ppermute x62 -> x56, starting transfers between devices: 36.4 us -> 34.3 us  [swap(): return lax.ppermute(value, axis, [(i, i ^ bits) for i in range(size)])]
  transfers between devices with their start and end apart: 146 -> 92, of which waited for: 51 -> 45; matrix products, arithmetic and copies ran while one was open for 9% -> 6% of each run, Pallas kernels for 12% -> 24%
where the time goes in v2:
time: 359 us; the launch traced here: 358 us
  waiting for transfers between devices  125 us (35%)
  Pallas kernels  105 us (29%)
  starting transfers between devices  72 us (20%)
  local copies, waits for them, and re-layouts  26.4 us (7%)
  between operations  15.3 us (4%)
  other arithmetic  8.33 us (2%)
  blocking collectives  5.4 us (2%)
    pallas_call x28, Pallas kernels, call(): pl.pallas_call(split, grid=(steps,), in_specs=[pl.BlockSpec(memory_space=...  105 us
    ppermute x56, waiting for transfers between devices, swap(): return lax.ppermute(value, axis, [(i, i ^ bits) for i in range(size)])  60.9 us
    ppermute x21, waiting for transfers between devices, fetch_step(): lax.ppermute(pieces[k + 1 if k < 0 else k - 1], 'blk', forth if k < 0 els...  50.6 us
    ppermute x56, starting transfers between devices, swap(): return lax.ppermute(value, axis, [(i, i ^ bits) for i in range(size)])  34.3 us
    ppermute x21, starting transfers between devices, fetch_step(): lax.ppermute(pieces[k + 1 if k < 0 else k - 1], 'blk', forth if k < 0 els...  22.9 us
    unnamed x197, local copies, waits for them, and re-layouts  16.8 us
    ppermute x6, waiting for transfers between devices, reduce_step(): lax.ppermute(behind, 'blk', back)  9.85 us
    ppermute x6, starting transfers between devices, reduce_step(): lax.ppermute(behind, 'blk', back)  7.75 us
  transfers between devices with their start and end apart: 92, of which 45 were waited for; matrix products, arithmetic and copies ran while one was open for 6% of the time, Pallas kernels for 24%

profile of v2, /device:TPU:0, one launch (start us, length us, event | category | flops | bytes accessed | tf_op | source)
XLA Modules:
  0.0 357.6 jit_solution(13263735832372163949)
XLA Ops:
  22.7 4.2 %collective-permute-done.2.refs_7_ = bf16[96,768]{1,0:T(8,128)(2,1)S(1)} collective-permute-done((bf16[96,768]{1,0:T(8,128)(2,1)S(1)}, bf16[96,768]{1,0:T(8,128)(2,1)S(1)}, u32[]{:S(2)}, u32[]{:S(2)}) %collective-permute-start.2) | collective-permute-done | bytes 147488 | tf_op jit(solution)/shard_map/ppermute | solution.py:74
  31.6 5.4 %all_gather.6 = bf16[2,40,768]{2,0,1:T(2,128)(2,1)S(1)} all-gather(bf16[2,10,768]{2,0,1:T(2,128)(2,1)S(1)} %copy.70), channel_id=1, replica_groups=mesh['blk'=8,'head'=4] {'head'}, dimensions={1}, use_global_device_ids=true | all-gather | bytes 153600 | tf_op jit(solution)/shard_map/all_gather | solution.py:1008
  38.2 3.9 %collective-permute-done.7.refs_10_ = bf16[96,768]{1,0:T(8,128)(2,1)S(1)} collective-permute-done((bf16[96,768]{1,0:T(8,128)(2,1)S(1)}, bf16[96,768]{1,0:T(8,128)(2,1)S(1)}, u32[]{:S(2)}, u32[]{:S(2)}) %collective-permute-start.7) | collective-permute-done | bytes 147488 | tf_op jit(solution)/shard_map/ppermute | solution.py:74
  44.2 3.7 %collective-permute-done.9.refs_11_ = bf16[96,768]{1,0:T(8,128)(2,1)S(1)} collective-permute-done((bf16[96,768]{1,0:T(8,128)(2,1)S(1)}, bf16[96,768]{1,0:T(8,128)(2,1)S(1)}, u32[]{:S(2)}, u32[]{:S(2)}) %collective-permute-start.9) | collective-permute-done | bytes 147488 | tf_op jit(solution)/shard_map/ppermute | solution.py:74
  53.1 10.0 %shard_map.427 = (bf16[4,256,576]{2,1,0:T(8,128)(2,1)}, bf16[4,3,256,256]{3,2,1,0:T(8,128)(2,1)}, bf16[4,256,192]{2,1,0:T(8,128)(2,1)}, f32[4,64,768]{2,1,0:T(8,...) custom-call(s32[14]{0:T(128)S(1)} %pad_add_fusion.info_ref, ...), custom_call_target="tpu_custom_call" | custom-call | flops 2013265920 | bytes 9437184 | tf_op jit(solution)/shard_map/pallas_call | solution.py:225
  66.0 10.3 %collective-permute-done.12.refs_8_ = bf16[96,1536]{1,0:T(8,128)(2,1)S(1)} collective-permute-done((bf16[96,1536]{1,0:T(8,128)(2,1)S(1)}, bf16[96,1536]{1,0:T(8,128)(2,1)S(1)}, u32[]{:S(2)}, u32[]{:S(2)}) %collective-permute-start.12) | collective-permute-done | bytes 294944 | tf_op jit(solution)/shard_map/ppermute | solution.py:74
  82.3 6.7 %collective-permute-done.16.refs_7_ = bf16[96,1536]{1,0:T(8,128)(2,1)S(1)} collective-permute-done((bf16[96,1536]{1,0:T(8,128)(2,1)S(1)}, bf16[96,1536]{1,0:T(8,128)(2,1)S(1)}, u32[]{:S(2)}, u32[]{:S(2)}) %collective-permute-start.16) | collective-permute-done | bytes 294944 | tf_op jit(solution)/shard_map/ppermute | solution.py:74
  94.8 7.4 %collective-permute-done.20.refs_9_ = bf16[96,1536]{1,0:T(8,128)(2,1)S(1)} collective-permute-done((bf16[96,1536]{1,0:T(8,128)(2,1)S(1)}, bf16[96,1536]{1,0:T(8,128)(2,1)S(1)}, u32[]{:S(2)}, u32[]{:S(2)}) %collective-permute-start.20) | collective-permute-done | bytes 294944 | tf_op jit(solution)/shard_map/ppermute | solution.py:74
  106.1 9.3 %shard_map.429 = (bf16[4,256,768]{2,1,0:T(8,128)(2,1)}, bf16[4,256,768]{2,1,0:T(8,128)(2,1)}, f32[4,64,768]{2,1,0:T(8,128)S(1)}, bf16[4,64,768]{2,1,0:T(8,128)(2...) custom-call(s32[14]{0:T(128)S(1)} %pad_add_fusion.info_ref, ...), custom_call_target="tpu_custom_call" | custom-call | flops 2415919104 | bytes 11796480 | tf_op jit(solution)/shard_map/pallas_call | solution.py:225
  136.0 6.9 %collective-permute-done.34.refs_4_ = bf16[48,768]{1,0:T(8,128)(2,1)S(1)} collective-permute-done((bf16[48,768]{1,0:T(8,128)(2,1)S(1)}, bf16[48,768]{1,0:T(8,128)(2,1)S(1)}, u32[]{:S(2)}, u32[]{:S(2)}) %collective-permute-start.34) | collective-permute-done | bytes 73760 | tf_op jit(solution)/shard_map/ppermute | solution.py:26
  153.7 5.7 %shard_map.433 = (bf16[4,256,384]{2,1,0:T(8,128)(2,1)}, f32[48,384]{1,0:T(8,128)S(1)}) custom-call(s32[14]{0:T(128)S(1)} %pad_add_fusion.info_ref, bf16[4,64,768]{2,1,0:T(8,128)(2,1)} %shard_map.431.refs_0_, bf16[4,64,768]{2,1,0:T(8,128)(2,1)} %copy-done.51, bf16[4,64,768]{2,1,0:T(8,128)(2,1)} %copy-done.50, bf16[4,64,768]{2,1,0:T(8,128)(2,1)} %copy-done.52, ...), custom_call_target="tpu_custom_call" | custom-call | flops 603979776 | bytes 3041472 | tf_op jit(solution)/shard_map/pallas_call | solution.py:225
  163.2 3.8 %shard_map.435 = (bf16[768,768]{1,0:T(8,128)(2,1)}, bf16[768,768]{1,0:T(8,128)(2,1)}, f32[48,768]{1,0:T(8,128)S(1)}) custom-call(s32[14]{0:T(128)S(1)} %pad_add_fusion.info_ref, bf16[48,768]{1,0:T(8,128)(2,1)S(1)} %get-tuple-element.887.refs_0_.refs_1_.refs_11_, bf16[96,1536]{1,0:T(8,128)(2,1)} %copy-done.53, bf16[96,1536]{1,0:T(8,128)(2,1)} %copy-done.65, ...), custom_call_target="tpu_custom_call" | custom-call | flops 56623104 | bytes 4939776 | tf_op jit(solution)/shard_map/pallas_call | solution.py:225
  174.1 5.0 %collective-permute-done.41.refs_1_ = f32[48,384]{1,0:T(8,128)S(1)} collective-permute-done((f32[48,384]{1,0:T(8,128)S(1)}, f32[48,384]{1,0:T(8,128)S(1)}, u32[]{:S(2)}, u32[]{:S(2)}) %collective-permute-start.41) | collective-permute-done | bytes 73760 | tf_op jit(solution)/shard_map/ppermute | solution.py:26
  195.6 7.7 %shard_map.440 = (bf16[4,256,384]{2,1,0:T(8,128)(2,1)}, f32[4,64,768]{2,1,0:T(8,128)S(1)}, bf16[4,64,768]{2,1,0:T(8,128)(2,1)S(1)}, f32[4,64,768]{2,1,0:T(8,128)...) custom-call(s32[14]{0:T(128)S(1)} %pad_add_fusion.info_ref, ...), custom_call_target="tpu_custom_call" | custom-call | flops 603979776 | bytes 5901504 | tf_op jit(solution)/shard_map/pallas_call | solution.py:225
  207.5 4.8 %shard_map.441.refs_10_ = f32[768,384]{1,0:T(8,128)} custom-call(s32[14]{0:T(128)S(1)} %pad_add_fusion.info_ref, bf16[4,64,768]{2,1,0:T(8,128)(2,1)} %shard_map.431.refs_0_, bf16[4,64,768]{2,1,0:T(8,128)(2,1)} %copy-done.51, bf16[4,64,768]{2,1,0:T(8,128)(2,1)} %copy-done.50, bf16[4,64,768]{2,1,0:T(8,128)(2,1)} %copy-done.52, ...), custom_call_target="tpu_custom_call" | custom-call | flops 603979776 | bytes 3538944 | tf_op jit(solution)/shard_map/pallas_call | solution.py:225
  212.4 4.6 %collective-permute-done.50.refs_3_ = bf16[4,64,768]{2,1,0:T(8,128)(2,1)S(1)} collective-permute-done((bf16[4,64,768]{2,1,0:T(8,128)(2,1)S(1)}, bf16[4,64,768]{2,1,0:T(8,128)(2,1)S(1)}, u32[]{:S(2)}, u32[]{:S(2)}) %collective-permute-start.50) | collective-permute-done | bytes 393248 | tf_op jit(solution)/shard_map/ppermute | solution.py:26
  219.2 3.9 %collective-permute-done.54 = f32[48,192]{1,0:T(8,128)S(1)} collective-permute-done((f32[48,192]{1,0:T(8,128)S(1)}, f32[48,192]{1,0:T(8,128)S(1)}, u32[]{:S(2)}, u32[]{:S(2)}) %collective-permute-start.54) | collective-permute-done | bytes 36896 | tf_op jit(solution)/shard_map/ppermute | solution.py:26
  223.5 4.9 %collective-permute-done.55 = f32[48,192]{1,0:T(8,128)S(1)} collective-permute-done((f32[48,192]{1,0:T(8,128)S(1)}, f32[48,192]{1,0:T(8,128)S(1)}, u32[]{:S(2)}, u32[]{:S(2)}) %collective-permute-start.55) | collective-permute-done | bytes 36896 | tf_op jit(solution)/shard_map/ppermute | solution.py:26
  232.2 6.5 %shard_map.444 = (bf16[4,256,768]{2,1,0:T(8,128)(2,1)}, f32[4,64,768]{2,1,0:T(8,128)S(1)}, bf16[4,64,768]{2,1,0:T(8,128)(2,1)S(1)}, f32[4,64,768]{2,1,0:T(8,128)S(1)}, bf16[4,64,768]{2,1,0:T(8,128)(2,1)S(1)}) custom-call(s32[14]{0:T(128)S(1)} %pad_add_fusion.info_ref, bf16[4,64,768]{2,1,0:T(8,128)(2,1)} %copy-done.49, bf16[4,64,768]{2,1,0:T(8,128)(2,1)} %copy-done.85, ...), custom_call_target="tpu_custom_call" | custom-call | flops 2415919104 | bytes 9437184 | tf_op jit(solution)/shard_map/pallas_call | solution.py:225
  242.2 9.9 %shard_map.445 = (f32[96,1920]{1,0:T(8,128)}, bf16[96,1920]{1,0:T(8,128)(2,1)S(1)}, bf16[96,1920]{1,0:T(8,128)(2,1)S(1)}, bf16[96,1920]{1,0:T(8,128)(2,1)S(1)}, ...) custom-call(s32[14]{0:T(128)S(1)} %pad_add_fusion.info_ref, ...), custom_call_target="tpu_custom_call" | custom-call | flops 3019898880 | bytes 10788864 | tf_op jit(solution)/shard_map/pallas_call | solution.py:225
  257.6 4.3 %shard_map.447 = (f32[48,768]{1,0:T(8,128)S(1)}, bf16[48,768]{1,0:T(8,128)(2,1)S(1)}, f32[48,768]{1,0:T(8,128)S(1)}, bf16[48,576]{1,0:T(8,128)(2,1)S(1)}, f32[96,768]{1,0:T(8,128)}, /*index=5*/bf16[96,768]{1,0:T(8,128)(2,1)}) custom-call(s32[14]{0:T(128)S(1)} %pad_add_fusion.info_ref, f32[48,768]{1,0:T(8,128)S(1)} %get-tuple-element.609.refs_0_, ...), custom_call_target="tpu_custom_call" | custom-call | flops 113246208 | bytes 4055040 | tf_op jit(solution)/shard_map/pallas_call | solution.py:225
  276.4 13.6 %shard_map.448 = (f32[4,64,768]{2,1,0:T(8,128)S(1)}, bf16[4,64,768]{2,1,0:T(8,128)(2,1)}, f32[4,64,768]{2,1,0:T(8,128)S(1)}, bf16[4,64,768]{2,1,0:T(8,128)(2,1)}...) custom-call(s32[14]{0:T(128)S(1)} %pad_add_fusion.info_ref, ...), custom_call_target="tpu_custom_call" | custom-call | flops 4429185024 | bytes 11166720 | tf_op jit(solution)/shard_map/pallas_call | solution.py:225
  311.9 9.4 %collective-permute-done.80 = bf16[96,768]{1,0:T(8,128)(2,1)S(1)} collective-permute-done((bf16[96,768]{1,0:T(8,128)(2,1)S(1)}, bf16[96,768]{1,0:T(8,128)(2,1)S(1)}, u32[]{:S(2)}, u32[]{:S(2)}) %collective-permute-start.80) | collective-permute-done | bytes 147488 | tf_op jit(solution)/shard_map/ppermute | solution.py:100
  328.8 4.3 %collective-permute-done.87 = f32[5,768]{1,0:T(8,128)S(1)} collective-permute-done((f32[5,768]{1,0:T(8,128)S(1)}, f32[5,768]{1,0:T(8,128)S(1)}, u32[]{:S(2)}, u32[]{:S(2)}) %collective-permute-start.87) | collective-permute-done | bytes 15392 | tf_op jit(solution)/shard_map/ppermute | solution.py:26
  (439 shorter events, 186.0 us)
Async XLA Ops:
  7.2 110.7 %all-gather.2.cloned.1.call-start = ((), (), s32[]{:S(2)}) async-start(), calls=%async_computation | async-start | bytes 2654208 | tf_op jit(solution)/shard_map/all_gather | solution.py:59
  29.3 12.8 %collective-permute-start.8 = (bf16[4,64,768]{2,1,0:T(8,128)(2,1)S(1)}, bf16[4,64,768]{2,1,0:T(8,128)(2,1)}, u32[]{:S(2)}, u32[]{:S(2)}) collective-permute-start(bf16[4,64,768]{2,1,0:T(8,128)(2,1)S(1)} %collective-permute-done.5.refs_2_.refs_6_), channel_id=1, source_target_pairs={{0,1},{1,0},{2,3},{3,2},{4,5},{5,4},{6,7},{7,6},{8,9},{9,8},{10,11... | collective-permute-start | bytes 1179656 | tf_op jit(solution)/shard_map/ppermute | solution.py:26
  51.0 14.9 %collective-permute-start.11 = (bf16[96,1536]{1,0:T(8,128)(2,1)S(1)}, bf16[96,1536]{1,0:T(8,128)(2,1)S(1)}, u32[]{:S(2)}, u32[]{:S(2)}) collective-permute-start(bf16[96,1536]{1,0:T(8,128)(2,1)S(1)} %pad_maximum_fusion.refs_4_), channel_id=1, source_target_pairs={{0,8},{8,16},{16,24},{24,28},{28,20},{20,12},{12,4},{4,0},{1,9},{9... | collective-permute-start | bytes 884744 | tf_op jit(solution)/shard_map/ppermute | solution.py:74
  52.3 24.0 %collective-permute-start.12 = (bf16[96,1536]{1,0:T(8,128)(2,1)S(1)}, bf16[96,1536]{1,0:T(8,128)(2,1)S(1)}, u32[]{:S(2)}, u32[]{:S(2)}) collective-permute-start(bf16[96,1536]{1,0:T(8,128)(2,1)S(1)} %collective-permute-done.10.refs_6_), channel_id=1, source_target_pairs={{8,0},{16,8},{24,16},{28,24},{20,28},{12,20},{4,12},{0,4},{9,1},{1... | collective-permute-start | bytes 884744 | tf_op jit(solution)/shard_map/ppermute | solution.py:74
  78.7 11.2 %collective-permute-start.15 = (bf16[4,64,768]{2,1,0:T(8,128)(2,1)S(1)}, bf16[4,64,768]{2,1,0:T(8,128)(2,1)S(1)}, u32[]{:S(2)}, u32[]{:S(2)}) collective-permute-start(bf16[4,64,768]{2,1,0:T(8,128)(2,1)S(1)} %add_convert_fusion.4), channel_id=1, source_target_pairs={{0,2},{1,3},{2,0},{3,1},{4,6},{5,7},{6,4},{7,5},{8,10},{9,11},{10,... | collective-permute-start | bytes 1179656 | tf_op jit(solution)/shard_map/ppermute | solution.py:26
  104.0 11.4 %collective-permute-start.24 = (bf16[96,1536]{1,0:T(8,128)(2,1)S(1)}, bf16[96,1536]{1,0:T(8,128)(2,1)S(1)}, u32[]{:S(2)}, u32[]{:S(2)}) collective-permute-start(bf16[96,1536]{1,0:T(8,128)(2,1)S(1)} %pad_maximum_fusion.1.refs_1_), channel_id=1, source_target_pairs={{8,0},{16,8},{24,16},{28,24},{20,28},{12,20},{4,12},{0,4},{9,1},{1... | collective-permute-start | bytes 884744 | tf_op jit(solution)/shard_map/ppermute | solution.py:74
  119.1 11.2 %collective-permute-start.27 = (bf16[4,64,768]{2,1,0:T(8,128)(2,1)S(1)}, bf16[4,64,768]{2,1,0:T(8,128)(2,1)S(1)}, u32[]{:S(2)}, u32[]{:S(2)}) collective-permute-start(bf16[4,64,768]{2,1,0:T(8,128)(2,1)S(1)} %add_convert_fusion.3), channel_id=1, source_target_pairs={{0,2},{1,3},{2,0},{3,1},{4,6},{5,7},{6,4},{7,5},{8,10},{9,11},{10,... | collective-permute-start | bytes 1179656 | tf_op jit(solution)/shard_map/ppermute | solution.py:26
  132.3 16.6 %collective-permute-start.31 = (bf16[4,64,768]{2,1,0:T(8,128)(2,1)}, bf16[4,64,768]{2,1,0:T(8,128)(2,1)S(1)}, u32[]{:S(2)}, u32[]{:S(2)}) collective-permute-start(bf16[4,64,768]{2,1,0:T(8,128)(2,1)} %shard_map.431.refs_0_), channel_id=1, source_target_pairs={{0,2},{1,3},{2,0},{3,1},{4,6},{5,7},{6,4},{7,5},{8,10},{9,11},{10,... | collective-permute-start | bytes 1179656 | tf_op jit(solution)/shard_map/ppermute | solution.py:26
  133.3 15.7 %collective-permute-start.30 = (bf16[4,64,768]{2,1,0:T(8,128)(2,1)}, bf16[4,64,768]{2,1,0:T(8,128)(2,1)S(1)}, u32[]{:S(2)}, u32[]{:S(2)}) collective-permute-start(bf16[4,64,768]{2,1,0:T(8,128)(2,1)} %shard_map.431.refs_0_), channel_id=1, source_target_pairs={{0,1},{1,0},{2,3},{3,2},{4,5},{5,4},{6,7},{7,6},{8,9},{9,8},{10,11... | collective-permute-start | bytes 1179656 | tf_op jit(solution)/shard_map/ppermute | solution.py:26
  133.3 15.7 %collective-permute-start.35 = (bf16[96,1536]{1,0:T(8,128)(2,1)S(1)}, bf16[96,1536]{1,0:T(8,128)(2,1)S(1)}, u32[]{:S(2)}, u32[]{:S(2)}) collective-permute-start(bf16[96,1536]{1,0:T(8,128)(2,1)S(1)} %collective-permute-done.28.refs_4_), channel_id=1, source_target_pairs={{0,8},{8,16},{16,24},{24,28},{28,20},{20,12},{12,4},{4,0},{1,9},{9... | collective-permute-start | bytes 884744 | tf_op jit(solution)/shard_map/ppermute | solution.py:74
  134.3 14.6 %collective-permute-start.36 = (bf16[96,1536]{1,0:T(8,128)(2,1)S(1)}, bf16[96,1536]{1,0:T(8,128)(2,1)S(1)}, u32[]{:S(2)}, u32[]{:S(2)}) collective-permute-start(bf16[96,1536]{1,0:T(8,128)(2,1)S(1)} %collective-permute-done.29.refs_5_), channel_id=1, source_target_pairs={{8,0},{16,8},{24,16},{28,24},{20,28},{12,20},{4,12},{0,4},{9,1},{1... | collective-permute-start | bytes 884744 | tf_op jit(solution)/shard_map/ppermute | solution.py:74
  205.8 11.2 %collective-permute-start.50 = (bf16[4,64,768]{2,1,0:T(8,128)(2,1)S(1)}, bf16[4,64,768]{2,1,0:T(8,128)(2,1)S(1)}, u32[]{:S(2)}, u32[]{:S(2)}) collective-permute-start(bf16[4,64,768]{2,1,0:T(8,128)(2,1)S(1)} %add_convert_fusion.2), channel_id=1, source_target_pairs={{0,2},{1,3},{2,0},{3,1},{4,6},{5,7},{6,4},{7,5},{8,10},{9,11},{10,... | collective-permute-start | bytes 1179656 | tf_op jit(solution)/shard_map/ppermute | solution.py:26
  241.2 11.6 %collective-permute-start.62 = (bf16[4,64,768]{2,1,0:T(8,128)(2,1)S(1)}, bf16[4,64,768]{2,1,0:T(8,128)(2,1)S(1)}, u32[]{:S(2)}, u32[]{:S(2)}) collective-permute-start(bf16[4,64,768]{2,1,0:T(8,128)(2,1)S(1)} %add_convert_fusion.1), channel_id=1, source_target_pairs={{0,2},{1,3},{2,0},{3,1},{4,6},{5,7},{6,4},{7,5},{8,10},{9,11},{10,... | collective-permute-start | bytes 1179656 | tf_op jit(solution)/shard_map/ppermute | solution.py:26
  254.4 12.2 %collective-permute-start.64 = (bf16[4,64,768]{2,1,0:T(8,128)(2,1)S(1)}, bf16[4,64,768]{2,1,0:T(8,128)(2,1)}, u32[]{:S(2)}, u32[]{:S(2)}) collective-permute-start(bf16[4,64,768]{2,1,0:T(8,128)(2,1)S(1)} %get-tuple-element.715.refs_0_), channel_id=1, source_target_pairs={{0,2},{1,3},{2,0},{3,1},{4,6},{5,7},{6,4},{7,5},{8,10},{9,11},{10,... | collective-permute-start | bytes 1179656 | tf_op jit(solution)/shard_map/ppermute | solution.py:26
  270.3 22.4 %collective-permute-start.72 = (bf16[96,768]{1,0:T(8,128)(2,1)}, bf16[96,768]{1,0:T(8,128)(2,1)S(1)}, u32[]{:S(2)}, u32[]{:S(2)}) collective-permute-start(bf16[96,768]{1,0:T(8,128)(2,1)} %get-tuple-element.742), channel_id=1, source_target_pairs={{0,3},{1,2},{2,1},{3,0},{4,7},{5,6},{6,5},{7,4},{8,11},{9,10},{10,... | collective-permute-start | bytes 442376 | tf_op jit(solution)/shard_map/ppermute | solution.py:26
  270.9 21.7 %collective-permute-start.71 = (bf16[96,768]{1,0:T(8,128)(2,1)}, bf16[96,768]{1,0:T(8,128)(2,1)S(1)}, u32[]{:S(2)}, u32[]{:S(2)}) collective-permute-start(bf16[96,768]{1,0:T(8,128)(2,1)} %get-tuple-element.742), channel_id=1, source_target_pairs={{0,2},{1,3},{2,0},{3,1},{4,6},{5,7},{6,4},{7,5},{8,10},{9,11},{10,... | collective-permute-start | bytes 442376 | tf_op jit(solution)/shard_map/ppermute | solution.py:26
  272.1 20.6 %collective-permute-start.70 = (bf16[96,768]{1,0:T(8,128)(2,1)}, bf16[96,768]{1,0:T(8,128)(2,1)S(1)}, u32[]{:S(2)}, u32[]{:S(2)}) collective-permute-start(bf16[96,768]{1,0:T(8,128)(2,1)} %get-tuple-element.742), channel_id=1, source_target_pairs={{0,1},{1,0},{2,3},{3,2},{4,5},{5,4},{6,7},{7,6},{8,9},{9,8},{10,11... | collective-permute-start | bytes 442376 | tf_op jit(solution)/shard_map/ppermute | solution.py:26
  273.2 19.4 %collective-permute-start.68 = (bf16[96,1920]{1,0:T(8,128)(2,1)S(1)}, bf16[96,1920]{1,0:T(8,128)(2,1)S(1)}, u32[]{:S(2)}, u32[]{:S(2)}) collective-permute-start(bf16[96,1920]{1,0:T(8,128)(2,1)S(1)} %add_convert_fusion.9), channel_id=1, source_target_pairs={{0,8},{8,16},{16,24},{24,28},{28,20},{20,12},{12,4},{4,0},{1,9},{9... | collective-permute-start | bytes 1105928 | tf_op jit(solution)/shard_map/ppermute | solution.py:99
  274.0 18.6 %collective-permute-start.69 = (bf16[96,1920]{1,0:T(8,128)(2,1)S(1)}, bf16[96,1920]{1,0:T(8,128)(2,1)S(1)}, u32[]{:S(2)}, u32[]{:S(2)}) collective-permute-start(bf16[96,1920]{1,0:T(8,128)(2,1)S(1)} %add_convert_fusion.8), channel_id=1, source_target_pairs={{8,0},{16,8},{24,16},{28,24},{20,28},{12,20},{4,12},{0,4},{9,1},{1... | collective-permute-start | bytes 1105928 | tf_op jit(solution)/shard_map/ppermute | solution.py:100
  306.2 15.1 %collective-permute-start.82 = (bf16[96,1920]{1,0:T(8,128)(2,1)S(1)}, bf16[96,1920]{1,0:T(8,128)(2,1)S(1)}, u32[]{:S(2)}, u32[]{:S(2)}) collective-permute-start(bf16[96,1920]{1,0:T(8,128)(2,1)S(1)} %add_convert_fusion.7), channel_id=1, source_target_pairs={{0,8},{8,16},{16,24},{24,28},{28,20},{20,12},{12,4},{4,0},{1,9},{9... | collective-permute-start | bytes 1105928 | tf_op jit(solution)/shard_map/ppermute | solution.py:99
  308.7 12.6 %collective-permute-start.78 = (bf16[4,64,768]{2,1,0:T(8,128)(2,1)S(1)}, bf16[4,64,768]{2,1,0:T(8,128)(2,1)S(1)}, u32[]{:S(2)}, u32[]{:S(2)}) collective-permute-start(bf16[4,64,768]{2,1,0:T(8,128)(2,1)S(1)} %add_convert_fusion), channel_id=1, source_target_pairs={{0,2},{1,3},{2,0},{3,1},{4,6},{5,7},{6,4},{7,5},{8,10},{9,11},{10,... | collective-permute-start | bytes 1179656 | tf_op jit(solution)/shard_map/ppermute | solution.py:26
  309.7 11.6 %collective-permute-start.83 = (bf16[96,1920]{1,0:T(8,128)(2,1)S(1)}, bf16[96,1920]{1,0:T(8,128)(2,1)S(1)}, u32[]{:S(2)}, u32[]{:S(2)}) collective-permute-start(bf16[96,1920]{1,0:T(8,128)(2,1)S(1)} %add_convert_fusion.6), channel_id=1, source_target_pairs={{8,0},{16,8},{24,16},{28,24},{20,28},{12,20},{4,12},{0,4},{9,1},{1... | collective-permute-start | bytes 1105928 | tf_op jit(solution)/shard_map/ppermute | solution.py:100
  321.4 11.7 %collective-permute-start.84 = (bf16[96,768]{1,0:T(8,128)(2,1)S(1)}, bf16[96,768]{1,0:T(8,128)(2,1)S(1)}, u32[]{:S(2)}, u32[]{:S(2)}) collective-permute-start(bf16[96,768]{1,0:T(8,128)(2,1)S(1)} %add_convert_fusion.12), channel_id=1, source_target_pairs={{0,8},{8,16},{16,24},{24,28},{28,20},{20,12},{12,4},{4,0},{1,9},{9... | collective-permute-start | bytes 442376 | tf_op jit(solution)/shard_map/ppermute | solution.py:99
  334.7 14.2 %collective-permute-start.88 = (bf16[96,768]{1,0:T(8,128)(2,1)S(1)}, bf16[96,768]{1,0:T(8,128)(2,1)S(1)}, u32[]{:S(2)}, u32[]{:S(2)}) collective-permute-start(bf16[96,768]{1,0:T(8,128)(2,1)S(1)} %add_convert_fusion.10), channel_id=1, source_target_pairs={{0,8},{8,16},{16,24},{24,28},{28,20},{20,12},{12,4},{4,0},{1,9},{9... | collective-permute-start | bytes 442376 | tf_op jit(solution)/shard_map/ppermute | solution.py:99
  (162 other events, 1405.7 us)
Sparse Core Ops, SparseCore 0:
  18.8 60.2 all-gather.1

commit v3 on v2

--- a/solution.py
+++ b/solution.py
@@ -12,8 +12,9 @@
 SCALE = HDIM ** (-0.5)
 LANES = 128
 EPS = 1e-06
-VMEM_LIMIT = 40 * 1024 * 1024
+VMEM_LIMIT = 24 * 1024 * 1024
 LARGE = 1 << 18
+RIDERS = 48
 masked_score = -1000000000.0
 f32 = jnp.float32
 bf16 = jnp.bfloat16
@@ -81,23 +82,72 @@
     return [pieces[k] if k in pieces else pieces[-k] for k in OFFSETS]
 
 
-def add_low(a, b):
-    return (a.astype(f32) + b.astype(f32)).astype(bf16)
-
-
-def reduce_step(pieces, moving, step):
+@jax.tree_util.register_pytree_node_class
+class Part:
+    def __init__(self, array, start, width):
+        self.array, self.start, self.width = array, start, width
+
+    def tree_flatten(self):
+        return (self.array,), (self.start, self.width)
+
+    @classmethod
+    def tree_unflatten(cls, places, arrays):
+        return cls(*arrays, *places)
+
+    def read(self, ref):
+        return ref[:, self.start : self.start + self.width]
+
+
+def part(value):
+    return value if isinstance(value, Part) else Part(value, 0, value.shape[1])
+
+
+def reduce_step(info, *rings):
     count = lax.axis_size("blk")
     if count != 8:
-        return []
+        return [[] for _ in rings]
     forth, back = ring_steps(count)
-    by = dict(zip(OFFSETS, pieces, strict=True))
-    if step == 1:
-        ahead, behind = by[-4], by[-3]
+    plan = [[], []]
+    for pieces, moving, step in rings:
+        by = dict(zip(OFFSETS, pieces, strict=True))
+        plan[0].append([*([] if step == 1 else [moving[0]]), by[(-4, 3, 2, 1)[step - 1]]])
+        if step < 4:
+            plan[1].append([*([] if step == 1 else [moving[1]]), by[(-3, -2, -1)[step - 1]]])
+    plan = [p for p in plan if p]
+    if len(rings) == 1 and rings[0][2] == 1:
+        sent = [p[0][0] for p in plan]
     else:
-        ahead = add_low(moving[0], by[5 - step])
-        behind = add_low(moving[1], by[step - 4]) if step < 4 else None
-    ahead = lax.ppermute(ahead, "blk", forth)
-    return [ahead, moving[1] if behind is None else lax.ppermute(behind, "blk", back)]
+        parts = [part(v) for p in plan for terms in p for v in terms]
+
+        def body(info, _, ins, __, outs, ___):
+            found = iter(zip(parts, ins, strict=True))
+            for out, p in zip(outs, plan, strict=True):
+                column = 0
+                for terms in p:
+                    values = [piece.read(ref) for piece, ref in (next(found) for _ in terms)]
+                    total = values[0]
+                    if len(values) == 2:
+                        total = (total.astype(f32) + values[1].astype(f32)).astype(bf16)
+                    out[:, column : column + total.shape[1]] = total
+                    column += total.shape[1]
+
+        rows = rings[0][0][0].shape[0]
+        wide = [sum(part(terms[0]).width for terms in p) for p in plan]
+        shapes = [like((rows, w), bf16) for w in wide]
+        sent = call(body, info, [], [p.array for p in parts], [], shapes, near=True)
+    came = [lax.ppermute(v, "blk", way) for v, way in zip(sent, (forth, back), strict=False)]
+    results, column = [], 0
+    for k, (pieces, moving, step) in enumerate(rings):
+        wide = pieces[0].shape[1]
+        found = [Part(came[0], column, wide)]
+        if step == 4:
+            found.append(moving[1])
+        else:
+            before = sum(r[0][0].shape[1] for r in rings[:k] if r[2] < 4)
+            found.append(Part(came[1], before, wide))
+        results.append(found)
+        column += wide
+    return results
 
 
 def reduce_terms(pieces, moving):
@@ -146,12 +196,12 @@
     return [slice(at, at + HDIM) for at in range(0, width, HDIM)]
 
 
-def assemble(info, pieces, targets, signals):
+def assemble(info, pieces, targets, signals, column_from=0):
     rows = pieces[0].shape[0]
     copies = []
     for t, piece in enumerate(pieces):
         at = pl.ds(pl.multiple_of(info[PLACES + t] * rows, 16), rows)
-        column = 0
+        column = column_from
         for k, target in enumerate(targets):
             wide = target.shape[1]
             copies.append(
@@ -193,14 +243,17 @@
 
 
 def call(
-    body, info, stepped, fixed, out_stepped, out_fixed, scratch=(), flops=0, steps=1, near=False
+    body, info, stepped, fixed, out_stepped, out_fixed, scratch=(), flops=0, steps=1, near=False, least=LARGE
 ):
     def by_step(shape):
-        return pl.BlockSpec((1, *shape[1:]), lambda b: (b,) + (0,) * (len(shape) - 1))
+        last = shape[0] - 1
+        return pl.BlockSpec((1, *shape[1:]), lambda b: (jnp.minimum(b, last),) + (0,) * (len(shape) - 1))
 
     def whole(a):
         if isinstance(a, Far):
             return pl.BlockSpec(memory_space=pltpu.HBM)
+        if isinstance(a, Rider):
+            return pl.BlockSpec(a.shape, lambda b: (a.index, 0, 0))
         index = (0, a.index) if type(a) is Columns else (0,) * len(a.shape)
         return pl.BlockSpec(a.shape, lambda b: index)
 
@@ -211,14 +264,16 @@
         body(info_ref, *(refs[e - c : e] for c, e in zip(counts, stops, strict=True)))
 
     def large(a):
-        return not near and math.prod(a.shape) * a.dtype.itemsize >= LARGE
+        return not near and math.prod(a.shape) * a.dtype.itemsize >= least
 
     def given(a):
-        array = a.array if isinstance(a, (Columns, Far)) else a
+        array = a.array if isinstance(a, (Columns, Far, Rider)) else a
         return pltpu.with_memory_space_constraint(array, pltpu.HBM) if large(a) else array
 
     def made(a):
-        return a.array if isinstance(a, Near) else pltpu.HBM(a.shape, a.dtype) if large(a) else a
+        if isinstance(a, Later) or (large(a) and not isinstance(a, Near)):
+            return pltpu.HBM(a.shape, a.dtype)
+        return a.array if isinstance(a, Near) else a
 
     arrays = [*stepped, *fixed, *out_stepped, *out_fixed]
     moved = sum(math.prod(a.shape) * a.dtype.itemsize for a in arrays)
@@ -256,6 +311,16 @@
         self.array, self.shape, self.dtype = array, array.shape, array.dtype
 
 
+class Later(Near):
+    pass
+
+
+class Rider:
+    def __init__(self, array, index):
+        self.array, self.index, self.dtype = array, index, array.dtype
+        self.shape = (1, *array.shape[1:])
+
+
 class Far:
     def __init__(self, array):
         self.array, self.shape, self.dtype = array, array.shape, array.dtype
@@ -265,30 +330,52 @@
     return jax.ShapeDtypeStruct(tuple(shape), dtype)
 
 
-def by_rows(fn, info, stepped, fixed, dtypes, gain=False):
+def by_rows(fn, info, stepped, fixed, dtypes, gain=False, riders=None, kept=True):
     steps, _, width = stepped[0].shape
+    count = 0 if riders is None else riders.shape[0] // RIDERS
+    alone = [like(stepped[0].shape, d) for d in dtypes]
+    outs = alone if riders is None or kept else alone[:-1]
+    more = 0 if riders is None else riders.shape[0] // count
+    together = [like((steps + count, *stepped[0].shape[1:]), dtypes[-1])] if more else []
 
     def body(info_ref, ins, whole, outs, sums, _):
-        results = fn(*(r[0].astype(f32) for r in ins), *(r[...] for r in whole))
-        for out, value in zip(outs, results, strict=False):
-            out[0] = value.astype(out.dtype)
-        for total in sums:
-
-            @pl.when(pl.program_id(0) == 0)
+        b = pl.program_id(0)
+        if more:
+            whole, rows = whole[:-1], whole[-1]
+
+        @pl.when(b < steps)
+        def _():
+            results = fn(*(r[0].astype(f32) for r in ins), *(r[...] for r in whole))
+            for out, value in zip(outs, results, strict=False):
+                out[0] = value.astype(out.dtype)
+            if more:
+                outs[-1][0] = results[len(dtypes) - 1].astype(outs[-1].dtype)
+            for total in sums:
+                found = jnp.sum(results[-1], axis=0, keepdims=True)
+
+                @pl.when(b == 0)
+                def _():
+                    total[...] = found
+
+                @pl.when(b > 0)
+                def _():
+                    total[...] += found
+
+        for k in range(count):
+
+            @pl.when(b == steps + k)
             def _():
-                total[...] = jnp.zeros_like(total)
-
-            total[...] += jnp.sum(results[-1], axis=0, keepdims=True)
+                outs[-1][0, :more, :] = rows[k * more : (k + 1) * more, :]
 
     return call(
         body,
         info,
         stepped,
-        fixed,
-        [like(stepped[0].shape, d) for d in dtypes],
+        [*fixed, riders] if more else fixed,
+        [*outs, *together],
         [like((1, width), f32)] * gain,
         flops=10 * math.prod(stepped[0].shape),
-        steps=steps,
+        steps=steps + count,
         near=True,
     )
 
@@ -298,7 +385,7 @@
 
 
 def piece_shapes(rows, columns):
-    return [like((rows, columns), f32), *[Near(like((rows, columns), bf16))] * 7]
+    return [Later(like((rows, columns), d)) for d in (f32, *[bf16] * 7)]
 
 
 def encoder_attention(info, normed, pieces):
@@ -323,9 +410,10 @@
         allowed = slots_used(info, b, part, slot)
         for k, at in enumerate(heads_in(size)):
             query, keys, vals = (qkv[0, :, j * size + at.start : j * size + at.stop] for j in range(3))
-            scores = jnp.where(allowed, dot_t(query, keys) * SCALE, masked_score)
+            scores = jnp.where(allowed, dot_t(query * SCALE, keys), masked_score)
             spread_out = jnp.exp(scores - jnp.max(scores, axis=-1, keepdims=True))
-            weight = (spread_out / jnp.sum(spread_out, axis=-1, keepdims=True)).astype(bf16)
+            inverse = 1.0 / jnp.sum(spread_out, axis=-1, keepdims=True)
+            weight = (spread_out * inverse).astype(bf16)
             probs[0, k] = weight
             context[0, :, at] = dot(weight, vals).astype(bf16)
         emit(dot_t(context[0], w_out[...]), outs[3:])
@@ -412,10 +500,9 @@
     return results[:4], results[4:12], results[12]
 
 
-def encoder_ffn(info, normed, pieces):
+def encoder_ffn(info, normed, pieces, hidden):
     blocks, part, width = normed[0].shape
     slot = part * len(normed)
-    hidden = pieces[0].shape[1] // 2
 
     def body(info, rows, pieces, outs, weights, scratch):
         active, slope = outs[:2]
@@ -444,7 +531,7 @@
 
 
 def encoder_ffn_back(info, grads, slope, w_inner, w_outer):
-    blocks, part, width = grads[0].shape
+    blocks, (_, part, width) = slope.shape[0], grads[0].shape
     slot = part * len(grads)
     hidden = w_inner.shape[1]
 
@@ -467,14 +554,13 @@
     )
 
 
-def weight_grads(info, pairs, more=()):
-    blocks, part, width = pairs[0][0][0].shape
+def weight_grads(info, pairs, more=(), cut=True):
+    blocks, (_, part, width) = pairs[0][1].shape[0], pairs[0][0][0].shape
     widths = [right.shape[2] for _, right in pairs]
-    total_width = sum(widths) + sum(m.shape[1] for m in more)
-
-    def body(info, stepped, more, _, ends, totals):
+
+    def body(info, stepped, more, __, ends, totals):
         b = pl.program_id(0)
-        totals = totals if more else ends
+        totals = totals if cut else ends
         for k, total in enumerate(totals):
             left, right = stepped[5 * k : 5 * k + 4], stepped[5 * k + 4]
             found = t_dot(token_rows(left), right[0])
@@ -487,11 +573,11 @@
             def _():
                 total[...] += found
 
-        if more:
+        if cut:
 
             @pl.when(b == blocks - 1)
             def _():
-                hand_out(info, (*more, *totals), ends)
+                hand_out(info, (*totals, *more), ends)
 
     return call(
         body,
@@ -499,41 +585,50 @@
         [a for left, right in pairs for a in (*left, right)],
         more,
         [],
-        piece_shapes(width // 8, total_width)
-        if more
+        piece_shapes(width // 8, sum(widths) + sum(m.shape[1] for m in more))
+        if cut
         else [like((width, w), f32) for w in widths],
-        [pltpu.VMEM((width, w), f32) for w in widths] if more else [],
-        flops=2 * blocks * part * 4 * width * total_width,
+        [pltpu.VMEM((width, w), f32) for w in widths] if cut else [],
+        flops=2 * blocks * part * 4 * width * sum(widths),
         steps=blocks,
     )
 
 
 def finish(info, terms, widths, turned):
-    rows = terms[0].shape[0]
+    terms = [part(t) for t in terms]
+    rows = terms[0].array.shape[0]
     shapes = [(w, rows) if t else (rows, w) for w, t in zip(widths, turned, strict=True)]
 
     def body(info, _, ins, __, outs, ___):
-        total = summed(ins)
+        total = terms[0].read(ins[0])
+        for term, ref in zip(terms[1:], ins[1:], strict=True):
+            total = total + term.read(ref).astype(f32)
         column = 0
         for out, wide, turn in zip(outs, widths, turned, strict=True):
             found = total[:, column : column + wide]
             out[...] = found.T if turn else found
             column += wide
 
-    return call(body, info, [], terms, [], [like(s, f32) for s in shapes])
-
-
-def cross_forward(info, states, weight, queries, own_question, count_pass):
-    blocks, part, width = states[0].shape
+    return call(body, info, [], [t.array for t in terms], [], [like(s, f32) for s in shapes])
+
+
+def cross_forward(info, states, pieces, column_from, queries, own_question, count_q, count_pass):
+    blocks = count_q * count_pass
+    _, part, width = states[0].shape
     slot = part * len(states)
     size = queries.shape[1]
     rows_dec = queries.shape[0]
 
     def body(info, rows, fixed, outs, ends, scratch):
-        weight, queries, question = fixed
-        stats = ends[0]
-        held = scratch[0]
+        pieces, queries, question = fixed[:-2], fixed[-2], fixed[-1]
+        stats, weight = ends
+        held, signals = scratch
         b = pl.program_id(0)
+
+        @pl.when(b == 0)
+        def _():
+            assemble(info, pieces, (weight,), signals, column_from)
+
         made = dot(token_rows(rows), weight[...]).astype(bf16)
         outs[0][0] = made
         held[pl.ds(pl.multiple_of(b * slot, slot), slot), :] = made
@@ -562,42 +657,56 @@
         body,
         info,
         states,
-        [weight, queries, own_question],
+        [*(Far(p) for p in pieces), queries, own_question],
         [like((blocks, slot, 2 * size), bf16)],
-        [like((rows_dec, size // HDIM * LANES), f32)],
-        [pltpu.VMEM((blocks * slot, 2 * size), bf16)],
+        [like((rows_dec, size // HDIM * LANES), f32), like((width, 2 * size), bf16)],
+        [
+            pltpu.VMEM((blocks * slot, 2 * size), bf16),
+            pltpu.SemaphoreType.DMA((1, len(pieces))),
+        ],
         flops=4 * blocks * slot * width * size,
         steps=blocks,
     )
 
 
+def merged(first, second):
+    lane = lax.broadcasted_iota(jnp.int32, (first.shape[0], HDIM), 1)
+    found = []
+    for at in range(0, first.shape[1], LANES):
+        tops = [v[:, at + HDIM : at + HDIM + 1] for v in (first, second)]
+        totals = [v[:, at + HDIM + 1 : at + HDIM + 2] for v in (first, second)]
+        top = jnp.maximum(*tops)
+        scales = [jnp.exp(t - top) for t in tops]
+        total = totals[0] * scales[0] + totals[1] * scales[1]
+        found.append(first[:, at : at + HDIM] * scales[0] + second[:, at : at + HDIM] * scales[1])
+        found.append(jnp.where(lane == 0, top, total))
+    return jnp.concatenate(found, axis=1)
+
+
+def in_order(info, bits, own, other):
+    later = (info[BLK] & bits) != 0
+    return jnp.where(later, other, own), jnp.where(later, own, other)
+
+
 def merge(info, own, other, bits):
     def body(info, _, ins, __, outs, ___):
-        mine, yours = ins[0][...], ins[1][...]
-        later = (info[BLK] & bits) != 0
-        first, second = jnp.where(later, yours, mine), jnp.where(later, mine, yours)
-        lane = lax.broadcasted_iota(jnp.int32, (first.shape[0], HDIM), 1)
-        for at in range(0, first.shape[1], LANES):
-            pairs = [(v[:, at + HDIM : at + HDIM + 1], v[:, at + HDIM + 1 : at + HDIM + 2]) for v in (first, second)]
-            top = jnp.maximum(pairs[0][0], pairs[1][0])
-            by_first, by_second = jnp.exp(pairs[0][0] - top), jnp.exp(pairs[1][0] - top)
-            total = pairs[0][1] * by_first + pairs[1][1] * by_second
-            outs[0][:, at : at + HDIM] = (
-                first[:, at : at + HDIM] * by_first + second[:, at : at + HDIM] * by_second
-            )
-            outs[0][:, at + HDIM : at + LANES] = jnp.where(lane == 0, top, total)
+        outs[0][...] = merged(*in_order(info, bits, ins[0][...], ins[1][...]))
 
     return call(body, info, [], [own, other], [], [like(own.shape, f32)])[0]
 
 
-def cross_out(info, stats, w_output):
-    rows, columns = stats.shape
+def cross_out(info, stats, bits, w_output):
+    rows, columns = stats[0].shape
     size = columns // LANES * HDIM
     width = w_output.shape[0]
 
     def body(info, _, ins, __, outs, scratch):
-        stats, w_output = ins
+        w_output = ins[-1]
         out, log_total, context, own, sent = outs
+        values = [r[...] for r in ins[:-1]]
+        near = merged(*in_order(info, bits[0], *values[:2]))
+        far = merged(*in_order(info, bits[0], *values[2:]))
+        stats = merged(*in_order(info, bits[1], near, far))
         log_total[...] = jnp.zeros_like(log_total)
         for k, at in enumerate(heads_in(size)):
             base = k * LANES
@@ -613,12 +722,12 @@
         body,
         info,
         [],
-        [stats, w_output],
+        [*stats, w_output],
         [],
         [
             like((rows, size), f32),
             like((rows, LANES), f32),
-            like((rows, size), bf16),
+            Later(like((rows, size), bf16)),
             like((rows, width), f32),
             like((rows, width), bf16),
         ],
@@ -676,9 +785,9 @@
         [cotangent, after_cross, *terms, gains, w_output, out, log_total, queries, weight, own_question],
         [like(key_vals.shape, bf16), *partial_rows(blocks, part, width)],
         [
-            like((rows_dec, width), f32),
-            like((rows_dec, width), bf16),
-            like((rows_dec, width), f32),
+            Later(like((rows_dec, width), f32)),
+            Later(like((rows_dec, width), bf16)),
+            Later(like((rows_dec, width), f32)),
             like((rows_dec, size), f32),
         ],
         [pltpu.VMEM((rows_dec, size), bf16), pltpu.VMEM((rows_dec, LANES), f32)],
@@ -688,19 +797,28 @@
 
 
 def summed(refs):
+    count = refs[0].shape[0]
+
+    def rows(ref):
+        return ref[...] if len(ref.shape) == 2 else ref[0, : min(count, RIDERS), :]
+
+    terms = [rows(ref).astype(f32) for ref in refs[1:]]
+    each = len(terms) // 3
+    if each == 2:
+        terms = [jnp.concatenate(terms[k : k + 2], axis=0) for k in (0, 2, 4)]
     total = refs[0][...]
-    for ref in refs[1:]:
-        total = total + ref[...].astype(f32)
+    for term in terms:
+        total = total + term
     return total
 
 
-def decoder_self(info, rows, gains, weight, order):
+def decoder_self(info, rows, gains, pieces, column_from, size, order):
     count, width = rows.shape
-    size = weight.shape[1] // 4
 
     def body(info, _, ins, __, outs, scratch):
-        rows, gains, order_q, order_k, weight = ins
-        normed, qkv, probs, context, own, sent = outs
+        rows, gains, order_q, order_k = ins[:4]
+        normed, qkv, probs, context, own, sent, weight = outs
+        assemble(info, ins[4:], (weight,), scratch[0], column_from)
         normed[...] = norm_rows(rows[...].astype(f32), gains[0:1, :]).astype(bf16)
         qkv[...] = dot(normed[...], weight[:, : 3 * size]).astype(bf16)
         query_at, key_at = order_q[...], order_k[...]
@@ -721,27 +839,30 @@
         body,
         info,
         [],
-        [rows, gains, *order, weight],
+        [rows, gains, *order, *(Far(p) for p in pieces)],
         [],
         [
-            like((count, width), bf16),
-            like((count, 3 * size), bf16),
-            like((size // HDIM, count, count), f32),
-            like((count, size), bf16),
+            Later(like((count, width), bf16)),
+            Later(like((count, 3 * size), bf16)),
+            Later(like((size // HDIM, count, count), f32)),
+            Later(like((count, size), bf16)),
             like((count, width), f32),
             like((count, width), bf16),
+            Later(like((width, 4 * size), bf16)),
         ],
+        [pltpu.SemaphoreType.DMA((1, len(pieces)))],
         flops=2 * count * width * size * 4,
     )
 
 
-def decoder_queries(info, rows, terms, gains, weight):
+def decoder_queries(info, rows, terms, gains, pieces, column_from, size):
     count, width = rows.shape
-    size = weight.shape[1] // 2
 
     def body(info, _, ins, __, outs, scratch):
-        rows, own, r1, r2, r3, gains, weight = ins
+        rows, own, r1, r2, r3, gains = ins[:6]
         after_self, normed, queries, w_query, w_output = outs
+        weight, signals = scratch
+        assemble(info, ins[6:], (weight,), signals, column_from)
         w_query[...] = weight[:, :size]
         w_output[...] = weight[:, size:]
         after_self[...] = rows[...].astype(f32) + summed((own, r1, r2, r3))
@@ -752,15 +873,16 @@
         body,
         info,
         [],
-        [rows, *terms, gains, weight],
+        [rows, *terms, gains, *(Far(p) for p in pieces)],
         [],
         [
             like((count, width), f32),
-            like((count, width), bf16),
+            Later(like((count, width), bf16)),
             like((count, size), bf16),
-            like((width, size), bf16),
+            Later(like((width, size), bf16)),
             like((width, size), bf16),
         ],
+        [pltpu.VMEM((width, 2 * size), bf16), pltpu.SemaphoreType.DMA((1, len(pieces)))],
         flops=2 * count * width * size,
     )
 
@@ -809,9 +931,9 @@
         [],
         [
             like((count, width), f32),
-            like((count, width), bf16),
-            like((count, hidden), bf16),
-            like((count, hidden), bf16),
+            Later(like((count, width), bf16)),
+            Later(like((count, hidden), bf16)),
+            Later(like((count, hidden), bf16)),
             like((count, width), f32),
             like((count, width), bf16),
         ],
@@ -819,21 +941,27 @@
     )
 
 
-def project_rows(info, rows, weight):
-    count, width = rows.shape[0], weight.shape[0]
+def query_back(info, terms, weight):
+    (count, size), width = terms[0].shape, weight.shape[0]
 
     def body(info, _, ins, __, outs, scratch):
-        outs[0][...] = dot_t(ins[0][...].astype(bf16), ins[1][...])
-        outs[1][...] = outs[0][...].astype(bf16)
+        low, own, sent = outs
+        low[...] = ((ins[0][...] + ins[1][...]) + (ins[2][...] + ins[3][...])).astype(bf16)
+        own[...] = dot_t(low[...], ins[4][...])
+        sent[...] = own[...].astype(bf16)
 
     return call(
         body,
         info,
         [],
-        [rows, weight],
-        [],
-        [like((count, width), f32), like((count, width), bf16)],
-        flops=2 * count * width * weight.shape[1],
+        [*terms, weight],
+        [],
+        [
+            Later(like((count, size), bf16)),
+            like((count, width), f32),
+            like((count, width), bf16),
+        ],
+        flops=2 * count * width * size,
     )
 
 
@@ -844,9 +972,9 @@
     size = weight.shape[1] // 4
 
     def body(info, _, ins, __, outs, scratch):
-        dcross, after_self, own, r1, r2, r3, gains, weight, qkv, probs, active, w_outer = ins
+        dcross, after_self, *terms, gains, weight, qkv, probs, active, w_outer = ins
         dself, dself_low, gain_rows, moved, own_back, sent_back = outs
-        back, gain_rows[...] = norm_back(after_self[...], gains[1:2, :], summed((own, r1, r2, r3)))
+        back, gain_rows[...] = norm_back(after_self[...], gains[1:2, :], summed(terms))
         dself[...] = dcross[...] + back
         dself_low[...] = dself[...].astype(bf16)
         dcontext = dot(dself_low[...], weight[:, 3 * size :]).astype(bf16)
@@ -875,9 +1003,9 @@
         [],
         [
             like((count, width), f32),
-            like((count, width), bf16),
+            Later(like((count, width), bf16)),
             like((count, width), f32),
-            like((count, 3 * size), bf16),
+            Later(like((count, 3 * size), bf16)),
             like((2 * count, width), f32),
             like((2 * count, width), bf16),
         ],
@@ -885,24 +1013,31 @@
     )
 
 
-def decoder_ends(info, rows, dself, terms, gains, after_cross):
+def decoder_ends(info, rows, dself, terms, gains, after_cross, gain_rows, gain_sums, dec_own):
     count, width = dself.shape
 
     def body(info, _, ins, __, outs, scratch):
         rows, dself, after_cross, gains = ins[:4]
-        grad, gain_rows, states = outs
-        total = summed(ins[4:8])
-        back, gain_rows[...] = norm_back(rows[...].astype(f32), gains[0:1, :], total[:count])
+        three, four, zero, one = ins[-4:]
+        grad, states, found = outs
+        total = summed(ins[4:-4])
+        back, two = norm_back(rows[...].astype(f32), gains[0:1, :], total[:count])
         grad[...] = dself[...] + back
         states[...] = (after_cross[...] + total[count:]).astype(bf16)
+        row = lax.div(lax.broadcasted_iota(jnp.int32, (count, 1), 0), dec_own)
+        mine = (row == info[HEAD]) & (info[BLK] == 0)
+        found[0:1, :] = zero[...]
+        found[1:2, :] = one[...]
+        for k, values in enumerate((two, three[...], four[...])):
+            found[2 + k : 3 + k, :] = jnp.sum(jnp.where(mine, values, 0.0), axis=0, keepdims=True)
 
     return call(
         body,
         info,
         [],
-        [rows, dself, after_cross, gains, *terms],
-        [],
-        [like((count, width), f32), like((count, width), f32), like((count, width), bf16)],
+        [rows, dself, after_cross, gains, *terms, *gain_rows, *gain_sums],
+        [],
+        [like((count, width), f32), like((count, width), bf16), like((5, width), f32)],
     )
 
 
@@ -913,18 +1048,21 @@
         row = lax.broadcasted_iota(jnp.int32, (own, width), 0) + info[BLK] * own
         column = lax.broadcasted_iota(jnp.int32, (own, width), 1)
         pick = jnp.where(row == column, 1.0, 0.0).astype(bf16)
-        n = 2 * len(pairs_in)
-        for k, out in enumerate(outs):
-            left, right = ins[2 * k][...], ins[2 * k + 1][...]
-            if 2 * k < n:
-                out[...] = t_dot(dot_t(left, pick).astype(bf16), right)
-            else:
-                out[...] = t_dot(left, dot_t(right, pick).astype(bf16))
-
-    outs = [like((own, r.shape[1]), f32) for _, r in pairs_in]
+        outs, ins = iter(outs), iter(ins)
+        for _, _, arrays in pairs_in:
+            left, right = next(ins)[...], next(ins)[...]
+            found = t_dot(dot_t(left, pick).astype(bf16), right)
+            wide = found.shape[1] // arrays
+            for k in range(arrays):
+                next(outs)[...] = found[:, k * wide : (k + 1) * wide]
+        for _ in pairs_out:
+            left, right = next(ins)[...], next(ins)[...]
+            next(outs)[...] = t_dot(left, dot_t(right, pick).astype(bf16))
+
+    outs = [like((own, r.shape[1] // n), f32) for _, r, n in pairs_in for _ in range(n)]
     outs += [like((l.shape[1], own), f32) for l, _ in pairs_out]
-    flat = [a for pair in (*pairs_in, *pairs_out) for a in pair]
-    return call(body, info, [], flat, [], outs, flops=2 * count * own * width * 10)
+    flat = [a for pair in pairs_in for a in pair[:2]] + [a for pair in pairs_out for a in pair]
+    return call(body, info, [], flat, [], outs, flops=2 * count * own * width * 10, least=0)
 
 
 def shards(
@@ -981,25 +1119,26 @@
     first = by_rows(
         lambda x, g: (norm_rows(x, g[0:1]),), info, [inputs], [encoder_gains], [bf16]
     )[0]
-    cross_self = jnp.concatenate(
+    attention, first = sync(attention, first)
+
+    attention = fetch_step(attention, -2, 2)
+    first_all = [first, swap(first, "head", 1), swap(first, "head", 2)]
+    ffn = jnp.concatenate(
         [
+            encoder_inner,
+            encoder_outer.T,
+            decoder_query,
+            decoder_key,
+            decoder_value,
+            decoder_output.T,
             cross_key,
             cross_value,
             cross_query,
             cross_output.T,
-            decoder_query,
-            decoder_key,
-            decoder_value,
-            decoder_output.T,
         ],
         axis=1,
     )
-    attention, first, cross_self = sync(attention, first, cross_self)
-
-    cross_self = gather_rows(cross_self)
-    attention = fetch_step(attention, -2, 2)
-    first_all = [first, swap(first, "head", 1), swap(first, "head", 2)]
-    ffn = jnp.concatenate([encoder_inner, encoder_outer.T], axis=1)
+    at_self, at_cross = 2 * units, 2 * units + 4 * size
     attention, first_all, ffn = sync(attention, first_all, ffn)
 
     attention = fetch_step(attention, -3, 3)
@@ -1013,10 +1152,10 @@
     dec_ffn = jnp.concatenate([decoder_inner, decoder_outer.T], axis=1)
     attention, ffn, first_all, dec_ffn = sync(attention, ffn, first_all, dec_ffn)
 
+    ffn = fetch_step(ffn, -1, 2)
     qkv, probs, context, *partial, w_in, w_out = encoder_attention(
         info, first_all, in_turn(attention)
     )
-    ffn = fetch_step(ffn, -1, 2)
     partial, ffn = sync(partial, ffn)
 
     def to_core(partial):
@@ -1038,21 +1177,26 @@
     hidden, second = by_rows(
         enter_ffn, info, [inputs, partial[0], beside[0], across], [encoder_gains], [f32, bf16]
     )
-    second, ffn = sync(second, ffn)
+    def spread(rows):
+        return [rows, swap(rows, "head", 1), swap(rows, "head", 2)]
+
+    def riders(all_rows, count=1):
+        return [Rider(rows, blocks + k) for rows in all_rows[1:] for k in range(count)]
+
+    second, ffn, dec_ffn = sync(second, ffn, dec_ffn)
+    second_all = spread(second)
     ffn = fetch_step(ffn, -3, 4)
-    second_all = [second, swap(second, "head", 1), swap(second, "head", 2)]
+    second_all, ffn = sync(second_all, ffn)
+    second_all.append(swap(second_all[2], "head", 1))
     second_all, ffn, dec_ffn = sync(second_all, ffn, dec_ffn)
-    second_all.append(swap(second_all[2], "head", 1))
-    second_all, dec_ffn = sync(second_all, dec_ffn)
+    ffn = in_turn(ffn)
 
     dec_ffn = fetch_step(fetch_start(dec_ffn), -1, 1)
-    active, slope, *partial, w_inner, w_outer = encoder_ffn(info, second_all, in_turn(ffn))
+    active, slope, *partial, w_inner, w_outer = encoder_ffn(info, second_all, ffn, units)
     partial, dec_ffn = sync(partial, dec_ffn)
     beside = to_core(partial)
-    partial, beside, cross_self, both, dec_ffn = sync(partial, beside, cross_self, both, dec_ffn)
+    partial, beside, both, dec_ffn = sync(partial, beside, both, dec_ffn)
     dec_in, cotangent = both[0], both[1]
-    w_cross, w_cross_qo = (Columns(cross_self, 2 * size, k) for k in (0, 1))
-    w_self = Columns(cross_self, 4 * size, 1)
 
     index = np.arange(filled)
     question = (index % dec_own) // dec_part
@@ -1062,41 +1206,52 @@
     question = jnp.asarray(question[:, None].astype(np.int32))
 
     across = to_chip(partial, beside)
-    third, dec_qkv, dec_probs, dec_context, mine, sent = decoder_self(
-        info, dec_in, decoder_gains, w_self, order
-    )
     dec_ffn = fetch_step(dec_ffn, -2, 2)
+    third, dec_qkv, dec_probs, dec_context, mine, sent, w_self = decoder_self(
+        info, dec_in, decoder_gains, ffn, at_self, size, order
+    )
     partial, beside, across, mine, sent, dec_ffn = sync(
         partial, beside, across, mine, sent, dec_ffn
     )
-    states = by_rows(
+    states, states_sent = by_rows(
         lambda h, a, b, c: (h + a + b + c,),
         info,
         [hidden, partial[0], beside[0], across],
         [],
         [bf16],
-    )[0]
-    states, sent, dec_ffn = sync(states, sent, dec_ffn)
-    states_all = [states, swap(states, "head", 1), swap(states, "head", 2)]
-    terms = [mine, *share(sent)]
+        riders=sent,
+    )
+    states_sent, dec_ffn = sync(states_sent, dec_ffn)
+    states_all = spread(states_sent)
     dec_ffn = fetch_step(dec_ffn, -3, 3)
-    states_all, terms, dec_ffn = sync(states_all, terms, dec_ffn)
+    states_all, dec_ffn = sync(states_all, dec_ffn)
     states_all.append(swap(states_all[2], "head", 1))
+    states_all, dec_ffn = sync(states_all, dec_ffn)
     after_self, fourth, queries, w_cross_query, w_cross_output = decoder_queries(
-        info, dec_in, terms, decoder_gains, w_cross_qo
-    )
-    states_all, queries, dec_ffn = sync(states_all, queries, dec_ffn)
-
-    key_vals, stats = cross_forward(info, states_all, w_cross, queries, question, count_pass)
+        info,
+        dec_in,
+        [mine, *riders(states_all)],
+        decoder_gains,
+        ffn,
+        at_cross + 2 * size,
+        size,
+    )
+
     dec_ffn = fetch_step(dec_ffn, -4)
+    key_vals, stats, w_cross = cross_forward(
+        info, states_all, ffn, at_cross, queries, question, count_q, count_pass
+    )
     bits = [1 << k for k in range((blk_count - 1).bit_length())]
+    last_two = (bits[-2], bits[-1], bits[-2] + bits[-1])
+    for k in bits[:-2]:
+        stats = merge(info, stats, swap(stats, "blk", k), k)
     stats, dec_ffn = sync(stats, dec_ffn)
+    stats_all = [stats, *(swap(stats, "blk", k) for k in last_two)]
     w_dec_inner, w_dec_outer, outer_back = decoder_back(info, cotangent, in_turn(dec_ffn))
-    for k in bits:
-        stats = merge(info, stats, swap(stats, "blk", k), k)
-        if k == bits[0]:
-            stats, outer_back = sync(stats, outer_back)
-    out, log_total, cross_context, mine, sent = cross_out(info, stats, w_cross_output)
+    stats_all, outer_back = sync(stats_all, outer_back)
+    out, log_total, cross_context, mine, sent = cross_out(
+        info, stats_all, bits[-2:], w_cross_output
+    )
     after_cross, fifth, dec_active, dec_dinner, mine, sent = decoder_ffn(
         info, after_self, [mine, *share(sent)], outer_back, decoder_gains, w_dec_inner
     )
@@ -1128,64 +1283,41 @@
 
     partial, dqueries, dkey_vals = sync(partial, dqueries, dkey_vals)
     beside = to_core(partial)
+    dqueries = some(dqueries, bits[:-2])
     partial, beside, dkey_vals, dqueries = sync(partial, beside, dkey_vals, dqueries)
     across = to_chip(partial, beside)
-    dqueries = some(dqueries, bits[:1])
-    cross_sum = weight_grads(info, [(states_all, dkey_vals)])[0]
-    partial, beside, across, cross_sum, dqueries = sync(
-        partial, beside, across, cross_sum, dqueries
-    )
+    terms = [dqueries, *(swap(dqueries, "blk", k) for k in last_two)]
+    cross_sum = weight_grads(info, [(states_all, dkey_vals)], cut=False)[0]
+    partial, beside, across, cross_sum, terms = sync(partial, beside, across, cross_sum, terms)
 
     def enter_back(cot, a, b, c):
         grad = cot + a + b + c
         return grad, grad
 
+    dqueries, mine, sent = query_back(info, terms, w_cross_query)
     dstates, dstates_low = by_rows(
         enter_back,
         info,
         [encoder_cotangent.reshape(blocks, part, width), partial[0], beside[0], across],
         [],
         [f32, bf16],
-    )
-    dstates_low, dqueries = sync(dstates_low, dqueries)
-    dstates_all = [dstates_low, swap(dstates_low, "head", 1), swap(dstates_low, "head", 2)]
-    dqueries = some(dqueries, bits[1:]).astype(bf16)
-    dstates_all, dqueries = sync(dstates_all, dqueries)
-    dstates_all.append(swap(dstates_all[2], "head", 1))
-    mine, sent = project_rows(info, dqueries, w_cross_query)
-    dstates_all, sent = sync(dstates_all, sent)
+        riders=sent,
+        kept=False,
+    )
+    dstates_low, cross_sum = sync(dstates_low, cross_sum)
+    dstates_all = spread(dstates_low)
+    dstates_all = sync(*dstates_all)
+    dstates_all = sync(*dstates_all, swap(dstates_all[2], "head", 1))
     dinner, *partial = encoder_ffn_back(info, dstates_all, slope, w_inner, w_outer)
-    terms = [mine, *share(sent)]
-    partial, dinner, terms = sync(partial, dinner, terms)
+    partial, dinner = sync(partial, dinner)
     beside = to_core(partial)
-    partial, beside, dinner = sync(partial, beside, dinner)
+    partial, beside, dinner, dstates_all = sync(partial, beside, dinner, dstates_all)
     across = to_chip(partial, beside)
-    ffn_sums = weight_grads(
-        info, [(second_all, dinner), (dstates_all, active)], [cross_sum]
-    )
-    partial, beside, across, ffn_sums, terms = sync(partial, beside, across, ffn_sums, terms)
-
-    def middle_back(dy, h, a, b, c, g):
-        back, gain_rows = norm_back(h, g[1:2], a + b + c)
-        grad = dy + back
-        return grad, grad, gain_rows
-
-    dhidden, dhidden_low, gain_one = by_rows(
-        middle_back,
-        info,
-        [dstates, hidden, partial[0], beside[0], across],
-        [encoder_gains],
-        [f32, bf16],
-        gain=True,
-    )
-    dhidden_low, ffn_sums, terms = sync(dhidden_low, ffn_sums, terms)
-    dhidden_all = [dhidden_low, swap(dhidden_low, "head", 1), swap(dhidden_low, "head", 2)]
-    ffn_moving = reduce_step(ffn_sums, None, 1)
     dself, dself_low, gain_three, dself_qkv, own_back, sent_back = decoder_self_back(
         info,
         dcross,
         after_self,
-        terms,
+        [mine, *riders(dstates_all)],
         decoder_gains,
         w_self,
         dec_qkv,
@@ -1193,62 +1325,96 @@
         dec_active,
         w_dec_outer,
     )
-    dhidden_all, ffn_moving, sent_back = sync(dhidden_all, ffn_moving, sent_back)
+    ffn_sums = weight_grads(
+        info, [(second_all, dinner), (dstates_all, active)], [cross_sum]
+    )
+    partial, beside, across, ffn_sums, sent_back = sync(
+        partial, beside, across, ffn_sums, sent_back
+    )
+
+    def middle_back(dy, h, a, b, c, g):
+        back, gain_rows = norm_back(h, g[1:2], a + b + c)
+        grad = dy + back
+        return grad, grad, gain_rows
+
+    dhidden, dhidden_low, gain_one = by_rows(
+        middle_back,
+        info,
+        [dstates, hidden, partial[0], beside[0], across],
+        [encoder_gains],
+        [f32, bf16],
+        gain=True,
+        riders=sent_back,
+        kept=False,
+    )
+    dhidden_low, ffn_sums = sync(dhidden_low, ffn_sums)
+    dhidden_all = spread(dhidden_low)
+    ffn_moving = reduce_step(info, (ffn_sums, None, 1))[0]
+    dhidden_all, ffn_moving = sync(dhidden_all, ffn_moving)
     dhidden_all.append(swap(dhidden_all[2], "head", 1))
-    dhidden_all, ffn_moving, sent_back = sync(dhidden_all, ffn_moving, sent_back)
-
+    dhidden_all, ffn_moving = sync(dhidden_all, ffn_moving)
+    terms = [own_back, *riders(dhidden_all, 2)]
+
+    ffn_moving = reduce_step(info, (ffn_sums, ffn_moving, 2))[0]
     partial, sums, gain_zero = encoder_attention_back(
         info, dhidden_all, first_all, qkv, probs, context, w_in, w_out, encoder_gains
     )
-    ffn_moving = reduce_step(ffn_sums, ffn_moving, 2)
-    terms = [own_back, *share(sent_back)]
-    partial, sums, ffn_moving, gain_zero, terms = sync(
-        partial, sums, ffn_moving, gain_zero, terms
-    )
-    moving = reduce_step(sums, None, 1)
+    partial, sums, ffn_moving, gain_zero = sync(partial, sums, ffn_moving, gain_zero)
+    ffn_moving, moving = reduce_step(info, (ffn_sums, ffn_moving, 3), (sums, None, 1))
     beside = to_core(partial)
-    dec_grad, gain_two, dec_states = decoder_ends(
-        info, dec_in, dself, terms, decoder_gains, after_cross
+    dec_grad, dec_states, gains = decoder_ends(
+        info,
+        dec_in,
+        dself,
+        terms,
+        decoder_gains,
+        after_cross,
+        [gain_three, gain_four],
+        [gain_zero, gain_one],
+        dec_own,
+    )
+    gains = gains + swap(gains, "head", 1)
+    (
+        grad_dec_query,
+        grad_dec_key,
+        grad_dec_value,
+        grad_cross_query,
+        grad_dec_inner,
+        grad_dec_outer,
+        grad_dec_output,
+        grad_cross_output,
+    ) = decoder_weight_grads(
+        info,
+        own,
+        [
+            (third, dself_qkv, 3),
+            (fourth, dqueries, 1),
+            (fifth, dec_dinner, 1),
+            (cotangent, dec_active, 1),
+        ],
+        [(dec_context, dself_low), (cross_context, dcross_low)],
+    )
+    partial, beside, moving, gains, ffn_moving, grad_dec_query = sync(
+        partial, beside, moving, gains, ffn_moving, grad_dec_query
     )
 
     def own_rows(values):
         return lax.dynamic_slice_in_dim(values, head * dec_own, dec_own, 0)
 
-    leading = (blk == 0).astype(f32)
-    dec_gains = [
-        jnp.sum(own_rows(g), axis=0, keepdims=True) * leading
-        for g in (gain_two, gain_three, gain_four)
-    ]
-    gains = jnp.concatenate([gain_zero, gain_one, *dec_gains], axis=0)
-    gains = gains + swap(gains, "head", 1)
-    partial, beside, moving, gains, ffn_moving = sync(partial, beside, moving, gains, ffn_moving)
+    ffn_moving, moving = reduce_step(info, (ffn_sums, ffn_moving, 4), (sums, moving, 2))
     across = to_chip(partial, beside)
-    moving = reduce_step(sums, moving, 2)
-    ffn_moving = reduce_step(ffn_sums, ffn_moving, 3)
     gains = gains + swap(gains, "head", 2)
-    (
-        grad_dec_qkv,
-        grad_cross_query,
-        grad_dec_inner,
-        grad_dec_output,
-        grad_cross_output,
-        grad_dec_outer,
-    ) = decoder_weight_grads(
-        info,
-        own,
-        [(third, dself_qkv), (fourth, dqueries), (fifth, dec_dinner)],
-        [(dec_context, dself_low), (cross_context, dcross_low), (dec_active, cotangent)],
-    )
-    partial, beside, across, moving, gains, ffn_moving = sync(
-        partial, beside, across, moving, gains, ffn_moving
+    gains = some(gains, bits[:1])
+    dec_states, dec_grad = own_rows(dec_states), own_rows(dec_grad)
+    partial, beside, across, moving, gains, ffn_moving, dec_states, dec_grad = sync(
+        partial, beside, across, moving, gains, ffn_moving, dec_states, dec_grad
     )
 
     def last_back(dh, x, a, b, c, g):
         return (dh + norm_back(x, g[0:1], a + b + c)[0],)
 
-    moving = reduce_step(sums, moving, 3)
-    ffn_moving = reduce_step(ffn_sums, ffn_moving, 4)
-    gains = some(gains, bits[:1])
+    moving = reduce_step(info, (sums, moving, 3))[0]
+    gains = some(gains, bits[1:-1])
     input_grad = by_rows(
         last_back,
         info,
@@ -1256,21 +1422,22 @@
         [encoder_gains],
         [f32],
     )[0]
-    moving, ffn_moving, gains = sync(moving, ffn_moving, gains)
-    moving = reduce_step(sums, moving, 4)
-    gains = some(gains, bits[1:])
-    grad_cross_key, grad_cross_value, grad_inner, grad_outer = finish(
+    grad_inner, grad_outer, grad_cross_key, grad_cross_value = finish(
         info,
         reduce_terms(ffn_sums, ffn_moving),
-        (size, size, units, units),
-        (False, False, False, True),
-    )
+        (units, units, size, size),
+        (False,) * 4,
+    )
+    moving, gains, input_grad, grad_inner = sync(moving, gains, input_grad, grad_inner)
+    moving = reduce_step(info, (sums, moving, 4))[0]
+    last = swap(gains, "blk", bits[-1])
+    enc_gain_grads, dec_gain_grads = gains[:2] + last[:2], gains[2:] + last[2:]
     grad_query, grad_key, grad_value, grad_output = finish(
         info, reduce_terms(sums, moving), (size,) * 4, (False, False, False, True)
     )
 
     def dec_shape(values):
-        return own_rows(values).reshape(count_q, dec_part, width)
+        return values.reshape(count_q, dec_part, width)
 
     return (
         states.reshape(encoder_input.shape),
@@ -1282,19 +1449,19 @@
         grad_value,
         grad_output,
         grad_inner,
-        grad_outer,
-        grad_dec_qkv[:, :size],
-        grad_dec_qkv[:, size : 2 * size],
-        grad_dec_qkv[:, 2 * size :],
+        grad_outer.T,
+        grad_dec_query,
+        grad_dec_key,
+        grad_dec_value,
         grad_dec_output,
         grad_cross_query,
         grad_cross_key,
         grad_cross_value,
         grad_cross_output,
         grad_dec_inner,
-        grad_dec_outer,
-        gains[:2],
-        gains[2:],
+        grad_dec_outer.T,
+        enc_gain_grads,
+        dec_gain_grads,
     )
 
 

time: 359 us -> 344 us (0.958)
  local copies, waits for them, and re-layouts: 26.4 us -> 12.3 us
  between operations: 15.3 us -> 1.84 us
  Pallas kernels: 105 us -> 116 us
  waiting for transfers between devices: 125 us -> 134 us
  other arithmetic: 8.33 us -> 3.48 us
    ppermute x56 -> x49, waiting for transfers between devices: 60.9 us -> 77.7 us  [swap(): return lax.ppermute(value, axis, [(i, i ^ bits) for i in range(size)])]
    ppermute x21, waiting for transfers between devices: 50.6 us -> 38 us  [fetch_step(): lax.ppermute(pieces[k + 1 if k < 0 else k - 1], 'blk', forth if k < 0 els...]
    pallas_call x28 -> x31, Pallas kernels: 105 us -> 116 us  [call(): pl.pallas_call(split, grid=(steps,), in_specs=[pl.BlockSpec(memory_space=...]
    unnamed x197 -> x169, local copies, waits for them, and re-layouts: 16.8 us -> 9.6 us
    ppermute x14 -> x11, waiting for transfers between devices: 13.6 us -> 18.3 us  [reduce_step(): lax.ppermute(v, 'blk', way)]
    convert_element_type x11 -> x0, other arithmetic: 4.63 us -> none  [the longest x10 4.62 us: add_low(): return (a.astype(f32) + b.astype(f32)).astype(bf16)]
    ppermute x14 -> x11, starting transfers between devices: 14.8 us -> 11.5 us  [reduce_step(): lax.ppermute(v, 'blk', way)]
    ppermute x56 -> x49, starting transfers between devices: 34.3 us -> 35.2 us  [swap(): return lax.ppermute(value, axis, [(i, i ^ bits) for i in range(size)])]
  transfers between devices with their start and end apart: 92 -> 81, of which waited for: 45 -> 47; matrix products, arithmetic and copies ran while one was open for 6% -> 2% of each run, Pallas kernels for 24% -> 24%
where the time goes in v3:
time: 344 us; the launch traced here: 342 us
  waiting for transfers between devices  134 us (39%)
  Pallas kernels  116 us (34%)
  starting transfers between devices  69.3 us (20%)
  local copies, waits for them, and re-layouts  12.3 us (4%)
  blocking collectives  5.4 us (2%)
  other arithmetic  3.48 us (1%)
    pallas_call x31, Pallas kernels, call(): pl.pallas_call(split, grid=(steps,), in_specs=[pl.BlockSpec(memory_space=...  116 us
    ppermute x49, waiting for transfers between devices, swap(): return lax.ppermute(value, axis, [(i, i ^ bits) for i in range(size)])  77.7 us
    ppermute x21, waiting for transfers between devices, fetch_step(): lax.ppermute(pieces[k + 1 if k < 0 else k - 1], 'blk', forth if k < 0 els...  38 us
    ppermute x49, starting transfers between devices, swap(): return lax.ppermute(value, axis, [(i, i ^ bits) for i in range(size)])  35.2 us
    ppermute x21, starting transfers between devices, fetch_step(): lax.ppermute(pieces[k + 1 if k < 0 else k - 1], 'blk', forth if k < 0 els...  22.6 us
    ppermute x11, waiting for transfers between devices, reduce_step(): lax.ppermute(v, 'blk', way)  18.3 us
    ppermute x11, starting transfers between devices, reduce_step(): lax.ppermute(v, 'blk', way)  11.5 us
    unnamed x169, local copies, waits for them, and re-layouts  9.6 us
  transfers between devices with their start and end apart: 81, of which 47 were waited for; matrix products, arithmetic and copies ran while one was open for 2% of the time, Pallas kernels for 24%

profile of v3, /device:TPU:0, one launch (start us, length us, event | category | flops | bytes accessed | tf_op | source)
XLA Modules:
  0.0 342.1 jit_solution(16263977927665309145)
XLA Ops:
  24.8 5.4 %all_gather.3 = bf16[2,40,768]{2,0,1:T(2,128)(2,1)S(1)} all-gather(bf16[2,10,768]{2,0,1:T(2,128)(2,1)S(1)} %copy.68), channel_id=1, replica_groups=mesh['blk'=8,'head'=4] {'head'}, dimensions={1}, use_global_device_ids=true | all-gather | bytes 153600 | tf_op jit(solution)/shard_map/all_gather | solution.py:1147
  32.4 4.8 %collective-permute-done.9.refs_11_ = bf16[96,768]{1,0:T(8,128)(2,1)S(1)} collective-permute-done((bf16[96,768]{1,0:T(8,128)(2,1)S(1)}, bf16[96,768]{1,0:T(8,128)(2,1)S(1)}, u32[]{:S(2)}, u32[]{:S(2)}) %collective-permute-start.9) | collective-permute-done | bytes 147488 | tf_op jit(solution)/shard_map/ppermute | solution.py:75
  37.2 8.7 %collective-permute-done.10.refs_6_.refs_8_ = bf16[96,3072]{1,0:T(8,128)(2,1)S(1)} collective-permute-done((bf16[96,3072]{1,0:T(8,128)(2,1)S(1)}, bf16[96,3072]{1,0:T(8,128)(2,1)S(1)}, u32[]{:S(2)}, u32[]{:S(2)}) %collective-permute-start.10) | collective-permute-done | bytes 589856 | tf_op jit(solution)/shard_map/ppermute | solution.py:75
  47.9 10.0 %shard_map.427 = (bf16[4,256,576]{2,1,0:T(8,128)(2,1)}, bf16[4,3,256,256]{3,2,1,0:T(8,128)(2,1)}, bf16[4,256,192]{2,1,0:T(8,128)(2,1)}, f32[4,64,768]{2,1,0:T(8,...) custom-call(s32[14]{0:T(128)S(1)} %pad_add_fusion.info_ref, ...), custom_call_target="tpu_custom_call" | custom-call | flops 2013265920 | bytes 9437184 | tf_op jit(solution)/shard_map/pallas_call | solution.py:280
  67.9 9.1 %collective-permute-done.15.refs_3_ = bf16[4,64,768]{2,1,0:T(8,128)(2,1)S(1)} collective-permute-done((bf16[4,64,768]{2,1,0:T(8,128)(2,1)S(1)}, bf16[4,64,768]{2,1,0:T(8,128)(2,1)S(1)}, u32[]{:S(2)}, u32[]{:S(2)}) %collective-permute-start.15) | collective-permute-done | bytes 393248 | tf_op jit(solution)/shard_map/ppermute | solution.py:27
  86.0 9.8 %collective-permute-done.19.refs_2_ = bf16[4,64,768]{2,1,0:T(8,128)(2,1)S(1)} collective-permute-done((bf16[4,64,768]{2,1,0:T(8,128)(2,1)S(1)}, bf16[4,64,768]{2,1,0:T(8,128)(2,1)S(1)}, u32[]{:S(2)}, u32[]{:S(2)}) %collective-permute-start.19) | collective-permute-done | bytes 393248 | tf_op jit(solution)/shard_map/ppermute | solution.py:27
  101.5 8.9 %shard_map.429 = (bf16[4,256,768]{2,1,0:T(8,128)(2,1)}, bf16[4,256,768]{2,1,0:T(8,128)(2,1)}, f32[4,64,768]{2,1,0:T(8,128)S(1)}, bf16[4,64,768]{2,1,0:T(8,128)(2...) custom-call(s32[14]{0:T(128)S(1)} %pad_add_fusion.info_ref, ...), custom_call_target="tpu_custom_call" | custom-call | flops 2415919104 | bytes 14155776 | tf_op jit(solution)/shard_map/pallas_call | solution.py:280
  116.6 4.0 %shard_map.430 = (bf16[48,768]{1,0:T(8,128)(2,1)}, bf16[48,576]{1,0:T(8,128)(2,1)}, f32[3,48,48]{2,1,0:T(8,128)}, bf16[48,192]{1,0:T(8,128)(2,1)}, f32[48,768]{1...) custom-call(s32[14]{0:T(128)S(1)} %pad_add_fusion.info_ref, ...), custom_call_target="tpu_custom_call" | custom-call | flops 56623104 | bytes 6377856 | tf_op jit(solution)/shard_map/pallas_call | solution.py:280
  130.4 7.0 %collective-permute-done.32.refs_6_ = bf16[96,1536]{1,0:T(8,128)(2,1)S(1)} collective-permute-done((bf16[96,1536]{1,0:T(8,128)(2,1)S(1)}, bf16[96,1536]{1,0:T(8,128)(2,1)S(1)}, u32[]{:S(2)}, u32[]{:S(2)}) %collective-permute-start.32) | collective-permute-done | bytes 294944 | tf_op jit(solution)/shard_map/ppermute | solution.py:75
  146.3 6.8 %shard_map.433 = (bf16[4,256,384]{2,1,0:T(8,128)(2,1)}, f32[48,384]{1,0:T(8,128)S(1)}, bf16[768,384]{1,0:T(8,128)(2,1)}) custom-call(s32[14]{0:T(128)S(1)} %pad_add_fusion.info_ref, bf16[5,64,768]{2,1,0:T(8,128)(2,1)} %copy-done.13, bf16[5,64,768]{2,1,0:T(8,128)(2,1)} %copy-done, bf16[5,64,768]{2,1,0:T(8,128)(2,1)} %copy-done.1, ...), custom_call_target="tpu_custom_call" | custom-call | flops 603979776 | bytes 8153280 | tf_op jit(solution)/shard_map/pallas_call | solution.py:280
  154.1 3.5 %collective-permute-done.35.refs_1_ = f32[48,384]{1,0:T(8,128)S(1)} collective-permute-done((f32[48,384]{1,0:T(8,128)S(1)}, f32[48,384]{1,0:T(8,128)S(1)}, u32[]{:S(2)}, u32[]{:S(2)}) %collective-permute-start.35) | collective-permute-done | bytes 73760 | tf_op jit(solution)/shard_map/ppermute | solution.py:27
  159.4 3.4 %collective-permute-start.39 = (f32[48,384]{1,0:T(8,128)S(1)}, f32[48,384]{1,0:T(8,128)S(1)}, u32[]{:S(2)}, u32[]{:S(2)}) collective-permute-start(f32[48,384]{1,0:T(8,128)S(1)} %shard_map.434.refs_0_), channel_id=1, source_target_pairs={{0,24},{4,28},{8,16},{12,20},{16,8},{20,12},{24,0},{28,4},{1,25},{... | collective-permute-start | bytes 221192 | tf_op jit(solution)/shard_map/ppermute | solution.py:27
  162.8 3.8 %shard_map.435 = (bf16[768,768]{1,0:T(8,128)(2,1)}, bf16[768,768]{1,0:T(8,128)(2,1)}, f32[48,768]{1,0:T(8,128)S(1)}) custom-call(s32[14]{0:T(128)S(1)} %pad_add_fusion.info_ref, bf16[48,768]{1,0:T(8,128)(2,1)S(1)} %get-tuple-element.902.refs_0_.refs_1_.refs_6_, bf16[96,1536]{1,0:T(8,128)(2,1)} %copy-done.57, bf16[96,1536]{1,0:T(8,128)(2,1)} %copy-done.58, ...), custom_call_target="tpu_custom_call" | custom-call | flops 56623104 | bytes 4939776 | tf_op jit(solution)/shard_map/pallas_call | solution.py:280
  183.9 7.8 %shard_map.438 = (bf16[4,256,384]{2,1,0:T(8,128)(2,1)}, f32[4,64,768]{2,1,0:T(8,128)S(1)}, bf16[4,64,768]{2,1,0:T(8,128)(2,1)S(1)}, f32[4,64,768]{2,1,0:T(8,128)...) custom-call(s32[14]{0:T(128)S(1)} %pad_add_fusion.info_ref, ...), custom_call_target="tpu_custom_call" | custom-call | flops 603979776 | bytes 5901504 | tf_op jit(solution)/shard_map/pallas_call | solution.py:280
  201.9 4.8 %shard_map.439.refs_10_ = f32[768,384]{1,0:T(8,128)} custom-call(s32[14]{0:T(128)S(1)} %pad_add_fusion.info_ref, bf16[5,64,768]{2,1,0:T(8,128)(2,1)} %copy-done.13, bf16[5,64,768]{2,1,0:T(8,128)(2,1)} %copy-done, bf16[5,64,768]{2,1,0:T(8,128)(2,1)} %copy-done.1, bf16[5,64,768]{2,1,0:T(8,128)(2,1)} %copy-done.2, bf16[4,256,384]{2,1,0:T(8,128)(2,1)} %get-tuple-element.640.refs_4_), custom_call_target="tpu_custom_call" | custom-call | flops 603979776 | bytes 3932160 | tf_op jit(solution)/shard_map/pallas_call | solution.py:280
  211.2 11.8 %collective-permute-done.54.refs_2_.refs_7_.refs_4_ = bf16[5,64,768]{2,1,0:T(8,128)(2,1)S(1)} collective-permute-done((bf16[5,64,768]{2,1,0:T(8,128)(2,1)S(1)}, bf16[5,64,768]{2,1,0:T(8,128)(2,1)S(1)}, u32[]{:S(2)}, u32[]{:S(2)}) %collective-permute-start.54) | collective-permute-done | bytes 491552 | tf_op jit(solution)/shard_map/ppermute | solution.py:27
  225.6 6.5 %shard_map.442 = (bf16[4,256,768]{2,1,0:T(8,128)(2,1)}, f32[4,64,768]{2,1,0:T(8,128)S(1)}, bf16[4,64,768]{2,1,0:T(8,128)(2,1)S(1)}, f32[4,64,768]{2,1,0:T(8,128)S(1)}, bf16[4,64,768]{2,1,0:T(8,128)(2,1)S(1)}) custom-call(s32[14]{0:T(128)S(1)} %pad_add_fusion.info_ref, bf16[5,64,768]{2,1,0:T(8,128)(2,1)} %copy-done.47, bf16[5,64,768]{2,1,0:T(8,128)(2,1)} %copy-done.15, ...), custom_call_target="tpu_custom_call" | custom-call | flops 2415919104 | bytes 9830400 | tf_op jit(solution)/shard_map/pallas_call | solution.py:280
  235.9 4.2 %shard_map.444 = (f32[48,768]{1,0:T(8,128)S(1)}, bf16[48,768]{1,0:T(8,128)(2,1)}, f32[48,768]{1,0:T(8,128)S(1)}, bf16[48,576]{1,0:T(8,128)(2,1)}, f32[96,768]{1,0:T(8,128)}, /*index=5*/bf16[96,768]{1,0:T(8,128)(2,1)S(1)}) custom-call(s32[14]{0:T(128)S(1)} %pad_add_fusion.info_ref, f32[48,768]{1,0:T(8,128)S(1)} %copy-done.31, ...), custom_call_target="tpu_custom_call" | custom-call | flops 113246208 | bytes 4128768 | tf_op jit(solution)/shard_map/pallas_call | solution.py:280
  240.1 10.7 %shard_map.443 = (f32[96,1920]{1,0:T(8,128)}, bf16[96,1920]{1,0:T(8,128)(2,1)}, bf16[96,1920]{1,0:T(8,128)(2,1)}, bf16[96,1920]{1,0:T(8,128)(2,1)}, bf16[96,1920...) custom-call(s32[14]{0:T(128)S(1)} %pad_add_fusion.info_ref, ...), custom_call_target="tpu_custom_call" | custom-call | flops 2415919104 | bytes 11182080 | tf_op jit(solution)/shard_map/pallas_call | solution.py:280
  255.6 8.6 %collective-permute-done.61.refs_0_ = bf16[96,1920]{1,0:T(8,128)(2,1)S(1)} collective-permute-done((bf16[96,1920]{1,0:T(8,128)(2,1)S(1)}, bf16[96,1920]{1,0:T(8,128)(2,1)S(1)}, u32[]{:S(2)}, u32[]{:S(2)}) %collective-permute-start.61) | collective-permute-done | bytes 368672 | tf_op jit(solution)/shard_map/ppermute | solution.py:138
  273.2 13.9 %shard_map.446 = (f32[4,64,768]{2,1,0:T(8,128)S(1)}, bf16[4,64,768]{2,1,0:T(8,128)(2,1)S(1)}, f32[4,64,768]{2,1,0:T(8,128)S(1)}, bf16[4,64,768]{2,1,0:T(8,128)(2...) custom-call(s32[14]{0:T(128)S(1)} %pad_add_fusion.info_ref, ...), custom_call_target="tpu_custom_call" | custom-call | flops 4429185024 | bytes 11953152 | tf_op jit(solution)/shard_map/pallas_call | solution.py:280
  297.3 5.9 %collective-permute-done.68.refs_0_.refs_2_ = bf16[96,2688]{1,0:T(8,128)(2,1)S(1)} collective-permute-done((bf16[96,2688]{1,0:T(8,128)(2,1)S(1)}, bf16[96,2688]{1,0:T(8,128)(2,1)S(1)}, u32[]{:S(2)}, u32[]{:S(2)}) %collective-permute-start.68) | collective-permute-done | bytes 516128 | tf_op jit(solution)/shard_map/ppermute | solution.py:138
  310.5 6.6 %collective-permute-done.74 = f32[5,768]{1,0:T(8,128)S(1)} collective-permute-done((f32[5,768]{1,0:T(8,128)S(1)}, f32[5,768]{1,0:T(8,128)S(1)}, u32[]{:S(2)}, u32[]{:S(2)}) %collective-permute-start.74) | collective-permute-done | bytes 15392 | tf_op jit(solution)/shard_map/ppermute | solution.py:27
  328.3 3.6 %shard_map.453 = f32[4,64,768]{2,1,0:T(8,128)} custom-call(s32[14]{0:T(128)S(1)} %pad_add_fusion.info_ref, f32[4,64,768]{2,1,0:T(8,128)S(1)} %get-tuple-element.805.refs_0_, bf16[4,64,768]{2,1,0:T(8,128)(2,1)S(1)} %bitcast.21, f32[4,64,768]{2,1,0:T(8,128)S(1)} %get-tuple-element.806.refs_2_, bf16[4,64,768]{2,1,0:T(8,128)(2,1)S(1)} %collective-permute-done.66.refs_3_, ...), custom_call_target="tpu_custom_call" | custom-call | flops 1966080 | bytes 3545088 | tf_op jit(solution)/shard_map/pallas_call | solution.py:280
  (368 shorter events, 170.5 us)
Async XLA Ops:
  11.0 11.5 %collective-permute-start.5 = (bf16[4,64,768]{2,1,0:T(8,128)(2,1)S(1)}, bf16[4,64,768]{2,1,0:T(8,128)(2,1)S(1)}, u32[]{:S(2)}, u32[]{:S(2)}) collective-permute-start(bf16[4,64,768]{2,1,0:T(8,128)(2,1)S(1)} %shard_map.426.refs_0_.refs_4_), channel_id=1, source_target_pairs={{0,2},{1,3},{2,0},{3,1},{4,6},{5,7},{6,4},{7,5},{8,10},{9,11},{10,... | collective-permute-start | bytes 1179656 | tf_op jit(solution)/shard_map/ppermute | solution.py:27
  30.3 15.6 %collective-permute-start.10 = (bf16[96,3072]{1,0:T(8,128)(2,1)S(1)}, bf16[96,3072]{1,0:T(8,128)(2,1)S(1)}, u32[]{:S(2)}, u32[]{:S(2)}) collective-permute-start(bf16[96,3072]{1,0:T(8,128)(2,1)S(1)} %concatenate.15.refs_4_.refs_6_), channel_id=1, source_target_pairs={{8,0},{16,8},{24,16},{28,24},{20,28},{12,20},{4,12},{0,4},{9,1},{1... | collective-permute-start | bytes 1769480 | tf_op jit(solution)/shard_map/ppermute | solution.py:75
  45.9 14.8 %collective-permute-start.11 = (bf16[96,3072]{1,0:T(8,128)(2,1)S(1)}, bf16[96,3072]{1,0:T(8,128)(2,1)S(1)}, u32[]{:S(2)}, u32[]{:S(2)}) collective-permute-start(bf16[96,3072]{1,0:T(8,128)(2,1)S(1)} %concatenate.15.refs_4_.refs_6_), channel_id=1, source_target_pairs={{0,8},{8,16},{16,24},{24,28},{28,20},{20,12},{12,4},{4,0},{1,9},{9... | collective-permute-start | bytes 1769480 | tf_op jit(solution)/shard_map/ppermute | solution.py:75
  47.5 14.5 %collective-permute-start.12 = (bf16[96,3072]{1,0:T(8,128)(2,1)S(1)}, bf16[96,3072]{1,0:T(8,128)(2,1)S(1)}, u32[]{:S(2)}, u32[]{:S(2)}) collective-permute-start(bf16[96,3072]{1,0:T(8,128)(2,1)S(1)} %collective-permute-done.10.refs_6_.refs_8_), channel_id=1, source_target_pairs={{8,0},{16,8},{24,16},{28,24},{20,28},{12,20},{4,12},{0,4},{9,1},{1... | collective-permute-start | bytes 1769480 | tf_op jit(solution)/shard_map/ppermute | solution.py:75
  64.2 15.4 %collective-permute-start.16 = (bf16[96,3072]{1,0:T(8,128)(2,1)S(1)}, bf16[96,3072]{1,0:T(8,128)(2,1)S(1)}, u32[]{:S(2)}, u32[]{:S(2)}) collective-permute-start(bf16[96,3072]{1,0:T(8,128)(2,1)S(1)} %collective-permute-done.11.refs_5_.refs_7_), channel_id=1, source_target_pairs={{0,8},{8,16},{16,24},{24,28},{28,20},{20,12},{12,4},{4,0},{1,9},{9... | collective-permute-start | bytes 1769480 | tf_op jit(solution)/shard_map/ppermute | solution.py:75
  65.8 15.1 %collective-permute-start.17 = (bf16[96,3072]{1,0:T(8,128)(2,1)S(1)}, bf16[96,3072]{1,0:T(8,128)(2,1)S(1)}, u32[]{:S(2)}, u32[]{:S(2)}) collective-permute-start(bf16[96,3072]{1,0:T(8,128)(2,1)S(1)} %collective-permute-done.12.refs_8_.refs_10_), channel_id=1, source_target_pairs={{8,0},{16,8},{24,16},{28,24},{20,28},{12,20},{4,12},{0,4},{9,1},{1... | collective-permute-start | bytes 1769480 | tf_op jit(solution)/shard_map/ppermute | solution.py:75
  82.2 14.3 %collective-permute-start.20 = (bf16[96,3072]{1,0:T(8,128)(2,1)S(1)}, bf16[96,3072]{1,0:T(8,128)(2,1)S(1)}, u32[]{:S(2)}, u32[]{:S(2)}) collective-permute-start(bf16[96,3072]{1,0:T(8,128)(2,1)S(1)} %collective-permute-done.16.refs_7_.refs_9_), channel_id=1, source_target_pairs={{0,8},{8,16},{16,24},{24,28},{28,20},{20,12},{12,4},{4,0},{1,9},{9... | collective-permute-start | bytes 1769480 | tf_op jit(solution)/shard_map/ppermute | solution.py:75
  83.7 13.9 %collective-permute-start.21 = (bf16[96,3072]{1,0:T(8,128)(2,1)S(1)}, bf16[96,3072]{1,0:T(8,128)(2,1)S(1)}, u32[]{:S(2)}, u32[]{:S(2)}) collective-permute-start(bf16[96,3072]{1,0:T(8,128)(2,1)S(1)} %collective-permute-done.17.refs_10_.refs_12_), channel_id=1, source_target_pairs={{8,0},{16,8},{24,16},{28,24},{20,28},{12,20},{4,12},{0,4},{9,1},{1... | collective-permute-start | bytes 1769480 | tf_op jit(solution)/shard_map/ppermute | solution.py:75
  84.2 11.5 %collective-permute-start.19 = (bf16[4,64,768]{2,1,0:T(8,128)(2,1)S(1)}, bf16[4,64,768]{2,1,0:T(8,128)(2,1)S(1)}, u32[]{:S(2)}, u32[]{:S(2)}) collective-permute-start(bf16[4,64,768]{2,1,0:T(8,128)(2,1)S(1)} %get-tuple-element.521.refs_0_), channel_id=1, source_target_pairs={{0,2},{1,3},{2,0},{3,1},{4,6},{5,7},{6,4},{7,5},{8,10},{9,11},{10,... | collective-permute-start | bytes 1179656 | tf_op jit(solution)/shard_map/ppermute | solution.py:27
  112.9 11.2 %collective-permute-start.27 = (bf16[4,64,768]{2,1,0:T(8,128)(2,1)S(1)}, bf16[4,64,768]{2,1,0:T(8,128)(2,1)S(1)}, u32[]{:S(2)}, u32[]{:S(2)}) collective-permute-start(bf16[4,64,768]{2,1,0:T(8,128)(2,1)S(1)} %add_convert_fusion.3), channel_id=1, source_target_pairs={{0,2},{1,3},{2,0},{3,1},{4,6},{5,7},{6,4},{7,5},{8,10},{9,11},{10,... | collective-permute-start | bytes 1179656 | tf_op jit(solution)/shard_map/ppermute | solution.py:27
  126.8 11.5 %collective-permute-start.30 = (bf16[5,64,768]{2,1,0:T(8,128)(2,1)S(1)}, bf16[5,64,768]{2,1,0:T(8,128)(2,1)S(1)}, u32[]{:S(2)}, u32[]{:S(2)}) collective-permute-start(bf16[5,64,768]{2,1,0:T(8,128)(2,1)S(1)} %get-tuple-element.583.refs_0_), channel_id=1, source_target_pairs={{0,1},{1,0},{2,3},{3,2},{4,5},{5,4},{6,7},{7,6},{8,9},{9,8},{10,11... | collective-permute-start | bytes 1474568 | tf_op jit(solution)/shard_map/ppermute | solution.py:27
  126.8 13.6 %collective-permute-start.31 = (bf16[5,64,768]{2,1,0:T(8,128)(2,1)S(1)}, bf16[5,64,768]{2,1,0:T(8,128)(2,1)S(1)}, u32[]{:S(2)}, u32[]{:S(2)}) collective-permute-start(bf16[5,64,768]{2,1,0:T(8,128)(2,1)S(1)} %get-tuple-element.583.refs_0_), channel_id=1, source_target_pairs={{0,2},{1,3},{2,0},{3,1},{4,6},{5,7},{6,4},{7,5},{8,10},{9,11},{10,... | collective-permute-start | bytes 1474568 | tf_op jit(solution)/shard_map/ppermute | solution.py:27
  142.3 16.1 %collective-permute-start.36 = (bf16[96,1536]{1,0:T(8,128)(2,1)S(1)}, bf16[96,1536]{1,0:T(8,128)(2,1)S(1)}, u32[]{:S(2)}, u32[]{:S(2)}) collective-permute-start(bf16[96,1536]{1,0:T(8,128)(2,1)S(1)} %collective-permute-done.32.refs_6_), channel_id=1, source_target_pairs={{0,8},{8,16},{16,24},{24,28},{28,20},{20,12},{12,4},{4,0},{1,9},{9... | collective-permute-start | bytes 884744 | tf_op jit(solution)/shard_map/ppermute | solution.py:75
  209.4 13.6 %collective-permute-start.54 = (bf16[5,64,768]{2,1,0:T(8,128)(2,1)S(1)}, bf16[5,64,768]{2,1,0:T(8,128)(2,1)S(1)}, u32[]{:S(2)}, u32[]{:S(2)}) collective-permute-start(bf16[5,64,768]{2,1,0:T(8,128)(2,1)S(1)} %get-tuple-element.680.refs_0_.refs_5_), channel_id=1, source_target_pairs={{0,2},{1,3},{2,0},{3,1},{4,6},{5,7},{6,4},{7,5},{8,10},{9,11},{10,... | collective-permute-start | bytes 1474568 | tf_op jit(solution)/shard_map/ppermute | solution.py:27
  234.6 16.2 %collective-permute-start.58 = (bf16[4,64,768]{2,1,0:T(8,128)(2,1)S(1)}, bf16[4,64,768]{2,1,0:T(8,128)(2,1)S(1)}, u32[]{:S(2)}, u32[]{:S(2)}) collective-permute-start(bf16[4,64,768]{2,1,0:T(8,128)(2,1)S(1)} %add_convert_fusion.1), channel_id=1, source_target_pairs={{0,2},{1,3},{2,0},{3,1},{4,6},{5,7},{6,4},{7,5},{8,10},{9,11},{10,... | collective-permute-start | bytes 1179656 | tf_op jit(solution)/shard_map/ppermute | solution.py:27
  252.5 12.6 %collective-permute-start.59 = (bf16[6,64,768]{2,1,0:T(8,128)(2,1)S(1)}, bf16[6,64,768]{2,1,0:T(8,128)(2,1)S(1)}, u32[]{:S(2)}, u32[]{:S(2)}) collective-permute-start(bf16[6,64,768]{2,1,0:T(8,128)(2,1)S(1)} %get-tuple-element.723.refs_0_), channel_id=1, source_target_pairs={{0,1},{1,0},{2,3},{3,2},{4,5},{5,4},{6,7},{7,6},{8,9},{9,8},{10,11... | collective-permute-start | bytes 1769480 | tf_op jit(solution)/shard_map/ppermute | solution.py:27
  252.6 15.7 %collective-permute-start.60 = (bf16[6,64,768]{2,1,0:T(8,128)(2,1)S(1)}, bf16[6,64,768]{2,1,0:T(8,128)(2,1)S(1)}, u32[]{:S(2)}, u32[]{:S(2)}) collective-permute-start(bf16[6,64,768]{2,1,0:T(8,128)(2,1)S(1)} %get-tuple-element.723.refs_0_), channel_id=1, source_target_pairs={{0,2},{1,3},{2,0},{3,1},{4,6},{5,7},{6,4},{7,5},{8,10},{9,11},{10,... | collective-permute-start | bytes 1769480 | tf_op jit(solution)/shard_map/ppermute | solution.py:27
  271.1 16.1 %collective-permute-start.64 = (bf16[96,1920]{1,0:T(8,128)(2,1)S(1)}, bf16[96,1920]{1,0:T(8,128)(2,1)S(1)}, u32[]{:S(2)}, u32[]{:S(2)}) collective-permute-start(bf16[96,1920]{1,0:T(8,128)(2,1)S(1)} %get-tuple-element.748), channel_id=1, source_target_pairs={{0,8},{8,16},{16,24},{24,28},{28,20},{20,12},{12,4},{4,0},{1,9},{9... | collective-permute-start | bytes 1105928 | tf_op jit(solution)/shard_map/ppermute | solution.py:138
  272.4 14.8 %collective-permute-start.65 = (bf16[96,1920]{1,0:T(8,128)(2,1)S(1)}, bf16[96,1920]{1,0:T(8,128)(2,1)S(1)}, u32[]{:S(2)}, u32[]{:S(2)}) collective-permute-start(bf16[96,1920]{1,0:T(8,128)(2,1)S(1)} %get-tuple-element.749), channel_id=1, source_target_pairs={{8,0},{16,8},{24,16},{28,24},{20,28},{12,20},{4,12},{0,4},{9,1},{1... | collective-permute-start | bytes 1105928 | tf_op jit(solution)/shard_map/ppermute | solution.py:138
  289.9 13.3 %collective-permute-start.68 = (bf16[96,2688]{1,0:T(8,128)(2,1)S(1)}, bf16[96,2688]{1,0:T(8,128)(2,1)S(1)}, u32[]{:S(2)}, u32[]{:S(2)}) collective-permute-start(bf16[96,2688]{1,0:T(8,128)(2,1)S(1)} %get-tuple-element.761), channel_id=1, source_target_pairs={{0,8},{8,16},{16,24},{24,28},{28,20},{20,12},{12,4},{4,0},{1,9},{9... | collective-permute-start | bytes 1548296 | tf_op jit(solution)/shard_map/ppermute | solution.py:138
  291.1 13.0 %collective-permute-start.69 = (bf16[96,2688]{1,0:T(8,128)(2,1)S(1)}, bf16[96,2688]{1,0:T(8,128)(2,1)S(1)}, u32[]{:S(2)}, u32[]{:S(2)}) collective-permute-start(bf16[96,2688]{1,0:T(8,128)(2,1)S(1)} %get-tuple-element.762), channel_id=1, source_target_pairs={{8,0},{16,8},{24,16},{28,24},{20,28},{12,20},{4,12},{0,4},{9,1},{1... | collective-permute-start | bytes 1548296 | tf_op jit(solution)/shard_map/ppermute | solution.py:138
  305.6 15.4 %collective-permute-start.72 = (bf16[96,2688]{1,0:T(8,128)(2,1)}, bf16[96,2688]{1,0:T(8,128)(2,1)S(1)}, u32[]{:S(2)}, u32[]{:S(2)}) collective-permute-start(bf16[96,2688]{1,0:T(8,128)(2,1)} %get-tuple-element.791), channel_id=1, source_target_pairs={{0,8},{8,16},{16,24},{24,28},{28,20},{20,12},{12,4},{4,0},{1,9},{9... | collective-permute-start | bytes 1548296 | tf_op jit(solution)/shard_map/ppermute | solution.py:138
  307.0 14.0 %collective-permute-start.71 = (bf16[4,64,768]{2,1,0:T(8,128)(2,1)}, bf16[4,64,768]{2,1,0:T(8,128)(2,1)}, u32[]{:S(2)}, u32[]{:S(2)}) collective-permute-start(bf16[4,64,768]{2,1,0:T(8,128)(2,1)} %add_convert_fusion), channel_id=1, source_target_pairs={{0,2},{1,3},{2,0},{3,1},{4,6},{5,7},{6,4},{7,5},{8,10},{9,11},{10,... | collective-permute-start | bytes 1179656 | tf_op jit(solution)/shard_map/ppermute | solution.py:27
  307.8 13.2 %collective-permute-start.73 = (bf16[96,768]{1,0:T(8,128)(2,1)S(1)}, bf16[96,768]{1,0:T(8,128)(2,1)S(1)}, u32[]{:S(2)}, u32[]{:S(2)}) collective-permute-start(bf16[96,768]{1,0:T(8,128)(2,1)S(1)} %get-tuple-element.792), channel_id=1, source_target_pairs={{8,0},{16,8},{24,16},{28,24},{20,28},{12,20},{4,12},{0,4},{9,1},{1... | collective-permute-start | bytes 442376 | tf_op jit(solution)/shard_map/ppermute | solution.py:138
  (138 other events, 1345.6 us)

commit v4 on v3

--- a/solution.py
+++ b/solution.py
@@ -14,7 +14,6 @@
 EPS = 1e-06
 VMEM_LIMIT = 24 * 1024 * 1024
 LARGE = 1 << 18
-RIDERS = 48
 masked_score = -1000000000.0
 f32 = jnp.float32
 bf16 = jnp.bfloat16
@@ -194,6 +193,11 @@
 
 def heads_in(width):
     return [slice(at, at + HDIM) for at in range(0, width, HDIM)]
+
+
+def head_parts(values, count):
+    size = values.shape[1] // count
+    return [[values[:, j * size :][:, at] for at in heads_in(size)] for j in range(count)]
 
 
 def assemble(info, pieces, targets, signals, column_from=0):
@@ -227,13 +231,15 @@
 
 
 def token_rows(refs):
-    return jnp.concatenate([r[0] for r in refs], axis=0)
+    return jnp.concatenate([r[k] for k in range(refs[0].shape[0]) for r in refs], axis=0)
 
 
 def emit(partial, outs):
-    part = outs[0].shape[1]
-    for r, out in enumerate(outs):
-        out[0] = partial[r * part : (r + 1) * part].astype(out.dtype)
+    each, part, _ = outs[0].shape
+    for k in range(each):
+        for r, out in enumerate(outs):
+            at = (k * len(outs) + r) * part
+            out[k] = partial[at : at + part].astype(out.dtype)
 
 
 def slots_used(info, b, part, slot):
@@ -242,12 +248,22 @@
     return position < info[LENGTHS + b]
 
 
+def keys_used(info, question, passages, part, slot, count_pass):
+    return jnp.concatenate(
+        [
+            slots_used(info, k, part, slot) & (question[...] == k // count_pass)
+            for k in passages
+        ],
+        axis=1,
+    )
+
+
 def call(
-    body, info, stepped, fixed, out_stepped, out_fixed, scratch=(), flops=0, steps=1, near=False, least=LARGE
+    body, info, stepped, fixed, out_stepped, out_fixed, scratch=(), flops=0, steps=1, near=False, least=LARGE, each=1
 ):
     def by_step(shape):
-        last = shape[0] - 1
-        return pl.BlockSpec((1, *shape[1:]), lambda b: (jnp.minimum(b, last),) + (0,) * (len(shape) - 1))
+        last = shape[0] // each - 1
+        return pl.BlockSpec((each, *shape[1:]), lambda b: (jnp.minimum(b, last),) + (0,) * (len(shape) - 1))
 
     def whole(a):
         if isinstance(a, Far):
@@ -332,10 +348,10 @@
 
 def by_rows(fn, info, stepped, fixed, dtypes, gain=False, riders=None, kept=True):
     steps, _, width = stepped[0].shape
-    count = 0 if riders is None else riders.shape[0] // RIDERS
+    count = 0 if riders is None else 1
     alone = [like(stepped[0].shape, d) for d in dtypes]
     outs = alone if riders is None or kept else alone[:-1]
-    more = 0 if riders is None else riders.shape[0] // count
+    more = 0 if riders is None else riders.shape[0]
     together = [like((steps + count, *stepped[0].shape[1:]), dtypes[-1])] if more else []
 
     def body(info_ref, ins, whole, outs, sums, _):
@@ -361,11 +377,11 @@
                 def _():
                     total[...] += found
 
-        for k in range(count):
-
-            @pl.when(b == steps + k)
+        if more:
+
+            @pl.when(b == steps)
             def _():
-                outs[-1][0, :more, :] = rows[k * more : (k + 1) * more, :]
+                outs[-1][0, :more, :] = rows[...]
 
     return call(
         body,
@@ -388,16 +404,22 @@
     return [Later(like((rows, columns), d)) for d in (f32, *[bf16] * 7)]
 
 
+def attention_scratch(width, size, pieces):
+    return [
+        *(pltpu.VMEM((width, k * size), bf16) for k in (3, 1, 4)),
+        pltpu.SemaphoreType.DMA((1, len(pieces))),
+    ]
+
+
 def encoder_attention(info, normed, pieces):
     blocks, part, width = normed[0].shape
     slot = part * len(normed)
     size = pieces[0].shape[1] // 4
     count = size // HDIM
 
-    def body(info, rows, pieces, outs, weights, scratch):
+    def body(info, rows, pieces, outs, _, scratch):
         qkv, probs, context = outs[:3]
-        w_in, w_out = weights
-        together, signals = scratch
+        w_in, w_out, together, signals = scratch
         b = pl.program_id(0)
 
         @pl.when(b == 0)
@@ -408,14 +430,16 @@
 
         qkv[0] = dot(token_rows(rows), w_in[...]).astype(bf16)
         allowed = slots_used(info, b, part, slot)
-        for k, at in enumerate(heads_in(size)):
-            query, keys, vals = (qkv[0, :, j * size + at.start : j * size + at.stop] for j in range(3))
-            scores = jnp.where(allowed, dot_t(query * SCALE, keys), masked_score)
+        query, keys, vals = head_parts(qkv[0], 3)
+        found = []
+        for k, scores in enumerate([dot_t(q * SCALE, t) for q, t in zip(query, keys, strict=True)]):
+            scores = jnp.where(allowed, scores, masked_score)
             spread_out = jnp.exp(scores - jnp.max(scores, axis=-1, keepdims=True))
             inverse = 1.0 / jnp.sum(spread_out, axis=-1, keepdims=True)
-            weight = (spread_out * inverse).astype(bf16)
-            probs[0, k] = weight
-            context[0, :, at] = dot(weight, vals).astype(bf16)
+            found.append((spread_out * inverse).astype(bf16))
+            probs[0, k] = found[-1]
+        found = [dot(w, v) for w, v in zip(found, vals, strict=True)]
+        context[0] = jnp.concatenate(found, axis=1).astype(bf16)
         emit(dot_t(context[0], w_out[...]), outs[3:])
 
     return call(
@@ -429,28 +453,31 @@
             like((blocks, slot, size), bf16),
             *partial_rows(blocks, part, width),
         ],
-        [like((width, 3 * size), bf16), like((width, size), bf16)],
-        [pltpu.VMEM((width, 4 * size), bf16), pltpu.SemaphoreType.DMA((1, len(pieces)))],
+        [],
+        attention_scratch(width, size, pieces),
         flops=2 * blocks * slot * (width * size * 4 + 8 * slot * size),
         steps=blocks,
     )
 
 
-def encoder_attention_back(info, grads, normed, qkv, probs, context, w_in, w_out, gains):
+def encoder_attention_back(info, grads, normed, qkv, probs, context, pieces, gains):
     blocks, part, width = normed[0].shape
     slot = part * len(normed)
-    size = w_out.shape[1]
+    size = context.shape[2]
 
     def body(info, stepped, fixed, outs, ends, scratch):
         grad_refs, normed_refs = stepped[:4], stepped[4:8]
         qkv, probs, context = stepped[8:]
-        w_in, w_out, gains = fixed
+        weight_pieces, gains = fixed[:-1], fixed[-1]
         pieces, gain_out = ends[:-1], ends[-1]
-        total_in, total_out, moved = scratch
+        w_in, w_out, together, signals, total_in, total_out, moved = scratch
         b = pl.program_id(0)
 
         @pl.when(b == 0)
         def _():
+            assemble(info, weight_pieces, (together,), signals)
+            w_in[...] = together[:, : 3 * size]
+            w_out[...] = together[:, 3 * size :]
             total_in[...] = jnp.zeros_like(total_in)
             total_out[...] = jnp.zeros_like(total_out)
             gain_out[...] = jnp.zeros_like(gain_out)
@@ -458,20 +485,18 @@
         grad = token_rows(grad_refs)
         rows = token_rows(normed_refs)
         dcontext = dot(grad, w_out[...]).astype(bf16)
-        for k, at in enumerate(heads_in(size)):
-            query, keys, vals = (qkv[0, :, j * size + at.start : j * size + at.stop] for j in range(3))
-            weight = probs[0, k]
-            dprobs = dot_t(dcontext[:, at], vals)
-            wide = weight.astype(f32)
-            dscores = wide * (dprobs - jnp.sum(wide * dprobs, axis=-1, keepdims=True))
-            dscores = dscores.astype(bf16)
-            terms = (
-                dot(dscores, keys) * SCALE,
-                t_dot(dscores, query) * SCALE,
-                t_dot(weight, dcontext[:, at]),
-            )
-            for j, term in enumerate(terms):
-                moved[:, j * size + at.start : j * size + at.stop] = term.astype(bf16)
+        query, keys, vals = head_parts(qkv[0], 3)
+        cuts = head_parts(dcontext, 1)[0]
+        backs = [dot_t(c, v) for c, v in zip(cuts, vals, strict=True)]
+        dvals = [t_dot(probs[0, k], c) for k, c in enumerate(cuts)]
+        lows = []
+        for k, back in enumerate(backs):
+            wide = probs[0, k].astype(f32)
+            low = wide * (back - jnp.sum(wide * back, axis=-1, keepdims=True))
+            lows.append(low.astype(bf16))
+        dquery = [dot(d, t) * SCALE for d, t in zip(lows, keys, strict=True)]
+        dkeys = [t_dot(d, q) * SCALE for d, q in zip(lows, query, strict=True)]
+        moved[...] = jnp.concatenate([*dquery, *dkeys, *dvals], axis=1).astype(bf16)
         partial = dot_t(moved[...], w_in[...])
         emit(partial, outs)
         gain_out[...] += jnp.sum(partial * rows.astype(f32), axis=0, keepdims=True) / gains[0:1, :]
@@ -486,10 +511,11 @@
         body,
         info,
         [*grads, *normed, qkv, probs, context],
-        [w_in, w_out, gains],
+        [*(Far(p) for p in pieces), gains],
         partial_rows(blocks, part, width),
         [*piece_shapes(width // 8, 4 * size), like((1, width), f32)],
         [
+            *attention_scratch(width, size, pieces),
             pltpu.VMEM((width, 3 * size), f32),
             pltpu.VMEM((width, size), f32),
             pltpu.VMEM((slot, 3 * size), bf16),
@@ -500,22 +526,30 @@
     return results[:4], results[4:12], results[12]
 
 
+def ffn_scratch(width, hidden, pieces):
+    return [
+        *[pltpu.VMEM((width, hidden), bf16)] * 2,
+        pltpu.SemaphoreType.DMA((2, len(pieces))),
+    ]
+
+
 def encoder_ffn(info, normed, pieces, hidden):
     blocks, part, width = normed[0].shape
     slot = part * len(normed)
 
-    def body(info, rows, pieces, outs, weights, scratch):
+    def body(info, rows, pieces, outs, _, scratch):
         active, slope = outs[:2]
-        w_inner, w_outer = weights
+        w_inner, w_outer, signals = scratch
 
         @pl.when(pl.program_id(0) == 0)
         def _():
-            assemble(info, pieces, weights, scratch[0])
+            assemble(info, pieces, (w_inner, w_outer), signals)
 
         value, bend = gelu_both(dot(token_rows(rows), w_inner[...]))
-        active[0] = value.astype(bf16)
-        slope[0] = bend.astype(bf16)
-        emit(dot_t(active[0], w_outer[...]), outs[2:])
+        low = value.astype(bf16)
+        active[...] = low.reshape(active.shape)
+        slope[...] = bend.astype(bf16).reshape(slope.shape)
+        emit(dot_t(low, w_outer[...]), outs[2:])
 
     return call(
         body,
@@ -523,34 +557,43 @@
         normed,
         [Far(p) for p in pieces],
         [*[like((blocks, slot, hidden), bf16)] * 2, *partial_rows(blocks, part, width)],
-        [like((width, hidden), bf16)] * 2,
-        [pltpu.SemaphoreType.DMA((2, len(pieces)))],
+        [],
+        ffn_scratch(width, hidden, pieces),
         flops=4 * blocks * slot * width * hidden,
-        steps=blocks,
-    )
-
-
-def encoder_ffn_back(info, grads, slope, w_inner, w_outer):
+        steps=blocks // 2,
+        each=2,
+    )
+
+
+def encoder_ffn_back(info, grads, slope, pieces):
     blocks, (_, part, width) = slope.shape[0], grads[0].shape
     slot = part * len(grads)
-    hidden = w_inner.shape[1]
-
-    def body(info, stepped, weights, outs, ends, _):
+    hidden = slope.shape[2]
+
+    def body(info, stepped, pieces, outs, ends, scratch):
         dinner = outs[0]
-        w_inner, w_outer = weights
+        w_inner, w_outer, signals = scratch
+
+        @pl.when(pl.program_id(0) == 0)
+        def _():
+            assemble(info, pieces, (w_inner, w_outer), signals)
+
         back = dot(token_rows(stepped[:4]), w_outer[...])
-        dinner[0] = (back * stepped[4][0].astype(f32)).astype(bf16)
-        emit(dot_t(dinner[0], w_inner[...]), outs[1:])
+        low = (back * stepped[4][...].reshape(back.shape).astype(f32)).astype(bf16)
+        dinner[...] = low.reshape(dinner.shape)
+        emit(dot_t(low, w_inner[...]), outs[1:])
 
     return call(
         body,
         info,
         [*grads, slope],
-        [w_inner, w_outer],
+        [Far(p) for p in pieces],
         [like((blocks, slot, hidden), bf16), *partial_rows(blocks, part, width)],
         [],
+        ffn_scratch(width, hidden, pieces),
         flops=4 * blocks * slot * width * hidden,
-        steps=blocks,
+        steps=blocks // 2,
+        each=2,
     )
 
 
@@ -559,25 +602,12 @@
     widths = [right.shape[2] for _, right in pairs]
 
     def body(info, stepped, more, __, ends, totals):
-        b = pl.program_id(0)
         totals = totals if cut else ends
         for k, total in enumerate(totals):
-            left, right = stepped[5 * k : 5 * k + 4], stepped[5 * k + 4]
-            found = t_dot(token_rows(left), right[0])
-
-            @pl.when(b == 0)
-            def _():
-                total[...] = found
-
-            @pl.when(b > 0)
-            def _():
-                total[...] += found
-
+            left, right = token_rows(stepped[5 * k : 5 * k + 4]), stepped[5 * k + 4]
+            total[...] = t_dot(left, right[...].reshape(left.shape[0], total.shape[1]))
         if cut:
-
-            @pl.when(b == blocks - 1)
-            def _():
-                hand_out(info, (*totals, *more), ends)
+            hand_out(info, (*totals, *more), ends)
 
     return call(
         body,
@@ -590,7 +620,7 @@
         else [like((width, w), f32) for w in widths],
         [pltpu.VMEM((width, w), f32) for w in widths] if cut else [],
         flops=2 * blocks * part * 4 * width * sum(widths),
-        steps=blocks,
+        each=blocks,
     )
 
 
@@ -612,60 +642,76 @@
     return call(body, info, [], [t.array for t in terms], [], [like(s, f32) for s in shapes])
 
 
-def cross_forward(info, states, pieces, column_from, queries, own_question, count_q, count_pass):
+def cross_forward(info, states, pieces, column_from, decoder, own_question, count_q, count_pass):
+    rows_in, terms, gains = decoder
     blocks = count_q * count_pass
     _, part, width = states[0].shape
     slot = part * len(states)
-    size = queries.shape[1]
-    rows_dec = queries.shape[0]
+    rows_dec = rows_in.shape[0]
+    size = (pieces[0].shape[1] - column_from) // 4
+    steps = 2
 
     def body(info, rows, fixed, outs, ends, scratch):
-        pieces, queries, question = fixed[:-2], fixed[-2], fixed[-1]
-        stats, weight = ends
-        held, signals = scratch
+        pieces, question = fixed[: len(pieces_given)], fixed[-1]
+        rows_in, *terms, gains = fixed[len(pieces_given) : -1]
+        after_self, normed, queries, w_query, w_output, stats, weight = ends
+        held, asked, signals = scratch
         b = pl.program_id(0)
 
         @pl.when(b == 0)
         def _():
-            assemble(info, pieces, (weight,), signals, column_from)
+            assemble(info, pieces, (weight, asked), signals, column_from)
+            w_query[...] = asked[:, :size]
+            w_output[...] = asked[:, size:]
+            after_self[...] = rows_in[...].astype(f32) + summed(terms)
+            normed[...] = norm_rows(after_self[...], gains[1:2, :]).astype(bf16)
+            queries[...] = dot(normed[...], w_query[...]).astype(bf16)
 
         made = dot(token_rows(rows), weight[...]).astype(bf16)
-        outs[0][0] = made
-        held[pl.ds(pl.multiple_of(b * slot, slot), slot), :] = made
-
-        @pl.when(b == blocks - 1)
+        outs[0][...] = made.reshape(outs[0].shape)
+        each = made.shape[0]
+        held[pl.ds(pl.multiple_of(b * each, each), each), :] = made
+
+        @pl.when(b == steps - 1)
         def _():
-            allowed = jnp.concatenate(
-                [
-                    slots_used(info, k, part, slot) & (question[...] == k // count_pass)
-                    for k in range(blocks)
-                ],
-                axis=1,
-            )
+            allowed = keys_used(info, question, range(blocks), part, slot, count_pass)
             lane = lax.broadcasted_iota(jnp.int32, (rows_dec, HDIM), 1)
-            for k, at in enumerate(heads_in(size)):
-                scores = dot_t(queries[:, at], held[:, at]) * SCALE
-                scores = jnp.where(allowed, scores, masked_score)
-                top = jnp.max(scores, axis=-1, keepdims=True)
-                spread_out = jnp.exp(scores - top)
+            keys, vals = head_parts(held[...], 2)
+            asking = head_parts(queries[...], 1)[0]
+            scores = [dot_t(q * SCALE, t) for q, t in zip(asking, keys, strict=True)]
+            for k, score in enumerate(scores):
+                score = jnp.where(allowed, score, masked_score)
+                top = jnp.max(score, axis=-1, keepdims=True)
+                spread_out = jnp.exp(score - top)
                 total = jnp.sum(spread_out, axis=-1, keepdims=True)
-                vals = held[:, size + at.start : size + at.stop]
-                stats[:, k * LANES : k * LANES + HDIM] = dot(spread_out.astype(bf16), vals)
-                stats[:, k * LANES + HDIM : (k + 1) * LANES] = jnp.where(lane == 0, top, total)
-
+                at = k * LANES
+                stats[:, at : at + HDIM] = dot(spread_out.astype(bf16), vals[k])
+                stats[:, at + HDIM : at + LANES] = jnp.where(lane == 0, top, total)
+
+    pieces_given = pieces
     return call(
         body,
         info,
         states,
-        [*(Far(p) for p in pieces), queries, own_question],
+        [*(Far(p) for p in pieces), rows_in, *terms, gains, own_question],
         [like((blocks, slot, 2 * size), bf16)],
-        [like((rows_dec, size // HDIM * LANES), f32), like((width, 2 * size), bf16)],
+        [
+            Later(like((rows_dec, width), f32)),
+            Later(like((rows_dec, width), bf16)),
+            like((rows_dec, size), bf16),
+            Later(like((width, size), bf16)),
+            like((width, size), bf16),
+            like((rows_dec, size // HDIM * LANES), f32),
+            like((width, 2 * size), bf16),
+        ],
         [
             pltpu.VMEM((blocks * slot, 2 * size), bf16),
-            pltpu.SemaphoreType.DMA((1, len(pieces))),
+            pltpu.VMEM((width, 2 * size), bf16),
+            pltpu.SemaphoreType.DMA((2, len(pieces))),
         ],
         flops=4 * blocks * slot * width * size,
-        steps=blocks,
+        steps=steps,
+        each=blocks // steps,
     )
 
 
@@ -746,37 +792,31 @@
         key_vals = stepped[0]
         dkey_vals = outs[0]
         dcross, dcross_low, gain_out, dqueries = ends
-        dcontext, row_terms = scratch
-        b = pl.program_id(0)
-
-        @pl.when(b == 0)
-        def _():
-            total = own[...] + r1[...].astype(f32) + r2[...].astype(f32) + r3[...].astype(f32)
-            back, gain_rows = norm_back(after_cross[...], gains[2:3, :], total)
-            dcross[...] = cotangent[...].astype(f32) + back
-            dcross_low[...] = dcross[...].astype(bf16)
-            gain_out[...] = gain_rows
-            dcontext[...] = dot(dcross_low[...], w_output[...]).astype(bf16)
-            for k, at in enumerate(heads_in(size)):
-                row_terms[:, k : k + 1] = jnp.sum(
-                    dcontext[:, at].astype(f32) * out[:, at], axis=-1, keepdims=True
-                )
-            dqueries[...] = jnp.zeros_like(dqueries)
-
-        allowed = slots_used(info, b, part, slot) & (question[...] == lax.div(b, count_pass))
-        for k, at in enumerate(heads_in(size)):
-            keys, vals = key_vals[0, :, at], key_vals[0, :, size + at.start : size + at.stop]
-            scores = dot_t(queries[:, at], keys) * SCALE
-            scores = jnp.where(allowed, scores, masked_score)
-            probs = jnp.exp(scores - log_total[:, k : k + 1])
-            dprobs = dot_t(dcontext[:, at], vals)
-            dscores = (probs * (dprobs - row_terms[:, k : k + 1])).astype(bf16)
-            dqueries[:, at] += dot(dscores, keys) * SCALE
-            dkey_vals[0, :, at] = (t_dot(dscores, queries[:, at]) * SCALE).astype(bf16)
-            dkey_vals[0, :, size + at.start : size + at.stop] = t_dot(
-                probs.astype(bf16), dcontext[:, at]
-            ).astype(bf16)
-        emit(dot_t(dkey_vals[0], weight[...]), outs[1:])
+        total = summed((own, r1, r2, r3))
+        back, gain_out[...] = norm_back(after_cross[...], gains[2:3, :], total)
+        dcross[...] = cotangent[...].astype(f32) + back
+        dcross_low[...] = dcross[...].astype(bf16)
+        dcontext = dot(dcross_low[...], w_output[...]).astype(bf16)
+        allowed = keys_used(info, question, range(blocks), part, slot, count_pass)
+        keys, vals = head_parts(key_vals[...].reshape(blocks * slot, 2 * size), 2)
+        asking = head_parts(queries[...], 1)[0]
+        cuts = head_parts(dcontext, 1)[0]
+        outs_of = head_parts(out[...], 1)[0]
+        scores = [dot_t(q * SCALE, t) for q, t in zip(asking, keys, strict=True)]
+        backs = [dot_t(c, v) for c, v in zip(cuts, vals, strict=True)]
+        probs, lows = [], []
+        for k, score in enumerate(scores):
+            row_term = jnp.sum(cuts[k].astype(f32) * outs_of[k], axis=-1, keepdims=True)
+            score = jnp.where(allowed, score, masked_score)
+            probs.append(jnp.exp(score - log_total[:, k : k + 1]))
+            lows.append((probs[k] * (backs[k] - row_term)).astype(bf16))
+        dvals = [t_dot(p.astype(bf16), c) for p, c in zip(probs, cuts, strict=True)]
+        dkeys = [t_dot(d, q) * SCALE for d, q in zip(lows, asking, strict=True)]
+        found = [dot(d, t) * SCALE for d, t in zip(lows, keys, strict=True)]
+        dqueries[...] = jnp.concatenate(found, axis=1)
+        made = jnp.concatenate([*dkeys, *dvals], axis=1).astype(bf16)
+        dkey_vals[...] = made.reshape(dkey_vals.shape)
+        emit(dot_t(made, weight[...]), outs[1:])
 
     return call(
         body,
@@ -790,9 +830,8 @@
             Later(like((rows_dec, width), f32)),
             like((rows_dec, size), f32),
         ],
-        [pltpu.VMEM((rows_dec, size), bf16), pltpu.VMEM((rows_dec, LANES), f32)],
         flops=4 * blocks * slot * width * size,
-        steps=blocks,
+        each=blocks,
     )
 
 
@@ -800,12 +839,9 @@
     count = refs[0].shape[0]
 
     def rows(ref):
-        return ref[...] if len(ref.shape) == 2 else ref[0, : min(count, RIDERS), :]
+        return ref[...] if len(ref.shape) == 2 else ref[0, :count, :]
 
     terms = [rows(ref).astype(f32) for ref in refs[1:]]
-    each = len(terms) // 3
-    if each == 2:
-        terms = [jnp.concatenate(terms[k : k + 2], axis=0) for k in (0, 2, 4)]
     total = refs[0][...]
     for term in terms:
         total = total + term
@@ -855,38 +891,6 @@
     )
 
 
-def decoder_queries(info, rows, terms, gains, pieces, column_from, size):
-    count, width = rows.shape
-
-    def body(info, _, ins, __, outs, scratch):
-        rows, own, r1, r2, r3, gains = ins[:6]
-        after_self, normed, queries, w_query, w_output = outs
-        weight, signals = scratch
-        assemble(info, ins[6:], (weight,), signals, column_from)
-        w_query[...] = weight[:, :size]
-        w_output[...] = weight[:, size:]
-        after_self[...] = rows[...].astype(f32) + summed((own, r1, r2, r3))
-        normed[...] = norm_rows(after_self[...], gains[1:2, :]).astype(bf16)
-        queries[...] = dot(normed[...], w_query[...]).astype(bf16)
-
-    return call(
-        body,
-        info,
-        [],
-        [rows, *terms, gains, *(Far(p) for p in pieces)],
-        [],
-        [
-            like((count, width), f32),
-            Later(like((count, width), bf16)),
-            like((count, size), bf16),
-            Later(like((width, size), bf16)),
-            like((width, size), bf16),
-        ],
-        [pltpu.VMEM((width, 2 * size), bf16), pltpu.SemaphoreType.DMA((1, len(pieces)))],
-        flops=2 * count * width * size,
-    )
-
-
 def decoder_back(info, cotangent, pieces):
     count, width = cotangent.shape
     hidden = pieces[0].shape[1] // 2
@@ -941,13 +945,16 @@
     )
 
 
-def query_back(info, terms, weight):
+def rows_back(info, terms, weight):
     (count, size), width = terms[0].shape, weight.shape[0]
 
     def body(info, _, ins, __, outs, scratch):
         low, own, sent = outs
-        low[...] = ((ins[0][...] + ins[1][...]) + (ins[2][...] + ins[3][...])).astype(bf16)
-        own[...] = dot_t(low[...], ins[4][...])
+        total = ins[0][...]
+        for term in ins[1:-1]:
+            total = total + term[...]
+        low[...] = total.astype(bf16)
+        own[...] = dot_t(low[...], ins[-1][...])
         sent[...] = own[...].astype(bf16)
 
     return call(
@@ -966,13 +973,13 @@
 
 
 def decoder_self_back(
-    info, dcross, after_self, terms, gains, weight, qkv, probs, active, w_outer
+    info, dcross, after_self, terms, gains, weight, qkv, probs
 ):
     count, width = after_self.shape
     size = weight.shape[1] // 4
 
     def body(info, _, ins, __, outs, scratch):
-        dcross, after_self, *terms, gains, weight, qkv, probs, active, w_outer = ins
+        dcross, after_self, *terms, gains, weight, qkv, probs = ins
         dself, dself_low, gain_rows, moved, own_back, sent_back = outs
         back, gain_rows[...] = norm_back(after_self[...], gains[1:2, :], summed(terms))
         dself[...] = dcross[...] + back
@@ -991,39 +998,40 @@
             )
             for j, term in enumerate(found):
                 moved[:, j * size + at.start : j * size + at.stop] = term.astype(bf16)
-        own_back[:count, :] = dot_t(moved[...], weight[:, : 3 * size])
-        own_back[count:, :] = dot_t(active[...], w_outer[...])
+        own_back[...] = dot_t(moved[...], weight[:, : 3 * size])
         sent_back[...] = own_back[...].astype(bf16)
 
     return call(
         body,
         info,
         [],
-        [dcross, after_self, *terms, gains, weight, qkv, probs, active, w_outer],
+        [dcross, after_self, *terms, gains, weight, qkv, probs],
         [],
         [
             like((count, width), f32),
             Later(like((count, width), bf16)),
             like((count, width), f32),
             Later(like((count, 3 * size), bf16)),
-            like((2 * count, width), f32),
-            like((2 * count, width), bf16),
+            like((count, width), f32),
+            like((count, width), bf16),
         ],
         flops=2 * count * width * size * 8,
     )
 
 
-def decoder_ends(info, rows, dself, terms, gains, after_cross, gain_rows, gain_sums, dec_own):
+def decoder_ends(
+    info, rows, dself, terms, gains, after_cross, out_terms, gain_rows, gain_sums, dec_own
+):
     count, width = dself.shape
 
     def body(info, _, ins, __, outs, scratch):
         rows, dself, after_cross, gains = ins[:4]
         three, four, zero, one = ins[-4:]
         grad, states, found = outs
-        total = summed(ins[4:-4])
-        back, two = norm_back(rows[...].astype(f32), gains[0:1, :], total[:count])
+        total, out_total = summed(ins[4:8]), summed(ins[8:12])
+        back, two = norm_back(rows[...].astype(f32), gains[0:1, :], total)
         grad[...] = dself[...] + back
-        states[...] = (after_cross[...] + total[count:]).astype(bf16)
+        states[...] = (after_cross[...] + out_total).astype(bf16)
         row = lax.div(lax.broadcasted_iota(jnp.int32, (count, 1), 0), dec_own)
         mine = (row == info[HEAD]) & (info[BLK] == 0)
         found[0:1, :] = zero[...]
@@ -1035,7 +1043,7 @@
         body,
         info,
         [],
-        [rows, dself, after_cross, gains, *terms, *gain_rows, *gain_sums],
+        [rows, dself, after_cross, gains, *terms, *out_terms, *gain_rows, *gain_sums],
         [],
         [like((count, width), f32), like((count, width), bf16), like((5, width), f32)],
     )
@@ -1153,7 +1161,7 @@
     attention, ffn, first_all, dec_ffn = sync(attention, ffn, first_all, dec_ffn)
 
     ffn = fetch_step(ffn, -1, 2)
-    qkv, probs, context, *partial, w_in, w_out = encoder_attention(
+    qkv, probs, context, *partial = encoder_attention(
         info, first_all, in_turn(attention)
     )
     partial, ffn = sync(partial, ffn)
@@ -1180,8 +1188,8 @@
     def spread(rows):
         return [rows, swap(rows, "head", 1), swap(rows, "head", 2)]
 
-    def riders(all_rows, count=1):
-        return [Rider(rows, blocks + k) for rows in all_rows[1:] for k in range(count)]
+    def riders(all_rows):
+        return [Rider(rows, blocks) for rows in all_rows[1:]]
 
     second, ffn, dec_ffn = sync(second, ffn, dec_ffn)
     second_all = spread(second)
@@ -1192,7 +1200,7 @@
     ffn = in_turn(ffn)
 
     dec_ffn = fetch_step(fetch_start(dec_ffn), -1, 1)
-    active, slope, *partial, w_inner, w_outer = encoder_ffn(info, second_all, ffn, units)
+    active, slope, *partial = encoder_ffn(info, second_all, ffn, units)
     partial, dec_ffn = sync(partial, dec_ffn)
     beside = to_core(partial)
     partial, beside, both, dec_ffn = sync(partial, beside, both, dec_ffn)
@@ -1227,19 +1235,26 @@
     states_all, dec_ffn = sync(states_all, dec_ffn)
     states_all.append(swap(states_all[2], "head", 1))
     states_all, dec_ffn = sync(states_all, dec_ffn)
-    after_self, fourth, queries, w_cross_query, w_cross_output = decoder_queries(
-        info,
-        dec_in,
-        [mine, *riders(states_all)],
-        decoder_gains,
+
+    dec_ffn = fetch_step(dec_ffn, -4)
+    (
+        key_vals,
+        after_self,
+        fourth,
+        queries,
+        w_cross_query,
+        w_cross_output,
+        stats,
+        w_cross,
+    ) = cross_forward(
+        info,
+        states_all,
         ffn,
-        at_cross + 2 * size,
-        size,
-    )
-
-    dec_ffn = fetch_step(dec_ffn, -4)
-    key_vals, stats, w_cross = cross_forward(
-        info, states_all, ffn, at_cross, queries, question, count_q, count_pass
+        at_cross,
+        (dec_in, [mine, *riders(states_all)], decoder_gains),
+        question,
+        count_q,
+        count_pass,
     )
     bits = [1 << k for k in range((blk_count - 1).bit_length())]
     last_two = (bits[-2], bits[-1], bits[-2] + bits[-1])
@@ -1283,33 +1298,39 @@
 
     partial, dqueries, dkey_vals = sync(partial, dqueries, dkey_vals)
     beside = to_core(partial)
-    dqueries = some(dqueries, bits[:-2])
     partial, beside, dkey_vals, dqueries = sync(partial, beside, dkey_vals, dqueries)
     across = to_chip(partial, beside)
-    terms = [dqueries, *(swap(dqueries, "blk", k) for k in last_two)]
+    dqueries = some(dqueries, bits[:-1])
     cross_sum = weight_grads(info, [(states_all, dkey_vals)], cut=False)[0]
-    partial, beside, across, cross_sum, terms = sync(partial, beside, across, cross_sum, terms)
+    _, out_mine, out_sent = rows_back(info, [dec_active], w_dec_outer)
+    partial, beside, across, cross_sum, dqueries, out_sent = sync(
+        partial, beside, across, cross_sum, dqueries, out_sent
+    )
 
     def enter_back(cot, a, b, c):
         grad = cot + a + b + c
         return grad, grad
 
-    dqueries, mine, sent = query_back(info, terms, w_cross_query)
     dstates, dstates_low = by_rows(
         enter_back,
         info,
         [encoder_cotangent.reshape(blocks, part, width), partial[0], beside[0], across],
         [],
         [f32, bf16],
-        riders=sent,
+        riders=out_sent,
         kept=False,
     )
-    dstates_low, cross_sum = sync(dstates_low, cross_sum)
+    dstates_low, cross_sum, dqueries = sync(dstates_low, cross_sum, dqueries)
     dstates_all = spread(dstates_low)
-    dstates_all = sync(*dstates_all)
-    dstates_all = sync(*dstates_all, swap(dstates_all[2], "head", 1))
-    dinner, *partial = encoder_ffn_back(info, dstates_all, slope, w_inner, w_outer)
-    partial, dinner = sync(partial, dinner)
+    terms = [dqueries, swap(dqueries, "blk", bits[-1])]
+    dqueries, mine, sent = rows_back(info, terms, w_cross_query)
+    dstates_all, sent = sync(dstates_all, sent)
+    dstates_all.append(swap(dstates_all[2], "head", 1))
+    dstates_all, sent = sync(dstates_all, sent)
+    out_terms = [out_mine, *riders(dstates_all)]
+    dinner, *partial = encoder_ffn_back(info, dstates_all, slope, ffn)
+    terms = [mine, *share(sent)]
+    partial, dinner, terms = sync(partial, dinner, terms)
     beside = to_core(partial)
     partial, beside, dinner, dstates_all = sync(partial, beside, dinner, dstates_all)
     across = to_chip(partial, beside)
@@ -1317,13 +1338,11 @@
         info,
         dcross,
         after_self,
-        [mine, *riders(dstates_all)],
+        terms,
         decoder_gains,
         w_self,
         dec_qkv,
         dec_probs,
-        dec_active,
-        w_dec_outer,
     )
     ffn_sums = weight_grads(
         info, [(second_all, dinner), (dstates_all, active)], [cross_sum]
@@ -1353,11 +1372,11 @@
     dhidden_all, ffn_moving = sync(dhidden_all, ffn_moving)
     dhidden_all.append(swap(dhidden_all[2], "head", 1))
     dhidden_all, ffn_moving = sync(dhidden_all, ffn_moving)
-    terms = [own_back, *riders(dhidden_all, 2)]
+    terms = [own_back, *riders(dhidden_all)]
 
     ffn_moving = reduce_step(info, (ffn_sums, ffn_moving, 2))[0]
     partial, sums, gain_zero = encoder_attention_back(
-        info, dhidden_all, first_all, qkv, probs, context, w_in, w_out, encoder_gains
+        info, dhidden_all, first_all, qkv, probs, context, in_turn(attention), encoder_gains
     )
     partial, sums, ffn_moving, gain_zero = sync(partial, sums, ffn_moving, gain_zero)
     ffn_moving, moving = reduce_step(info, (ffn_sums, ffn_moving, 3), (sums, None, 1))
@@ -1369,6 +1388,7 @@
         terms,
         decoder_gains,
         after_cross,
+        out_terms,
         [gain_three, gain_four],
         [gain_zero, gain_one],
         dec_own,

time: 344 us -> 328 us (0.953)
  Pallas kernels: 116 us -> 104 us
  waiting for transfers between devices: 134 us -> 128 us
    pallas_call x31, Pallas kernels: 116 us -> 104 us  [call(): pl.pallas_call(split, grid=(steps,), in_specs=[pl.BlockSpec(memory_space=...]
    ppermute x49 -> x51, waiting for transfers between devices: 77.7 us -> 73.1 us  [swap(): return lax.ppermute(value, axis, [(i, i ^ bits) for i in range(size)])]
    ppermute x49 -> x51, starting transfers between devices: 35.2 us -> 35.2 us  [swap(): return lax.ppermute(value, axis, [(i, i ^ bits) for i in range(size)])]
  transfers between devices with their start and end apart: 81 -> 83, of which waited for: 47 -> 51; matrix products, arithmetic and copies ran while one was open for 2% -> 2% of each run, Pallas kernels for 24% -> 25%
where the time goes in v4:
time: 328 us; the launch traced here: 326 us
  waiting for transfers between devices  128 us (39%)
  Pallas kernels  104 us (32%)
  starting transfers between devices  69.5 us (21%)
  local copies, waits for them, and re-layouts  14.5 us (4%)
  blocking collectives  5.4 us (2%)
  other arithmetic  3.5 us (1%)
    pallas_call x31, Pallas kernels, call(): pl.pallas_call(split, grid=(steps,), in_specs=[pl.BlockSpec(memory_space=...  104 us
    ppermute x51, waiting for transfers between devices, swap(): return lax.ppermute(value, axis, [(i, i ^ bits) for i in range(size)])  73.1 us
    ppermute x21, waiting for transfers between devices, fetch_step(): lax.ppermute(pieces[k + 1 if k < 0 else k - 1], 'blk', forth if k < 0 els...  38.9 us
    ppermute x51, starting transfers between devices, swap(): return lax.ppermute(value, axis, [(i, i ^ bits) for i in range(size)])  35.2 us
    ppermute x21, starting transfers between devices, fetch_step(): lax.ppermute(pieces[k + 1 if k < 0 else k - 1], 'blk', forth if k < 0 els...  22.6 us
    ppermute x11, waiting for transfers between devices, reduce_step(): lax.ppermute(v, 'blk', way)  15.8 us
    unnamed x169, local copies, waits for them, and re-layouts  11.9 us
    ppermute x11, starting transfers between devices, reduce_step(): lax.ppermute(v, 'blk', way)  11.7 us
  transfers between devices with their start and end apart: 83, of which 51 were waited for; matrix products, arithmetic and copies ran while one was open for 2% of the time, Pallas kernels for 25%

profile of v4, /device:TPU:0, one launch (start us, length us, event | category | flops | bytes accessed | tf_op | source)
XLA Modules:
  0.0 326.1 jit_solution(7140394177498373383)
XLA Ops:
  24.9 5.4 %all_gather.3 = bf16[2,40,768]{2,0,1:T(2,128)(2,1)S(1)} all-gather(bf16[2,10,768]{2,0,1:T(2,128)(2,1)S(1)} %copy.68), channel_id=1, replica_groups=mesh['blk'=8,'head'=4] {'head'}, dimensions={1}, use_global_device_ids=true | all-gather | bytes 153600 | tf_op jit(solution)/shard_map/all_gather | solution.py:1155
  32.5 4.8 %collective-permute-done.9.refs_11_.refs_18_ = bf16[96,768]{1,0:T(8,128)(2,1)S(1)} collective-permute-done((bf16[96,768]{1,0:T(8,128)(2,1)S(1)}, bf16[96,768]{1,0:T(8,128)(2,1)S(1)}, u32[]{:S(2)}, u32[]{:S(2)}) %collective-permute-start.9) | collective-permute-done | bytes 147488 | tf_op jit(solution)/shard_map/ppermute | solution.py:74
  37.3 8.7 %collective-permute-done.10.refs_6_.refs_7_ = bf16[96,3072]{1,0:T(8,128)(2,1)S(1)} collective-permute-done((bf16[96,3072]{1,0:T(8,128)(2,1)S(1)}, bf16[96,3072]{1,0:T(8,128)(2,1)S(1)}, u32[]{:S(2)}, u32[]{:S(2)}) %collective-permute-start.10) | collective-permute-done | bytes 589856 | tf_op jit(solution)/shard_map/ppermute | solution.py:74
  48.0 9.3 %shard_map.427 = (bf16[4,256,576]{2,1,0:T(8,128)(2,1)}, bf16[4,3,256,256]{3,2,1,0:T(8,128)(2,1)}, bf16[4,256,192]{2,1,0:T(8,128)(2,1)}, f32[4,64,768]{2,1,0:T(8,...) custom-call(s32[14]{0:T(128)S(1)} %pad_add_fusion.info_ref, ...), custom_call_target="tpu_custom_call" | custom-call | flops 2013265920 | bytes 8257536 | tf_op jit(solution)/shard_map/pallas_call | solution.py:296
  57.3 3.4 %collective-permute-done.11.refs_5_.refs_6_ = bf16[96,3072]{1,0:T(8,128)(2,1)S(1)} collective-permute-done((bf16[96,3072]{1,0:T(8,128)(2,1)S(1)}, bf16[96,3072]{1,0:T(8,128)(2,1)S(1)}, u32[]{:S(2)}, u32[]{:S(2)}) %collective-permute-start.11) | collective-permute-done | bytes 589856 | tf_op jit(solution)/shard_map/ppermute | solution.py:74
  68.0 9.1 %collective-permute-done.15.refs_3_ = bf16[4,64,768]{2,1,0:T(8,128)(2,1)S(1)} collective-permute-done((bf16[4,64,768]{2,1,0:T(8,128)(2,1)S(1)}, bf16[4,64,768]{2,1,0:T(8,128)(2,1)S(1)}, u32[]{:S(2)}, u32[]{:S(2)}) %collective-permute-start.15) | collective-permute-done | bytes 393248 | tf_op jit(solution)/shard_map/ppermute | solution.py:26
  86.1 9.8 %collective-permute-done.19.refs_2_ = bf16[4,64,768]{2,1,0:T(8,128)(2,1)S(1)} collective-permute-done((bf16[4,64,768]{2,1,0:T(8,128)(2,1)S(1)}, bf16[4,64,768]{2,1,0:T(8,128)(2,1)S(1)}, u32[]{:S(2)}, u32[]{:S(2)}) %collective-permute-start.19) | collective-permute-done | bytes 393248 | tf_op jit(solution)/shard_map/ppermute | solution.py:26
  101.6 7.9 %shard_map.429 = (bf16[4,256,768]{2,1,0:T(8,128)(2,1)}, bf16[4,256,768]{2,1,0:T(8,128)(2,1)}, f32[4,64,768]{2,1,0:T(8,128)S(1)}, bf16[4,64,768]{2,1,0:T(8,128)(2...) custom-call(s32[14]{0:T(128)S(1)} %pad_add_fusion.info_ref, bf16[4,64,768]{2,1,0:T(8,128)(2,1)} %copy-done.46, ...), custom_call_target="tpu_custom_call" | custom-call | flops 2415919104 | bytes 11796480 | tf_op jit(solution)/shard_map/pallas_call | solution.py:296
  115.7 4.0 %shard_map.430 = (bf16[48,768]{1,0:T(8,128)(2,1)}, bf16[48,576]{1,0:T(8,128)(2,1)}, f32[3,48,48]{2,1,0:T(8,128)}, bf16[48,192]{1,0:T(8,128)(2,1)}, f32[48,768]{1...) custom-call(s32[14]{0:T(128)S(1)} %pad_add_fusion.info_ref, ...), custom_call_target="tpu_custom_call" | custom-call | flops 56623104 | bytes 6377856 | tf_op jit(solution)/shard_map/pallas_call | solution.py:296
  129.4 7.1 %collective-permute-done.32.refs_6_ = bf16[96,1536]{1,0:T(8,128)(2,1)S(1)} collective-permute-done((bf16[96,1536]{1,0:T(8,128)(2,1)S(1)}, bf16[96,1536]{1,0:T(8,128)(2,1)S(1)}, u32[]{:S(2)}, u32[]{:S(2)}) %collective-permute-start.32) | collective-permute-done | bytes 294944 | tf_op jit(solution)/shard_map/ppermute | solution.py:74
  142.5 6.3 %shard_map.432 = (bf16[4,256,384]{2,1,0:T(8,128)(2,1)}, f32[48,768]{1,0:T(8,128)}, bf16[48,768]{1,0:T(8,128)(2,1)}, bf16[48,192]{1,0:T(8,128)(2,1)S(1)}, bf16[76...) custom-call(s32[14]{0:T(128)S(1)} %pad_add_fusion.info_ref, ...), custom_call_target="tpu_custom_call" | custom-call | flops 603979776 | bytes 9489600 | tf_op jit(solution)/shard_map/pallas_call | solution.py:296
  149.9 3.5 %collective-permute-done.35.refs_1_ = f32[48,384]{1,0:T(8,128)S(1)} collective-permute-done((f32[48,384]{1,0:T(8,128)S(1)}, f32[48,384]{1,0:T(8,128)S(1)}, u32[]{:S(2)}, u32[]{:S(2)}) %collective-permute-start.35) | collective-permute-done | bytes 73760 | tf_op jit(solution)/shard_map/ppermute | solution.py:26
  158.6 3.8 %shard_map.434 = (bf16[768,768]{1,0:T(8,128)(2,1)}, bf16[768,768]{1,0:T(8,128)(2,1)}, f32[48,768]{1,0:T(8,128)S(1)}) custom-call(s32[14]{0:T(128)S(1)} %pad_add_fusion.info_ref, bf16[48,768]{1,0:T(8,128)(2,1)S(1)} %get-tuple-element.908.refs_0_.refs_1_.refs_6_, bf16[96,1536]{1,0:T(8,128)(2,1)} %copy-done.58, bf16[96,1536]{1,0:T(8,128)(2,1)} %copy-done.59, ...), custom_call_target="tpu_custom_call" | custom-call | flops 56623104 | bytes 4939776 | tf_op jit(solution)/shard_map/pallas_call | solution.py:296
  180.0 4.0 %shard_map.437 = (bf16[4,256,384]{2,1,0:T(8,128)(2,1)}, f32[4,64,768]{2,1,0:T(8,128)S(1)}, bf16[4,64,768]{2,1,0:T(8,128)(2,1)S(1)}, f32[4,64,768]{2,1,0:T(8,128)...) custom-call(s32[14]{0:T(128)S(1)} %pad_add_fusion.info_ref, ...), custom_call_target="tpu_custom_call" | custom-call | flops 603979776 | bytes 5901504 | tf_op jit(solution)/shard_map/pallas_call | solution.py:296
  193.0 3.7 %shard_map.438.refs_10_ = f32[768,384]{1,0:T(8,128)} custom-call(s32[14]{0:T(128)S(1)} %pad_add_fusion.info_ref, bf16[5,64,768]{2,1,0:T(8,128)(2,1)} %copy-done.4, bf16[5,64,768]{2,1,0:T(8,128)(2,1)} %copy-done.48, bf16[5,64,768]{2,1,0:T(8,128)(2,1)} %copy-done.49, bf16[5,64,768]{2,1,0:T(8,128)(2,1)} %copy-done.50, ...), custom_call_target="tpu_custom_call" | custom-call | flops 603979776 | bytes 3932160 | tf_op jit(solution)/shard_map/pallas_call | solution.py:296
  201.2 4.6 %collective-permute-done.53.refs_1_ = f32[48,192]{1,0:T(8,128)S(1)} collective-permute-done((f32[48,192]{1,0:T(8,128)S(1)}, f32[48,192]{1,0:T(8,128)S(1)}, u32[]{:S(2)}, u32[]{:S(2)}) %collective-permute-start.53) | collective-permute-done | bytes 36896 | tf_op jit(solution)/shard_map/ppermute | solution.py:26
  207.5 4.7 %collective-permute-done.52.refs_2_.refs_7_.refs_10_ = bf16[5,64,768]{2,1,0:T(8,128)(2,1)S(1)} collective-permute-done((bf16[5,64,768]{2,1,0:T(8,128)(2,1)S(1)}, bf16[5,64,768]{2,1,0:T(8,128)(2,1)S(1)}, u32[]{:S(2)}, u32[]{:S(2)}) %collective-permute-start.52) | collective-permute-done | bytes 491552 | tf_op jit(solution)/shard_map/ppermute | solution.py:26
  215.9 7.0 %shard_map.442 = (bf16[4,256,768]{2,1,0:T(8,128)(2,1)}, f32[4,64,768]{2,1,0:T(8,128)S(1)}, bf16[4,64,768]{2,1,0:T(8,128)(2,1)S(1)}, f32[4,64,768]{2,1,0:T(8,128)S(1)}, bf16[4,64,768]{2,1,0:T(8,128)(2,1)S(1)}) custom-call(s32[14]{0:T(128)S(1)} %pad_add_fusion.info_ref, bf16[5,64,768]{2,1,0:T(8,128)(2,1)} %copy-done.44, bf16[5,64,768]{2,1,0:T(8,128)(2,1)} %copy-done.7, ...), custom_call_target="tpu_custom_call" | custom-call | flops 2415919104 | bytes 12189696 | tf_op jit(solution)/shard_map/pallas_call | solution.py:296
  230.1 7.6 %shard_map.443 = (f32[96,1920]{1,0:T(8,128)}, bf16[96,1920]{1,0:T(8,128)(2,1)}, bf16[96,1920]{1,0:T(8,128)(2,1)}, bf16[96,1920]{1,0:T(8,128)(2,1)}, bf16[96,1920...) custom-call(s32[14]{0:T(128)S(1)} %pad_add_fusion.info_ref, ...), custom_call_target="tpu_custom_call" | custom-call | flops 2415919104 | bytes 11182080 | tf_op jit(solution)/shard_map/pallas_call | solution.py:296
  242.4 8.6 %collective-permute-done.63.refs_0_ = bf16[96,1920]{1,0:T(8,128)(2,1)S(1)} collective-permute-done((bf16[96,1920]{1,0:T(8,128)(2,1)S(1)}, bf16[96,1920]{1,0:T(8,128)(2,1)S(1)}, u32[]{:S(2)}, u32[]{:S(2)}) %collective-permute-start.63) | collective-permute-done | bytes 368672 | tf_op jit(solution)/shard_map/ppermute | solution.py:137
  257.8 13.8 %shard_map.446 = (f32[4,64,768]{2,1,0:T(8,128)S(1)}, bf16[4,64,768]{2,1,0:T(8,128)(2,1)S(1)}, f32[4,64,768]{2,1,0:T(8,128)S(1)}, bf16[4,64,768]{2,1,0:T(8,128)(2...) custom-call(s32[14]{0:T(128)S(1)} %pad_add_fusion.info_ref, ...), custom_call_target="tpu_custom_call" | custom-call | flops 4429185024 | bytes 11559936 | tf_op jit(solution)/shard_map/pallas_call | solution.py:296
  280.9 3.4 %shard_map.450 = (f32[96,192]{1,0:T(8,128)}, f32[96,192]{1,0:T(8,128)}, f32[96,192]{1,0:T(8,128)}, f32[96,192]{1,0:T(8,128)}, f32[96,768]{1,0:T(8,128)}, /*index...) custom-call(s32[14]{0:T(128)S(1)} %pad_add_fusion.info_ref, bf16[48,768]{1,0:T(8,128)(2,1)} %get-tuple-element.776.refs_0_, ...), custom_call_target="tpu_custom_call" | custom-call | flops 70778880 | bytes 1732608 | tf_op jit(solution)/shard_map/pallas_call | solution.py:296
  295.1 6.4 %collective-permute-done.76 = f32[5,768]{1,0:T(8,128)S(1)} collective-permute-done((f32[5,768]{1,0:T(8,128)S(1)}, f32[5,768]{1,0:T(8,128)S(1)}, u32[]{:S(2)}, u32[]{:S(2)}) %collective-permute-start.76) | collective-permute-done | bytes 15392 | tf_op jit(solution)/shard_map/ppermute | solution.py:26
  312.7 3.6 %shard_map.453 = f32[4,64,768]{2,1,0:T(8,128)} custom-call(s32[14]{0:T(128)S(1)} %pad_add_fusion.info_ref, f32[4,64,768]{2,1,0:T(8,128)S(1)} %get-tuple-element.811.refs_0_, bf16[4,64,768]{2,1,0:T(8,128)(2,1)S(1)} %bitcast.21, f32[4,64,768]{2,1,0:T(8,128)S(1)} %get-tuple-element.812.refs_2_, bf16[4,64,768]{2,1,0:T(8,128)(2,1)S(1)} %collective-permute-done.68.refs_3_, ...), custom_call_target="tpu_custom_call" | custom-call | flops 1966080 | bytes 3545088 | tf_op jit(solution)/shard_map/pallas_call | solution.py:296
  (373 shorter events, 173.8 us)
Async XLA Ops:
  11.0 11.6 %collective-permute-start.5 = (bf16[4,64,768]{2,1,0:T(8,128)(2,1)S(1)}, bf16[4,64,768]{2,1,0:T(8,128)(2,1)}, u32[]{:S(2)}, u32[]{:S(2)}) collective-permute-start(bf16[4,64,768]{2,1,0:T(8,128)(2,1)S(1)} %shard_map.426.refs_0_.refs_4_), channel_id=1, source_target_pairs={{0,2},{1,3},{2,0},{3,1},{4,6},{5,7},{6,4},{7,5},{8,10},{9,11},{10,... | collective-permute-start | bytes 1179656 | tf_op jit(solution)/shard_map/ppermute | solution.py:26
  30.4 15.6 %collective-permute-start.10 = (bf16[96,3072]{1,0:T(8,128)(2,1)S(1)}, bf16[96,3072]{1,0:T(8,128)(2,1)S(1)}, u32[]{:S(2)}, u32[]{:S(2)}) collective-permute-start(bf16[96,3072]{1,0:T(8,128)(2,1)S(1)} %concatenate.15.refs_4_.refs_5_), channel_id=1, source_target_pairs={{8,0},{16,8},{24,16},{28,24},{20,28},{12,20},{4,12},{0,4},{9,1},{1... | collective-permute-start | bytes 1769480 | tf_op jit(solution)/shard_map/ppermute | solution.py:74
  46.0 14.8 %collective-permute-start.11 = (bf16[96,3072]{1,0:T(8,128)(2,1)S(1)}, bf16[96,3072]{1,0:T(8,128)(2,1)S(1)}, u32[]{:S(2)}, u32[]{:S(2)}) collective-permute-start(bf16[96,3072]{1,0:T(8,128)(2,1)S(1)} %concatenate.15.refs_4_.refs_5_), channel_id=1, source_target_pairs={{0,8},{8,16},{16,24},{24,28},{28,20},{20,12},{12,4},{4,0},{1,9},{9... | collective-permute-start | bytes 1769480 | tf_op jit(solution)/shard_map/ppermute | solution.py:74
  47.6 14.5 %collective-permute-start.12 = (bf16[96,3072]{1,0:T(8,128)(2,1)S(1)}, bf16[96,3072]{1,0:T(8,128)(2,1)S(1)}, u32[]{:S(2)}, u32[]{:S(2)}) collective-permute-start(bf16[96,3072]{1,0:T(8,128)(2,1)S(1)} %collective-permute-done.10.refs_6_.refs_7_), channel_id=1, source_target_pairs={{8,0},{16,8},{24,16},{28,24},{20,28},{12,20},{4,12},{0,4},{9,1},{1... | collective-permute-start | bytes 1769480 | tf_op jit(solution)/shard_map/ppermute | solution.py:74
  64.3 15.4 %collective-permute-start.16 = (bf16[96,3072]{1,0:T(8,128)(2,1)S(1)}, bf16[96,3072]{1,0:T(8,128)(2,1)S(1)}, u32[]{:S(2)}, u32[]{:S(2)}) collective-permute-start(bf16[96,3072]{1,0:T(8,128)(2,1)S(1)} %collective-permute-done.11.refs_5_.refs_6_), channel_id=1, source_target_pairs={{0,8},{8,16},{16,24},{24,28},{28,20},{20,12},{12,4},{4,0},{1,9},{9... | collective-permute-start | bytes 1769480 | tf_op jit(solution)/shard_map/ppermute | solution.py:74
  65.9 15.1 %collective-permute-start.17 = (bf16[96,3072]{1,0:T(8,128)(2,1)S(1)}, bf16[96,3072]{1,0:T(8,128)(2,1)S(1)}, u32[]{:S(2)}, u32[]{:S(2)}) collective-permute-start(bf16[96,3072]{1,0:T(8,128)(2,1)S(1)} %collective-permute-done.12.refs_8_.refs_9_), channel_id=1, source_target_pairs={{8,0},{16,8},{24,16},{28,24},{20,28},{12,20},{4,12},{0,4},{9,1},{1... | collective-permute-start | bytes 1769480 | tf_op jit(solution)/shard_map/ppermute | solution.py:74
  82.3 14.3 %collective-permute-start.20 = (bf16[96,3072]{1,0:T(8,128)(2,1)S(1)}, bf16[96,3072]{1,0:T(8,128)(2,1)S(1)}, u32[]{:S(2)}, u32[]{:S(2)}) collective-permute-start(bf16[96,3072]{1,0:T(8,128)(2,1)S(1)} %collective-permute-done.16.refs_7_.refs_8_), channel_id=1, source_target_pairs={{0,8},{8,16},{16,24},{24,28},{28,20},{20,12},{12,4},{4,0},{1,9},{9... | collective-permute-start | bytes 1769480 | tf_op jit(solution)/shard_map/ppermute | solution.py:74
  83.8 13.9 %collective-permute-start.21 = (bf16[96,3072]{1,0:T(8,128)(2,1)S(1)}, bf16[96,3072]{1,0:T(8,128)(2,1)S(1)}, u32[]{:S(2)}, u32[]{:S(2)}) collective-permute-start(bf16[96,3072]{1,0:T(8,128)(2,1)S(1)} %collective-permute-done.17.refs_10_.refs_11_), channel_id=1, source_target_pairs={{8,0},{16,8},{24,16},{28,24},{20,28},{12,20},{4,12},{0,4},{9,1},{1... | collective-permute-start | bytes 1769480 | tf_op jit(solution)/shard_map/ppermute | solution.py:74
  84.3 11.5 %collective-permute-start.19 = (bf16[4,64,768]{2,1,0:T(8,128)(2,1)S(1)}, bf16[4,64,768]{2,1,0:T(8,128)(2,1)S(1)}, u32[]{:S(2)}, u32[]{:S(2)}) collective-permute-start(bf16[4,64,768]{2,1,0:T(8,128)(2,1)S(1)} %get-tuple-element.524.refs_0_), channel_id=1, source_target_pairs={{0,2},{1,3},{2,0},{3,1},{4,6},{5,7},{6,4},{7,5},{8,10},{9,11},{10,... | collective-permute-start | bytes 1179656 | tf_op jit(solution)/shard_map/ppermute | solution.py:26
  112.0 11.2 %collective-permute-start.27 = (bf16[4,64,768]{2,1,0:T(8,128)(2,1)S(1)}, bf16[4,64,768]{2,1,0:T(8,128)(2,1)S(1)}, u32[]{:S(2)}, u32[]{:S(2)}) collective-permute-start(bf16[4,64,768]{2,1,0:T(8,128)(2,1)S(1)} %add_convert_fusion.3), channel_id=1, source_target_pairs={{0,2},{1,3},{2,0},{3,1},{4,6},{5,7},{6,4},{7,5},{8,10},{9,11},{10,... | collective-permute-start | bytes 1179656 | tf_op jit(solution)/shard_map/ppermute | solution.py:26
  125.8 11.5 %collective-permute-start.30 = (bf16[5,64,768]{2,1,0:T(8,128)(2,1)S(1)}, bf16[5,64,768]{2,1,0:T(8,128)(2,1)S(1)}, u32[]{:S(2)}, u32[]{:S(2)}) collective-permute-start(bf16[5,64,768]{2,1,0:T(8,128)(2,1)S(1)} %get-tuple-element.586.refs_0_), channel_id=1, source_target_pairs={{0,1},{1,0},{2,3},{3,2},{4,5},{5,4},{6,7},{7,6},{8,9},{9,8},{10,11... | collective-permute-start | bytes 1474568 | tf_op jit(solution)/shard_map/ppermute | solution.py:26
  125.8 13.6 %collective-permute-start.31 = (bf16[5,64,768]{2,1,0:T(8,128)(2,1)S(1)}, bf16[5,64,768]{2,1,0:T(8,128)(2,1)S(1)}, u32[]{:S(2)}, u32[]{:S(2)}) collective-permute-start(bf16[5,64,768]{2,1,0:T(8,128)(2,1)S(1)} %get-tuple-element.586.refs_0_), channel_id=1, source_target_pairs={{0,2},{1,3},{2,0},{3,1},{4,6},{5,7},{6,4},{7,5},{8,10},{9,11},{10,... | collective-permute-start | bytes 1474568 | tf_op jit(solution)/shard_map/ppermute | solution.py:26
  141.3 12.8 %collective-permute-start.36 = (bf16[96,1536]{1,0:T(8,128)(2,1)S(1)}, bf16[96,1536]{1,0:T(8,128)(2,1)S(1)}, u32[]{:S(2)}, u32[]{:S(2)}) collective-permute-start(bf16[96,1536]{1,0:T(8,128)(2,1)S(1)} %collective-permute-done.32.refs_6_), channel_id=1, source_target_pairs={{0,8},{8,16},{16,24},{24,28},{28,20},{20,12},{12,4},{4,0},{1,9},{9... | collective-permute-start | bytes 884744 | tf_op jit(solution)/shard_map/ppermute | solution.py:74
  198.6 13.6 %collective-permute-start.52 = (bf16[5,64,768]{2,1,0:T(8,128)(2,1)S(1)}, bf16[5,64,768]{2,1,0:T(8,128)(2,1)S(1)}, u32[]{:S(2)}, u32[]{:S(2)}) collective-permute-start(bf16[5,64,768]{2,1,0:T(8,128)(2,1)S(1)} %get-tuple-element.686.refs_0_.refs_5_), channel_id=1, source_target_pairs={{0,2},{1,3},{2,0},{3,1},{4,6},{5,7},{6,4},{7,5},{8,10},{9,11},{10,... | collective-permute-start | bytes 1474568 | tf_op jit(solution)/shard_map/ppermute | solution.py:26
  225.5 12.2 %collective-permute-start.60 = (bf16[4,64,768]{2,1,0:T(8,128)(2,1)S(1)}, bf16[4,64,768]{2,1,0:T(8,128)(2,1)S(1)}, u32[]{:S(2)}, u32[]{:S(2)}) collective-permute-start(bf16[4,64,768]{2,1,0:T(8,128)(2,1)S(1)} %add_convert_fusion.1), channel_id=1, source_target_pairs={{0,2},{1,3},{2,0},{3,1},{4,6},{5,7},{6,4},{7,5},{8,10},{9,11},{10,... | collective-permute-start | bytes 1179656 | tf_op jit(solution)/shard_map/ppermute | solution.py:26
  239.4 12.7 %collective-permute-start.61 = (bf16[5,64,768]{2,1,0:T(8,128)(2,1)S(1)}, bf16[5,64,768]{2,1,0:T(8,128)(2,1)S(1)}, u32[]{:S(2)}, u32[]{:S(2)}) collective-permute-start(bf16[5,64,768]{2,1,0:T(8,128)(2,1)S(1)} %get-tuple-element.730.refs_0_), channel_id=1, source_target_pairs={{0,1},{1,0},{2,3},{3,2},{4,5},{5,4},{6,7},{7,6},{8,9},{9,8},{10,11... | collective-permute-start | bytes 1474568 | tf_op jit(solution)/shard_map/ppermute | solution.py:26
  239.5 13.6 %collective-permute-start.62 = (bf16[5,64,768]{2,1,0:T(8,128)(2,1)S(1)}, bf16[5,64,768]{2,1,0:T(8,128)(2,1)S(1)}, u32[]{:S(2)}, u32[]{:S(2)}) collective-permute-start(bf16[5,64,768]{2,1,0:T(8,128)(2,1)S(1)} %get-tuple-element.730.refs_0_), channel_id=1, source_target_pairs={{0,2},{1,3},{2,0},{3,1},{4,6},{5,7},{6,4},{7,5},{8,10},{9,11},{10,... | collective-permute-start | bytes 1474568 | tf_op jit(solution)/shard_map/ppermute | solution.py:26
  255.7 16.0 %collective-permute-start.66 = (bf16[96,1920]{1,0:T(8,128)(2,1)S(1)}, bf16[96,1920]{1,0:T(8,128)(2,1)S(1)}, u32[]{:S(2)}, u32[]{:S(2)}) collective-permute-start(bf16[96,1920]{1,0:T(8,128)(2,1)S(1)} %get-tuple-element.753), channel_id=1, source_target_pairs={{0,8},{8,16},{16,24},{24,28},{28,20},{20,12},{12,4},{4,0},{1,9},{9... | collective-permute-start | bytes 1105928 | tf_op jit(solution)/shard_map/ppermute | solution.py:137
  257.1 14.6 %collective-permute-start.67 = (bf16[96,1920]{1,0:T(8,128)(2,1)S(1)}, bf16[96,1920]{1,0:T(8,128)(2,1)S(1)}, u32[]{:S(2)}, u32[]{:S(2)}) collective-permute-start(bf16[96,1920]{1,0:T(8,128)(2,1)S(1)} %get-tuple-element.754), channel_id=1, source_target_pairs={{8,0},{16,8},{24,16},{28,24},{20,28},{12,20},{4,12},{0,4},{9,1},{1... | collective-permute-start | bytes 1105928 | tf_op jit(solution)/shard_map/ppermute | solution.py:137
  274.4 13.3 %collective-permute-start.70 = (bf16[96,2688]{1,0:T(8,128)(2,1)S(1)}, bf16[96,2688]{1,0:T(8,128)(2,1)S(1)}, u32[]{:S(2)}, u32[]{:S(2)}) collective-permute-start(bf16[96,2688]{1,0:T(8,128)(2,1)S(1)} %get-tuple-element.766), channel_id=1, source_target_pairs={{0,8},{8,16},{16,24},{24,28},{28,20},{20,12},{12,4},{4,0},{1,9},{9... | collective-permute-start | bytes 1548296 | tf_op jit(solution)/shard_map/ppermute | solution.py:137
  275.8 12.9 %collective-permute-start.71 = (bf16[96,2688]{1,0:T(8,128)(2,1)S(1)}, bf16[96,2688]{1,0:T(8,128)(2,1)S(1)}, u32[]{:S(2)}, u32[]{:S(2)}) collective-permute-start(bf16[96,2688]{1,0:T(8,128)(2,1)S(1)} %get-tuple-element.767), channel_id=1, source_target_pairs={{8,0},{16,8},{24,16},{28,24},{20,28},{12,20},{4,12},{0,4},{9,1},{1... | collective-permute-start | bytes 1548296 | tf_op jit(solution)/shard_map/ppermute | solution.py:137
  290.2 15.2 %collective-permute-start.74 = (bf16[96,2688]{1,0:T(8,128)(2,1)}, bf16[96,2688]{1,0:T(8,128)(2,1)S(1)}, u32[]{:S(2)}, u32[]{:S(2)}) collective-permute-start(bf16[96,2688]{1,0:T(8,128)(2,1)} %get-tuple-element.797), channel_id=1, source_target_pairs={{0,8},{8,16},{16,24},{24,28},{28,20},{20,12},{12,4},{4,0},{1,9},{9... | collective-permute-start | bytes 1548296 | tf_op jit(solution)/shard_map/ppermute | solution.py:137
  291.7 13.7 %collective-permute-start.73 = (bf16[4,64,768]{2,1,0:T(8,128)(2,1)}, bf16[4,64,768]{2,1,0:T(8,128)(2,1)}, u32[]{:S(2)}, u32[]{:S(2)}) collective-permute-start(bf16[4,64,768]{2,1,0:T(8,128)(2,1)} %add_convert_fusion), channel_id=1, source_target_pairs={{0,2},{1,3},{2,0},{3,1},{4,6},{5,7},{6,4},{7,5},{8,10},{9,11},{10,... | collective-permute-start | bytes 1179656 | tf_op jit(solution)/shard_map/ppermute | solution.py:26
  293.7 11.7 %collective-permute-start.75 = (bf16[96,768]{1,0:T(8,128)(2,1)S(1)}, bf16[96,768]{1,0:T(8,128)(2,1)S(1)}, u32[]{:S(2)}, u32[]{:S(2)}) collective-permute-start(bf16[96,768]{1,0:T(8,128)(2,1)S(1)} %get-tuple-element.798), channel_id=1, source_target_pairs={{8,0},{16,8},{24,16},{28,24},{20,28},{12,20},{4,12},{0,4},{9,1},{1... | collective-permute-start | bytes 442376 | tf_op jit(solution)/shard_map/ppermute | solution.py:137
  (140 other events, 1351.8 us)

commit v5 on v4

--- a/solution.py
+++ b/solution.py
@@ -133,7 +133,7 @@
         rows = rings[0][0][0].shape[0]
         wide = [sum(part(terms[0]).width for terms in p) for p in plan]
         shapes = [like((rows, w), bf16) for w in wide]
-        sent = call(body, info, [], [p.array for p in parts], [], shapes, near=True)
+        sent = call(body, info, [], [p.array for p in parts], [], [Near(v) for v in shapes], least=0)
     came = [lax.ppermute(v, "blk", way) for v, way in zip(sent, (forth, back), strict=False)]
     results, column = [], 0
     for k, (pieces, moving, step) in enumerate(rings):
@@ -284,7 +284,8 @@
 
     def given(a):
         array = a.array if isinstance(a, (Columns, Far, Rider)) else a
-        return pltpu.with_memory_space_constraint(array, pltpu.HBM) if large(a) else array
+        far = large(a) or isinstance(a, Rider)
+        return pltpu.with_memory_space_constraint(array, pltpu.HBM) if far else array
 
     def made(a):
         if isinstance(a, Later) or (large(a) and not isinstance(a, Near)):
@@ -1147,16 +1148,16 @@
         axis=1,
     )
     at_self, at_cross = 2 * units, 2 * units + 4 * size
-    attention, first_all, ffn = sync(attention, first_all, ffn)
+    attention, ffn = sync(attention, ffn)
 
     attention = fetch_step(attention, -3, 3)
-    first_all.append(swap(first_all[2], "head", 1))
     pair = jnp.stack([decoder_input, decoder_cotangent]).reshape(2, dec_own, width)
     both = lax.all_gather(pair, "head", axis=1, tiled=True)
     both = jnp.pad(both, ((0, 0), (0, filled - dec_rows), (0, 0)))
     attention, first_all, ffn, both = sync(attention, first_all, ffn, both)
 
     attention, ffn = fetch_step(attention, -4), fetch_step(fetch_start(ffn), 1)
+    first_all.append(swap(first_all[2], "head", 1))
     dec_ffn = jnp.concatenate([decoder_inner, decoder_outer.T], axis=1)
     attention, ffn, first_all, dec_ffn = sync(attention, ffn, first_all, dec_ffn)
 
@@ -1194,12 +1195,12 @@
     second, ffn, dec_ffn = sync(second, ffn, dec_ffn)
     second_all = spread(second)
     ffn = fetch_step(ffn, -3, 4)
+    second_all, ffn, dec_ffn = sync(second_all, ffn, dec_ffn)
+    dec_ffn = fetch_step(fetch_start(dec_ffn), -1, 1)
+    second_all.append(swap(second_all[2], "head", 1))
     second_all, ffn = sync(second_all, ffn)
-    second_all.append(swap(second_all[2], "head", 1))
-    second_all, ffn, dec_ffn = sync(second_all, ffn, dec_ffn)
     ffn = in_turn(ffn)
 
-    dec_ffn = fetch_step(fetch_start(dec_ffn), -1, 1)
     active, slope, *partial = encoder_ffn(info, second_all, ffn, units)
     partial, dec_ffn = sync(partial, dec_ffn)
     beside = to_core(partial)
@@ -1233,10 +1234,9 @@
     states_all = spread(states_sent)
     dec_ffn = fetch_step(dec_ffn, -3, 3)
     states_all, dec_ffn = sync(states_all, dec_ffn)
-    states_all.append(swap(states_all[2], "head", 1))
-    states_all, dec_ffn = sync(states_all, dec_ffn)
-
     dec_ffn = fetch_step(dec_ffn, -4)
+    states_all = sync(*states_all, swap(states_all[2], "head", 1))
+
     (
         key_vals,
         after_self,
@@ -1370,11 +1370,10 @@
     dhidden_all = spread(dhidden_low)
     ffn_moving = reduce_step(info, (ffn_sums, None, 1))[0]
     dhidden_all, ffn_moving = sync(dhidden_all, ffn_moving)
-    dhidden_all.append(swap(dhidden_all[2], "head", 1))
-    dhidden_all, ffn_moving = sync(dhidden_all, ffn_moving)
+    ffn_moving = reduce_step(info, (ffn_sums, ffn_moving, 2))[0]
+    dhidden_all = sync(*dhidden_all, swap(dhidden_all[2], "head", 1))
     terms = [own_back, *riders(dhidden_all)]
 
-    ffn_moving = reduce_step(info, (ffn_sums, ffn_moving, 2))[0]
     partial, sums, gain_zero = encoder_attention_back(
         info, dhidden_all, first_all, qkv, probs, context, in_turn(attention), encoder_gains
     )
@@ -1426,8 +1425,8 @@
     gains = gains + swap(gains, "head", 2)
     gains = some(gains, bits[:1])
     dec_states, dec_grad = own_rows(dec_states), own_rows(dec_grad)
-    partial, beside, across, moving, gains, ffn_moving, dec_states, dec_grad = sync(
-        partial, beside, across, moving, gains, ffn_moving, dec_states, dec_grad
+    partial, beside, across, moving, gains, ffn_moving = sync(
+        partial, beside, across, moving, gains, ffn_moving
     )
 
     def last_back(dh, x, a, b, c, g):
@@ -1442,15 +1441,15 @@
         [encoder_gains],
         [f32],
     )[0]
+    moving, gains, input_grad, ffn_moving = sync(moving, gains, input_grad, ffn_moving)
+    moving = reduce_step(info, (sums, moving, 4))[0]
+    last = swap(gains, "blk", bits[-1])
     grad_inner, grad_outer, grad_cross_key, grad_cross_value = finish(
         info,
         reduce_terms(ffn_sums, ffn_moving),
         (units, units, size, size),
         (False,) * 4,
     )
-    moving, gains, input_grad, grad_inner = sync(moving, gains, input_grad, grad_inner)
-    moving = reduce_step(info, (sums, moving, 4))[0]
-    last = swap(gains, "blk", bits[-1])
     enc_gain_grads, dec_gain_grads = gains[:2] + last[:2], gains[2:] + last[2:]
     grad_query, grad_key, grad_value, grad_output = finish(
         info, reduce_terms(sums, moving), (size,) * 4, (False, False, False, True)

time: 328 us -> 321 us (0.979)
  starting transfers between devices: 69.5 us -> 63.3 us
    ppermute x51, starting transfers between devices: 35.2 us -> 30.2 us  [swap(): return lax.ppermute(value, axis, [(i, i ^ bits) for i in range(size)])]
    unnamed x169 -> x147, local copies, waits for them, and re-layouts: 11.9 us -> 11.4 us
  transfers between devices with their start and end apart: 83 -> 83, of which waited for: 51 -> 49; matrix products, arithmetic and copies ran while one was open for 2% -> 2% of each run, Pallas kernels for 25% -> 26%
where the time goes in v5:
time: 321 us; the launch traced here: 320 us
  waiting for transfers between devices  127 us (40%)
  Pallas kernels  106 us (33%)
  starting transfers between devices  63.3 us (20%)
  local copies, waits for them, and re-layouts  14 us (4%)
  blocking collectives  5.4 us (2%)
    pallas_call x31, Pallas kernels, call(): pl.pallas_call(split, grid=(steps,), in_specs=[pl.BlockSpec(memory_space=...  106 us
    ppermute x51, waiting for transfers between devices, swap(): return lax.ppermute(value, axis, [(i, i ^ bits) for i in range(size)])  71.8 us
    ppermute x21, waiting for transfers between devices, fetch_step(): lax.ppermute(pieces[k + 1 if k < 0 else k - 1], 'blk', forth if k < 0 els...  37.2 us
    ppermute x51, starting transfers between devices, swap(): return lax.ppermute(value, axis, [(i, i ^ bits) for i in range(size)])  30.2 us
    ppermute x21, starting transfers between devices, fetch_step(): lax.ppermute(pieces[k + 1 if k < 0 else k - 1], 'blk', forth if k < 0 els...  22.1 us
    ppermute x11, waiting for transfers between devices, reduce_step(): lax.ppermute(v, 'blk', way)  17.7 us
    unnamed x147, local copies, waits for them, and re-layouts  11.4 us
    ppermute x11, starting transfers between devices, reduce_step(): lax.ppermute(v, 'blk', way)  11 us
  transfers between devices with their start and end apart: 83, of which 49 were waited for; matrix products, arithmetic and copies ran while one was open for 2% of the time, Pallas kernels for 26%

profile of v5, /device:TPU:0, one launch (start us, length us, event | category | flops | bytes accessed | tf_op | source)
XLA Modules:
  0.0 319.9 jit_solution(9754487091141570050)
XLA Ops:
  21.9 5.4 %all_gather.3 = bf16[2,40,768]{2,0,1:T(2,128)(2,1)S(1)} all-gather(bf16[2,10,768]{2,0,1:T(2,128)(2,1)S(1)} %copy.66), channel_id=1, replica_groups=mesh['blk'=8,'head'=4] {'head'}, dimensions={1}, use_global_device_ids=true | all-gather | bytes 153600 | tf_op jit(solution)/shard_map/all_gather | solution.py:1155
  29.6 4.6 %collective-permute-done.8.refs_11_.refs_18_ = bf16[96,768]{1,0:T(8,128)(2,1)S(1)} collective-permute-done((bf16[96,768]{1,0:T(8,128)(2,1)S(1)}, bf16[96,768]{1,0:T(8,128)(2,1)S(1)}, u32[]{:S(2)}, u32[]{:S(2)}) %collective-permute-start.8) | collective-permute-done | bytes 147488 | tf_op jit(solution)/shard_map/ppermute | solution.py:74
  34.2 8.9 %collective-permute-done.9.refs_6_.refs_7_ = bf16[96,3072]{1,0:T(8,128)(2,1)S(1)} collective-permute-done((bf16[96,3072]{1,0:T(8,128)(2,1)S(1)}, bf16[96,3072]{1,0:T(8,128)(2,1)S(1)}, u32[]{:S(2)}, u32[]{:S(2)}) %collective-permute-start.9) | collective-permute-done | bytes 589856 | tf_op jit(solution)/shard_map/ppermute | solution.py:74
  45.1 9.2 %shard_map.427 = (bf16[4,256,576]{2,1,0:T(8,128)(2,1)}, bf16[4,3,256,256]{3,2,1,0:T(8,128)(2,1)}, bf16[4,256,192]{2,1,0:T(8,128)(2,1)}, f32[4,64,768]{2,1,0:T(8,...) custom-call(s32[14]{0:T(128)S(1)} %pad_add_fusion.info_ref, ...), custom_call_target="tpu_custom_call" | custom-call | flops 2013265920 | bytes 8257536 | tf_op jit(solution)/shard_map/pallas_call | solution.py:297
  54.3 3.5 %collective-permute-done.11.refs_5_.refs_6_ = bf16[96,3072]{1,0:T(8,128)(2,1)S(1)} collective-permute-done((bf16[96,3072]{1,0:T(8,128)(2,1)S(1)}, bf16[96,3072]{1,0:T(8,128)(2,1)S(1)}, u32[]{:S(2)}, u32[]{:S(2)}) %collective-permute-start.11) | collective-permute-done | bytes 589856 | tf_op jit(solution)/shard_map/ppermute | solution.py:74
  64.1 10.1 %collective-permute-done.15.refs_3_ = bf16[4,64,768]{2,1,0:T(8,128)(2,1)S(1)} collective-permute-done((bf16[4,64,768]{2,1,0:T(8,128)(2,1)S(1)}, bf16[4,64,768]{2,1,0:T(8,128)(2,1)S(1)}, u32[]{:S(2)}, u32[]{:S(2)}) %collective-permute-start.15) | collective-permute-done | bytes 393248 | tf_op jit(solution)/shard_map/ppermute | solution.py:26
  83.0 9.8 %collective-permute-done.19.refs_2_ = bf16[4,64,768]{2,1,0:T(8,128)(2,1)S(1)} collective-permute-done((bf16[4,64,768]{2,1,0:T(8,128)(2,1)S(1)}, bf16[4,64,768]{2,1,0:T(8,128)(2,1)S(1)}, u32[]{:S(2)}, u32[]{:S(2)}) %collective-permute-start.19) | collective-permute-done | bytes 393248 | tf_op jit(solution)/shard_map/ppermute | solution.py:26
  97.2 7.9 %shard_map.429 = (bf16[4,256,768]{2,1,0:T(8,128)(2,1)}, bf16[4,256,768]{2,1,0:T(8,128)(2,1)}, f32[4,64,768]{2,1,0:T(8,128)S(1)}, bf16[4,64,768]{2,1,0:T(8,128)(2...) custom-call(s32[14]{0:T(128)S(1)} %pad_add_fusion.info_ref, bf16[4,64,768]{2,1,0:T(8,128)(2,1)} %copy-done.20, ...), custom_call_target="tpu_custom_call" | custom-call | flops 2415919104 | bytes 11796480 | tf_op jit(solution)/shard_map/pallas_call | solution.py:297
  110.3 4.0 %shard_map.430 = (bf16[48,768]{1,0:T(8,128)(2,1)}, bf16[48,576]{1,0:T(8,128)(2,1)}, f32[3,48,48]{2,1,0:T(8,128)}, bf16[48,192]{1,0:T(8,128)(2,1)}, f32[48,768]{1...) custom-call(s32[14]{0:T(128)S(1)} %pad_add_fusion.info_ref, ...), custom_call_target="tpu_custom_call" | custom-call | flops 56623104 | bytes 6377856 | tf_op jit(solution)/shard_map/pallas_call | solution.py:297
  124.0 7.1 %collective-permute-done.32.refs_6_ = bf16[96,1536]{1,0:T(8,128)(2,1)S(1)} collective-permute-done((bf16[96,1536]{1,0:T(8,128)(2,1)S(1)}, bf16[96,1536]{1,0:T(8,128)(2,1)S(1)}, u32[]{:S(2)}, u32[]{:S(2)}) %collective-permute-start.32) | collective-permute-done | bytes 294944 | tf_op jit(solution)/shard_map/ppermute | solution.py:74
  131.5 3.6 %collective-permute-done.31.refs_2_.refs_15_ = bf16[5,64,768]{2,1,0:T(8,128)(2,1)S(1)} collective-permute-done((bf16[5,64,768]{2,1,0:T(8,128)(2,1)S(1)}, bf16[5,64,768]{2,1,0:T(8,128)(2,1)S(1)}, u32[]{:S(2)}, u32[]{:S(2)}) %collective-permute-start.31) | collective-permute-done | bytes 491552 | tf_op jit(solution)/shard_map/ppermute | solution.py:26
  137.7 6.3 %shard_map.432 = (bf16[4,256,384]{2,1,0:T(8,128)(2,1)}, f32[48,768]{1,0:T(8,128)}, bf16[48,768]{1,0:T(8,128)(2,1)}, bf16[48,192]{1,0:T(8,128)(2,1)S(1)}, bf16[76...) custom-call(s32[14]{0:T(128)S(1)} %pad_add_fusion.info_ref, ...), custom_call_target="tpu_custom_call" | custom-call | flops 603979776 | bytes 9489600 | tf_op jit(solution)/shard_map/pallas_call | solution.py:297
  145.0 3.5 %collective-permute-done.35.refs_1_ = f32[48,384]{1,0:T(8,128)S(1)} collective-permute-done((f32[48,384]{1,0:T(8,128)S(1)}, f32[48,384]{1,0:T(8,128)S(1)}, u32[]{:S(2)}, u32[]{:S(2)}) %collective-permute-start.35) | collective-permute-done | bytes 73760 | tf_op jit(solution)/shard_map/ppermute | solution.py:26
  153.8 3.8 %shard_map.434 = (bf16[768,768]{1,0:T(8,128)(2,1)}, bf16[768,768]{1,0:T(8,128)(2,1)}, f32[48,768]{1,0:T(8,128)S(1)}) custom-call(s32[14]{0:T(128)S(1)} %pad_add_fusion.info_ref, bf16[48,768]{1,0:T(8,128)(2,1)S(1)} %get-tuple-element.858.refs_0_.refs_1_.refs_6_, bf16[96,1536]{1,0:T(8,128)(2,1)} %copy-done.35, bf16[96,1536]{1,0:T(8,128)(2,1)} %copy-done.46, ...), custom_call_target="tpu_custom_call" | custom-call | flops 56623104 | bytes 4939776 | tf_op jit(solution)/shard_map/pallas_call | solution.py:297
  174.4 4.0 %shard_map.437 = (bf16[4,256,384]{2,1,0:T(8,128)(2,1)}, f32[4,64,768]{2,1,0:T(8,128)S(1)}, bf16[4,64,768]{2,1,0:T(8,128)(2,1)S(1)}, f32[4,64,768]{2,1,0:T(8,128)...) custom-call(s32[14]{0:T(128)S(1)} %pad_add_fusion.info_ref, ...), custom_call_target="tpu_custom_call" | custom-call | flops 603979776 | bytes 5901504 | tf_op jit(solution)/shard_map/pallas_call | solution.py:297
  187.5 3.7 %shard_map.438.refs_10_ = f32[768,384]{1,0:T(8,128)} custom-call(s32[14]{0:T(128)S(1)} %pad_add_fusion.info_ref, bf16[5,64,768]{2,1,0:T(8,128)(2,1)} %copy-done.2, bf16[5,64,768]{2,1,0:T(8,128)(2,1)} %copy-done.22, bf16[5,64,768]{2,1,0:T(8,128)(2,1)} %copy-done.23, bf16[5,64,768]{2,1,0:T(8,128)(2,1)} %copy-done.24, ...), custom_call_target="tpu_custom_call" | custom-call | flops 603979776 | bytes 3932160 | tf_op jit(solution)/shard_map/pallas_call | solution.py:297
  194.6 5.6 %collective-permute-done.53.refs_1_ = f32[48,192]{1,0:T(8,128)S(1)} collective-permute-done((f32[48,192]{1,0:T(8,128)S(1)}, f32[48,192]{1,0:T(8,128)S(1)}, u32[]{:S(2)}, u32[]{:S(2)}) %collective-permute-start.53) | collective-permute-done | bytes 36896 | tf_op jit(solution)/shard_map/ppermute | solution.py:26
  201.9 5.1 %collective-permute-done.52.refs_2_.refs_7_.refs_10_ = bf16[5,64,768]{2,1,0:T(8,128)(2,1)S(1)} collective-permute-done((bf16[5,64,768]{2,1,0:T(8,128)(2,1)S(1)}, bf16[5,64,768]{2,1,0:T(8,128)(2,1)S(1)}, u32[]{:S(2)}, u32[]{:S(2)}) %collective-permute-start.52) | collective-permute-done | bytes 491552 | tf_op jit(solution)/shard_map/ppermute | solution.py:26
  210.7 6.9 %shard_map.442 = (bf16[4,256,768]{2,1,0:T(8,128)(2,1)}, f32[4,64,768]{2,1,0:T(8,128)S(1)}, bf16[4,64,768]{2,1,0:T(8,128)(2,1)S(1)}, f32[4,64,768]{2,1,0:T(8,128)S(1)}, bf16[4,64,768]{2,1,0:T(8,128)(2,1)S(1)}) custom-call(s32[14]{0:T(128)S(1)} %pad_add_fusion.info_ref, bf16[5,64,768]{2,1,0:T(8,128)(2,1)} %copy-done.18, bf16[5,64,768]{2,1,0:T(8,128)(2,1)} %copy-done.36, ...), custom_call_target="tpu_custom_call" | custom-call | flops 2415919104 | bytes 12189696 | tf_op jit(solution)/shard_map/pallas_call | solution.py:297
  224.4 7.6 %shard_map.444 = (f32[96,1920]{1,0:T(8,128)}, bf16[96,1920]{1,0:T(8,128)(2,1)}, bf16[96,1920]{1,0:T(8,128)(2,1)}, bf16[96,1920]{1,0:T(8,128)(2,1)}, bf16[96,1920...) custom-call(s32[14]{0:T(128)S(1)} %pad_add_fusion.info_ref, ...), custom_call_target="tpu_custom_call" | custom-call | flops 2415919104 | bytes 11182080 | tf_op jit(solution)/shard_map/pallas_call | solution.py:297
  237.0 8.6 %collective-permute-done.63.refs_0_ = bf16[96,1920]{1,0:T(8,128)(2,1)S(1)} collective-permute-done((bf16[96,1920]{1,0:T(8,128)(2,1)S(1)}, bf16[96,1920]{1,0:T(8,128)(2,1)S(1)}, u32[]{:S(2)}, u32[]{:S(2)}) %collective-permute-start.63) | collective-permute-done | bytes 368672 | tf_op jit(solution)/shard_map/ppermute | solution.py:137
  252.0 13.6 %shard_map.446 = (f32[4,64,768]{2,1,0:T(8,128)S(1)}, bf16[4,64,768]{2,1,0:T(8,128)(2,1)S(1)}, f32[4,64,768]{2,1,0:T(8,128)S(1)}, bf16[4,64,768]{2,1,0:T(8,128)(2...) custom-call(s32[14]{0:T(128)S(1)} %pad_add_fusion.info_ref, ...), custom_call_target="tpu_custom_call" | custom-call | flops 4429185024 | bytes 11559936 | tf_op jit(solution)/shard_map/pallas_call | solution.py:297
  275.6 6.0 %collective-permute-done.70.refs_0_.refs_2_ = bf16[96,2688]{1,0:T(8,128)(2,1)S(1)} collective-permute-done((bf16[96,2688]{1,0:T(8,128)(2,1)S(1)}, bf16[96,2688]{1,0:T(8,128)(2,1)S(1)}, u32[]{:S(2)}, u32[]{:S(2)}) %collective-permute-start.70) | collective-permute-done | bytes 516128 | tf_op jit(solution)/shard_map/ppermute | solution.py:137
  289.4 6.5 %collective-permute-done.76 = f32[5,768]{1,0:T(8,128)S(1)} collective-permute-done((f32[5,768]{1,0:T(8,128)S(1)}, f32[5,768]{1,0:T(8,128)S(1)}, u32[]{:S(2)}, u32[]{:S(2)}) %collective-permute-start.76) | collective-permute-done | bytes 15392 | tf_op jit(solution)/shard_map/ppermute | solution.py:26
  (351 shorter events, 163.0 us)
Async XLA Ops:
  11.0 16.3 %collective-permute-start.6 = (bf16[4,64,768]{2,1,0:T(8,128)(2,1)S(1)}, bf16[4,64,768]{2,1,0:T(8,128)(2,1)S(1)}, u32[]{:S(2)}, u32[]{:S(2)}) collective-permute-start(bf16[4,64,768]{2,1,0:T(8,128)(2,1)S(1)} %shard_map.426.refs_0_.refs_4_), channel_id=1, source_target_pairs={{0,1},{1,0},{2,3},{3,2},{4,5},{5,4},{6,7},{7,6},{8,9},{9,8},{10,11... | collective-permute-start | bytes 1179656 | tf_op jit(solution)/shard_map/ppermute | solution.py:26
  11.1 16.3 %collective-permute-start.7 = (bf16[4,64,768]{2,1,0:T(8,128)(2,1)S(1)}, bf16[4,64,768]{2,1,0:T(8,128)(2,1)}, u32[]{:S(2)}, u32[]{:S(2)}) collective-permute-start(bf16[4,64,768]{2,1,0:T(8,128)(2,1)S(1)} %shard_map.426.refs_0_.refs_4_), channel_id=1, source_target_pairs={{0,2},{1,3},{2,0},{3,1},{4,6},{5,7},{6,4},{7,5},{8,10},{9,11},{10,... | collective-permute-start | bytes 1179656 | tf_op jit(solution)/shard_map/ppermute | solution.py:26
  27.4 15.6 %collective-permute-start.9 = (bf16[96,3072]{1,0:T(8,128)(2,1)S(1)}, bf16[96,3072]{1,0:T(8,128)(2,1)S(1)}, u32[]{:S(2)}, u32[]{:S(2)}) collective-permute-start(bf16[96,3072]{1,0:T(8,128)(2,1)S(1)} %concatenate.15.refs_4_.refs_5_), channel_id=1, source_target_pairs={{8,0},{16,8},{24,16},{28,24},{20,28},{12,20},{4,12},{0,4},{9,1},{1... | collective-permute-start | bytes 1769480 | tf_op jit(solution)/shard_map/ppermute | solution.py:74
  43.0 14.8 %collective-permute-start.11 = (bf16[96,3072]{1,0:T(8,128)(2,1)S(1)}, bf16[96,3072]{1,0:T(8,128)(2,1)S(1)}, u32[]{:S(2)}, u32[]{:S(2)}) collective-permute-start(bf16[96,3072]{1,0:T(8,128)(2,1)S(1)} %concatenate.15.refs_4_.refs_5_), channel_id=1, source_target_pairs={{0,8},{8,16},{16,24},{24,28},{28,20},{20,12},{12,4},{4,0},{1,9},{9... | collective-permute-start | bytes 1769480 | tf_op jit(solution)/shard_map/ppermute | solution.py:74
  44.6 14.5 %collective-permute-start.12 = (bf16[96,3072]{1,0:T(8,128)(2,1)S(1)}, bf16[96,3072]{1,0:T(8,128)(2,1)S(1)}, u32[]{:S(2)}, u32[]{:S(2)}) collective-permute-start(bf16[96,3072]{1,0:T(8,128)(2,1)S(1)} %collective-permute-done.9.refs_6_.refs_7_), channel_id=1, source_target_pairs={{8,0},{16,8},{24,16},{28,24},{20,28},{12,20},{4,12},{0,4},{9,1},{1... | collective-permute-start | bytes 1769480 | tf_op jit(solution)/shard_map/ppermute | solution.py:74
  61.4 15.4 %collective-permute-start.16 = (bf16[96,3072]{1,0:T(8,128)(2,1)S(1)}, bf16[96,3072]{1,0:T(8,128)(2,1)S(1)}, u32[]{:S(2)}, u32[]{:S(2)}) collective-permute-start(bf16[96,3072]{1,0:T(8,128)(2,1)S(1)} %collective-permute-done.11.refs_5_.refs_6_), channel_id=1, source_target_pairs={{0,8},{8,16},{16,24},{24,28},{28,20},{20,12},{12,4},{4,0},{1,9},{9... | collective-permute-start | bytes 1769480 | tf_op jit(solution)/shard_map/ppermute | solution.py:74
  62.9 15.1 %collective-permute-start.17 = (bf16[96,3072]{1,0:T(8,128)(2,1)S(1)}, bf16[96,3072]{1,0:T(8,128)(2,1)S(1)}, u32[]{:S(2)}, u32[]{:S(2)}) collective-permute-start(bf16[96,3072]{1,0:T(8,128)(2,1)S(1)} %collective-permute-done.12.refs_8_.refs_9_), channel_id=1, source_target_pairs={{8,0},{16,8},{24,16},{28,24},{20,28},{12,20},{4,12},{0,4},{9,1},{1... | collective-permute-start | bytes 1769480 | tf_op jit(solution)/shard_map/ppermute | solution.py:74
  79.2 14.3 %collective-permute-start.20 = (bf16[96,3072]{1,0:T(8,128)(2,1)S(1)}, bf16[96,3072]{1,0:T(8,128)(2,1)S(1)}, u32[]{:S(2)}, u32[]{:S(2)}) collective-permute-start(bf16[96,3072]{1,0:T(8,128)(2,1)S(1)} %collective-permute-done.16.refs_7_.refs_8_), channel_id=1, source_target_pairs={{0,8},{8,16},{16,24},{24,28},{28,20},{20,12},{12,4},{4,0},{1,9},{9... | collective-permute-start | bytes 1769480 | tf_op jit(solution)/shard_map/ppermute | solution.py:74
  80.4 13.9 %collective-permute-start.21 = (bf16[96,3072]{1,0:T(8,128)(2,1)S(1)}, bf16[96,3072]{1,0:T(8,128)(2,1)S(1)}, u32[]{:S(2)}, u32[]{:S(2)}) collective-permute-start(bf16[96,3072]{1,0:T(8,128)(2,1)S(1)} %collective-permute-done.17.refs_10_.refs_11_), channel_id=1, source_target_pairs={{8,0},{16,8},{24,16},{28,24},{20,28},{12,20},{4,12},{0,4},{9,1},{1... | collective-permute-start | bytes 1769480 | tf_op jit(solution)/shard_map/ppermute | solution.py:74
  81.3 11.5 %collective-permute-start.19 = (bf16[4,64,768]{2,1,0:T(8,128)(2,1)S(1)}, bf16[4,64,768]{2,1,0:T(8,128)(2,1)S(1)}, u32[]{:S(2)}, u32[]{:S(2)}) collective-permute-start(bf16[4,64,768]{2,1,0:T(8,128)(2,1)S(1)} %get-tuple-element.506.refs_0_), channel_id=1, source_target_pairs={{0,2},{1,3},{2,0},{3,1},{4,6},{5,7},{6,4},{7,5},{8,10},{9,11},{10,... | collective-permute-start | bytes 1179656 | tf_op jit(solution)/shard_map/ppermute | solution.py:26
  121.5 13.6 %collective-permute-start.31 = (bf16[5,64,768]{2,1,0:T(8,128)(2,1)S(1)}, bf16[5,64,768]{2,1,0:T(8,128)(2,1)S(1)}, u32[]{:S(2)}, u32[]{:S(2)}) collective-permute-start(bf16[5,64,768]{2,1,0:T(8,128)(2,1)S(1)} %get-tuple-element.561.refs_0_), channel_id=1, source_target_pairs={{0,2},{1,3},{2,0},{3,1},{4,6},{5,7},{6,4},{7,5},{8,10},{9,11},{10,... | collective-permute-start | bytes 1474568 | tf_op jit(solution)/shard_map/ppermute | solution.py:26
  135.1 14.2 %collective-permute-start.36 = (bf16[96,1536]{1,0:T(8,128)(2,1)S(1)}, bf16[96,1536]{1,0:T(8,128)(2,1)S(1)}, u32[]{:S(2)}, u32[]{:S(2)}) collective-permute-start(bf16[96,1536]{1,0:T(8,128)(2,1)S(1)} %collective-permute-done.32.refs_6_), channel_id=1, source_target_pairs={{0,8},{8,16},{16,24},{24,28},{28,20},{20,12},{12,4},{4,0},{1,9},{9... | collective-permute-start | bytes 884744 | tf_op jit(solution)/shard_map/ppermute | solution.py:74
  180.9 11.5 %collective-permute-start.48 = (bf16[4,64,768]{2,1,0:T(8,128)(2,1)S(1)}, bf16[4,64,768]{2,1,0:T(8,128)(2,1)S(1)}, u32[]{:S(2)}, u32[]{:S(2)}) collective-permute-start(bf16[4,64,768]{2,1,0:T(8,128)(2,1)S(1)} %add_convert_fusion.2), channel_id=1, source_target_pairs={{0,2},{1,3},{2,0},{3,1},{4,6},{5,7},{6,4},{7,5},{8,10},{9,11},{10,... | collective-permute-start | bytes 1179656 | tf_op jit(solution)/shard_map/ppermute | solution.py:26
  193.3 13.6 %collective-permute-start.52 = (bf16[5,64,768]{2,1,0:T(8,128)(2,1)S(1)}, bf16[5,64,768]{2,1,0:T(8,128)(2,1)S(1)}, u32[]{:S(2)}, u32[]{:S(2)}) collective-permute-start(bf16[5,64,768]{2,1,0:T(8,128)(2,1)S(1)} %get-tuple-element.671.refs_0_.refs_5_), channel_id=1, source_target_pairs={{0,2},{1,3},{2,0},{3,1},{4,6},{5,7},{6,4},{7,5},{8,10},{9,11},{10,... | collective-permute-start | bytes 1474568 | tf_op jit(solution)/shard_map/ppermute | solution.py:26
  220.1 11.9 %collective-permute-start.60 = (bf16[4,64,768]{2,1,0:T(8,128)(2,1)S(1)}, bf16[4,64,768]{2,1,0:T(8,128)(2,1)S(1)}, u32[]{:S(2)}, u32[]{:S(2)}) collective-permute-start(bf16[4,64,768]{2,1,0:T(8,128)(2,1)S(1)} %add_convert_fusion.1), channel_id=1, source_target_pairs={{0,2},{1,3},{2,0},{3,1},{4,6},{5,7},{6,4},{7,5},{8,10},{9,11},{10,... | collective-permute-start | bytes 1179656 | tf_op jit(solution)/shard_map/ppermute | solution.py:26
  233.7 13.1 %collective-permute-start.61 = (bf16[5,64,768]{2,1,0:T(8,128)(2,1)S(1)}, bf16[5,64,768]{2,1,0:T(8,128)(2,1)S(1)}, u32[]{:S(2)}, u32[]{:S(2)}) collective-permute-start(bf16[5,64,768]{2,1,0:T(8,128)(2,1)S(1)} %get-tuple-element.711.refs_0_), channel_id=1, source_target_pairs={{0,1},{1,0},{2,3},{3,2},{4,5},{5,4},{6,7},{7,6},{8,9},{9,8},{10,11... | collective-permute-start | bytes 1474568 | tf_op jit(solution)/shard_map/ppermute | solution.py:26
  233.8 13.6 %collective-permute-start.62 = (bf16[5,64,768]{2,1,0:T(8,128)(2,1)S(1)}, bf16[5,64,768]{2,1,0:T(8,128)(2,1)S(1)}, u32[]{:S(2)}, u32[]{:S(2)}) collective-permute-start(bf16[5,64,768]{2,1,0:T(8,128)(2,1)S(1)} %get-tuple-element.711.refs_0_), channel_id=1, source_target_pairs={{0,2},{1,3},{2,0},{3,1},{4,6},{5,7},{6,4},{7,5},{8,10},{9,11},{10,... | collective-permute-start | bytes 1474568 | tf_op jit(solution)/shard_map/ppermute | solution.py:26
  249.1 16.5 %collective-permute-start.66 = (bf16[96,1920]{1,0:T(8,128)(2,1)S(1)}, bf16[96,1920]{1,0:T(8,128)(2,1)S(1)}, u32[]{:S(2)}, u32[]{:S(2)}) collective-permute-start(bf16[96,1920]{1,0:T(8,128)(2,1)S(1)} %get-tuple-element.731), channel_id=1, source_target_pairs={{0,8},{8,16},{16,24},{24,28},{28,20},{20,12},{12,4},{4,0},{1,9},{9... | collective-permute-start | bytes 1105928 | tf_op jit(solution)/shard_map/ppermute | solution.py:137
  250.5 15.1 %collective-permute-start.67 = (bf16[96,1920]{1,0:T(8,128)(2,1)S(1)}, bf16[96,1920]{1,0:T(8,128)(2,1)S(1)}, u32[]{:S(2)}, u32[]{:S(2)}) collective-permute-start(bf16[96,1920]{1,0:T(8,128)(2,1)S(1)} %get-tuple-element.732), channel_id=1, source_target_pairs={{8,0},{16,8},{24,16},{28,24},{20,28},{12,20},{4,12},{0,4},{9,1},{1... | collective-permute-start | bytes 1105928 | tf_op jit(solution)/shard_map/ppermute | solution.py:137
  268.1 13.5 %collective-permute-start.70 = (bf16[96,2688]{1,0:T(8,128)(2,1)S(1)}, bf16[96,2688]{1,0:T(8,128)(2,1)S(1)}, u32[]{:S(2)}, u32[]{:S(2)}) collective-permute-start(bf16[96,2688]{1,0:T(8,128)(2,1)S(1)} %get-tuple-element.747), channel_id=1, source_target_pairs={{0,8},{8,16},{16,24},{24,28},{28,20},{20,12},{12,4},{4,0},{1,9},{9... | collective-permute-start | bytes 1548296 | tf_op jit(solution)/shard_map/ppermute | solution.py:137
  269.5 13.1 %collective-permute-start.71 = (bf16[96,2688]{1,0:T(8,128)(2,1)S(1)}, bf16[96,2688]{1,0:T(8,128)(2,1)S(1)}, u32[]{:S(2)}, u32[]{:S(2)}) collective-permute-start(bf16[96,2688]{1,0:T(8,128)(2,1)S(1)} %get-tuple-element.748), channel_id=1, source_target_pairs={{8,0},{16,8},{24,16},{28,24},{20,28},{12,20},{4,12},{0,4},{9,1},{1... | collective-permute-start | bytes 1548296 | tf_op jit(solution)/shard_map/ppermute | solution.py:137
  285.1 14.7 %collective-permute-start.74 = (bf16[96,2688]{1,0:T(8,128)(2,1)S(1)}, bf16[96,2688]{1,0:T(8,128)(2,1)S(1)}, u32[]{:S(2)}, u32[]{:S(2)}) collective-permute-start(bf16[96,2688]{1,0:T(8,128)(2,1)S(1)} %get-tuple-element.771), channel_id=1, source_target_pairs={{0,8},{8,16},{16,24},{24,28},{28,20},{20,12},{12,4},{4,0},{1,9},{9... | collective-permute-start | bytes 1548296 | tf_op jit(solution)/shard_map/ppermute | solution.py:137
  285.7 14.1 %collective-permute-start.73 = (bf16[4,64,768]{2,1,0:T(8,128)(2,1)S(1)}, bf16[4,64,768]{2,1,0:T(8,128)(2,1)S(1)}, u32[]{:S(2)}, u32[]{:S(2)}) collective-permute-start(bf16[4,64,768]{2,1,0:T(8,128)(2,1)S(1)} %add_convert_fusion), channel_id=1, source_target_pairs={{0,2},{1,3},{2,0},{3,1},{4,6},{5,7},{6,4},{7,5},{8,10},{9,11},{10,... | collective-permute-start | bytes 1179656 | tf_op jit(solution)/shard_map/ppermute | solution.py:26
  287.0 12.8 %collective-permute-start.75 = (bf16[96,768]{1,0:T(8,128)(2,1)S(1)}, bf16[96,768]{1,0:T(8,128)(2,1)S(1)}, u32[]{:S(2)}, u32[]{:S(2)}) collective-permute-start(bf16[96,768]{1,0:T(8,128)(2,1)S(1)} %get-tuple-element.772), channel_id=1, source_target_pairs={{8,0},{16,8},{24,16},{28,24},{20,28},{12,20},{4,12},{0,4},{9,1},{1... | collective-permute-start | bytes 442376 | tf_op jit(solution)/shard_map/ppermute | solution.py:137
  (129 other events, 1145.7 us)

commit v6 on v5

--- a/solution.py
+++ b/solution.py
@@ -13,7 +13,7 @@
 LANES = 128
 EPS = 1e-06
 VMEM_LIMIT = 24 * 1024 * 1024
-LARGE = 1 << 18
+LARGE = 1 << 19
 masked_score = -1000000000.0
 f32 = jnp.float32
 bf16 = jnp.bfloat16
@@ -101,10 +101,10 @@
     return value if isinstance(value, Part) else Part(value, 0, value.shape[1])
 
 
-def reduce_step(info, *rings):
+def reduce_step(info, *rings, hold=None):
     count = lax.axis_size("blk")
     if count != 8:
-        return [[] for _ in rings]
+        return [[] for _ in rings] + [hold]
     forth, back = ring_steps(count)
     plan = [[], []]
     for pieces, moving, step in rings:
@@ -134,6 +134,8 @@
         wide = [sum(part(terms[0]).width for terms in p) for p in plan]
         shapes = [like((rows, w), bf16) for w in wide]
         sent = call(body, info, [], [p.array for p in parts], [], [Near(v) for v in shapes], least=0)
+    if hold is not None:
+        sent, hold = sync(sent, hold)
     came = [lax.ppermute(v, "blk", way) for v, way in zip(sent, (forth, back), strict=False)]
     results, column = [], 0
     for k, (pieces, moving, step) in enumerate(rings):
@@ -146,7 +148,7 @@
             found.append(Part(came[1], before, wide))
         results.append(found)
         column += wide
-    return results
+    return [*results, hold]
 
 
 def reduce_terms(pieces, moving):
@@ -266,7 +268,7 @@
         return pl.BlockSpec((each, *shape[1:]), lambda b: (jnp.minimum(b, last),) + (0,) * (len(shape) - 1))
 
     def whole(a):
-        if isinstance(a, Far):
+        if type(a) is Far:
             return pl.BlockSpec(memory_space=pltpu.HBM)
         if isinstance(a, Rider):
             return pl.BlockSpec(a.shape, lambda b: (a.index, 0, 0))
@@ -284,7 +286,7 @@
 
     def given(a):
         array = a.array if isinstance(a, (Columns, Far, Rider)) else a
-        far = large(a) or isinstance(a, Rider)
+        far = (large(a) and not isinstance(a, Close)) or isinstance(a, Rider)
         return pltpu.with_memory_space_constraint(array, pltpu.HBM) if far else array
 
     def made(a):
@@ -343,6 +345,10 @@
         self.array, self.shape, self.dtype = array, array.shape, array.dtype
 
 
+class Close(Far):
+    pass
+
+
 def like(shape, dtype):
     return jax.ShapeDtypeStruct(tuple(shape), dtype)
 
@@ -403,6 +409,28 @@
 
 def piece_shapes(rows, columns):
     return [Later(like((rows, columns), d)) for d in (f32, *[bf16] * 7)]
+
+
+def gathered(info, pieces, widths, column_from=0):
+    rows, wide = pieces[0].shape[0] * len(pieces), sum(widths)
+
+    def body(info, _, ins, __, outs, scratch):
+        together, signals = scratch
+        assemble(info, ins, (together,), signals, column_from)
+        column = 0
+        for out in outs:
+            out[...] = together[:, column : column + out.shape[1]]
+            column += out.shape[1]
+
+    return call(
+        body,
+        info,
+        [],
+        [Far(p) for p in pieces],
+        [],
+        [Near(like((rows, w), bf16)) for w in widths],
+        [pltpu.VMEM((rows, wide), bf16), pltpu.SemaphoreType.DMA((1, len(pieces)))],
+    )
 
 
 def attention_scratch(width, size, pieces):
@@ -461,7 +489,7 @@
     )
 
 
-def encoder_attention_back(info, grads, normed, qkv, probs, context, pieces, gains):
+def encoder_attention_back(info, grads, normed, qkv, probs, context, weights, gains):
     blocks, part, width = normed[0].shape
     slot = part * len(normed)
     size = context.shape[2]
@@ -469,16 +497,13 @@
     def body(info, stepped, fixed, outs, ends, scratch):
         grad_refs, normed_refs = stepped[:4], stepped[4:8]
         qkv, probs, context = stepped[8:]
-        weight_pieces, gains = fixed[:-1], fixed[-1]
+        w_in, w_out, gains = fixed
         pieces, gain_out = ends[:-1], ends[-1]
-        w_in, w_out, together, signals, total_in, total_out, moved = scratch
+        total_in, total_out, moved = scratch
         b = pl.program_id(0)
 
         @pl.when(b == 0)
         def _():
-            assemble(info, weight_pieces, (together,), signals)
-            w_in[...] = together[:, : 3 * size]
-            w_out[...] = together[:, 3 * size :]
             total_in[...] = jnp.zeros_like(total_in)
             total_out[...] = jnp.zeros_like(total_out)
             gain_out[...] = jnp.zeros_like(gain_out)
@@ -512,11 +537,10 @@
         body,
         info,
         [*grads, *normed, qkv, probs, context],
-        [*(Far(p) for p in pieces), gains],
+        [*(Close(w) for w in weights), gains],
         partial_rows(blocks, part, width),
         [*piece_shapes(width // 8, 4 * size), like((1, width), f32)],
         [
-            *attention_scratch(width, size, pieces),
             pltpu.VMEM((width, 3 * size), f32),
             pltpu.VMEM((width, size), f32),
             pltpu.VMEM((slot, 3 * size), bf16),
@@ -566,19 +590,14 @@
     )
 
 
-def encoder_ffn_back(info, grads, slope, pieces):
+def encoder_ffn_back(info, grads, slope, weights):
     blocks, (_, part, width) = slope.shape[0], grads[0].shape
     slot = part * len(grads)
     hidden = slope.shape[2]
 
-    def body(info, stepped, pieces, outs, ends, scratch):
+    def body(info, stepped, weights, outs, ends, scratch):
         dinner = outs[0]
-        w_inner, w_outer, signals = scratch
-
-        @pl.when(pl.program_id(0) == 0)
-        def _():
-            assemble(info, pieces, (w_inner, w_outer), signals)
-
+        w_inner, w_outer = weights
         back = dot(token_rows(stepped[:4]), w_outer[...])
         low = (back * stepped[4][...].reshape(back.shape).astype(f32)).astype(bf16)
         dinner[...] = low.reshape(dinner.shape)
@@ -588,10 +607,9 @@
         body,
         info,
         [*grads, slope],
-        [Far(p) for p in pieces],
+        [Close(w) for w in weights],
         [like((blocks, slot, hidden), bf16), *partial_rows(blocks, part, width)],
         [],
-        ffn_scratch(width, hidden, pieces),
         flops=4 * blocks * slot * width * hidden,
         steps=blocks // 2,
         each=2,
@@ -643,27 +661,23 @@
     return call(body, info, [], [t.array for t in terms], [], [like(s, f32) for s in shapes])
 
 
-def cross_forward(info, states, pieces, column_from, decoder, own_question, count_q, count_pass):
+def cross_forward(info, states, weights, decoder, own_question, count_q, count_pass):
     rows_in, terms, gains = decoder
     blocks = count_q * count_pass
     _, part, width = states[0].shape
     slot = part * len(states)
     rows_dec = rows_in.shape[0]
-    size = (pieces[0].shape[1] - column_from) // 4
+    size = weights[1].shape[1]
     steps = 2
 
     def body(info, rows, fixed, outs, ends, scratch):
-        pieces, question = fixed[: len(pieces_given)], fixed[-1]
-        rows_in, *terms, gains = fixed[len(pieces_given) : -1]
-        after_self, normed, queries, w_query, w_output, stats, weight = ends
-        held, asked, signals = scratch
+        weight, w_query, rows_in, *terms, gains, question = fixed
+        after_self, normed, queries, stats = ends
+        held = scratch[0]
         b = pl.program_id(0)
 
         @pl.when(b == 0)
         def _():
-            assemble(info, pieces, (weight, asked), signals, column_from)
-            w_query[...] = asked[:, :size]
-            w_output[...] = asked[:, size:]
             after_self[...] = rows_in[...].astype(f32) + summed(terms)
             normed[...] = norm_rows(after_self[...], gains[1:2, :]).astype(bf16)
             queries[...] = dot(normed[...], w_query[...]).astype(bf16)
@@ -689,27 +703,19 @@
                 stats[:, at : at + HDIM] = dot(spread_out.astype(bf16), vals[k])
                 stats[:, at + HDIM : at + LANES] = jnp.where(lane == 0, top, total)
 
-    pieces_given = pieces
     return call(
         body,
         info,
         states,
-        [*(Far(p) for p in pieces), rows_in, *terms, gains, own_question],
+        [*(Close(w) for w in weights), rows_in, *terms, gains, own_question],
         [like((blocks, slot, 2 * size), bf16)],
         [
             Later(like((rows_dec, width), f32)),
             Later(like((rows_dec, width), bf16)),
             like((rows_dec, size), bf16),
-            Later(like((width, size), bf16)),
-            like((width, size), bf16),
             like((rows_dec, size // HDIM * LANES), f32),
-            like((width, 2 * size), bf16),
         ],
-        [
-            pltpu.VMEM((blocks * slot, 2 * size), bf16),
-            pltpu.VMEM((width, 2 * size), bf16),
-            pltpu.SemaphoreType.DMA((2, len(pieces))),
-        ],
+        [pltpu.VMEM((blocks * slot, 2 * size), bf16)],
         flops=4 * blocks * slot * width * size,
         steps=steps,
         each=blocks // steps,
@@ -823,7 +829,18 @@
         body,
         info,
         [key_vals],
-        [cotangent, after_cross, *terms, gains, w_output, out, log_total, queries, weight, own_question],
+        [
+            cotangent,
+            after_cross,
+            *terms,
+            gains,
+            w_output,
+            out,
+            log_total,
+            queries,
+            Close(weight),
+            own_question,
+        ],
         [like(key_vals.shape, bf16), *partial_rows(blocks, part, width)],
         [
             Later(like((rows_dec, width), f32)),
@@ -907,7 +924,7 @@
         [],
         [cotangent, *(Far(p) for p in pieces)],
         [],
-        [*[like((width, hidden), bf16)] * 2, like((count, hidden), f32)],
+        [Near(like((width, hidden), bf16)), like((width, hidden), bf16), like((count, hidden), f32)],
         [pltpu.SemaphoreType.DMA((2, len(pieces)))],
         flops=2 * count * width * hidden,
     )
@@ -932,7 +949,7 @@
         body,
         info,
         [],
-        [after_self, *terms, back, gains, w_inner],
+        [after_self, *terms, back, gains, Close(w_inner)],
         [],
         [
             like((count, width), f32),
@@ -1168,33 +1185,32 @@
     partial, ffn = sync(partial, ffn)
 
     def to_core(partial):
-        return [swap(partial[1], "head", 1), swap(partial[3], "head", 1)]
-
-    def to_chip(partial, beside):
-        return swap((partial[2] + beside[1].astype(f32)).astype(bf16), "head", 2)
-
-    beside = to_core(partial)
-    partial, beside, ffn = sync(partial, beside, ffn)
-    across = to_chip(partial, beside)
+        return swap(partial[3], "head", 1)
+
+    def to_chip(partial, corner):
+        far = (partial[2] + corner.astype(f32)).astype(bf16)
+        return [swap(far, "head", 2), swap(partial[1], "head", 1)]
+
     ffn = fetch_step(ffn, -2, 3)
-    partial, beside, across, ffn = sync(partial, beside, across, ffn)
+    partial, corner = sync(partial, to_core(partial))
+    partial, arrived, ffn = sync(partial, to_chip(partial, corner), ffn)
 
     def enter_ffn(x, a, b, c, g):
         hidden = x + a + b + c
         return hidden, norm_rows(hidden, g[1:2])
 
     hidden, second = by_rows(
-        enter_ffn, info, [inputs, partial[0], beside[0], across], [encoder_gains], [f32, bf16]
-    )
+        enter_ffn, info, [inputs, partial[0], *arrived], [encoder_gains], [f32, bf16]
+    )
+    ffn = fetch_step(ffn, -3, 4)
     def spread(rows):
         return [rows, swap(rows, "head", 1), swap(rows, "head", 2)]
 
     def riders(all_rows):
         return [Rider(rows, blocks) for rows in all_rows[1:]]
 
-    second, ffn, dec_ffn = sync(second, ffn, dec_ffn)
+    second, dec_ffn = sync(second, dec_ffn)
     second_all = spread(second)
-    ffn = fetch_step(ffn, -3, 4)
     second_all, ffn, dec_ffn = sync(second_all, ffn, dec_ffn)
     dec_ffn = fetch_step(fetch_start(dec_ffn), -1, 1)
     second_all.append(swap(second_all[2], "head", 1))
@@ -1203,8 +1219,7 @@
 
     active, slope, *partial = encoder_ffn(info, second_all, ffn, units)
     partial, dec_ffn = sync(partial, dec_ffn)
-    beside = to_core(partial)
-    partial, beside, both, dec_ffn = sync(partial, beside, both, dec_ffn)
+    partial, corner, both, dec_ffn = sync(partial, to_core(partial), both, dec_ffn)
     dec_in, cotangent = both[0], both[1]
 
     index = np.arange(filled)
@@ -1214,18 +1229,16 @@
     order = (jnp.asarray(order[:, None]), jnp.asarray(order[None, :]))
     question = jnp.asarray(question[:, None].astype(np.int32))
 
-    across = to_chip(partial, beside)
+    arrived = to_chip(partial, corner)
     dec_ffn = fetch_step(dec_ffn, -2, 2)
     third, dec_qkv, dec_probs, dec_context, mine, sent, w_self = decoder_self(
         info, dec_in, decoder_gains, ffn, at_self, size, order
     )
-    partial, beside, across, mine, sent, dec_ffn = sync(
-        partial, beside, across, mine, sent, dec_ffn
-    )
+    partial, arrived, mine, sent, dec_ffn = sync(partial, arrived, mine, sent, dec_ffn)
     states, states_sent = by_rows(
         lambda h, a, b, c: (h + a + b + c,),
         info,
-        [hidden, partial[0], beside[0], across],
+        [hidden, partial[0], *arrived],
         [],
         [bf16],
         riders=sent,
@@ -1233,24 +1246,17 @@
     states_sent, dec_ffn = sync(states_sent, dec_ffn)
     states_all = spread(states_sent)
     dec_ffn = fetch_step(dec_ffn, -3, 3)
-    states_all, dec_ffn = sync(states_all, dec_ffn)
+    w_cross, w_cross_query, w_cross_output = gathered(
+        info, ffn, (2 * size, size, size), at_cross
+    )
+    states_all, dec_ffn, w_cross = sync(states_all, dec_ffn, w_cross)
     dec_ffn = fetch_step(dec_ffn, -4)
     states_all = sync(*states_all, swap(states_all[2], "head", 1))
 
-    (
-        key_vals,
-        after_self,
-        fourth,
-        queries,
-        w_cross_query,
-        w_cross_output,
-        stats,
-        w_cross,
-    ) = cross_forward(
+    key_vals, after_self, fourth, queries, stats = cross_forward(
         info,
         states_all,
-        ffn,
-        at_cross,
+        (w_cross, w_cross_query),
         (dec_in, [mine, *riders(states_all)], decoder_gains),
         question,
         count_q,
@@ -1297,14 +1303,13 @@
         return value
 
     partial, dqueries, dkey_vals = sync(partial, dqueries, dkey_vals)
-    beside = to_core(partial)
-    partial, beside, dkey_vals, dqueries = sync(partial, beside, dkey_vals, dqueries)
-    across = to_chip(partial, beside)
+    partial, corner, dkey_vals, dqueries = sync(partial, to_core(partial), dkey_vals, dqueries)
+    arrived = to_chip(partial, corner)
     dqueries = some(dqueries, bits[:-1])
     cross_sum = weight_grads(info, [(states_all, dkey_vals)], cut=False)[0]
     _, out_mine, out_sent = rows_back(info, [dec_active], w_dec_outer)
-    partial, beside, across, cross_sum, dqueries, out_sent = sync(
-        partial, beside, across, cross_sum, dqueries, out_sent
+    partial, arrived, cross_sum, dqueries, out_sent = sync(
+        partial, arrived, cross_sum, dqueries, out_sent
     )
 
     def enter_back(cot, a, b, c):
@@ -1314,7 +1319,7 @@
     dstates, dstates_low = by_rows(
         enter_back,
         info,
-        [encoder_cotangent.reshape(blocks, part, width), partial[0], beside[0], across],
+        [encoder_cotangent.reshape(blocks, part, width), partial[0], *arrived],
         [],
         [f32, bf16],
         riders=out_sent,
@@ -1324,16 +1329,16 @@
     dstates_all = spread(dstates_low)
     terms = [dqueries, swap(dqueries, "blk", bits[-1])]
     dqueries, mine, sent = rows_back(info, terms, w_cross_query)
-    dstates_all, sent = sync(dstates_all, sent)
+    w_ffn = gathered(info, ffn, (units, units))
+    dstates_all, sent, w_ffn = sync(dstates_all, sent, w_ffn)
     dstates_all.append(swap(dstates_all[2], "head", 1))
     dstates_all, sent = sync(dstates_all, sent)
     out_terms = [out_mine, *riders(dstates_all)]
-    dinner, *partial = encoder_ffn_back(info, dstates_all, slope, ffn)
+    dinner, *partial = encoder_ffn_back(info, dstates_all, slope, w_ffn)
     terms = [mine, *share(sent)]
     partial, dinner, terms = sync(partial, dinner, terms)
-    beside = to_core(partial)
-    partial, beside, dinner, dstates_all = sync(partial, beside, dinner, dstates_all)
-    across = to_chip(partial, beside)
+    partial, corner, dinner, dstates_all = sync(partial, to_core(partial), dinner, dstates_all)
+    arrived = to_chip(partial, corner)
     dself, dself_low, gain_three, dself_qkv, own_back, sent_back = decoder_self_back(
         info,
         dcross,
@@ -1347,9 +1352,7 @@
     ffn_sums = weight_grads(
         info, [(second_all, dinner), (dstates_all, active)], [cross_sum]
     )
-    partial, beside, across, ffn_sums, sent_back = sync(
-        partial, beside, across, ffn_sums, sent_back
-    )
+    partial, arrived, ffn_sums, sent_back = sync(partial, arrived, ffn_sums, sent_back)
 
     def middle_back(dy, h, a, b, c, g):
         back, gain_rows = norm_back(h, g[1:2], a + b + c)
@@ -1359,7 +1362,7 @@
     dhidden, dhidden_low, gain_one = by_rows(
         middle_back,
         info,
-        [dstates, hidden, partial[0], beside[0], across],
+        [dstates, hidden, partial[0], *arrived],
         [encoder_gains],
         [f32, bf16],
         gain=True,
@@ -1369,17 +1372,18 @@
     dhidden_low, ffn_sums = sync(dhidden_low, ffn_sums)
     dhidden_all = spread(dhidden_low)
     ffn_moving = reduce_step(info, (ffn_sums, None, 1))[0]
-    dhidden_all, ffn_moving = sync(dhidden_all, ffn_moving)
+    w_attention = gathered(info, in_turn(attention), (3 * size, size))
+    dhidden_all, ffn_moving, w_attention = sync(dhidden_all, ffn_moving, w_attention)
     ffn_moving = reduce_step(info, (ffn_sums, ffn_moving, 2))[0]
     dhidden_all = sync(*dhidden_all, swap(dhidden_all[2], "head", 1))
     terms = [own_back, *riders(dhidden_all)]
 
     partial, sums, gain_zero = encoder_attention_back(
-        info, dhidden_all, first_all, qkv, probs, context, in_turn(attention), encoder_gains
+        info, dhidden_all, first_all, qkv, probs, context, w_attention, encoder_gains
     )
     partial, sums, ffn_moving, gain_zero = sync(partial, sums, ffn_moving, gain_zero)
-    ffn_moving, moving = reduce_step(info, (ffn_sums, ffn_moving, 3), (sums, None, 1))
-    beside = to_core(partial)
+    ffn_moving, moving = reduce_step(info, (ffn_sums, ffn_moving, 3), (sums, None, 1))[:2]
+    corner = to_core(partial)
     dec_grad, dec_states, gains = decoder_ends(
         info,
         dec_in,
@@ -1392,7 +1396,8 @@
         [gain_zero, gain_one],
         dec_own,
     )
-    gains = gains + swap(gains, "head", 1)
+    for k in (1, 2):
+        gains = gains + swap(gains, "head", k)
     (
         grad_dec_query,
         grad_dec_key,
@@ -1413,20 +1418,22 @@
         ],
         [(dec_context, dself_low), (cross_context, dcross_low)],
     )
-    partial, beside, moving, gains, ffn_moving, grad_dec_query = sync(
-        partial, beside, moving, gains, ffn_moving, grad_dec_query
-    )
+    partial, corner, moving, gains, ffn_moving, grad_dec_query = sync(
+        partial, corner, moving, gains, ffn_moving, grad_dec_query
+    )
+
+    def dec_shape(values):
+        return values.reshape(count_q, dec_part, width)
 
     def own_rows(values):
         return lax.dynamic_slice_in_dim(values, head * dec_own, dec_own, 0)
 
-    ffn_moving, moving = reduce_step(info, (ffn_sums, ffn_moving, 4), (sums, moving, 2))
-    across = to_chip(partial, beside)
-    gains = gains + swap(gains, "head", 2)
+    ffn_moving, moving = reduce_step(info, (ffn_sums, ffn_moving, 4), (sums, moving, 2))[:2]
+    arrived = to_chip(partial, corner)
     gains = some(gains, bits[:1])
-    dec_states, dec_grad = own_rows(dec_states), own_rows(dec_grad)
-    partial, beside, across, moving, gains, ffn_moving = sync(
-        partial, beside, across, moving, gains, ffn_moving
+    dec_states, dec_grad = dec_shape(own_rows(dec_states)), dec_shape(own_rows(dec_grad))
+    partial, arrived, moving, gains, ffn_moving = sync(
+        partial, arrived, moving, gains, ffn_moving
     )
 
     def last_back(dh, x, a, b, c, g):
@@ -1437,12 +1444,14 @@
     input_grad = by_rows(
         last_back,
         info,
-        [dhidden, inputs, partial[0], beside[0], across],
+        [dhidden, inputs, partial[0], *arrived],
         [encoder_gains],
         [f32],
     )[0]
     moving, gains, input_grad, ffn_moving = sync(moving, gains, input_grad, ffn_moving)
-    moving = reduce_step(info, (sums, moving, 4))[0]
+    moving, (gains, ffn_moving, dec_states, dec_grad) = reduce_step(
+        info, (sums, moving, 4), hold=(gains, ffn_moving, dec_states, dec_grad)
+    )
     last = swap(gains, "blk", bits[-1])
     grad_inner, grad_outer, grad_cross_key, grad_cross_value = finish(
         info,
@@ -1455,14 +1464,11 @@
         info, reduce_terms(sums, moving), (size,) * 4, (False, False, False, True)
     )
 
-    def dec_shape(values):
-        return values.reshape(count_q, dec_part, width)
-
     return (
         states.reshape(encoder_input.shape),
-        dec_shape(dec_states),
+        dec_states,
         input_grad.reshape(encoder_input.shape),
-        dec_shape(dec_grad),
+        dec_grad,
         grad_query,
         grad_key,
         grad_value,

time: 321 us -> 306 us (0.953)
  waiting for transfers between devices: 127 us -> 116 us
  Pallas kernels: 106 us -> 101 us
    ppermute x51, waiting for transfers between devices: 71.8 us -> 57.3 us  [swap(): return lax.ppermute(value, axis, [(i, i ^ bits) for i in range(size)])]
    ppermute x21, waiting for transfers between devices: 37.2 us -> 46 us  [fetch_step(): lax.ppermute(pieces[k + 1 if k < 0 else k - 1], 'blk', forth if k < 0 els...]
    ppermute x11, waiting for transfers between devices: 17.7 us -> 12.2 us  [reduce_step(): lax.ppermute(v, 'blk', way)]
    pallas_call x31 -> x34, Pallas kernels: 106 us -> 101 us  [call(): pl.pallas_call(split, grid=(steps,), in_specs=[pl.BlockSpec(memory_space=...]
    unnamed x147 -> x133, local copies, waits for them, and re-layouts: 11.4 us -> 9.92 us
  transfers between devices with their start and end apart: 83 -> 83, of which waited for: 49 -> 43; matrix products, arithmetic and copies ran while one was open for 2% -> 3% of each run, Pallas kernels for 26% -> 26%
where the time goes in v6:
time: 306 us; the launch traced here: 304 us
  waiting for transfers between devices  116 us (38%)
  Pallas kernels  101 us (33%)
  starting transfers between devices  64.1 us (21%)
  local copies, waits for them, and re-layouts  12.5 us (4%)
  blocking collectives  5.4 us (2%)
  other arithmetic  4.23 us (1%)
    pallas_call x34, Pallas kernels, call(): pl.pallas_call(split, grid=(steps,), in_specs=[pl.BlockSpec(memory_space=...  101 us
    ppermute x51, waiting for transfers between devices, swap(): return lax.ppermute(value, axis, [(i, i ^ bits) for i in range(size)])  57.3 us
    ppermute x21, waiting for transfers between devices, fetch_step(): lax.ppermute(pieces[k + 1 if k < 0 else k - 1], 'blk', forth if k < 0 els...  46 us
    ppermute x51, starting transfers between devices, swap(): return lax.ppermute(value, axis, [(i, i ^ bits) for i in range(size)])  30.9 us
    ppermute x21, starting transfers between devices, fetch_step(): lax.ppermute(pieces[k + 1 if k < 0 else k - 1], 'blk', forth if k < 0 els...  21.9 us
    ppermute x11, waiting for transfers between devices, reduce_step(): lax.ppermute(v, 'blk', way)  12.2 us
    ppermute x11, starting transfers between devices, reduce_step(): lax.ppermute(v, 'blk', way)  11.3 us
    unnamed x133, local copies, waits for them, and re-layouts  9.92 us
  transfers between devices with their start and end apart: 83, of which 43 were waited for; matrix products, arithmetic and copies ran while one was open for 3% of the time, Pallas kernels for 26%

profile of v6, /device:TPU:0, one launch (start us, length us, event | category | flops | bytes accessed | tf_op | source)
XLA Modules:
  0.0 304.4 jit_solution(2968638462894258630)
XLA Ops:
  21.9 5.4 %all_gather.3 = bf16[2,40,768]{2,0,1:T(2,128)(2,1)S(1)} all-gather(bf16[2,10,768]{2,0,1:T(2,128)(2,1)S(1)} %copy.66), channel_id=1, replica_groups=mesh['blk'=8,'head'=4] {'head'}, dimensions={1}, use_global_device_ids=true | all-gather | bytes 153600 | tf_op jit(solution)/shard_map/all_gather | solution.py:1172
  29.6 4.6 %collective-permute-done.8.refs_11_.refs_7_ = bf16[96,768]{1,0:T(8,128)(2,1)S(1)} collective-permute-done((bf16[96,768]{1,0:T(8,128)(2,1)S(1)}, bf16[96,768]{1,0:T(8,128)(2,1)S(1)}, u32[]{:S(2)}, u32[]{:S(2)}) %collective-permute-start.8) | collective-permute-done | bytes 147488 | tf_op jit(solution)/shard_map/ppermute | solution.py:74
  34.2 8.9 %collective-permute-done.9.refs_6_.refs_2_ = bf16[96,3072]{1,0:T(8,128)(2,1)S(1)} collective-permute-done((bf16[96,3072]{1,0:T(8,128)(2,1)S(1)}, bf16[96,3072]{1,0:T(8,128)(2,1)S(1)}, u32[]{:S(2)}, u32[]{:S(2)}) %collective-permute-start.9) | collective-permute-done | bytes 589856 | tf_op jit(solution)/shard_map/ppermute | solution.py:74
  45.1 8.5 %shard_map.427 = (bf16[4,256,576]{2,1,0:T(8,128)(2,1)}, bf16[4,3,256,256]{3,2,1,0:T(8,128)(2,1)}, bf16[4,256,192]{2,1,0:T(8,128)(2,1)S(1)}, f32[4,64,768]{2,1,0:...) custom-call(s32[14]{0:T(128)S(1)} %pad_add_fusion.info_ref, ...), custom_call_target="tpu_custom_call" | custom-call | flops 2013265920 | bytes 8257536 | tf_op jit(solution)/shard_map/pallas_call | solution.py:299
  53.6 4.2 %collective-permute-done.11.refs_5_.refs_1_ = bf16[96,3072]{1,0:T(8,128)(2,1)S(1)} collective-permute-done((bf16[96,3072]{1,0:T(8,128)(2,1)S(1)}, bf16[96,3072]{1,0:T(8,128)(2,1)S(1)}, u32[]{:S(2)}, u32[]{:S(2)}) %collective-permute-start.11) | collective-permute-done | bytes 589856 | tf_op jit(solution)/shard_map/ppermute | solution.py:74
  61.8 13.0 %collective-permute-done.16.refs_7_.refs_3_ = bf16[96,3072]{1,0:T(8,128)(2,1)S(1)} collective-permute-done((bf16[96,3072]{1,0:T(8,128)(2,1)S(1)}, bf16[96,3072]{1,0:T(8,128)(2,1)S(1)}, u32[]{:S(2)}, u32[]{:S(2)}) %collective-permute-start.16) | collective-permute-done | bytes 589856 | tf_op jit(solution)/shard_map/ppermute | solution.py:74
  81.2 9.8 %collective-permute-done.19.refs_2_ = bf16[4,64,768]{2,1,0:T(8,128)(2,1)S(1)} collective-permute-done((bf16[4,64,768]{2,1,0:T(8,128)(2,1)S(1)}, bf16[4,64,768]{2,1,0:T(8,128)(2,1)S(1)}, u32[]{:S(2)}, u32[]{:S(2)}) %collective-permute-start.19) | collective-permute-done | bytes 393248 | tf_op jit(solution)/shard_map/ppermute | solution.py:26
  93.7 7.3 %shard_map.429 = (bf16[4,256,768]{2,1,0:T(8,128)(2,1)}, bf16[4,256,768]{2,1,0:T(8,128)(2,1)}, f32[4,64,768]{2,1,0:T(8,128)S(1)}, bf16[4,64,768]{2,1,0:T(8,128)(2...) custom-call(s32[14]{0:T(128)S(1)} %pad_add_fusion.info_ref, ...), custom_call_target="tpu_custom_call" | custom-call | flops 2415919104 | bytes 11796480 | tf_op jit(solution)/shard_map/pallas_call | solution.py:299
  105.9 4.0 %shard_map.430 = (bf16[48,768]{1,0:T(8,128)(2,1)}, bf16[48,576]{1,0:T(8,128)(2,1)}, f32[3,48,48]{2,1,0:T(8,128)}, bf16[48,192]{1,0:T(8,128)(2,1)}, f32[48,768]{1...) custom-call(s32[14]{0:T(128)S(1)} %pad_add_fusion.info_ref, ...), custom_call_target="tpu_custom_call" | custom-call | flops 56623104 | bytes 6377856 | tf_op jit(solution)/shard_map/pallas_call | solution.py:299
  109.9 3.4 %collective-permute-done.28.refs_4_ = bf16[96,1536]{1,0:T(8,128)(2,1)S(1)} collective-permute-done((bf16[96,1536]{1,0:T(8,128)(2,1)S(1)}, bf16[96,1536]{1,0:T(8,128)(2,1)S(1)}, u32[]{:S(2)}, u32[]{:S(2)}) %collective-permute-start.28) | collective-permute-done | bytes 294944 | tf_op jit(solution)/shard_map/ppermute | solution.py:74
  121.8 4.9 %collective-permute-done.32.refs_6_ = bf16[96,1536]{1,0:T(8,128)(2,1)S(1)} collective-permute-done((bf16[96,1536]{1,0:T(8,128)(2,1)S(1)}, bf16[96,1536]{1,0:T(8,128)(2,1)S(1)}, u32[]{:S(2)}, u32[]{:S(2)}) %collective-permute-start.32) | collective-permute-done | bytes 294944 | tf_op jit(solution)/shard_map/ppermute | solution.py:74
  126.9 3.8 %collective-permute-done.31.refs_2_.refs_9_ = bf16[5,64,768]{2,1,0:T(8,128)(2,1)S(1)} collective-permute-done((bf16[5,64,768]{2,1,0:T(8,128)(2,1)S(1)}, bf16[5,64,768]{2,1,0:T(8,128)(2,1)S(1)}, u32[]{:S(2)}, u32[]{:S(2)}) %collective-permute-start.31) | collective-permute-done | bytes 491552 | tf_op jit(solution)/shard_map/ppermute | solution.py:26
  133.4 4.3 %shard_map.433 = (bf16[4,256,384]{2,1,0:T(8,128)(2,1)}, f32[48,768]{1,0:T(8,128)}, bf16[48,768]{1,0:T(8,128)(2,1)}, bf16[48,192]{1,0:T(8,128)(2,1)S(1)}, f32[48,384]{1,0:T(8,128)S(1)}) custom-call(s32[14]{0:T(128)S(1)} %pad_add_fusion.info_ref, bf16[5,64,768]{2,1,0:T(8,128)(2,1)S(1)} %get-tuple-element.557.refs_0_, bf16[5,64,768]{2,1,0:T(8,128)(2,1)} %copy-done, ...), custom_call_target="tpu_custom_call" | custom-call | flops 603979776 | bytes 4476096 | tf_op jit(solution)/shard_map/pallas_call | solution.py:299
  155.8 3.2 %collective-permute-done.41.refs_3_ = bf16[48,768]{1,0:T(8,128)(2,1)S(1)} collective-permute-done((bf16[48,768]{1,0:T(8,128)(2,1)S(1)}, bf16[48,768]{1,0:T(8,128)(2,1)S(1)}, u32[]{:S(2)}, u32[]{:S(2)}) %collective-permute-start.41) | collective-permute-done | bytes 73760 | tf_op jit(solution)/shard_map/ppermute | solution.py:26
  167.5 3.8 %shard_map.438 = (bf16[4,256,384]{2,1,0:T(8,128)(2,1)}, f32[4,64,768]{2,1,0:T(8,128)S(1)}, bf16[4,64,768]{2,1,0:T(8,128)(2,1)S(1)}, f32[4,64,768]{2,1,0:T(8,128)...) custom-call(s32[14]{0:T(128)S(1)} %pad_add_fusion.info_ref, ...), custom_call_target="tpu_custom_call" | custom-call | flops 603979776 | bytes 5901504 | tf_op jit(solution)/shard_map/pallas_call | solution.py:299
  193.9 5.2 %collective-permute-done.52.refs_2_.refs_7_.refs_10_ = bf16[5,64,768]{2,1,0:T(8,128)(2,1)S(1)} collective-permute-done((bf16[5,64,768]{2,1,0:T(8,128)(2,1)S(1)}, bf16[5,64,768]{2,1,0:T(8,128)(2,1)S(1)}, u32[]{:S(2)}, u32[]{:S(2)}) %collective-permute-start.52) | collective-permute-done | bytes 491552 | tf_op jit(solution)/shard_map/ppermute | solution.py:26
  202.8 4.6 %shard_map.444 = (bf16[4,256,768]{2,1,0:T(8,128)(2,1)}, f32[4,64,768]{2,1,0:T(8,128)S(1)}, bf16[4,64,768]{2,1,0:T(8,128)(2,1)S(1)}, f32[4,64,768]{2,1,0:T(8,128)S(1)}, bf16[4,64,768]{2,1,0:T(8,128)(2,1)S(1)}) custom-call(s32[14]{0:T(128)S(1)} %pad_add_fusion.info_ref, bf16[5,64,768]{2,1,0:T(8,128)(2,1)S(1)} %get-tuple-element.661.refs_0_.refs_5_, ...), custom_call_target="tpu_custom_call" | custom-call | flops 2415919104 | bytes 9830400 | tf_op jit(solution)/shard_map/pallas_call | solution.py:299
  210.8 3.3 %shard_map.446 = (f32[48,768]{1,0:T(8,128)S(1)}, bf16[48,768]{1,0:T(8,128)(2,1)}, f32[48,768]{1,0:T(8,128)S(1)}, bf16[48,576]{1,0:T(8,128)(2,1)}, f32[48,768]{1,0:T(8,128)S(1)}, /*index=5*/bf16[48,768]{1,0:T(8,128)(2,1)S(1)}) custom-call(s32[14]{0:T(128)S(1)} %pad_add_fusion.info_ref, f32[48,768]{1,0:T(8,128)S(1)} %copy-done.24, f32[48,768]{1,0:T(8,128)S(1)} %copy-done.13, ...), custom_call_target="tpu_custom_call" | custom-call | flops 113246208 | bytes 2580480 | tf_op jit(solution)/shard_map/pallas_call | solution.py:299
  214.1 6.6 %shard_map.445 = (f32[96,1920]{1,0:T(8,128)}, bf16[96,1920]{1,0:T(8,128)(2,1)}, bf16[96,1920]{1,0:T(8,128)(2,1)}, bf16[96,1920]{1,0:T(8,128)(2,1)}, bf16[96,1920...) custom-call(s32[14]{0:T(128)S(1)} %pad_add_fusion.info_ref, ...), custom_call_target="tpu_custom_call" | custom-call | flops 2415919104 | bytes 11182080 | tf_op jit(solution)/shard_map/pallas_call | solution.py:299
  228.3 6.1 %collective-permute-done.63.refs_0_ = bf16[96,1920]{1,0:T(8,128)(2,1)S(1)} collective-permute-done((bf16[96,1920]{1,0:T(8,128)(2,1)S(1)}, bf16[96,1920]{1,0:T(8,128)(2,1)S(1)}, u32[]{:S(2)}, u32[]{:S(2)}) %collective-permute-start.63) | collective-permute-done | bytes 368672 | tf_op jit(solution)/shard_map/ppermute | solution.py:139
  239.9 11.4 %shard_map.449 = (f32[4,64,768]{2,1,0:T(8,128)S(1)}, bf16[4,64,768]{2,1,0:T(8,128)(2,1)}, f32[4,64,768]{2,1,0:T(8,128)S(1)}, bf16[4,64,768]{2,1,0:T(8,128)(2,1)S...) custom-call(s32[14]{0:T(128)S(1)} %pad_add_fusion.info_ref, ...), custom_call_target="tpu_custom_call" | custom-call | flops 4429185024 | bytes 11559936 | tf_op jit(solution)/shard_map/pallas_call | solution.py:299
  260.0 3.4 %shard_map.453 = (f32[96,192]{1,0:T(8,128)}, f32[96,192]{1,0:T(8,128)}, f32[96,192]{1,0:T(8,128)}, f32[96,192]{1,0:T(8,128)}, f32[96,768]{1,0:T(8,128)}, /*index...) custom-call(s32[14]{0:T(128)S(1)} %pad_add_fusion.info_ref, bf16[48,768]{1,0:T(8,128)(2,1)} %get-tuple-element.753.refs_0_, ...), custom_call_target="tpu_custom_call" | custom-call | flops 70778880 | bytes 1732608 | tf_op jit(solution)/shard_map/pallas_call | solution.py:299
  263.4 3.9 %collective-permute-done.69.refs_0_.refs_2_ = bf16[96,2688]{1,0:T(8,128)(2,1)S(1)} collective-permute-done((bf16[96,2688]{1,0:T(8,128)(2,1)S(1)}, bf16[96,2688]{1,0:T(8,128)(2,1)S(1)}, u32[]{:S(2)}, u32[]{:S(2)}) %collective-permute-start.69) | collective-permute-done | bytes 516128 | tf_op jit(solution)/shard_map/ppermute | solution.py:139
  276.6 8.3 %collective-permute-done.77 = f32[5,768]{1,0:T(8,128)} collective-permute-done((f32[5,768]{1,0:T(8,128)S(1)}, f32[5,768]{1,0:T(8,128)}, u32[]{:S(2)}, u32[]{:S(2)}) %collective-permute-start.77) | collective-permute-done | bytes 15392 | tf_op jit(solution)/shard_map/ppermute | solution.py:26
  (340 shorter events, 160.9 us)
Async XLA Ops:
  11.0 16.3 %collective-permute-start.6 = (bf16[4,64,768]{2,1,0:T(8,128)(2,1)S(1)}, bf16[4,64,768]{2,1,0:T(8,128)(2,1)S(1)}, u32[]{:S(2)}, u32[]{:S(2)}) collective-permute-start(bf16[4,64,768]{2,1,0:T(8,128)(2,1)S(1)} %shard_map.426.refs_0_.refs_4_), channel_id=1, source_target_pairs={{0,1},{1,0},{2,3},{3,2},{4,5},{5,4},{6,7},{7,6},{8,9},{9,8},{10,11... | collective-permute-start | bytes 1179656 | tf_op jit(solution)/shard_map/ppermute | solution.py:26
  11.1 16.3 %collective-permute-start.7 = (bf16[4,64,768]{2,1,0:T(8,128)(2,1)S(1)}, bf16[4,64,768]{2,1,0:T(8,128)(2,1)S(1)}, u32[]{:S(2)}, u32[]{:S(2)}) collective-permute-start(bf16[4,64,768]{2,1,0:T(8,128)(2,1)S(1)} %shard_map.426.refs_0_.refs_4_), channel_id=1, source_target_pairs={{0,2},{1,3},{2,0},{3,1},{4,6},{5,7},{6,4},{7,5},{8,10},{9,11},{10,... | collective-permute-start | bytes 1179656 | tf_op jit(solution)/shard_map/ppermute | solution.py:26
  27.4 15.6 %collective-permute-start.9 = (bf16[96,3072]{1,0:T(8,128)(2,1)S(1)}, bf16[96,3072]{1,0:T(8,128)(2,1)S(1)}, u32[]{:S(2)}, u32[]{:S(2)}) collective-permute-start(bf16[96,3072]{1,0:T(8,128)(2,1)S(1)} %concatenate.15.refs_4_.refs_0_), channel_id=1, source_target_pairs={{8,0},{16,8},{24,16},{28,24},{20,28},{12,20},{4,12},{0,4},{9,1},{1... | collective-permute-start | bytes 1769480 | tf_op jit(solution)/shard_map/ppermute | solution.py:74
  43.0 14.8 %collective-permute-start.11 = (bf16[96,3072]{1,0:T(8,128)(2,1)S(1)}, bf16[96,3072]{1,0:T(8,128)(2,1)S(1)}, u32[]{:S(2)}, u32[]{:S(2)}) collective-permute-start(bf16[96,3072]{1,0:T(8,128)(2,1)S(1)} %concatenate.15.refs_4_.refs_0_), channel_id=1, source_target_pairs={{0,8},{8,16},{16,24},{24,28},{28,20},{20,12},{12,4},{4,0},{1,9},{9... | collective-permute-start | bytes 1769480 | tf_op jit(solution)/shard_map/ppermute | solution.py:74
  44.6 14.5 %collective-permute-start.12 = (bf16[96,3072]{1,0:T(8,128)(2,1)S(1)}, bf16[96,3072]{1,0:T(8,128)(2,1)S(1)}, u32[]{:S(2)}, u32[]{:S(2)}) collective-permute-start(bf16[96,3072]{1,0:T(8,128)(2,1)S(1)} %collective-permute-done.9.refs_6_.refs_2_), channel_id=1, source_target_pairs={{8,0},{16,8},{24,16},{28,24},{20,28},{12,20},{4,12},{0,4},{9,1},{1... | collective-permute-start | bytes 1769480 | tf_op jit(solution)/shard_map/ppermute | solution.py:74
  59.1 15.7 %collective-permute-start.16 = (bf16[96,3072]{1,0:T(8,128)(2,1)S(1)}, bf16[96,3072]{1,0:T(8,128)(2,1)S(1)}, u32[]{:S(2)}, u32[]{:S(2)}) collective-permute-start(bf16[96,3072]{1,0:T(8,128)(2,1)S(1)} %collective-permute-done.11.refs_5_.refs_1_), channel_id=1, source_target_pairs={{0,8},{8,16},{16,24},{24,28},{28,20},{20,12},{12,4},{4,0},{1,9},{9... | collective-permute-start | bytes 1769480 | tf_op jit(solution)/shard_map/ppermute | solution.py:74
  60.6 15.5 %collective-permute-start.17 = (bf16[96,3072]{1,0:T(8,128)(2,1)S(1)}, bf16[96,3072]{1,0:T(8,128)(2,1)S(1)}, u32[]{:S(2)}, u32[]{:S(2)}) collective-permute-start(bf16[96,3072]{1,0:T(8,128)(2,1)S(1)} %collective-permute-done.12.refs_8_.refs_4_), channel_id=1, source_target_pairs={{8,0},{16,8},{24,16},{28,24},{20,28},{12,20},{4,12},{0,4},{9,1},{1... | collective-permute-start | bytes 1769480 | tf_op jit(solution)/shard_map/ppermute | solution.py:74
  61.2 14.9 %collective-permute-start.14 = (bf16[4,64,768]{2,1,0:T(8,128)(2,1)S(1)}, bf16[4,64,768]{2,1,0:T(8,128)(2,1)S(1)}, u32[]{:S(2)}, u32[]{:S(2)}) collective-permute-start(bf16[4,64,768]{2,1,0:T(8,128)(2,1)S(1)} %add_convert_fusion.4), channel_id=1, source_target_pairs={{0,2},{1,3},{2,0},{3,1},{4,6},{5,7},{6,4},{7,5},{8,10},{9,11},{10,... | collective-permute-start | bytes 1179656 | tf_op jit(solution)/shard_map/ppermute | solution.py:26
  61.8 14.3 %collective-permute-start.15 = (bf16[4,64,768]{2,1,0:T(8,128)(2,1)S(1)}, bf16[4,64,768]{2,1,0:T(8,128)(2,1)S(1)}, u32[]{:S(2)}, u32[]{:S(2)}) collective-permute-start(bf16[4,64,768]{2,1,0:T(8,128)(2,1)S(1)} %get-tuple-element.469), channel_id=1, source_target_pairs={{0,1},{1,0},{2,3},{3,2},{4,5},{5,4},{6,7},{7,6},{8,9},{9,8},{10,11... | collective-permute-start | bytes 1179656 | tf_op jit(solution)/shard_map/ppermute | solution.py:26
  76.1 14.9 %collective-permute-start.20 = (bf16[96,3072]{1,0:T(8,128)(2,1)S(1)}, bf16[96,3072]{1,0:T(8,128)(2,1)S(1)}, u32[]{:S(2)}, u32[]{:S(2)}) collective-permute-start(bf16[96,3072]{1,0:T(8,128)(2,1)S(1)} %collective-permute-done.16.refs_7_.refs_3_), channel_id=1, source_target_pairs={{0,8},{8,16},{16,24},{24,28},{28,20},{20,12},{12,4},{4,0},{1,9},{9... | collective-permute-start | bytes 1769480 | tf_op jit(solution)/shard_map/ppermute | solution.py:74
  77.3 14.4 %collective-permute-start.21 = (bf16[96,3072]{1,0:T(8,128)(2,1)S(1)}, bf16[96,3072]{1,0:T(8,128)(2,1)S(1)}, u32[]{:S(2)}, u32[]{:S(2)}) collective-permute-start(bf16[96,3072]{1,0:T(8,128)(2,1)S(1)} %collective-permute-done.17.refs_10_.refs_6_), channel_id=1, source_target_pairs={{8,0},{16,8},{24,16},{28,24},{20,28},{12,20},{4,12},{0,4},{9,1},{1... | collective-permute-start | bytes 1769480 | tf_op jit(solution)/shard_map/ppermute | solution.py:74
  79.5 11.5 %collective-permute-start.19 = (bf16[4,64,768]{2,1,0:T(8,128)(2,1)S(1)}, bf16[4,64,768]{2,1,0:T(8,128)(2,1)S(1)}, u32[]{:S(2)}, u32[]{:S(2)}) collective-permute-start(bf16[4,64,768]{2,1,0:T(8,128)(2,1)S(1)} %get-tuple-element.501.refs_0_), channel_id=1, source_target_pairs={{0,2},{1,3},{2,0},{3,1},{4,6},{5,7},{6,4},{7,5},{8,10},{9,11},{10,... | collective-permute-start | bytes 1179656 | tf_op jit(solution)/shard_map/ppermute | solution.py:26
  117.0 13.6 %collective-permute-start.31 = (bf16[5,64,768]{2,1,0:T(8,128)(2,1)S(1)}, bf16[5,64,768]{2,1,0:T(8,128)(2,1)S(1)}, u32[]{:S(2)}, u32[]{:S(2)}) collective-permute-start(bf16[5,64,768]{2,1,0:T(8,128)(2,1)S(1)} %get-tuple-element.557.refs_0_), channel_id=1, source_target_pairs={{0,2},{1,3},{2,0},{3,1},{4,6},{5,7},{6,4},{7,5},{8,10},{9,11},{10,... | collective-permute-start | bytes 1474568 | tf_op jit(solution)/shard_map/ppermute | solution.py:26
  130.7 12.2 %collective-permute-start.36 = (bf16[96,1536]{1,0:T(8,128)(2,1)S(1)}, bf16[96,1536]{1,0:T(8,128)(2,1)S(1)}, u32[]{:S(2)}, u32[]{:S(2)}) collective-permute-start(bf16[96,1536]{1,0:T(8,128)(2,1)S(1)} %collective-permute-done.32.refs_6_), channel_id=1, source_target_pairs={{0,8},{8,16},{16,24},{24,28},{28,20},{20,12},{12,4},{4,0},{1,9},{9... | collective-permute-start | bytes 884744 | tf_op jit(solution)/shard_map/ppermute | solution.py:74
  185.4 13.6 %collective-permute-start.52 = (bf16[5,64,768]{2,1,0:T(8,128)(2,1)S(1)}, bf16[5,64,768]{2,1,0:T(8,128)(2,1)S(1)}, u32[]{:S(2)}, u32[]{:S(2)}) collective-permute-start(bf16[5,64,768]{2,1,0:T(8,128)(2,1)S(1)} %get-tuple-element.661.refs_0_.refs_5_), channel_id=1, source_target_pairs={{0,2},{1,3},{2,0},{3,1},{4,6},{5,7},{6,4},{7,5},{8,10},{9,11},{10,... | collective-permute-start | bytes 1474568 | tf_op jit(solution)/shard_map/ppermute | solution.py:26
  209.4 11.5 %collective-permute-start.59 = (bf16[4,64,768]{2,1,0:T(8,128)(2,1)S(1)}, bf16[4,64,768]{2,1,0:T(8,128)(2,1)S(1)}, u32[]{:S(2)}, u32[]{:S(2)}) collective-permute-start(bf16[4,64,768]{2,1,0:T(8,128)(2,1)S(1)} %add_convert_fusion.1), channel_id=1, source_target_pairs={{0,2},{1,3},{2,0},{3,1},{4,6},{5,7},{6,4},{7,5},{8,10},{9,11},{10,... | collective-permute-start | bytes 1179656 | tf_op jit(solution)/shard_map/ppermute | solution.py:26
  222.5 13.1 %collective-permute-start.61 = (bf16[5,64,768]{2,1,0:T(8,128)(2,1)S(1)}, bf16[5,64,768]{2,1,0:T(8,128)(2,1)S(1)}, u32[]{:S(2)}, u32[]{:S(2)}) collective-permute-start(bf16[5,64,768]{2,1,0:T(8,128)(2,1)S(1)} %get-tuple-element.705.refs_0_), channel_id=1, source_target_pairs={{0,1},{1,0},{2,3},{3,2},{4,5},{5,4},{6,7},{7,6},{8,9},{9,8},{10,11... | collective-permute-start | bytes 1474568 | tf_op jit(solution)/shard_map/ppermute | solution.py:26
  222.9 13.3 %collective-permute-start.62 = (bf16[5,64,768]{2,1,0:T(8,128)(2,1)S(1)}, bf16[5,64,768]{2,1,0:T(8,128)(2,1)S(1)}, u32[]{:S(2)}, u32[]{:S(2)}) collective-permute-start(bf16[5,64,768]{2,1,0:T(8,128)(2,1)S(1)} %get-tuple-element.705.refs_0_), channel_id=1, source_target_pairs={{0,2},{1,3},{2,0},{3,1},{4,6},{5,7},{6,4},{7,5},{8,10},{9,11},{10,... | collective-permute-start | bytes 1474568 | tf_op jit(solution)/shard_map/ppermute | solution.py:26
  237.9 13.5 %collective-permute-start.66 = (bf16[96,1920]{1,0:T(8,128)(2,1)S(1)}, bf16[96,1920]{1,0:T(8,128)(2,1)S(1)}, u32[]{:S(2)}, u32[]{:S(2)}) collective-permute-start(bf16[96,1920]{1,0:T(8,128)(2,1)S(1)} %get-tuple-element.730), channel_id=1, source_target_pairs={{0,8},{8,16},{16,24},{24,28},{28,20},{20,12},{12,4},{4,0},{1,9},{9... | collective-permute-start | bytes 1105928 | tf_op jit(solution)/shard_map/ppermute | solution.py:139
  239.3 12.1 %collective-permute-start.67 = (bf16[96,1920]{1,0:T(8,128)(2,1)S(1)}, bf16[96,1920]{1,0:T(8,128)(2,1)S(1)}, u32[]{:S(2)}, u32[]{:S(2)}) collective-permute-start(bf16[96,1920]{1,0:T(8,128)(2,1)S(1)} %get-tuple-element.731), channel_id=1, source_target_pairs={{8,0},{16,8},{24,16},{28,24},{20,28},{12,20},{4,12},{0,4},{9,1},{1... | collective-permute-start | bytes 1105928 | tf_op jit(solution)/shard_map/ppermute | solution.py:139
  253.9 13.5 %collective-permute-start.69 = (bf16[96,2688]{1,0:T(8,128)(2,1)S(1)}, bf16[96,2688]{1,0:T(8,128)(2,1)S(1)}, u32[]{:S(2)}, u32[]{:S(2)}) collective-permute-start(bf16[96,2688]{1,0:T(8,128)(2,1)S(1)} %get-tuple-element.743), channel_id=1, source_target_pairs={{0,8},{8,16},{16,24},{24,28},{28,20},{20,12},{12,4},{4,0},{1,9},{9... | collective-permute-start | bytes 1548296 | tf_op jit(solution)/shard_map/ppermute | solution.py:139
  255.3 13.1 %collective-permute-start.70 = (bf16[96,2688]{1,0:T(8,128)(2,1)S(1)}, bf16[96,2688]{1,0:T(8,128)(2,1)S(1)}, u32[]{:S(2)}, u32[]{:S(2)}) collective-permute-start(bf16[96,2688]{1,0:T(8,128)(2,1)S(1)} %get-tuple-element.744), channel_id=1, source_target_pairs={{8,0},{16,8},{24,16},{28,24},{20,28},{12,20},{4,12},{0,4},{9,1},{1... | collective-permute-start | bytes 1548296 | tf_op jit(solution)/shard_map/ppermute | solution.py:139
  271.9 13.8 %collective-permute-start.75 = (bf16[96,2688]{1,0:T(8,128)(2,1)}, bf16[96,2688]{1,0:T(8,128)(2,1)S(1)}, u32[]{:S(2)}, u32[]{:S(2)}) collective-permute-start(bf16[96,2688]{1,0:T(8,128)(2,1)} %get-tuple-element.774), channel_id=1, source_target_pairs={{0,8},{8,16},{16,24},{24,28},{28,20},{20,12},{12,4},{4,0},{1,9},{9... | collective-permute-start | bytes 1548296 | tf_op jit(solution)/shard_map/ppermute | solution.py:139
  273.7 12.0 %collective-permute-start.73 = (bf16[4,64,768]{2,1,0:T(8,128)(2,1)}, bf16[4,64,768]{2,1,0:T(8,128)(2,1)S(1)}, u32[]{:S(2)}, u32[]{:S(2)}) collective-permute-start(bf16[4,64,768]{2,1,0:T(8,128)(2,1)} %add_convert_fusion), channel_id=1, source_target_pairs={{0,2},{1,3},{2,0},{3,1},{4,6},{5,7},{6,4},{7,5},{8,10},{9,11},{10,... | collective-permute-start | bytes 1179656 | tf_op jit(solution)/shard_map/ppermute | solution.py:26
  (122 other events, 1070.3 us)

commit v7 on v6

--- a/solution.py
+++ b/solution.py
@@ -133,7 +133,9 @@
         rows = rings[0][0][0].shape[0]
         wide = [sum(part(terms[0]).width for terms in p) for p in plan]
         shapes = [like((rows, w), bf16) for w in wide]
-        sent = call(body, info, [], [p.array for p in parts], [], [Near(v) for v in shapes], least=0)
+        came_in = {id(m.array) for _, moving, _ in rings for m in moving or ()}
+        given = [Close(p.array) if id(p.array) in came_in else p.array for p in parts]
+        sent = call(body, info, [], given, [], [Near(v) for v in shapes], least=0)
     if hold is not None:
         sent, hold = sync(sent, hold)
     came = [lax.ppermute(v, "blk", way) for v, way in zip(sent, (forth, back), strict=False)]
@@ -1037,6 +1039,13 @@
     )
 
 
+def own_rows(info, values, dec_own):
+    found = values[:dec_own]
+    for k in range(1, values.shape[0] // dec_own):
+        found = jnp.where(info[HEAD] == k, values[k * dec_own : (k + 1) * dec_own], found)
+    return found
+
+
 def decoder_ends(
     info, rows, dself, terms, gains, after_cross, out_terms, gain_rows, gain_sums, dec_own
 ):
@@ -1048,8 +1057,8 @@
         grad, states, found = outs
         total, out_total = summed(ins[4:8]), summed(ins[8:12])
         back, two = norm_back(rows[...].astype(f32), gains[0:1, :], total)
-        grad[...] = dself[...] + back
-        states[...] = (after_cross[...] + out_total).astype(bf16)
+        grad[...] = own_rows(info, dself[...] + back, dec_own)
+        states[...] = own_rows(info, after_cross[...] + out_total, dec_own).astype(bf16)
         row = lax.div(lax.broadcasted_iota(jnp.int32, (count, 1), 0), dec_own)
         mine = (row == info[HEAD]) & (info[BLK] == 0)
         found[0:1, :] = zero[...]
@@ -1063,7 +1072,7 @@
         [],
         [rows, dself, after_cross, gains, *terms, *out_terms, *gain_rows, *gain_sums],
         [],
-        [like((count, width), f32), like((count, width), bf16), like((5, width), f32)],
+        [like((dec_own, width), f32), like((dec_own, width), bf16), like((5, width), f32)],
     )
 
 
@@ -1331,11 +1340,10 @@
     dqueries, mine, sent = rows_back(info, terms, w_cross_query)
     w_ffn = gathered(info, ffn, (units, units))
     dstates_all, sent, w_ffn = sync(dstates_all, sent, w_ffn)
-    dstates_all.append(swap(dstates_all[2], "head", 1))
-    dstates_all, sent = sync(dstates_all, sent)
+    terms = [mine, *share(sent)]
+    dstates_all = sync(*dstates_all, swap(dstates_all[2], "head", 1))
     out_terms = [out_mine, *riders(dstates_all)]
     dinner, *partial = encoder_ffn_back(info, dstates_all, slope, w_ffn)
-    terms = [mine, *share(sent)]
     partial, dinner, terms = sync(partial, dinner, terms)
     partial, corner, dinner, dstates_all = sync(partial, to_core(partial), dinner, dstates_all)
     arrived = to_chip(partial, corner)
@@ -1425,13 +1433,9 @@
     def dec_shape(values):
         return values.reshape(count_q, dec_part, width)
 
-    def own_rows(values):
-        return lax.dynamic_slice_in_dim(values, head * dec_own, dec_own, 0)
-
     ffn_moving, moving = reduce_step(info, (ffn_sums, ffn_moving, 4), (sums, moving, 2))[:2]
     arrived = to_chip(partial, corner)
     gains = some(gains, bits[:1])
-    dec_states, dec_grad = dec_shape(own_rows(dec_states)), dec_shape(own_rows(dec_grad))
     partial, arrived, moving, gains, ffn_moving = sync(
         partial, arrived, moving, gains, ffn_moving
     )
@@ -1449,9 +1453,7 @@
         [f32],
     )[0]
     moving, gains, input_grad, ffn_moving = sync(moving, gains, input_grad, ffn_moving)
-    moving, (gains, ffn_moving, dec_states, dec_grad) = reduce_step(
-        info, (sums, moving, 4), hold=(gains, ffn_moving, dec_states, dec_grad)
-    )
+    moving, (gains, ffn_moving) = reduce_step(info, (sums, moving, 4), hold=(gains, ffn_moving))
     last = swap(gains, "blk", bits[-1])
     grad_inner, grad_outer, grad_cross_key, grad_cross_value = finish(
         info,
@@ -1466,9 +1468,9 @@
 
     return (
         states.reshape(encoder_input.shape),
-        dec_states,
+        dec_shape(dec_states),
         input_grad.reshape(encoder_input.shape),
-        dec_grad,
+        dec_shape(dec_grad),
         grad_query,
         grad_key,
         grad_value,

time: 306 us -> 298 us (0.974)
  local copies, waits for them, and re-layouts: 12.5 us -> 8.58 us
    unnamed x133 -> x109, local copies, waits for them, and re-layouts: 9.92 us -> 6.69 us
  transfers between devices with their start and end apart: 83 -> 83, of which waited for: 43 -> 42; matrix products, arithmetic and copies ran while one was open for 3% -> 2% of each run, Pallas kernels for 26% -> 27%
where the time goes in v7:
time: 298 us; the launch traced here: 297 us
  waiting for transfers between devices  115 us (39%)
  Pallas kernels  98.7 us (33%)
  starting transfers between devices  65.4 us (22%)
  local copies, waits for them, and re-layouts  8.58 us (3%)
  blocking collectives  5.4 us (2%)
    pallas_call x34, Pallas kernels, call(): pl.pallas_call(split, grid=(steps,), in_specs=[pl.BlockSpec(memory_space=...  98.7 us
    ppermute x51, waiting for transfers between devices, swap(): return lax.ppermute(value, axis, [(i, i ^ bits) for i in range(size)])  55.5 us
    ppermute x21, waiting for transfers between devices, fetch_step(): lax.ppermute(pieces[k + 1 if k < 0 else k - 1], 'blk', forth if k < 0 els...  46.7 us
    ppermute x51, starting transfers between devices, swap(): return lax.ppermute(value, axis, [(i, i ^ bits) for i in range(size)])  31.8 us
    ppermute x21, starting transfers between devices, fetch_step(): lax.ppermute(pieces[k + 1 if k < 0 else k - 1], 'blk', forth if k < 0 els...  21.9 us
    ppermute x11, waiting for transfers between devices, reduce_step(): lax.ppermute(v, 'blk', way)  12.8 us
    ppermute x11, starting transfers between devices, reduce_step(): lax.ppermute(v, 'blk', way)  11.7 us
    unnamed x109, local copies, waits for them, and re-layouts  6.69 us
  transfers between devices with their start and end apart: 83, of which 42 were waited for; matrix products, arithmetic and copies ran while one was open for 2% of the time, Pallas kernels for 27%

profile of v7, /device:TPU:0, one launch (start us, length us, event | category | flops | bytes accessed | tf_op | source)
XLA Modules:
  0.0 297.2 jit_solution(15836390343537859975)
XLA Ops:
  21.9 5.4 %all_gather.3 = bf16[2,40,768]{2,0,1:T(2,128)(2,1)S(1)} all-gather(bf16[2,10,768]{2,0,1:T(2,128)(2,1)S(1)} %copy.68), channel_id=1, replica_groups=mesh['blk'=8,'head'=4] {'head'}, dimensions={1}, use_global_device_ids=true | all-gather | bytes 153600 | tf_op jit(solution)/shard_map/all_gather | solution.py:1181
  29.6 4.6 %collective-permute-done.8.refs_11_.refs_7_ = bf16[96,768]{1,0:T(8,128)(2,1)S(1)} collective-permute-done((bf16[96,768]{1,0:T(8,128)(2,1)S(1)}, bf16[96,768]{1,0:T(8,128)(2,1)S(1)}, u32[]{:S(2)}, u32[]{:S(2)}) %collective-permute-start.8) | collective-permute-done | bytes 147488 | tf_op jit(solution)/shard_map/ppermute | solution.py:74
  34.1 8.9 %collective-permute-done.9.refs_6_.refs_2_ = bf16[96,3072]{1,0:T(8,128)(2,1)S(1)} collective-permute-done((bf16[96,3072]{1,0:T(8,128)(2,1)S(1)}, bf16[96,3072]{1,0:T(8,128)(2,1)S(1)}, u32[]{:S(2)}, u32[]{:S(2)}) %collective-permute-start.9) | collective-permute-done | bytes 589856 | tf_op jit(solution)/shard_map/ppermute | solution.py:74
  45.0 8.5 %shard_map.427 = (bf16[4,256,576]{2,1,0:T(8,128)(2,1)}, bf16[4,3,256,256]{3,2,1,0:T(8,128)(2,1)}, bf16[4,256,192]{2,1,0:T(8,128)(2,1)S(1)}, f32[4,64,768]{2,1,0:...) custom-call(s32[14]{0:T(128)S(1)} %pad_add_fusion.info_ref, ...), custom_call_target="tpu_custom_call" | custom-call | flops 2013265920 | bytes 8257536 | tf_op jit(solution)/shard_map/pallas_call | solution.py:301
  53.6 4.2 %collective-permute-done.11.refs_5_.refs_1_ = bf16[96,3072]{1,0:T(8,128)(2,1)S(1)} collective-permute-done((bf16[96,3072]{1,0:T(8,128)(2,1)S(1)}, bf16[96,3072]{1,0:T(8,128)(2,1)S(1)}, u32[]{:S(2)}, u32[]{:S(2)}) %collective-permute-start.11) | collective-permute-done | bytes 589856 | tf_op jit(solution)/shard_map/ppermute | solution.py:74
  61.8 13.0 %collective-permute-done.16.refs_7_.refs_3_ = bf16[96,3072]{1,0:T(8,128)(2,1)S(1)} collective-permute-done((bf16[96,3072]{1,0:T(8,128)(2,1)S(1)}, bf16[96,3072]{1,0:T(8,128)(2,1)S(1)}, u32[]{:S(2)}, u32[]{:S(2)}) %collective-permute-start.16) | collective-permute-done | bytes 589856 | tf_op jit(solution)/shard_map/ppermute | solution.py:74
  81.2 9.8 %collective-permute-done.19.refs_2_ = bf16[4,64,768]{2,1,0:T(8,128)(2,1)S(1)} collective-permute-done((bf16[4,64,768]{2,1,0:T(8,128)(2,1)S(1)}, bf16[4,64,768]{2,1,0:T(8,128)(2,1)S(1)}, u32[]{:S(2)}, u32[]{:S(2)}) %collective-permute-start.19) | collective-permute-done | bytes 393248 | tf_op jit(solution)/shard_map/ppermute | solution.py:26
  93.7 7.3 %shard_map.429 = (bf16[4,256,768]{2,1,0:T(8,128)(2,1)}, bf16[4,256,768]{2,1,0:T(8,128)(2,1)}, f32[4,64,768]{2,1,0:T(8,128)S(1)}, bf16[4,64,768]{2,1,0:T(8,128)(2...) custom-call(s32[14]{0:T(128)S(1)} %pad_add_fusion.info_ref, ...), custom_call_target="tpu_custom_call" | custom-call | flops 2415919104 | bytes 11796480 | tf_op jit(solution)/shard_map/pallas_call | solution.py:301
  105.9 3.9 %shard_map.430 = (bf16[48,768]{1,0:T(8,128)(2,1)}, bf16[48,576]{1,0:T(8,128)(2,1)}, f32[3,48,48]{2,1,0:T(8,128)}, bf16[48,192]{1,0:T(8,128)(2,1)}, f32[48,768]{1...) custom-call(s32[14]{0:T(128)S(1)} %pad_add_fusion.info_ref, ...), custom_call_target="tpu_custom_call" | custom-call | flops 56623104 | bytes 6377856 | tf_op jit(solution)/shard_map/pallas_call | solution.py:301
  109.8 3.4 %collective-permute-done.28.refs_4_ = bf16[96,1536]{1,0:T(8,128)(2,1)S(1)} collective-permute-done((bf16[96,1536]{1,0:T(8,128)(2,1)S(1)}, bf16[96,1536]{1,0:T(8,128)(2,1)S(1)}, u32[]{:S(2)}, u32[]{:S(2)}) %collective-permute-start.28) | collective-permute-done | bytes 294944 | tf_op jit(solution)/shard_map/ppermute | solution.py:74
  121.8 4.9 %collective-permute-done.32.refs_6_ = bf16[96,1536]{1,0:T(8,128)(2,1)S(1)} collective-permute-done((bf16[96,1536]{1,0:T(8,128)(2,1)S(1)}, bf16[96,1536]{1,0:T(8,128)(2,1)S(1)}, u32[]{:S(2)}, u32[]{:S(2)}) %collective-permute-start.32) | collective-permute-done | bytes 294944 | tf_op jit(solution)/shard_map/ppermute | solution.py:74
  126.9 3.8 %collective-permute-done.31.refs_2_.refs_9_ = bf16[5,64,768]{2,1,0:T(8,128)(2,1)S(1)} collective-permute-done((bf16[5,64,768]{2,1,0:T(8,128)(2,1)S(1)}, bf16[5,64,768]{2,1,0:T(8,128)(2,1)S(1)}, u32[]{:S(2)}, u32[]{:S(2)}) %collective-permute-start.31) | collective-permute-done | bytes 491552 | tf_op jit(solution)/shard_map/ppermute | solution.py:26
  133.3 4.3 %shard_map.433 = (bf16[4,256,384]{2,1,0:T(8,128)(2,1)}, f32[48,768]{1,0:T(8,128)}, bf16[48,768]{1,0:T(8,128)(2,1)}, bf16[48,192]{1,0:T(8,128)(2,1)S(1)}, f32[48,384]{1,0:T(8,128)S(1)}) custom-call(s32[14]{0:T(128)S(1)} %pad_add_fusion.info_ref, bf16[5,64,768]{2,1,0:T(8,128)(2,1)S(1)} %get-tuple-element.554.refs_0_, bf16[5,64,768]{2,1,0:T(8,128)(2,1)} %copy-done, ...), custom_call_target="tpu_custom_call" | custom-call | flops 603979776 | bytes 4476096 | tf_op jit(solution)/shard_map/pallas_call | solution.py:301
  167.5 3.8 %shard_map.438 = (bf16[4,256,384]{2,1,0:T(8,128)(2,1)}, f32[4,64,768]{2,1,0:T(8,128)S(1)}, bf16[4,64,768]{2,1,0:T(8,128)(2,1)S(1)}, f32[4,64,768]{2,1,0:T(8,128)...) custom-call(s32[14]{0:T(128)S(1)} %pad_add_fusion.info_ref, ...), custom_call_target="tpu_custom_call" | custom-call | flops 603979776 | bytes 5901504 | tf_op jit(solution)/shard_map/pallas_call | solution.py:301
  179.9 3.2 %shard_map.439.refs_10_ = f32[768,384]{1,0:T(8,128)} custom-call(s32[14]{0:T(128)S(1)} %pad_add_fusion.info_ref, bf16[5,64,768]{2,1,0:T(8,128)(2,1)S(1)} %get-tuple-element.554.refs_0_, bf16[5,64,768]{2,1,0:T(8,128)(2,1)S(1)} %copy-done.1, bf16[5,64,768]{2,1,0:T(8,128)(2,1)S(1)} %copy-done.3, bf16[5,64,768]{2,1,0:T(8,128)(2,1)S(1)} %copy-done.5, ...), custom_call_target="tpu_custom_call" | custom-call | flops 603979776 | bytes 3932160 | tf_op jit(solution)/shard_map/pallas_call | solution.py:301
  193.9 5.1 %collective-permute-done.52.refs_2_.refs_7_.refs_10_ = bf16[5,64,768]{2,1,0:T(8,128)(2,1)S(1)} collective-permute-done((bf16[5,64,768]{2,1,0:T(8,128)(2,1)S(1)}, bf16[5,64,768]{2,1,0:T(8,128)(2,1)S(1)}, u32[]{:S(2)}, u32[]{:S(2)}) %collective-permute-start.52) | collective-permute-done | bytes 491552 | tf_op jit(solution)/shard_map/ppermute | solution.py:26
  200.9 4.8 %shard_map.444 = (bf16[4,256,768]{2,1,0:T(8,128)(2,1)}, f32[4,64,768]{2,1,0:T(8,128)S(1)}, bf16[4,64,768]{2,1,0:T(8,128)(2,1)S(1)}, f32[4,64,768]{2,1,0:T(8,128)S(1)}, bf16[4,64,768]{2,1,0:T(8,128)(2,1)S(1)}) custom-call(s32[14]{0:T(128)S(1)} %pad_add_fusion.info_ref, bf16[5,64,768]{2,1,0:T(8,128)(2,1)S(1)} %get-tuple-element.667.refs_0_.refs_5_, ...), custom_call_target="tpu_custom_call" | custom-call | flops 2415919104 | bytes 9830400 | tf_op jit(solution)/shard_map/pallas_call | solution.py:301
  209.4 3.3 %shard_map.445 = (f32[48,768]{1,0:T(8,128)S(1)}, bf16[48,768]{1,0:T(8,128)(2,1)}, f32[48,768]{1,0:T(8,128)S(1)}, bf16[48,576]{1,0:T(8,128)(2,1)}, f32[48,768]{1,0:T(8,128)S(1)}, /*index=5*/bf16[48,768]{1,0:T(8,128)(2,1)S(1)}) custom-call(s32[14]{0:T(128)S(1)} %pad_add_fusion.info_ref, f32[48,768]{1,0:T(8,128)S(1)} %copy-done.20, f32[48,768]{1,0:T(8,128)S(1)} %copy-done.9, ...), custom_call_target="tpu_custom_call" | custom-call | flops 113246208 | bytes 2580480 | tf_op jit(solution)/shard_map/pallas_call | solution.py:301
  212.8 6.7 %shard_map.446 = (f32[96,1920]{1,0:T(8,128)}, bf16[96,1920]{1,0:T(8,128)(2,1)}, bf16[96,1920]{1,0:T(8,128)(2,1)}, bf16[96,1920]{1,0:T(8,128)(2,1)}, bf16[96,1920...) custom-call(s32[14]{0:T(128)S(1)} %pad_add_fusion.info_ref, ...), custom_call_target="tpu_custom_call" | custom-call | flops 2415919104 | bytes 11182080 | tf_op jit(solution)/shard_map/pallas_call | solution.py:301
  227.0 6.1 %collective-permute-done.63.refs_0_ = bf16[96,1920]{1,0:T(8,128)(2,1)S(1)} collective-permute-done((bf16[96,1920]{1,0:T(8,128)(2,1)S(1)}, bf16[96,1920]{1,0:T(8,128)(2,1)S(1)}, u32[]{:S(2)}, u32[]{:S(2)}) %collective-permute-start.63) | collective-permute-done | bytes 368672 | tf_op jit(solution)/shard_map/ppermute | solution.py:141
  238.4 11.4 %shard_map.449 = (f32[4,64,768]{2,1,0:T(8,128)S(1)}, bf16[4,64,768]{2,1,0:T(8,128)(2,1)S(1)}, f32[4,64,768]{2,1,0:T(8,128)S(1)}, bf16[4,64,768]{2,1,0:T(8,128)(2...) custom-call(s32[14]{0:T(128)S(1)} %pad_add_fusion.info_ref, ...), custom_call_target="tpu_custom_call" | custom-call | flops 4429185024 | bytes 11559936 | tf_op jit(solution)/shard_map/pallas_call | solution.py:301
  257.4 3.4 %shard_map.453 = (f32[96,192]{1,0:T(8,128)}, f32[96,192]{1,0:T(8,128)}, f32[96,192]{1,0:T(8,128)}, f32[96,192]{1,0:T(8,128)}, f32[96,768]{1,0:T(8,128)}, /*index...) custom-call(s32[14]{0:T(128)S(1)} %pad_add_fusion.info_ref, bf16[48,768]{1,0:T(8,128)(2,1)} %get-tuple-element.750.refs_0_, ...), custom_call_target="tpu_custom_call" | custom-call | flops 70778880 | bytes 1732608 | tf_op jit(solution)/shard_map/pallas_call | solution.py:301
  260.8 3.9 %collective-permute-done.69.refs_0_.refs_2_ = bf16[96,2688]{1,0:T(8,128)(2,1)S(1)} collective-permute-done((bf16[96,2688]{1,0:T(8,128)(2,1)S(1)}, bf16[96,2688]{1,0:T(8,128)(2,1)S(1)}, u32[]{:S(2)}, u32[]{:S(2)}) %collective-permute-start.69) | collective-permute-done | bytes 516128 | tf_op jit(solution)/shard_map/ppermute | solution.py:141
  271.2 8.7 %collective-permute-done.77 = f32[5,768]{1,0:T(8,128)S(1)} collective-permute-done((f32[5,768]{1,0:T(8,128)S(1)}, f32[5,768]{1,0:T(8,128)S(1)}, u32[]{:S(2)}, u32[]{:S(2)}) %collective-permute-start.77) | collective-permute-done | bytes 15392 | tf_op jit(solution)/shard_map/ppermute | solution.py:26
  (314 shorter events, 153.2 us)
Async XLA Ops:
  11.0 16.3 %collective-permute-start.6 = (bf16[4,64,768]{2,1,0:T(8,128)(2,1)S(1)}, bf16[4,64,768]{2,1,0:T(8,128)(2,1)S(1)}, u32[]{:S(2)}, u32[]{:S(2)}) collective-permute-start(bf16[4,64,768]{2,1,0:T(8,128)(2,1)S(1)} %shard_map.426.refs_0_.refs_4_), channel_id=1, source_target_pairs={{0,1},{1,0},{2,3},{3,2},{4,5},{5,4},{6,7},{7,6},{8,9},{9,8},{10,11... | collective-permute-start | bytes 1179656 | tf_op jit(solution)/shard_map/ppermute | solution.py:26
  11.1 16.3 %collective-permute-start.7 = (bf16[4,64,768]{2,1,0:T(8,128)(2,1)S(1)}, bf16[4,64,768]{2,1,0:T(8,128)(2,1)S(1)}, u32[]{:S(2)}, u32[]{:S(2)}) collective-permute-start(bf16[4,64,768]{2,1,0:T(8,128)(2,1)S(1)} %shard_map.426.refs_0_.refs_4_), channel_id=1, source_target_pairs={{0,2},{1,3},{2,0},{3,1},{4,6},{5,7},{6,4},{7,5},{8,10},{9,11},{10,... | collective-permute-start | bytes 1179656 | tf_op jit(solution)/shard_map/ppermute | solution.py:26
  27.4 15.6 %collective-permute-start.9 = (bf16[96,3072]{1,0:T(8,128)(2,1)S(1)}, bf16[96,3072]{1,0:T(8,128)(2,1)S(1)}, u32[]{:S(2)}, u32[]{:S(2)}) collective-permute-start(bf16[96,3072]{1,0:T(8,128)(2,1)S(1)} %concatenate.15.refs_4_.refs_0_), channel_id=1, source_target_pairs={{8,0},{16,8},{24,16},{28,24},{20,28},{12,20},{4,12},{0,4},{9,1},{1... | collective-permute-start | bytes 1769480 | tf_op jit(solution)/shard_map/ppermute | solution.py:74
  43.0 14.8 %collective-permute-start.11 = (bf16[96,3072]{1,0:T(8,128)(2,1)S(1)}, bf16[96,3072]{1,0:T(8,128)(2,1)S(1)}, u32[]{:S(2)}, u32[]{:S(2)}) collective-permute-start(bf16[96,3072]{1,0:T(8,128)(2,1)S(1)} %concatenate.15.refs_4_.refs_0_), channel_id=1, source_target_pairs={{0,8},{8,16},{16,24},{24,28},{28,20},{20,12},{12,4},{4,0},{1,9},{9... | collective-permute-start | bytes 1769480 | tf_op jit(solution)/shard_map/ppermute | solution.py:74
  44.6 14.5 %collective-permute-start.12 = (bf16[96,3072]{1,0:T(8,128)(2,1)S(1)}, bf16[96,3072]{1,0:T(8,128)(2,1)S(1)}, u32[]{:S(2)}, u32[]{:S(2)}) collective-permute-start(bf16[96,3072]{1,0:T(8,128)(2,1)S(1)} %collective-permute-done.9.refs_6_.refs_2_), channel_id=1, source_target_pairs={{8,0},{16,8},{24,16},{28,24},{20,28},{12,20},{4,12},{0,4},{9,1},{1... | collective-permute-start | bytes 1769480 | tf_op jit(solution)/shard_map/ppermute | solution.py:74
  59.1 15.7 %collective-permute-start.16 = (bf16[96,3072]{1,0:T(8,128)(2,1)S(1)}, bf16[96,3072]{1,0:T(8,128)(2,1)S(1)}, u32[]{:S(2)}, u32[]{:S(2)}) collective-permute-start(bf16[96,3072]{1,0:T(8,128)(2,1)S(1)} %collective-permute-done.11.refs_5_.refs_1_), channel_id=1, source_target_pairs={{0,8},{8,16},{16,24},{24,28},{28,20},{20,12},{12,4},{4,0},{1,9},{9... | collective-permute-start | bytes 1769480 | tf_op jit(solution)/shard_map/ppermute | solution.py:74
  60.6 15.5 %collective-permute-start.17 = (bf16[96,3072]{1,0:T(8,128)(2,1)S(1)}, bf16[96,3072]{1,0:T(8,128)(2,1)S(1)}, u32[]{:S(2)}, u32[]{:S(2)}) collective-permute-start(bf16[96,3072]{1,0:T(8,128)(2,1)S(1)} %collective-permute-done.12.refs_8_.refs_4_), channel_id=1, source_target_pairs={{8,0},{16,8},{24,16},{28,24},{20,28},{12,20},{4,12},{0,4},{9,1},{1... | collective-permute-start | bytes 1769480 | tf_op jit(solution)/shard_map/ppermute | solution.py:74
  61.2 14.9 %collective-permute-start.14 = (bf16[4,64,768]{2,1,0:T(8,128)(2,1)S(1)}, bf16[4,64,768]{2,1,0:T(8,128)(2,1)S(1)}, u32[]{:S(2)}, u32[]{:S(2)}) collective-permute-start(bf16[4,64,768]{2,1,0:T(8,128)(2,1)S(1)} %add_convert_fusion.4), channel_id=1, source_target_pairs={{0,2},{1,3},{2,0},{3,1},{4,6},{5,7},{6,4},{7,5},{8,10},{9,11},{10,... | collective-permute-start | bytes 1179656 | tf_op jit(solution)/shard_map/ppermute | solution.py:26
  61.8 14.3 %collective-permute-start.15 = (bf16[4,64,768]{2,1,0:T(8,128)(2,1)S(1)}, bf16[4,64,768]{2,1,0:T(8,128)(2,1)S(1)}, u32[]{:S(2)}, u32[]{:S(2)}) collective-permute-start(bf16[4,64,768]{2,1,0:T(8,128)(2,1)S(1)} %get-tuple-element.466), channel_id=1, source_target_pairs={{0,1},{1,0},{2,3},{3,2},{4,5},{5,4},{6,7},{7,6},{8,9},{9,8},{10,11... | collective-permute-start | bytes 1179656 | tf_op jit(solution)/shard_map/ppermute | solution.py:26
  76.1 14.9 %collective-permute-start.20 = (bf16[96,3072]{1,0:T(8,128)(2,1)S(1)}, bf16[96,3072]{1,0:T(8,128)(2,1)S(1)}, u32[]{:S(2)}, u32[]{:S(2)}) collective-permute-start(bf16[96,3072]{1,0:T(8,128)(2,1)S(1)} %collective-permute-done.16.refs_7_.refs_3_), channel_id=1, source_target_pairs={{0,8},{8,16},{16,24},{24,28},{28,20},{20,12},{12,4},{4,0},{1,9},{9... | collective-permute-start | bytes 1769480 | tf_op jit(solution)/shard_map/ppermute | solution.py:74
  77.3 14.4 %collective-permute-start.21 = (bf16[96,3072]{1,0:T(8,128)(2,1)S(1)}, bf16[96,3072]{1,0:T(8,128)(2,1)S(1)}, u32[]{:S(2)}, u32[]{:S(2)}) collective-permute-start(bf16[96,3072]{1,0:T(8,128)(2,1)S(1)} %collective-permute-done.17.refs_10_.refs_6_), channel_id=1, source_target_pairs={{8,0},{16,8},{24,16},{28,24},{20,28},{12,20},{4,12},{0,4},{9,1},{1... | collective-permute-start | bytes 1769480 | tf_op jit(solution)/shard_map/ppermute | solution.py:74
  79.5 11.5 %collective-permute-start.19 = (bf16[4,64,768]{2,1,0:T(8,128)(2,1)S(1)}, bf16[4,64,768]{2,1,0:T(8,128)(2,1)S(1)}, u32[]{:S(2)}, u32[]{:S(2)}) collective-permute-start(bf16[4,64,768]{2,1,0:T(8,128)(2,1)S(1)} %get-tuple-element.498.refs_0_), channel_id=1, source_target_pairs={{0,2},{1,3},{2,0},{3,1},{4,6},{5,7},{6,4},{7,5},{8,10},{9,11},{10,... | collective-permute-start | bytes 1179656 | tf_op jit(solution)/shard_map/ppermute | solution.py:26
  117.0 13.6 %collective-permute-start.31 = (bf16[5,64,768]{2,1,0:T(8,128)(2,1)S(1)}, bf16[5,64,768]{2,1,0:T(8,128)(2,1)S(1)}, u32[]{:S(2)}, u32[]{:S(2)}) collective-permute-start(bf16[5,64,768]{2,1,0:T(8,128)(2,1)S(1)} %get-tuple-element.554.refs_0_), channel_id=1, source_target_pairs={{0,2},{1,3},{2,0},{3,1},{4,6},{5,7},{6,4},{7,5},{8,10},{9,11},{10,... | collective-permute-start | bytes 1474568 | tf_op jit(solution)/shard_map/ppermute | solution.py:26
  130.7 12.2 %collective-permute-start.36 = (bf16[96,1536]{1,0:T(8,128)(2,1)S(1)}, bf16[96,1536]{1,0:T(8,128)(2,1)S(1)}, u32[]{:S(2)}, u32[]{:S(2)}) collective-permute-start(bf16[96,1536]{1,0:T(8,128)(2,1)S(1)} %collective-permute-done.32.refs_6_), channel_id=1, source_target_pairs={{0,8},{8,16},{16,24},{24,28},{28,20},{20,12},{12,4},{4,0},{1,9},{9... | collective-permute-start | bytes 884744 | tf_op jit(solution)/shard_map/ppermute | solution.py:74
  185.4 13.6 %collective-permute-start.52 = (bf16[5,64,768]{2,1,0:T(8,128)(2,1)S(1)}, bf16[5,64,768]{2,1,0:T(8,128)(2,1)S(1)}, u32[]{:S(2)}, u32[]{:S(2)}) collective-permute-start(bf16[5,64,768]{2,1,0:T(8,128)(2,1)S(1)} %get-tuple-element.667.refs_0_.refs_5_), channel_id=1, source_target_pairs={{0,2},{1,3},{2,0},{3,1},{4,6},{5,7},{6,4},{7,5},{8,10},{9,11},{10,... | collective-permute-start | bytes 1474568 | tf_op jit(solution)/shard_map/ppermute | solution.py:26
  208.0 11.5 %collective-permute-start.59 = (bf16[4,64,768]{2,1,0:T(8,128)(2,1)S(1)}, bf16[4,64,768]{2,1,0:T(8,128)(2,1)S(1)}, u32[]{:S(2)}, u32[]{:S(2)}) collective-permute-start(bf16[4,64,768]{2,1,0:T(8,128)(2,1)S(1)} %add_convert_fusion.1), channel_id=1, source_target_pairs={{0,2},{1,3},{2,0},{3,1},{4,6},{5,7},{6,4},{7,5},{8,10},{9,11},{10,... | collective-permute-start | bytes 1179656 | tf_op jit(solution)/shard_map/ppermute | solution.py:26
  221.1 13.1 %collective-permute-start.61 = (bf16[5,64,768]{2,1,0:T(8,128)(2,1)S(1)}, bf16[5,64,768]{2,1,0:T(8,128)(2,1)S(1)}, u32[]{:S(2)}, u32[]{:S(2)}) collective-permute-start(bf16[5,64,768]{2,1,0:T(8,128)(2,1)S(1)} %get-tuple-element.709.refs_0_), channel_id=1, source_target_pairs={{0,1},{1,0},{2,3},{3,2},{4,5},{5,4},{6,7},{7,6},{8,9},{9,8},{10,11... | collective-permute-start | bytes 1474568 | tf_op jit(solution)/shard_map/ppermute | solution.py:26
  221.6 13.2 %collective-permute-start.62 = (bf16[5,64,768]{2,1,0:T(8,128)(2,1)S(1)}, bf16[5,64,768]{2,1,0:T(8,128)(2,1)S(1)}, u32[]{:S(2)}, u32[]{:S(2)}) collective-permute-start(bf16[5,64,768]{2,1,0:T(8,128)(2,1)S(1)} %get-tuple-element.709.refs_0_), channel_id=1, source_target_pairs={{0,2},{1,3},{2,0},{3,1},{4,6},{5,7},{6,4},{7,5},{8,10},{9,11},{10,... | collective-permute-start | bytes 1474568 | tf_op jit(solution)/shard_map/ppermute | solution.py:26
  236.3 13.5 %collective-permute-start.66 = (bf16[96,1920]{1,0:T(8,128)(2,1)S(1)}, bf16[96,1920]{1,0:T(8,128)(2,1)S(1)}, u32[]{:S(2)}, u32[]{:S(2)}) collective-permute-start(bf16[96,1920]{1,0:T(8,128)(2,1)S(1)} %get-tuple-element.731), channel_id=1, source_target_pairs={{0,8},{8,16},{16,24},{24,28},{28,20},{20,12},{12,4},{4,0},{1,9},{9... | collective-permute-start | bytes 1105928 | tf_op jit(solution)/shard_map/ppermute | solution.py:141
  237.7 12.1 %collective-permute-start.67 = (bf16[96,1920]{1,0:T(8,128)(2,1)S(1)}, bf16[96,1920]{1,0:T(8,128)(2,1)S(1)}, u32[]{:S(2)}, u32[]{:S(2)}) collective-permute-start(bf16[96,1920]{1,0:T(8,128)(2,1)S(1)} %get-tuple-element.732), channel_id=1, source_target_pairs={{8,0},{16,8},{24,16},{28,24},{20,28},{12,20},{4,12},{0,4},{9,1},{1... | collective-permute-start | bytes 1105928 | tf_op jit(solution)/shard_map/ppermute | solution.py:141
  251.3 13.5 %collective-permute-start.69 = (bf16[96,2688]{1,0:T(8,128)(2,1)S(1)}, bf16[96,2688]{1,0:T(8,128)(2,1)S(1)}, u32[]{:S(2)}, u32[]{:S(2)}) collective-permute-start(bf16[96,2688]{1,0:T(8,128)(2,1)S(1)} %get-tuple-element.747), channel_id=1, source_target_pairs={{0,8},{8,16},{16,24},{24,28},{28,20},{20,12},{12,4},{4,0},{1,9},{9... | collective-permute-start | bytes 1548296 | tf_op jit(solution)/shard_map/ppermute | solution.py:141
  252.7 13.1 %collective-permute-start.70 = (bf16[96,2688]{1,0:T(8,128)(2,1)S(1)}, bf16[96,2688]{1,0:T(8,128)(2,1)S(1)}, u32[]{:S(2)}, u32[]{:S(2)}) collective-permute-start(bf16[96,2688]{1,0:T(8,128)(2,1)S(1)} %get-tuple-element.748), channel_id=1, source_target_pairs={{8,0},{16,8},{24,16},{28,24},{20,28},{12,20},{4,12},{0,4},{9,1},{1... | collective-permute-start | bytes 1548296 | tf_op jit(solution)/shard_map/ppermute | solution.py:141
  267.1 12.8 %collective-permute-start.75 = (bf16[96,2688]{1,0:T(8,128)(2,1)S(1)}, bf16[96,2688]{1,0:T(8,128)(2,1)S(1)}, u32[]{:S(2)}, u32[]{:S(2)}) collective-permute-start(bf16[96,2688]{1,0:T(8,128)(2,1)S(1)} %get-tuple-element.771), channel_id=1, source_target_pairs={{0,8},{8,16},{16,24},{24,28},{28,20},{20,12},{12,4},{4,0},{1,9},{9... | collective-permute-start | bytes 1548296 | tf_op jit(solution)/shard_map/ppermute | solution.py:141
  268.2 11.7 %collective-permute-start.73 = (bf16[4,64,768]{2,1,0:T(8,128)(2,1)S(1)}, bf16[4,64,768]{2,1,0:T(8,128)(2,1)S(1)}, u32[]{:S(2)}, u32[]{:S(2)}) collective-permute-start(bf16[4,64,768]{2,1,0:T(8,128)(2,1)S(1)} %add_convert_fusion), channel_id=1, source_target_pairs={{0,2},{1,3},{2,0},{3,1},{4,6},{5,7},{6,4},{7,5},{8,10},{9,11},{10,... | collective-permute-start | bytes 1179656 | tf_op jit(solution)/shard_map/ppermute | solution.py:26
  (110 other events, 958.4 us)

commit v8 on v7

--- a/solution.py
+++ b/solution.py
@@ -204,6 +204,13 @@
     return [[values[:, j * size :][:, at] for at in heads_in(size)] for j in range(count)]
 
 
+def by_passage(found, count):
+    rows = [
+        jnp.concatenate(found[at : at + count], axis=1) for at in range(0, len(found), count)
+    ]
+    return jnp.concatenate(rows, axis=0)
+
+
 def assemble(info, pieces, targets, signals, column_from=0):
     rows = pieces[0].shape[0]
     copies = []
@@ -288,7 +295,7 @@
 
     def given(a):
         array = a.array if isinstance(a, (Columns, Far, Rider)) else a
-        far = (large(a) and not isinstance(a, Close)) or isinstance(a, Rider)
+        far = (large(a) and not isinstance(a, Close)) or (isinstance(a, Rider) and a.far)
         return pltpu.with_memory_space_constraint(array, pltpu.HBM) if far else array
 
     def made(a):
@@ -337,8 +344,8 @@
 
 
 class Rider:
-    def __init__(self, array, index):
-        self.array, self.index, self.dtype = array, index, array.dtype
+    def __init__(self, array, index, far):
+        self.array, self.index, self.dtype, self.far = array, index, array.dtype, far
         self.shape = (1, *array.shape[1:])
 
 
@@ -447,6 +454,7 @@
     slot = part * len(normed)
     size = pieces[0].shape[1] // 4
     count = size // HDIM
+    each = 2
 
     def body(info, rows, pieces, outs, _, scratch):
         qkv, probs, context = outs[:3]
@@ -459,19 +467,23 @@
             w_in[...] = together[:, : 3 * size]
             w_out[...] = together[:, 3 * size :]
 
-        qkv[0] = dot(token_rows(rows), w_in[...]).astype(bf16)
-        allowed = slots_used(info, b, part, slot)
-        query, keys, vals = head_parts(qkv[0], 3)
+        made = dot(token_rows(rows), w_in[...]).astype(bf16)
+        qkv[...] = made.reshape(qkv.shape)
+        parts = [head_parts(made[p * slot : (p + 1) * slot], 3) for p in range(each)]
+        pairs = [(p, k) for p in range(each) for k in range(count)]
+        scores = [dot_t(parts[p][0][k] * SCALE, parts[p][1][k]) for p, k in pairs]
+        allowed = [slots_used(info, b * each + p, part, slot) for p in range(each)]
         found = []
-        for k, scores in enumerate([dot_t(q * SCALE, t) for q, t in zip(query, keys, strict=True)]):
-            scores = jnp.where(allowed, scores, masked_score)
-            spread_out = jnp.exp(scores - jnp.max(scores, axis=-1, keepdims=True))
+        for (p, k), score in zip(pairs, scores, strict=True):
+            score = jnp.where(allowed[p], score, masked_score)
+            spread_out = jnp.exp(score - jnp.max(score, axis=-1, keepdims=True))
             inverse = 1.0 / jnp.sum(spread_out, axis=-1, keepdims=True)
             found.append((spread_out * inverse).astype(bf16))
-            probs[0, k] = found[-1]
-        found = [dot(w, v) for w, v in zip(found, vals, strict=True)]
-        context[0] = jnp.concatenate(found, axis=1).astype(bf16)
-        emit(dot_t(context[0], w_out[...]), outs[3:])
+            probs[p, k] = found[-1]
+        found = [dot(w, parts[p][2][k]) for (p, k), w in zip(pairs, found, strict=True)]
+        joined = by_passage(found, count).astype(bf16)
+        context[...] = joined.reshape(context.shape)
+        emit(dot_t(joined, w_out[...]), outs[3:])
 
     return call(
         body,
@@ -487,7 +499,8 @@
         [],
         attention_scratch(width, size, pieces),
         flops=2 * blocks * slot * (width * size * 4 + 8 * slot * size),
-        steps=blocks,
+        steps=blocks // each,
+        each=each,
     )
 
 
@@ -495,13 +508,14 @@
     blocks, part, width = normed[0].shape
     slot = part * len(normed)
     size = context.shape[2]
+    each = 2
 
     def body(info, stepped, fixed, outs, ends, scratch):
         grad_refs, normed_refs = stepped[:4], stepped[4:8]
         qkv, probs, context = stepped[8:]
         w_in, w_out, gains = fixed
         pieces, gain_out = ends[:-1], ends[-1]
-        total_in, total_out, moved = scratch
+        total_in, total_out = scratch
         b = pl.program_id(0)
 
         @pl.when(b == 0)
@@ -513,25 +527,29 @@
         grad = token_rows(grad_refs)
         rows = token_rows(normed_refs)
         dcontext = dot(grad, w_out[...]).astype(bf16)
-        query, keys, vals = head_parts(qkv[0], 3)
-        cuts = head_parts(dcontext, 1)[0]
-        backs = [dot_t(c, v) for c, v in zip(cuts, vals, strict=True)]
-        dvals = [t_dot(probs[0, k], c) for k, c in enumerate(cuts)]
+        parts = [head_parts(qkv[p], 3) for p in range(each)]
+        cuts = [c for p in range(each) for c in head_parts(dcontext[p * slot : (p + 1) * slot], 1)[0]]
+        pairs = [(p, k) for p in range(each) for k in range(size // HDIM)]
+        backs = [dot_t(c, parts[p][2][k]) for (p, k), c in zip(pairs, cuts, strict=True)]
+        dvals = [t_dot(probs[p, k], c) for (p, k), c in zip(pairs, cuts, strict=True)]
         lows = []
-        for k, back in enumerate(backs):
-            wide = probs[0, k].astype(f32)
+        for (p, k), back in zip(pairs, backs, strict=True):
+            wide = probs[p, k].astype(f32)
             low = wide * (back - jnp.sum(wide * back, axis=-1, keepdims=True))
             lows.append(low.astype(bf16))
-        dquery = [dot(d, t) * SCALE for d, t in zip(lows, keys, strict=True)]
-        dkeys = [t_dot(d, q) * SCALE for d, q in zip(lows, query, strict=True)]
-        moved[...] = jnp.concatenate([*dquery, *dkeys, *dvals], axis=1).astype(bf16)
-        partial = dot_t(moved[...], w_in[...])
+        dquery = [dot(d, parts[p][1][k]) * SCALE for (p, k), d in zip(pairs, lows, strict=True)]
+        dkeys = [t_dot(d, parts[p][0][k]) * SCALE for (p, k), d in zip(pairs, lows, strict=True)]
+        count = size // HDIM
+        moved = jnp.concatenate(
+            [by_passage(found, count) for found in (dquery, dkeys, dvals)], axis=1
+        ).astype(bf16)
+        partial = dot_t(moved, w_in[...])
         emit(partial, outs)
         gain_out[...] += jnp.sum(partial * rows.astype(f32), axis=0, keepdims=True) / gains[0:1, :]
-        total_in[...] += t_dot(rows, moved[...])
-        total_out[...] += t_dot(grad, context[0])
-
-        @pl.when(b == blocks - 1)
+        total_in[...] += t_dot(rows, moved)
+        total_out[...] += t_dot(grad, context[...].reshape(grad.shape[0], size))
+
+        @pl.when(b == blocks // each - 1)
         def _():
             hand_out(info, (total_in, total_out), pieces)
 
@@ -545,10 +563,10 @@
         [
             pltpu.VMEM((width, 3 * size), f32),
             pltpu.VMEM((width, size), f32),
-            pltpu.VMEM((slot, 3 * size), bf16),
         ],
         flops=2 * blocks * slot * (width * size * 8 + 20 * slot * size),
-        steps=blocks,
+        steps=blocks // each,
+        each=each,
     )
     return results[:4], results[4:12], results[12]
 
@@ -1215,8 +1233,8 @@
     def spread(rows):
         return [rows, swap(rows, "head", 1), swap(rows, "head", 2)]
 
-    def riders(all_rows):
-        return [Rider(rows, blocks) for rows in all_rows[1:]]
+    def riders(all_rows, far=True):
+        return [Rider(rows, blocks, far) for rows in all_rows[1:]]
 
     second, dec_ffn = sync(second, dec_ffn)
     second_all = spread(second)
@@ -1244,21 +1262,23 @@
         info, dec_in, decoder_gains, ffn, at_self, size, order
     )
     partial, arrived, mine, sent, dec_ffn = sync(partial, arrived, mine, sent, dec_ffn)
-    states, states_sent = by_rows(
+    (states_sent,) = by_rows(
         lambda h, a, b, c: (h + a + b + c,),
         info,
         [hidden, partial[0], *arrived],
         [],
         [bf16],
         riders=sent,
+        kept=False,
     )
     states_sent, dec_ffn = sync(states_sent, dec_ffn)
+    states = states_sent[:blocks]
     states_all = spread(states_sent)
     dec_ffn = fetch_step(dec_ffn, -3, 3)
     w_cross, w_cross_query, w_cross_output = gathered(
         info, ffn, (2 * size, size, size), at_cross
     )
-    states_all, dec_ffn, w_cross = sync(states_all, dec_ffn, w_cross)
+    states_all, dec_ffn, w_cross, states = sync(states_all, dec_ffn, w_cross, states)
     dec_ffn = fetch_step(dec_ffn, -4)
     states_all = sync(*states_all, swap(states_all[2], "head", 1))
 
@@ -1266,7 +1286,7 @@
         info,
         states_all,
         (w_cross, w_cross_query),
-        (dec_in, [mine, *riders(states_all)], decoder_gains),
+        (dec_in, [mine, *riders(states_all, False)], decoder_gains),
         question,
         count_q,
         count_pass,

time: 298 us -> 294 us (0.987)
  Pallas kernels: 98.7 us -> 92.9 us
  waiting for transfers between devices: 115 us -> 120 us
  starting transfers between devices: 65.4 us -> 62.3 us
    pallas_call x34, Pallas kernels: 98.7 us -> 92.9 us  [call(): pl.pallas_call(split, grid=(steps,), in_specs=[pl.BlockSpec(memory_space=...]
    ppermute x51, waiting for transfers between devices: 55.5 us -> 59.4 us  [swap(): return lax.ppermute(value, axis, [(i, i ^ bits) for i in range(size)])]
    ppermute x51, starting transfers between devices: 31.8 us -> 28.5 us  [swap(): return lax.ppermute(value, axis, [(i, i ^ bits) for i in range(size)])]
    unnamed x109 -> x97, local copies, waits for them, and re-layouts: 6.69 us -> 5.88 us
  transfers between devices with their start and end apart: 83 -> 83, of which waited for: 42 -> 43; matrix products, arithmetic and copies ran while one was open for 2% -> 2% of each run, Pallas kernels for 27% -> 26%
where the time goes in v8:
time: 294 us; the launch traced here: 293 us
  waiting for transfers between devices  120 us (41%)
  Pallas kernels  92.9 us (32%)
  starting transfers between devices  62.3 us (21%)
  local copies, waits for them, and re-layouts  8.54 us (3%)
  blocking collectives  5.4 us (2%)
    pallas_call x34, Pallas kernels, call(): pl.pallas_call(split, grid=(steps,), in_specs=[pl.BlockSpec(memory_space=...  92.9 us
    ppermute x51, waiting for transfers between devices, swap(): return lax.ppermute(value, axis, [(i, i ^ bits) for i in range(size)])  59.4 us
    ppermute x21, waiting for transfers between devices, fetch_step(): lax.ppermute(pieces[k + 1 if k < 0 else k - 1], 'blk', forth if k < 0 els...  47.7 us
    ppermute x51, starting transfers between devices, swap(): return lax.ppermute(value, axis, [(i, i ^ bits) for i in range(size)])  28.5 us
    ppermute x21, starting transfers between devices, fetch_step(): lax.ppermute(pieces[k + 1 if k < 0 else k - 1], 'blk', forth if k < 0 els...  21.9 us
    ppermute x11, waiting for transfers between devices, reduce_step(): lax.ppermute(v, 'blk', way)  12.6 us
    ppermute x11, starting transfers between devices, reduce_step(): lax.ppermute(v, 'blk', way)  11.9 us
  transfers between devices with their start and end apart: 83, of which 43 were waited for; matrix products, arithmetic and copies ran while one was open for 2% of the time, Pallas kernels for 26%

profile of v8, /device:TPU:0, one launch (start us, length us, event | category | flops | bytes accessed | tf_op | source)
XLA Modules:
  0.0 293.1 jit_solution(9038550374553279419)
XLA Ops:
  21.9 5.4 %all_gather.3 = bf16[2,40,768]{2,0,1:T(2,128)(2,1)S(1)} all-gather(bf16[2,10,768]{2,0,1:T(2,128)(2,1)S(1)} %copy.68), channel_id=1, replica_groups=mesh['blk'=8,'head'=4] {'head'}, dimensions={1}, use_global_device_ids=true | all-gather | bytes 153600 | tf_op jit(solution)/shard_map/all_gather | solution.py:1199
  29.6 4.6 %collective-permute-done.8.refs_11_.refs_7_ = bf16[96,768]{1,0:T(8,128)(2,1)S(1)} collective-permute-done((bf16[96,768]{1,0:T(8,128)(2,1)S(1)}, bf16[96,768]{1,0:T(8,128)(2,1)S(1)}, u32[]{:S(2)}, u32[]{:S(2)}) %collective-permute-start.8) | collective-permute-done | bytes 147488 | tf_op jit(solution)/shard_map/ppermute | solution.py:74
  34.1 8.9 %collective-permute-done.9.refs_6_.refs_2_ = bf16[96,3072]{1,0:T(8,128)(2,1)S(1)} collective-permute-done((bf16[96,3072]{1,0:T(8,128)(2,1)S(1)}, bf16[96,3072]{1,0:T(8,128)(2,1)S(1)}, u32[]{:S(2)}, u32[]{:S(2)}) %collective-permute-start.9) | collective-permute-done | bytes 589856 | tf_op jit(solution)/shard_map/ppermute | solution.py:74
  45.0 6.6 %shard_map.427 = (bf16[4,256,576]{2,1,0:T(8,128)(2,1)}, bf16[4,3,256,256]{3,2,1,0:T(8,128)(2,1)}, bf16[4,256,192]{2,1,0:T(8,128)(2,1)S(1)}, f32[4,64,768]{2,1,0:...) custom-call(s32[14]{0:T(128)S(1)} %pad_add_fusion.info_ref, ...), custom_call_target="tpu_custom_call" | custom-call | flops 2013265920 | bytes 8257536 | tf_op jit(solution)/shard_map/pallas_call | solution.py:308
  51.7 6.1 %collective-permute-done.11.refs_5_.refs_1_ = bf16[96,3072]{1,0:T(8,128)(2,1)S(1)} collective-permute-done((bf16[96,3072]{1,0:T(8,128)(2,1)S(1)}, bf16[96,3072]{1,0:T(8,128)(2,1)S(1)}, u32[]{:S(2)}, u32[]{:S(2)}) %collective-permute-start.11) | collective-permute-done | bytes 589856 | tf_op jit(solution)/shard_map/ppermute | solution.py:74
  61.8 13.0 %collective-permute-done.16.refs_7_.refs_3_ = bf16[96,3072]{1,0:T(8,128)(2,1)S(1)} collective-permute-done((bf16[96,3072]{1,0:T(8,128)(2,1)S(1)}, bf16[96,3072]{1,0:T(8,128)(2,1)S(1)}, u32[]{:S(2)}, u32[]{:S(2)}) %collective-permute-start.16) | collective-permute-done | bytes 589856 | tf_op jit(solution)/shard_map/ppermute | solution.py:74
  81.2 9.8 %collective-permute-done.19.refs_2_ = bf16[4,64,768]{2,1,0:T(8,128)(2,1)S(1)} collective-permute-done((bf16[4,64,768]{2,1,0:T(8,128)(2,1)S(1)}, bf16[4,64,768]{2,1,0:T(8,128)(2,1)S(1)}, u32[]{:S(2)}, u32[]{:S(2)}) %collective-permute-start.19) | collective-permute-done | bytes 393248 | tf_op jit(solution)/shard_map/ppermute | solution.py:26
  93.7 7.3 %shard_map.429 = (bf16[4,256,768]{2,1,0:T(8,128)(2,1)}, bf16[4,256,768]{2,1,0:T(8,128)(2,1)}, f32[4,64,768]{2,1,0:T(8,128)S(1)}, bf16[4,64,768]{2,1,0:T(8,128)(2...) custom-call(s32[14]{0:T(128)S(1)} %pad_add_fusion.info_ref, ...), custom_call_target="tpu_custom_call" | custom-call | flops 2415919104 | bytes 11796480 | tf_op jit(solution)/shard_map/pallas_call | solution.py:308
  105.9 3.9 %shard_map.430 = (bf16[48,768]{1,0:T(8,128)(2,1)}, bf16[48,576]{1,0:T(8,128)(2,1)}, f32[3,48,48]{2,1,0:T(8,128)}, bf16[48,192]{1,0:T(8,128)(2,1)}, f32[48,768]{1...) custom-call(s32[14]{0:T(128)S(1)} %pad_add_fusion.info_ref, ...), custom_call_target="tpu_custom_call" | custom-call | flops 56623104 | bytes 6377856 | tf_op jit(solution)/shard_map/pallas_call | solution.py:308
  109.8 3.4 %collective-permute-done.28.refs_4_ = bf16[96,1536]{1,0:T(8,128)(2,1)S(1)} collective-permute-done((bf16[96,1536]{1,0:T(8,128)(2,1)S(1)}, bf16[96,1536]{1,0:T(8,128)(2,1)S(1)}, u32[]{:S(2)}, u32[]{:S(2)}) %collective-permute-start.28) | collective-permute-done | bytes 294944 | tf_op jit(solution)/shard_map/ppermute | solution.py:74
  121.0 4.1 %collective-permute-done.32.refs_6_ = bf16[96,1536]{1,0:T(8,128)(2,1)S(1)} collective-permute-done((bf16[96,1536]{1,0:T(8,128)(2,1)S(1)}, bf16[96,1536]{1,0:T(8,128)(2,1)S(1)}, u32[]{:S(2)}, u32[]{:S(2)}) %collective-permute-start.32) | collective-permute-done | bytes 294944 | tf_op jit(solution)/shard_map/ppermute | solution.py:74
  125.2 3.8 %collective-permute-done.31.refs_2_.refs_9_ = bf16[5,64,768]{2,1,0:T(8,128)(2,1)S(1)} collective-permute-done((bf16[5,64,768]{2,1,0:T(8,128)(2,1)S(1)}, bf16[5,64,768]{2,1,0:T(8,128)(2,1)S(1)}, u32[]{:S(2)}, u32[]{:S(2)}) %collective-permute-start.31) | collective-permute-done | bytes 491552 | tf_op jit(solution)/shard_map/ppermute | solution.py:26
  130.9 3.6 %shard_map.433 = (bf16[4,256,384]{2,1,0:T(8,128)(2,1)}, f32[48,768]{1,0:T(8,128)}, bf16[48,768]{1,0:T(8,128)(2,1)}, bf16[48,192]{1,0:T(8,128)(2,1)S(1)}, f32[48,384]{1,0:T(8,128)S(1)}) custom-call(s32[14]{0:T(128)S(1)} %pad_add_fusion.info_ref, bf16[5,64,768]{2,1,0:T(8,128)(2,1)S(1)} %shard_map.431.refs_0_, ...), custom_call_target="tpu_custom_call" | custom-call | flops 603979776 | bytes 4476096 | tf_op jit(solution)/shard_map/pallas_call | solution.py:308
  135.8 4.2 %collective-permute-done.35.refs_1_ = f32[48,384]{1,0:T(8,128)S(1)} collective-permute-done((f32[48,384]{1,0:T(8,128)S(1)}, f32[48,384]{1,0:T(8,128)S(1)}, u32[]{:S(2)}, u32[]{:S(2)}) %collective-permute-start.35) | collective-permute-done | bytes 73760 | tf_op jit(solution)/shard_map/ppermute | solution.py:26
  141.2 4.1 %collective-permute-start.39 = (f32[48,384]{1,0:T(8,128)S(1)}, f32[48,384]{1,0:T(8,128)S(1)}, u32[]{:S(2)}, u32[]{:S(2)}) collective-permute-start(f32[48,384]{1,0:T(8,128)S(1)} %shard_map.434.refs_0_), channel_id=1, source_target_pairs={{0,24},{4,28},{8,16},{12,20},{16,8},{20,12},{24,0},{28,4},{1,25},{... | collective-permute-start | bytes 221192 | tf_op jit(solution)/shard_map/ppermute | solution.py:26
  161.4 3.4 %collective-permute-done.44.refs_5_ = bf16[48,768]{1,0:T(8,128)(2,1)S(1)} collective-permute-done((bf16[48,768]{1,0:T(8,128)(2,1)S(1)}, bf16[48,768]{1,0:T(8,128)(2,1)S(1)}, u32[]{:S(2)}, u32[]{:S(2)}) %collective-permute-start.44) | collective-permute-done | bytes 73760 | tf_op jit(solution)/shard_map/ppermute | solution.py:26
  165.1 3.8 %shard_map.438 = (bf16[4,256,384]{2,1,0:T(8,128)(2,1)}, f32[4,64,768]{2,1,0:T(8,128)S(1)}, bf16[4,64,768]{2,1,0:T(8,128)(2,1)S(1)}, f32[4,64,768]{2,1,0:T(8,128)...) custom-call(s32[14]{0:T(128)S(1)} %pad_add_fusion.info_ref, ...), custom_call_target="tpu_custom_call" | custom-call | flops 603979776 | bytes 5901504 | tf_op jit(solution)/shard_map/pallas_call | solution.py:308
  191.3 5.6 %collective-permute-done.52.refs_2_.refs_7_.refs_10_ = bf16[5,64,768]{2,1,0:T(8,128)(2,1)S(1)} collective-permute-done((bf16[5,64,768]{2,1,0:T(8,128)(2,1)S(1)}, bf16[5,64,768]{2,1,0:T(8,128)(2,1)S(1)}, u32[]{:S(2)}, u32[]{:S(2)}) %collective-permute-start.52) | collective-permute-done | bytes 491552 | tf_op jit(solution)/shard_map/ppermute | solution.py:26
  198.8 4.9 %shard_map.444 = (bf16[4,256,768]{2,1,0:T(8,128)(2,1)}, f32[4,64,768]{2,1,0:T(8,128)S(1)}, bf16[4,64,768]{2,1,0:T(8,128)(2,1)S(1)}, f32[4,64,768]{2,1,0:T(8,128)S(1)}, bf16[4,64,768]{2,1,0:T(8,128)(2,1)S(1)}) custom-call(s32[14]{0:T(128)S(1)} %pad_add_fusion.info_ref, bf16[5,64,768]{2,1,0:T(8,128)(2,1)S(1)} %get-tuple-element.665.refs_0_.refs_5_, ...), custom_call_target="tpu_custom_call" | custom-call | flops 2415919104 | bytes 9830400 | tf_op jit(solution)/shard_map/pallas_call | solution.py:308
  210.3 6.7 %shard_map.446 = (f32[96,1920]{1,0:T(8,128)}, bf16[96,1920]{1,0:T(8,128)(2,1)}, bf16[96,1920]{1,0:T(8,128)(2,1)}, bf16[96,1920]{1,0:T(8,128)(2,1)}, bf16[96,1920...) custom-call(s32[14]{0:T(128)S(1)} %pad_add_fusion.info_ref, ...), custom_call_target="tpu_custom_call" | custom-call | flops 2415919104 | bytes 11182080 | tf_op jit(solution)/shard_map/pallas_call | solution.py:308
  224.9 5.8 %collective-permute-done.63.refs_0_ = bf16[96,1920]{1,0:T(8,128)(2,1)S(1)} collective-permute-done((bf16[96,1920]{1,0:T(8,128)(2,1)S(1)}, bf16[96,1920]{1,0:T(8,128)(2,1)S(1)}, u32[]{:S(2)}, u32[]{:S(2)}) %collective-permute-start.63) | collective-permute-done | bytes 368672 | tf_op jit(solution)/shard_map/ppermute | solution.py:141
  236.4 10.0 %shard_map.449 = (f32[4,64,768]{2,1,0:T(8,128)S(1)}, bf16[4,64,768]{2,1,0:T(8,128)(2,1)S(1)}, f32[4,64,768]{2,1,0:T(8,128)S(1)}, bf16[4,64,768]{2,1,0:T(8,128)(2...) custom-call(s32[14]{0:T(128)S(1)} %pad_add_fusion.info_ref, ...), custom_call_target="tpu_custom_call" | custom-call | flops 4429185024 | bytes 11559936 | tf_op jit(solution)/shard_map/pallas_call | solution.py:308
  257.0 4.3 %collective-permute-done.69.refs_0_.refs_2_ = bf16[96,2688]{1,0:T(8,128)(2,1)S(1)} collective-permute-done((bf16[96,2688]{1,0:T(8,128)(2,1)S(1)}, bf16[96,2688]{1,0:T(8,128)(2,1)S(1)}, u32[]{:S(2)}, u32[]{:S(2)}) %collective-permute-start.69) | collective-permute-done | bytes 516128 | tf_op jit(solution)/shard_map/ppermute | solution.py:141
  267.4 9.1 %collective-permute-done.77 = f32[5,768]{1,0:T(8,128)S(1)} collective-permute-done((f32[5,768]{1,0:T(8,128)S(1)}, f32[5,768]{1,0:T(8,128)S(1)}, u32[]{:S(2)}, u32[]{:S(2)}) %collective-permute-start.77) | collective-permute-done | bytes 15392 | tf_op jit(solution)/shard_map/ppermute | solution.py:26
  (303 shorter events, 149.3 us)
Async XLA Ops:
  11.0 16.3 %collective-permute-start.6 = (bf16[4,64,768]{2,1,0:T(8,128)(2,1)S(1)}, bf16[4,64,768]{2,1,0:T(8,128)(2,1)S(1)}, u32[]{:S(2)}, u32[]{:S(2)}) collective-permute-start(bf16[4,64,768]{2,1,0:T(8,128)(2,1)S(1)} %shard_map.426.refs_0_.refs_4_), channel_id=1, source_target_pairs={{0,1},{1,0},{2,3},{3,2},{4,5},{5,4},{6,7},{7,6},{8,9},{9,8},{10,11... | collective-permute-start | bytes 1179656 | tf_op jit(solution)/shard_map/ppermute | solution.py:26
  11.1 16.3 %collective-permute-start.7 = (bf16[4,64,768]{2,1,0:T(8,128)(2,1)S(1)}, bf16[4,64,768]{2,1,0:T(8,128)(2,1)S(1)}, u32[]{:S(2)}, u32[]{:S(2)}) collective-permute-start(bf16[4,64,768]{2,1,0:T(8,128)(2,1)S(1)} %shard_map.426.refs_0_.refs_4_), channel_id=1, source_target_pairs={{0,2},{1,3},{2,0},{3,1},{4,6},{5,7},{6,4},{7,5},{8,10},{9,11},{10,... | collective-permute-start | bytes 1179656 | tf_op jit(solution)/shard_map/ppermute | solution.py:26
  27.4 15.6 %collective-permute-start.9 = (bf16[96,3072]{1,0:T(8,128)(2,1)S(1)}, bf16[96,3072]{1,0:T(8,128)(2,1)S(1)}, u32[]{:S(2)}, u32[]{:S(2)}) collective-permute-start(bf16[96,3072]{1,0:T(8,128)(2,1)S(1)} %concatenate.15.refs_4_.refs_0_), channel_id=1, source_target_pairs={{8,0},{16,8},{24,16},{28,24},{20,28},{12,20},{4,12},{0,4},{9,1},{1... | collective-permute-start | bytes 1769480 | tf_op jit(solution)/shard_map/ppermute | solution.py:74
  43.0 14.8 %collective-permute-start.11 = (bf16[96,3072]{1,0:T(8,128)(2,1)S(1)}, bf16[96,3072]{1,0:T(8,128)(2,1)S(1)}, u32[]{:S(2)}, u32[]{:S(2)}) collective-permute-start(bf16[96,3072]{1,0:T(8,128)(2,1)S(1)} %concatenate.15.refs_4_.refs_0_), channel_id=1, source_target_pairs={{0,8},{8,16},{16,24},{24,28},{28,20},{20,12},{12,4},{4,0},{1,9},{9... | collective-permute-start | bytes 1769480 | tf_op jit(solution)/shard_map/ppermute | solution.py:74
  44.6 14.5 %collective-permute-start.12 = (bf16[96,3072]{1,0:T(8,128)(2,1)S(1)}, bf16[96,3072]{1,0:T(8,128)(2,1)S(1)}, u32[]{:S(2)}, u32[]{:S(2)}) collective-permute-start(bf16[96,3072]{1,0:T(8,128)(2,1)S(1)} %collective-permute-done.9.refs_6_.refs_2_), channel_id=1, source_target_pairs={{8,0},{16,8},{24,16},{28,24},{20,28},{12,20},{4,12},{0,4},{9,1},{1... | collective-permute-start | bytes 1769480 | tf_op jit(solution)/shard_map/ppermute | solution.py:74
  59.1 15.7 %collective-permute-start.16 = (bf16[96,3072]{1,0:T(8,128)(2,1)S(1)}, bf16[96,3072]{1,0:T(8,128)(2,1)S(1)}, u32[]{:S(2)}, u32[]{:S(2)}) collective-permute-start(bf16[96,3072]{1,0:T(8,128)(2,1)S(1)} %collective-permute-done.11.refs_5_.refs_1_), channel_id=1, source_target_pairs={{0,8},{8,16},{16,24},{24,28},{28,20},{20,12},{12,4},{4,0},{1,9},{9... | collective-permute-start | bytes 1769480 | tf_op jit(solution)/shard_map/ppermute | solution.py:74
  60.6 15.5 %collective-permute-start.17 = (bf16[96,3072]{1,0:T(8,128)(2,1)S(1)}, bf16[96,3072]{1,0:T(8,128)(2,1)S(1)}, u32[]{:S(2)}, u32[]{:S(2)}) collective-permute-start(bf16[96,3072]{1,0:T(8,128)(2,1)S(1)} %collective-permute-done.12.refs_8_.refs_4_), channel_id=1, source_target_pairs={{8,0},{16,8},{24,16},{28,24},{20,28},{12,20},{4,12},{0,4},{9,1},{1... | collective-permute-start | bytes 1769480 | tf_op jit(solution)/shard_map/ppermute | solution.py:74
  61.2 14.9 %collective-permute-start.14 = (bf16[4,64,768]{2,1,0:T(8,128)(2,1)S(1)}, bf16[4,64,768]{2,1,0:T(8,128)(2,1)S(1)}, u32[]{:S(2)}, u32[]{:S(2)}) collective-permute-start(bf16[4,64,768]{2,1,0:T(8,128)(2,1)S(1)} %add_convert_fusion.4), channel_id=1, source_target_pairs={{0,2},{1,3},{2,0},{3,1},{4,6},{5,7},{6,4},{7,5},{8,10},{9,11},{10,... | collective-permute-start | bytes 1179656 | tf_op jit(solution)/shard_map/ppermute | solution.py:26
  61.8 14.3 %collective-permute-start.15 = (bf16[4,64,768]{2,1,0:T(8,128)(2,1)S(1)}, bf16[4,64,768]{2,1,0:T(8,128)(2,1)S(1)}, u32[]{:S(2)}, u32[]{:S(2)}) collective-permute-start(bf16[4,64,768]{2,1,0:T(8,128)(2,1)S(1)} %get-tuple-element.465), channel_id=1, source_target_pairs={{0,1},{1,0},{2,3},{3,2},{4,5},{5,4},{6,7},{7,6},{8,9},{9,8},{10,11... | collective-permute-start | bytes 1179656 | tf_op jit(solution)/shard_map/ppermute | solution.py:26
  76.1 14.9 %collective-permute-start.20 = (bf16[96,3072]{1,0:T(8,128)(2,1)S(1)}, bf16[96,3072]{1,0:T(8,128)(2,1)S(1)}, u32[]{:S(2)}, u32[]{:S(2)}) collective-permute-start(bf16[96,3072]{1,0:T(8,128)(2,1)S(1)} %collective-permute-done.16.refs_7_.refs_3_), channel_id=1, source_target_pairs={{0,8},{8,16},{16,24},{24,28},{28,20},{20,12},{12,4},{4,0},{1,9},{9... | collective-permute-start | bytes 1769480 | tf_op jit(solution)/shard_map/ppermute | solution.py:74
  77.3 14.4 %collective-permute-start.21 = (bf16[96,3072]{1,0:T(8,128)(2,1)S(1)}, bf16[96,3072]{1,0:T(8,128)(2,1)S(1)}, u32[]{:S(2)}, u32[]{:S(2)}) collective-permute-start(bf16[96,3072]{1,0:T(8,128)(2,1)S(1)} %collective-permute-done.17.refs_10_.refs_6_), channel_id=1, source_target_pairs={{8,0},{16,8},{24,16},{28,24},{20,28},{12,20},{4,12},{0,4},{9,1},{1... | collective-permute-start | bytes 1769480 | tf_op jit(solution)/shard_map/ppermute | solution.py:74
  79.5 11.5 %collective-permute-start.19 = (bf16[4,64,768]{2,1,0:T(8,128)(2,1)S(1)}, bf16[4,64,768]{2,1,0:T(8,128)(2,1)S(1)}, u32[]{:S(2)}, u32[]{:S(2)}) collective-permute-start(bf16[4,64,768]{2,1,0:T(8,128)(2,1)S(1)} %get-tuple-element.497.refs_0_), channel_id=1, source_target_pairs={{0,2},{1,3},{2,0},{3,1},{4,6},{5,7},{6,4},{7,5},{8,10},{9,11},{10,... | collective-permute-start | bytes 1179656 | tf_op jit(solution)/shard_map/ppermute | solution.py:26
  115.4 13.6 %collective-permute-start.31 = (bf16[5,64,768]{2,1,0:T(8,128)(2,1)S(1)}, bf16[5,64,768]{2,1,0:T(8,128)(2,1)S(1)}, u32[]{:S(2)}, u32[]{:S(2)}) collective-permute-start(bf16[5,64,768]{2,1,0:T(8,128)(2,1)S(1)} %shard_map.431.refs_0_), channel_id=1, source_target_pairs={{0,2},{1,3},{2,0},{3,1},{4,6},{5,7},{6,4},{7,5},{8,10},{9,11},{10,... | collective-permute-start | bytes 1474568 | tf_op jit(solution)/shard_map/ppermute | solution.py:26
  129.0 11.8 %collective-permute-start.36 = (bf16[96,1536]{1,0:T(8,128)(2,1)S(1)}, bf16[96,1536]{1,0:T(8,128)(2,1)S(1)}, u32[]{:S(2)}, u32[]{:S(2)}) collective-permute-start(bf16[96,1536]{1,0:T(8,128)(2,1)S(1)} %collective-permute-done.32.refs_6_), channel_id=1, source_target_pairs={{0,8},{8,16},{16,24},{24,28},{28,20},{20,12},{12,4},{4,0},{1,9},{9... | collective-permute-start | bytes 884744 | tf_op jit(solution)/shard_map/ppermute | solution.py:74
  170.8 11.5 %collective-permute-start.47 = (bf16[4,64,768]{2,1,0:T(8,128)(2,1)S(1)}, bf16[4,64,768]{2,1,0:T(8,128)(2,1)S(1)}, u32[]{:S(2)}, u32[]{:S(2)}) collective-permute-start(bf16[4,64,768]{2,1,0:T(8,128)(2,1)S(1)} %add_convert_fusion.2), channel_id=1, source_target_pairs={{0,2},{1,3},{2,0},{3,1},{4,6},{5,7},{6,4},{7,5},{8,10},{9,11},{10,... | collective-permute-start | bytes 1179656 | tf_op jit(solution)/shard_map/ppermute | solution.py:26
  183.3 13.6 %collective-permute-start.52 = (bf16[5,64,768]{2,1,0:T(8,128)(2,1)S(1)}, bf16[5,64,768]{2,1,0:T(8,128)(2,1)S(1)}, u32[]{:S(2)}, u32[]{:S(2)}) collective-permute-start(bf16[5,64,768]{2,1,0:T(8,128)(2,1)S(1)} %get-tuple-element.665.refs_0_.refs_5_), channel_id=1, source_target_pairs={{0,2},{1,3},{2,0},{3,1},{4,6},{5,7},{6,4},{7,5},{8,10},{9,11},{10,... | collective-permute-start | bytes 1474568 | tf_op jit(solution)/shard_map/ppermute | solution.py:26
  206.0 11.5 %collective-permute-start.59 = (bf16[4,64,768]{2,1,0:T(8,128)(2,1)S(1)}, bf16[4,64,768]{2,1,0:T(8,128)(2,1)S(1)}, u32[]{:S(2)}, u32[]{:S(2)}) collective-permute-start(bf16[4,64,768]{2,1,0:T(8,128)(2,1)S(1)} %add_convert_fusion.1), channel_id=1, source_target_pairs={{0,2},{1,3},{2,0},{3,1},{4,6},{5,7},{6,4},{7,5},{8,10},{9,11},{10,... | collective-permute-start | bytes 1179656 | tf_op jit(solution)/shard_map/ppermute | solution.py:26
  219.1 12.7 %collective-permute-start.61 = (bf16[5,64,768]{2,1,0:T(8,128)(2,1)S(1)}, bf16[5,64,768]{2,1,0:T(8,128)(2,1)S(1)}, u32[]{:S(2)}, u32[]{:S(2)}) collective-permute-start(bf16[5,64,768]{2,1,0:T(8,128)(2,1)S(1)} %get-tuple-element.707.refs_0_), channel_id=1, source_target_pairs={{0,1},{1,0},{2,3},{3,2},{4,5},{5,4},{6,7},{7,6},{8,9},{9,8},{10,11... | collective-permute-start | bytes 1474568 | tf_op jit(solution)/shard_map/ppermute | solution.py:26
  219.2 13.6 %collective-permute-start.62 = (bf16[5,64,768]{2,1,0:T(8,128)(2,1)S(1)}, bf16[5,64,768]{2,1,0:T(8,128)(2,1)S(1)}, u32[]{:S(2)}, u32[]{:S(2)}) collective-permute-start(bf16[5,64,768]{2,1,0:T(8,128)(2,1)S(1)} %get-tuple-element.707.refs_0_), channel_id=1, source_target_pairs={{0,2},{1,3},{2,0},{3,1},{4,6},{5,7},{6,4},{7,5},{8,10},{9,11},{10,... | collective-permute-start | bytes 1474568 | tf_op jit(solution)/shard_map/ppermute | solution.py:26
  234.3 12.1 %collective-permute-start.66 = (bf16[96,1920]{1,0:T(8,128)(2,1)S(1)}, bf16[96,1920]{1,0:T(8,128)(2,1)S(1)}, u32[]{:S(2)}, u32[]{:S(2)}) collective-permute-start(bf16[96,1920]{1,0:T(8,128)(2,1)S(1)} %get-tuple-element.729), channel_id=1, source_target_pairs={{0,8},{8,16},{16,24},{24,28},{28,20},{20,12},{12,4},{4,0},{1,9},{9... | collective-permute-start | bytes 1105928 | tf_op jit(solution)/shard_map/ppermute | solution.py:141
  247.9 13.5 %collective-permute-start.69 = (bf16[96,2688]{1,0:T(8,128)(2,1)S(1)}, bf16[96,2688]{1,0:T(8,128)(2,1)S(1)}, u32[]{:S(2)}, u32[]{:S(2)}) collective-permute-start(bf16[96,2688]{1,0:T(8,128)(2,1)S(1)} %get-tuple-element.745), channel_id=1, source_target_pairs={{0,8},{8,16},{16,24},{24,28},{28,20},{20,12},{12,4},{4,0},{1,9},{9... | collective-permute-start | bytes 1548296 | tf_op jit(solution)/shard_map/ppermute | solution.py:141
  249.3 13.1 %collective-permute-start.70 = (bf16[96,2688]{1,0:T(8,128)(2,1)S(1)}, bf16[96,2688]{1,0:T(8,128)(2,1)S(1)}, u32[]{:S(2)}, u32[]{:S(2)}) collective-permute-start(bf16[96,2688]{1,0:T(8,128)(2,1)S(1)} %get-tuple-element.746), channel_id=1, source_target_pairs={{8,0},{16,8},{24,16},{28,24},{20,28},{12,20},{4,12},{0,4},{9,1},{1... | collective-permute-start | bytes 1548296 | tf_op jit(solution)/shard_map/ppermute | solution.py:141
  263.7 12.8 %collective-permute-start.75 = (bf16[96,2688]{1,0:T(8,128)(2,1)S(1)}, bf16[96,2688]{1,0:T(8,128)(2,1)S(1)}, u32[]{:S(2)}, u32[]{:S(2)}) collective-permute-start(bf16[96,2688]{1,0:T(8,128)(2,1)S(1)} %get-tuple-element.769), channel_id=1, source_target_pairs={{0,8},{8,16},{16,24},{24,28},{28,20},{20,12},{12,4},{4,0},{1,9},{9... | collective-permute-start | bytes 1548296 | tf_op jit(solution)/shard_map/ppermute | solution.py:141
  264.3 12.2 %collective-permute-start.73 = (bf16[4,64,768]{2,1,0:T(8,128)(2,1)S(1)}, bf16[4,64,768]{2,1,0:T(8,128)(2,1)S(1)}, u32[]{:S(2)}, u32[]{:S(2)}) collective-permute-start(bf16[4,64,768]{2,1,0:T(8,128)(2,1)S(1)} %add_convert_fusion), channel_id=1, source_target_pairs={{0,2},{1,3},{2,0},{3,1},{4,6},{5,7},{6,4},{7,5},{8,10},{9,11},{10,... | collective-permute-start | bytes 1179656 | tf_op jit(solution)/shard_map/ppermute | solution.py:26
  (104 other events, 918.2 us)

commit v9 on v8

--- a/solution.py
+++ b/solution.py
@@ -13,7 +13,7 @@
 LANES = 128
 EPS = 1e-06
 VMEM_LIMIT = 24 * 1024 * 1024
-LARGE = 1 << 19
+LARGE = 1 << 20
 masked_score = -1000000000.0
 f32 = jnp.float32
 bf16 = jnp.bfloat16

time: 294 us -> 293 us (level)
  Pallas kernels: 92.9 us -> 85.7 us
  waiting for transfers between devices: 120 us -> 126 us
    pallas_call x34, Pallas kernels: 92.9 us -> 85.7 us  [call(): pl.pallas_call(split, grid=(steps,), in_specs=[pl.BlockSpec(memory_space=...]
    ppermute x21, waiting for transfers between devices: 47.7 us -> 51.5 us  [fetch_step(): lax.ppermute(pieces[k + 1 if k < 0 else k - 1], 'blk', forth if k < 0 els...]
  transfers between devices with their start and end apart: 83 -> 83, of which waited for: 43 -> 45; matrix products, arithmetic and copies ran while one was open for 2% -> 2% of each run, Pallas kernels for 26% -> 24%
where the time goes in v9:
time: 293 us; the launch traced here: 292 us
  waiting for transfers between devices  126 us (43%)
  Pallas kernels  85.7 us (29%)
  starting transfers between devices  62.2 us (21%)
  local copies, waits for them, and re-layouts  8.51 us (3%)
  blocking collectives  5.4 us (2%)
    pallas_call x34, Pallas kernels, call(): pl.pallas_call(split, grid=(steps,), in_specs=[pl.BlockSpec(memory_space=...  85.7 us
    ppermute x51, waiting for transfers between devices, swap(): return lax.ppermute(value, axis, [(i, i ^ bits) for i in range(size)])  61.5 us
    ppermute x21, waiting for transfers between devices, fetch_step(): lax.ppermute(pieces[k + 1 if k < 0 else k - 1], 'blk', forth if k < 0 els...  51.5 us
    ppermute x51, starting transfers between devices, swap(): return lax.ppermute(value, axis, [(i, i ^ bits) for i in range(size)])  28.5 us
    ppermute x21, starting transfers between devices, fetch_step(): lax.ppermute(pieces[k + 1 if k < 0 else k - 1], 'blk', forth if k < 0 els...  21.8 us
    ppermute x11, waiting for transfers between devices, reduce_step(): lax.ppermute(v, 'blk', way)  13.2 us
    ppermute x11, starting transfers between devices, reduce_step(): lax.ppermute(v, 'blk', way)  11.9 us
  transfers between devices with their start and end apart: 83, of which 45 were waited for; matrix products, arithmetic and copies ran while one was open for 2% of the time, Pallas kernels for 24%

profile of v9, /device:TPU:0, one launch (start us, length us, event | category | flops | bytes accessed | tf_op | source)
XLA Modules:
  0.0 292.2 jit_solution(6860041086532271113)
XLA Ops:
  21.9 5.4 %all_gather.3 = bf16[2,40,768]{2,0,1:T(2,128)(2,1)S(1)} all-gather(bf16[2,10,768]{2,0,1:T(2,128)(2,1)S(1)} %copy.68), channel_id=1, replica_groups=mesh['blk'=8,'head'=4] {'head'}, dimensions={1}, use_global_device_ids=true | all-gather | bytes 153600 | tf_op jit(solution)/shard_map/all_gather | solution.py:1199
  29.6 4.6 %collective-permute-done.8.refs_11_.refs_7_ = bf16[96,768]{1,0:T(8,128)(2,1)S(1)} collective-permute-done((bf16[96,768]{1,0:T(8,128)(2,1)S(1)}, bf16[96,768]{1,0:T(8,128)(2,1)S(1)}, u32[]{:S(2)}, u32[]{:S(2)}) %collective-permute-start.8) | collective-permute-done | bytes 147488 | tf_op jit(solution)/shard_map/ppermute | solution.py:74
  34.1 8.9 %collective-permute-done.9.refs_6_.refs_2_ = bf16[96,3072]{1,0:T(8,128)(2,1)S(1)} collective-permute-done((bf16[96,3072]{1,0:T(8,128)(2,1)S(1)}, bf16[96,3072]{1,0:T(8,128)(2,1)S(1)}, u32[]{:S(2)}, u32[]{:S(2)}) %collective-permute-start.9) | collective-permute-done | bytes 589856 | tf_op jit(solution)/shard_map/ppermute | solution.py:74
  45.0 6.6 %shard_map.427 = (bf16[4,256,576]{2,1,0:T(8,128)(2,1)}, bf16[4,3,256,256]{3,2,1,0:T(8,128)(2,1)}, bf16[4,256,192]{2,1,0:T(8,128)(2,1)S(1)}, f32[4,64,768]{2,1,0:...) custom-call(s32[14]{0:T(128)S(1)} %pad_add_fusion.info_ref, ...), custom_call_target="tpu_custom_call" | custom-call | flops 2013265920 | bytes 8257536 | tf_op jit(solution)/shard_map/pallas_call | solution.py:308
  51.7 6.1 %collective-permute-done.11.refs_5_.refs_1_ = bf16[96,3072]{1,0:T(8,128)(2,1)S(1)} collective-permute-done((bf16[96,3072]{1,0:T(8,128)(2,1)S(1)}, bf16[96,3072]{1,0:T(8,128)(2,1)S(1)}, u32[]{:S(2)}, u32[]{:S(2)}) %collective-permute-start.11) | collective-permute-done | bytes 589856 | tf_op jit(solution)/shard_map/ppermute | solution.py:74
  61.8 13.0 %collective-permute-done.16.refs_7_.refs_3_ = bf16[96,3072]{1,0:T(8,128)(2,1)S(1)} collective-permute-done((bf16[96,3072]{1,0:T(8,128)(2,1)S(1)}, bf16[96,3072]{1,0:T(8,128)(2,1)S(1)}, u32[]{:S(2)}, u32[]{:S(2)}) %collective-permute-start.16) | collective-permute-done | bytes 589856 | tf_op jit(solution)/shard_map/ppermute | solution.py:74
  81.1 9.8 %collective-permute-done.19.refs_2_ = bf16[4,64,768]{2,1,0:T(8,128)(2,1)S(1)} collective-permute-done((bf16[4,64,768]{2,1,0:T(8,128)(2,1)S(1)}, bf16[4,64,768]{2,1,0:T(8,128)(2,1)S(1)}, u32[]{:S(2)}, u32[]{:S(2)}) %collective-permute-start.19) | collective-permute-done | bytes 393248 | tf_op jit(solution)/shard_map/ppermute | solution.py:26
  93.6 6.0 %shard_map.429 = (bf16[4,256,768]{2,1,0:T(8,128)(2,1)}, bf16[4,256,768]{2,1,0:T(8,128)(2,1)}, f32[4,64,768]{2,1,0:T(8,128)S(1)}, bf16[4,64,768]{2,1,0:T(8,128)(2...) custom-call(s32[14]{0:T(128)S(1)} %pad_add_fusion.info_ref, ...), custom_call_target="tpu_custom_call" | custom-call | flops 2415919104 | bytes 11796480 | tf_op jit(solution)/shard_map/pallas_call | solution.py:308
  108.7 4.5 %collective-permute-done.28.refs_4_ = bf16[96,1536]{1,0:T(8,128)(2,1)S(1)} collective-permute-done((bf16[96,1536]{1,0:T(8,128)(2,1)S(1)}, bf16[96,1536]{1,0:T(8,128)(2,1)S(1)}, u32[]{:S(2)}, u32[]{:S(2)}) %collective-permute-start.28) | collective-permute-done | bytes 294944 | tf_op jit(solution)/shard_map/ppermute | solution.py:74
  119.8 5.2 %collective-permute-done.32.refs_6_ = bf16[96,1536]{1,0:T(8,128)(2,1)S(1)} collective-permute-done((bf16[96,1536]{1,0:T(8,128)(2,1)S(1)}, bf16[96,1536]{1,0:T(8,128)(2,1)S(1)}, u32[]{:S(2)}, u32[]{:S(2)}) %collective-permute-start.32) | collective-permute-done | bytes 294944 | tf_op jit(solution)/shard_map/ppermute | solution.py:74
  125.2 3.8 %collective-permute-done.31.refs_2_.refs_9_ = bf16[5,64,768]{2,1,0:T(8,128)(2,1)S(1)} collective-permute-done((bf16[5,64,768]{2,1,0:T(8,128)(2,1)S(1)}, bf16[5,64,768]{2,1,0:T(8,128)(2,1)S(1)}, u32[]{:S(2)}, u32[]{:S(2)}) %collective-permute-start.31) | collective-permute-done | bytes 491552 | tf_op jit(solution)/shard_map/ppermute | solution.py:26
  130.8 3.4 %shard_map.433 = (bf16[4,256,384]{2,1,0:T(8,128)(2,1)S(1)}, f32[48,768]{1,0:T(8,128)}, bf16[48,768]{1,0:T(8,128)(2,1)}, bf16[48,192]{1,0:T(8,128)(2,1)S(1)}, f32[48,384]{1,0:T(8,128)S(1)}) custom-call(s32[14]{0:T(128)S(1)} %pad_add_fusion.info_ref, bf16[5,64,768]{2,1,0:T(8,128)(2,1)S(1)} %shard_map.431.refs_0_, ...), custom_call_target="tpu_custom_call" | custom-call | flops 603979776 | bytes 4476096 | tf_op jit(solution)/shard_map/pallas_call | solution.py:308
  135.6 4.3 %collective-permute-done.35.refs_1_ = f32[48,384]{1,0:T(8,128)S(1)} collective-permute-done((f32[48,384]{1,0:T(8,128)S(1)}, f32[48,384]{1,0:T(8,128)S(1)}, u32[]{:S(2)}, u32[]{:S(2)}) %collective-permute-start.35) | collective-permute-done | bytes 73760 | tf_op jit(solution)/shard_map/ppermute | solution.py:26
  141.2 4.1 %collective-permute-start.39 = (f32[48,384]{1,0:T(8,128)S(1)}, f32[48,384]{1,0:T(8,128)S(1)}, u32[]{:S(2)}, u32[]{:S(2)}) collective-permute-start(f32[48,384]{1,0:T(8,128)S(1)} %shard_map.434.refs_0_), channel_id=1, source_target_pairs={{0,24},{4,28},{8,16},{12,20},{16,8},{20,12},{24,0},{28,4},{1,25},{... | collective-permute-start | bytes 221192 | tf_op jit(solution)/shard_map/ppermute | solution.py:26
  161.3 3.4 %collective-permute-done.44.refs_5_ = bf16[48,768]{1,0:T(8,128)(2,1)S(1)} collective-permute-done((bf16[48,768]{1,0:T(8,128)(2,1)S(1)}, bf16[48,768]{1,0:T(8,128)(2,1)S(1)}, u32[]{:S(2)}, u32[]{:S(2)}) %collective-permute-start.44) | collective-permute-done | bytes 73760 | tf_op jit(solution)/shard_map/ppermute | solution.py:26
  185.8 3.6 %collective-permute-done.53.refs_1_ = f32[48,192]{1,0:T(8,128)S(1)} collective-permute-done((f32[48,192]{1,0:T(8,128)S(1)}, f32[48,192]{1,0:T(8,128)S(1)}, u32[]{:S(2)}, u32[]{:S(2)}) %collective-permute-start.53) | collective-permute-done | bytes 36896 | tf_op jit(solution)/shard_map/ppermute | solution.py:26
  190.6 5.5 %collective-permute-done.52.refs_2_.refs_7_.refs_10_ = bf16[5,64,768]{2,1,0:T(8,128)(2,1)S(1)} collective-permute-done((bf16[5,64,768]{2,1,0:T(8,128)(2,1)S(1)}, bf16[5,64,768]{2,1,0:T(8,128)(2,1)S(1)}, u32[]{:S(2)}, u32[]{:S(2)}) %collective-permute-start.52) | collective-permute-done | bytes 491552 | tf_op jit(solution)/shard_map/ppermute | solution.py:26
  198.0 4.8 %shard_map.444 = (bf16[4,256,768]{2,1,0:T(8,128)(2,1)}, f32[4,64,768]{2,1,0:T(8,128)S(1)}, bf16[4,64,768]{2,1,0:T(8,128)(2,1)S(1)}, f32[4,64,768]{2,1,0:T(8,128)S(1)}, bf16[4,64,768]{2,1,0:T(8,128)(2,1)S(1)}) custom-call(s32[14]{0:T(128)S(1)} %pad_add_fusion.info_ref, bf16[5,64,768]{2,1,0:T(8,128)(2,1)S(1)} %get-tuple-element.665.refs_0_.refs_5_, ...), custom_call_target="tpu_custom_call" | custom-call | flops 2415919104 | bytes 9830400 | tf_op jit(solution)/shard_map/pallas_call | solution.py:308
  209.5 6.7 %shard_map.446 = (f32[96,1920]{1,0:T(8,128)}, bf16[96,1920]{1,0:T(8,128)(2,1)}, bf16[96,1920]{1,0:T(8,128)(2,1)}, bf16[96,1920]{1,0:T(8,128)(2,1)}, bf16[96,1920...) custom-call(s32[14]{0:T(128)S(1)} %pad_add_fusion.info_ref, ...), custom_call_target="tpu_custom_call" | custom-call | flops 2415919104 | bytes 11182080 | tf_op jit(solution)/shard_map/pallas_call | solution.py:308
  224.0 5.8 %collective-permute-done.63.refs_0_ = bf16[96,1920]{1,0:T(8,128)(2,1)S(1)} collective-permute-done((bf16[96,1920]{1,0:T(8,128)(2,1)S(1)}, bf16[96,1920]{1,0:T(8,128)(2,1)S(1)}, u32[]{:S(2)}, u32[]{:S(2)}) %collective-permute-start.63) | collective-permute-done | bytes 368672 | tf_op jit(solution)/shard_map/ppermute | solution.py:141
  235.5 10.0 %shard_map.449 = (f32[4,64,768]{2,1,0:T(8,128)S(1)}, bf16[4,64,768]{2,1,0:T(8,128)(2,1)S(1)}, f32[4,64,768]{2,1,0:T(8,128)S(1)}, bf16[4,64,768]{2,1,0:T(8,128)(2...) custom-call(s32[14]{0:T(128)S(1)} %pad_add_fusion.info_ref, ...), custom_call_target="tpu_custom_call" | custom-call | flops 4429185024 | bytes 11559936 | tf_op jit(solution)/shard_map/pallas_call | solution.py:308
  252.7 3.4 %shard_map.453 = (f32[96,192]{1,0:T(8,128)}, f32[96,192]{1,0:T(8,128)}, f32[96,192]{1,0:T(8,128)}, f32[96,192]{1,0:T(8,128)}, f32[96,768]{1,0:T(8,128)}, /*index...) custom-call(s32[14]{0:T(128)S(1)} %pad_add_fusion.info_ref, bf16[48,768]{1,0:T(8,128)(2,1)} %get-tuple-element.748.refs_0_, ...), custom_call_target="tpu_custom_call" | custom-call | flops 70778880 | bytes 1732608 | tf_op jit(solution)/shard_map/pallas_call | solution.py:308
  256.1 4.3 %collective-permute-done.69.refs_0_.refs_2_ = bf16[96,2688]{1,0:T(8,128)(2,1)S(1)} collective-permute-done((bf16[96,2688]{1,0:T(8,128)(2,1)S(1)}, bf16[96,2688]{1,0:T(8,128)(2,1)S(1)}, u32[]{:S(2)}, u32[]{:S(2)}) %collective-permute-start.69) | collective-permute-done | bytes 516128 | tf_op jit(solution)/shard_map/ppermute | solution.py:141
  266.5 9.1 %collective-permute-done.77 = f32[5,768]{1,0:T(8,128)S(1)} collective-permute-done((f32[5,768]{1,0:T(8,128)S(1)}, f32[5,768]{1,0:T(8,128)S(1)}, u32[]{:S(2)}, u32[]{:S(2)}) %collective-permute-start.77) | collective-permute-done | bytes 15392 | tf_op jit(solution)/shard_map/ppermute | solution.py:26
  (289 shorter events, 148.3 us)
Async XLA Ops:
  11.0 16.3 %collective-permute-start.6 = (bf16[4,64,768]{2,1,0:T(8,128)(2,1)S(1)}, bf16[4,64,768]{2,1,0:T(8,128)(2,1)S(1)}, u32[]{:S(2)}, u32[]{:S(2)}) collective-permute-start(bf16[4,64,768]{2,1,0:T(8,128)(2,1)S(1)} %shard_map.426.refs_0_.refs_4_), channel_id=1, source_target_pairs={{0,1},{1,0},{2,3},{3,2},{4,5},{5,4},{6,7},{7,6},{8,9},{9,8},{10,11... | collective-permute-start | bytes 1179656 | tf_op jit(solution)/shard_map/ppermute | solution.py:26
  11.1 16.3 %collective-permute-start.7 = (bf16[4,64,768]{2,1,0:T(8,128)(2,1)S(1)}, bf16[4,64,768]{2,1,0:T(8,128)(2,1)S(1)}, u32[]{:S(2)}, u32[]{:S(2)}) collective-permute-start(bf16[4,64,768]{2,1,0:T(8,128)(2,1)S(1)} %shard_map.426.refs_0_.refs_4_), channel_id=1, source_target_pairs={{0,2},{1,3},{2,0},{3,1},{4,6},{5,7},{6,4},{7,5},{8,10},{9,11},{10,... | collective-permute-start | bytes 1179656 | tf_op jit(solution)/shard_map/ppermute | solution.py:26
  27.4 15.6 %collective-permute-start.9 = (bf16[96,3072]{1,0:T(8,128)(2,1)S(1)}, bf16[96,3072]{1,0:T(8,128)(2,1)S(1)}, u32[]{:S(2)}, u32[]{:S(2)}) collective-permute-start(bf16[96,3072]{1,0:T(8,128)(2,1)S(1)} %concatenate.15.refs_4_.refs_0_), channel_id=1, source_target_pairs={{8,0},{16,8},{24,16},{28,24},{20,28},{12,20},{4,12},{0,4},{9,1},{1... | collective-permute-start | bytes 1769480 | tf_op jit(solution)/shard_map/ppermute | solution.py:74
  43.0 14.8 %collective-permute-start.11 = (bf16[96,3072]{1,0:T(8,128)(2,1)S(1)}, bf16[96,3072]{1,0:T(8,128)(2,1)S(1)}, u32[]{:S(2)}, u32[]{:S(2)}) collective-permute-start(bf16[96,3072]{1,0:T(8,128)(2,1)S(1)} %concatenate.15.refs_4_.refs_0_), channel_id=1, source_target_pairs={{0,8},{8,16},{16,24},{24,28},{28,20},{20,12},{12,4},{4,0},{1,9},{9... | collective-permute-start | bytes 1769480 | tf_op jit(solution)/shard_map/ppermute | solution.py:74
  44.6 14.5 %collective-permute-start.12 = (bf16[96,3072]{1,0:T(8,128)(2,1)S(1)}, bf16[96,3072]{1,0:T(8,128)(2,1)S(1)}, u32[]{:S(2)}, u32[]{:S(2)}) collective-permute-start(bf16[96,3072]{1,0:T(8,128)(2,1)S(1)} %collective-permute-done.9.refs_6_.refs_2_), channel_id=1, source_target_pairs={{8,0},{16,8},{24,16},{28,24},{20,28},{12,20},{4,12},{0,4},{9,1},{1... | collective-permute-start | bytes 1769480 | tf_op jit(solution)/shard_map/ppermute | solution.py:74
  59.1 15.7 %collective-permute-start.16 = (bf16[96,3072]{1,0:T(8,128)(2,1)S(1)}, bf16[96,3072]{1,0:T(8,128)(2,1)S(1)}, u32[]{:S(2)}, u32[]{:S(2)}) collective-permute-start(bf16[96,3072]{1,0:T(8,128)(2,1)S(1)} %collective-permute-done.11.refs_5_.refs_1_), channel_id=1, source_target_pairs={{0,8},{8,16},{16,24},{24,28},{28,20},{20,12},{12,4},{4,0},{1,9},{9... | collective-permute-start | bytes 1769480 | tf_op jit(solution)/shard_map/ppermute | solution.py:74
  60.6 15.5 %collective-permute-start.17 = (bf16[96,3072]{1,0:T(8,128)(2,1)S(1)}, bf16[96,3072]{1,0:T(8,128)(2,1)S(1)}, u32[]{:S(2)}, u32[]{:S(2)}) collective-permute-start(bf16[96,3072]{1,0:T(8,128)(2,1)S(1)} %collective-permute-done.12.refs_8_.refs_4_), channel_id=1, source_target_pairs={{8,0},{16,8},{24,16},{28,24},{20,28},{12,20},{4,12},{0,4},{9,1},{1... | collective-permute-start | bytes 1769480 | tf_op jit(solution)/shard_map/ppermute | solution.py:74
  61.2 14.9 %collective-permute-start.14 = (bf16[4,64,768]{2,1,0:T(8,128)(2,1)S(1)}, bf16[4,64,768]{2,1,0:T(8,128)(2,1)S(1)}, u32[]{:S(2)}, u32[]{:S(2)}) collective-permute-start(bf16[4,64,768]{2,1,0:T(8,128)(2,1)S(1)} %add_convert_fusion.4), channel_id=1, source_target_pairs={{0,2},{1,3},{2,0},{3,1},{4,6},{5,7},{6,4},{7,5},{8,10},{9,11},{10,... | collective-permute-start | bytes 1179656 | tf_op jit(solution)/shard_map/ppermute | solution.py:26
  61.8 14.3 %collective-permute-start.15 = (bf16[4,64,768]{2,1,0:T(8,128)(2,1)S(1)}, bf16[4,64,768]{2,1,0:T(8,128)(2,1)S(1)}, u32[]{:S(2)}, u32[]{:S(2)}) collective-permute-start(bf16[4,64,768]{2,1,0:T(8,128)(2,1)S(1)} %get-tuple-element.465), channel_id=1, source_target_pairs={{0,1},{1,0},{2,3},{3,2},{4,5},{5,4},{6,7},{7,6},{8,9},{9,8},{10,11... | collective-permute-start | bytes 1179656 | tf_op jit(solution)/shard_map/ppermute | solution.py:26
  76.1 14.8 %collective-permute-start.20 = (bf16[96,3072]{1,0:T(8,128)(2,1)S(1)}, bf16[96,3072]{1,0:T(8,128)(2,1)S(1)}, u32[]{:S(2)}, u32[]{:S(2)}) collective-permute-start(bf16[96,3072]{1,0:T(8,128)(2,1)S(1)} %collective-permute-done.16.refs_7_.refs_3_), channel_id=1, source_target_pairs={{0,8},{8,16},{16,24},{24,28},{28,20},{20,12},{12,4},{4,0},{1,9},{9... | collective-permute-start | bytes 1769480 | tf_op jit(solution)/shard_map/ppermute | solution.py:74
  77.2 14.4 %collective-permute-start.21 = (bf16[96,3072]{1,0:T(8,128)(2,1)S(1)}, bf16[96,3072]{1,0:T(8,128)(2,1)S(1)}, u32[]{:S(2)}, u32[]{:S(2)}) collective-permute-start(bf16[96,3072]{1,0:T(8,128)(2,1)S(1)} %collective-permute-done.17.refs_10_.refs_6_), channel_id=1, source_target_pairs={{8,0},{16,8},{24,16},{28,24},{20,28},{12,20},{4,12},{0,4},{9,1},{1... | collective-permute-start | bytes 1769480 | tf_op jit(solution)/shard_map/ppermute | solution.py:74
  79.4 11.5 %collective-permute-start.19 = (bf16[4,64,768]{2,1,0:T(8,128)(2,1)S(1)}, bf16[4,64,768]{2,1,0:T(8,128)(2,1)S(1)}, u32[]{:S(2)}, u32[]{:S(2)}) collective-permute-start(bf16[4,64,768]{2,1,0:T(8,128)(2,1)S(1)} %get-tuple-element.497.refs_0_), channel_id=1, source_target_pairs={{0,2},{1,3},{2,0},{3,1},{4,6},{5,7},{6,4},{7,5},{8,10},{9,11},{10,... | collective-permute-start | bytes 1179656 | tf_op jit(solution)/shard_map/ppermute | solution.py:26
  115.3 13.6 %collective-permute-start.31 = (bf16[5,64,768]{2,1,0:T(8,128)(2,1)S(1)}, bf16[5,64,768]{2,1,0:T(8,128)(2,1)S(1)}, u32[]{:S(2)}, u32[]{:S(2)}) collective-permute-start(bf16[5,64,768]{2,1,0:T(8,128)(2,1)S(1)} %shard_map.431.refs_0_), channel_id=1, source_target_pairs={{0,2},{1,3},{2,0},{3,1},{4,6},{5,7},{6,4},{7,5},{8,10},{9,11},{10,... | collective-permute-start | bytes 1474568 | tf_op jit(solution)/shard_map/ppermute | solution.py:26
  129.0 11.8 %collective-permute-start.36 = (bf16[96,1536]{1,0:T(8,128)(2,1)S(1)}, bf16[96,1536]{1,0:T(8,128)(2,1)S(1)}, u32[]{:S(2)}, u32[]{:S(2)}) collective-permute-start(bf16[96,1536]{1,0:T(8,128)(2,1)S(1)} %collective-permute-done.32.refs_6_), channel_id=1, source_target_pairs={{0,8},{8,16},{16,24},{24,28},{28,20},{20,12},{12,4},{4,0},{1,9},{9... | collective-permute-start | bytes 884744 | tf_op jit(solution)/shard_map/ppermute | solution.py:74
  170.1 11.5 %collective-permute-start.47 = (bf16[4,64,768]{2,1,0:T(8,128)(2,1)S(1)}, bf16[4,64,768]{2,1,0:T(8,128)(2,1)S(1)}, u32[]{:S(2)}, u32[]{:S(2)}) collective-permute-start(bf16[4,64,768]{2,1,0:T(8,128)(2,1)S(1)} %add_convert_fusion.2), channel_id=1, source_target_pairs={{0,2},{1,3},{2,0},{3,1},{4,6},{5,7},{6,4},{7,5},{8,10},{9,11},{10,... | collective-permute-start | bytes 1179656 | tf_op jit(solution)/shard_map/ppermute | solution.py:26
  182.5 13.6 %collective-permute-start.52 = (bf16[5,64,768]{2,1,0:T(8,128)(2,1)S(1)}, bf16[5,64,768]{2,1,0:T(8,128)(2,1)S(1)}, u32[]{:S(2)}, u32[]{:S(2)}) collective-permute-start(bf16[5,64,768]{2,1,0:T(8,128)(2,1)S(1)} %get-tuple-element.665.refs_0_.refs_5_), channel_id=1, source_target_pairs={{0,2},{1,3},{2,0},{3,1},{4,6},{5,7},{6,4},{7,5},{8,10},{9,11},{10,... | collective-permute-start | bytes 1474568 | tf_op jit(solution)/shard_map/ppermute | solution.py:26
  205.1 11.5 %collective-permute-start.59 = (bf16[4,64,768]{2,1,0:T(8,128)(2,1)S(1)}, bf16[4,64,768]{2,1,0:T(8,128)(2,1)S(1)}, u32[]{:S(2)}, u32[]{:S(2)}) collective-permute-start(bf16[4,64,768]{2,1,0:T(8,128)(2,1)S(1)} %add_convert_fusion.1), channel_id=1, source_target_pairs={{0,2},{1,3},{2,0},{3,1},{4,6},{5,7},{6,4},{7,5},{8,10},{9,11},{10,... | collective-permute-start | bytes 1179656 | tf_op jit(solution)/shard_map/ppermute | solution.py:26
  218.2 12.7 %collective-permute-start.61 = (bf16[5,64,768]{2,1,0:T(8,128)(2,1)S(1)}, bf16[5,64,768]{2,1,0:T(8,128)(2,1)S(1)}, u32[]{:S(2)}, u32[]{:S(2)}) collective-permute-start(bf16[5,64,768]{2,1,0:T(8,128)(2,1)S(1)} %get-tuple-element.707.refs_0_), channel_id=1, source_target_pairs={{0,1},{1,0},{2,3},{3,2},{4,5},{5,4},{6,7},{7,6},{8,9},{9,8},{10,11... | collective-permute-start | bytes 1474568 | tf_op jit(solution)/shard_map/ppermute | solution.py:26
  218.3 13.6 %collective-permute-start.62 = (bf16[5,64,768]{2,1,0:T(8,128)(2,1)S(1)}, bf16[5,64,768]{2,1,0:T(8,128)(2,1)S(1)}, u32[]{:S(2)}, u32[]{:S(2)}) collective-permute-start(bf16[5,64,768]{2,1,0:T(8,128)(2,1)S(1)} %get-tuple-element.707.refs_0_), channel_id=1, source_target_pairs={{0,2},{1,3},{2,0},{3,1},{4,6},{5,7},{6,4},{7,5},{8,10},{9,11},{10,... | collective-permute-start | bytes 1474568 | tf_op jit(solution)/shard_map/ppermute | solution.py:26
  233.4 12.1 %collective-permute-start.66 = (bf16[96,1920]{1,0:T(8,128)(2,1)S(1)}, bf16[96,1920]{1,0:T(8,128)(2,1)S(1)}, u32[]{:S(2)}, u32[]{:S(2)}) collective-permute-start(bf16[96,1920]{1,0:T(8,128)(2,1)S(1)} %get-tuple-element.729), channel_id=1, source_target_pairs={{0,8},{8,16},{16,24},{24,28},{28,20},{20,12},{12,4},{4,0},{1,9},{9... | collective-permute-start | bytes 1105928 | tf_op jit(solution)/shard_map/ppermute | solution.py:141
  247.0 13.5 %collective-permute-start.69 = (bf16[96,2688]{1,0:T(8,128)(2,1)S(1)}, bf16[96,2688]{1,0:T(8,128)(2,1)S(1)}, u32[]{:S(2)}, u32[]{:S(2)}) collective-permute-start(bf16[96,2688]{1,0:T(8,128)(2,1)S(1)} %get-tuple-element.745), channel_id=1, source_target_pairs={{0,8},{8,16},{16,24},{24,28},{28,20},{20,12},{12,4},{4,0},{1,9},{9... | collective-permute-start | bytes 1548296 | tf_op jit(solution)/shard_map/ppermute | solution.py:141
  248.4 13.1 %collective-permute-start.70 = (bf16[96,2688]{1,0:T(8,128)(2,1)S(1)}, bf16[96,2688]{1,0:T(8,128)(2,1)S(1)}, u32[]{:S(2)}, u32[]{:S(2)}) collective-permute-start(bf16[96,2688]{1,0:T(8,128)(2,1)S(1)} %get-tuple-element.746), channel_id=1, source_target_pairs={{8,0},{16,8},{24,16},{28,24},{20,28},{12,20},{4,12},{0,4},{9,1},{1... | collective-permute-start | bytes 1548296 | tf_op jit(solution)/shard_map/ppermute | solution.py:141
  262.8 12.8 %collective-permute-start.75 = (bf16[96,2688]{1,0:T(8,128)(2,1)S(1)}, bf16[96,2688]{1,0:T(8,128)(2,1)S(1)}, u32[]{:S(2)}, u32[]{:S(2)}) collective-permute-start(bf16[96,2688]{1,0:T(8,128)(2,1)S(1)} %get-tuple-element.769), channel_id=1, source_target_pairs={{0,8},{8,16},{16,24},{24,28},{28,20},{20,12},{12,4},{4,0},{1,9},{9... | collective-permute-start | bytes 1548296 | tf_op jit(solution)/shard_map/ppermute | solution.py:141
  263.4 12.2 %collective-permute-start.73 = (bf16[4,64,768]{2,1,0:T(8,128)(2,1)S(1)}, bf16[4,64,768]{2,1,0:T(8,128)(2,1)S(1)}, u32[]{:S(2)}, u32[]{:S(2)}) collective-permute-start(bf16[4,64,768]{2,1,0:T(8,128)(2,1)S(1)} %add_convert_fusion), channel_id=1, source_target_pairs={{0,2},{1,3},{2,0},{3,1},{4,6},{5,7},{6,4},{7,5},{8,10},{9,11},{10,... | collective-permute-start | bytes 1179656 | tf_op jit(solution)/shard_map/ppermute | solution.py:26
  (97 other events, 800.2 us)

commit v10 on v9

--- a/solution.py
+++ b/solution.py
@@ -13,7 +13,7 @@
 LANES = 128
 EPS = 1e-06
 VMEM_LIMIT = 24 * 1024 * 1024
-LARGE = 1 << 20
+LARGE = 1 << 21
 masked_score = -1000000000.0
 f32 = jnp.float32
 bf16 = jnp.bfloat16

time: 293 us -> 291 us (level)
  Pallas kernels: 85.7 us -> 77.9 us
  waiting for transfers between devices: 126 us -> 132 us
    pallas_call x34, Pallas kernels: 85.7 us -> 77.9 us  [call(): pl.pallas_call(split, grid=(steps,), in_specs=[pl.BlockSpec(memory_space=...]
    ppermute x51, waiting for transfers between devices: 61.5 us -> 66.1 us  [swap(): return lax.ppermute(value, axis, [(i, i ^ bits) for i in range(size)])]
    unnamed x83 -> x85, local copies, waits for them, and re-layouts: 5.85 us -> 5.87 us
  transfers between devices with their start and end apart: 83 -> 83, of which waited for: 45 -> 47; matrix products, arithmetic and copies ran while one was open for 2% -> 2% of each run, Pallas kernels for 24% -> 21%
where the time goes in v10:
time: 291 us; the launch traced here: 290 us
  waiting for transfers between devices  132 us (45%)
  Pallas kernels  77.9 us (27%)
  starting transfers between devices  61.9 us (21%)
  local copies, waits for them, and re-layouts  8.53 us (3%)
  blocking collectives  5.4 us (2%)
    pallas_call x34, Pallas kernels, call(): pl.pallas_call(split, grid=(steps,), in_specs=[pl.BlockSpec(memory_space=...  77.9 us
    ppermute x51, waiting for transfers between devices, swap(): return lax.ppermute(value, axis, [(i, i ^ bits) for i in range(size)])  66.1 us
    ppermute x21, waiting for transfers between devices, fetch_step(): lax.ppermute(pieces[k + 1 if k < 0 else k - 1], 'blk', forth if k < 0 els...  52.6 us
    ppermute x51, starting transfers between devices, swap(): return lax.ppermute(value, axis, [(i, i ^ bits) for i in range(size)])  28.1 us
    ppermute x21, starting transfers between devices, fetch_step(): lax.ppermute(pieces[k + 1 if k < 0 else k - 1], 'blk', forth if k < 0 els...  21.8 us
    ppermute x11, waiting for transfers between devices, reduce_step(): lax.ppermute(v, 'blk', way)  13.4 us
    ppermute x11, starting transfers between devices, reduce_step(): lax.ppermute(v, 'blk', way)  12 us
    unnamed x85, local copies, waits for them, and re-layouts  5.87 us
  transfers between devices with their start and end apart: 83, of which 47 were waited for; matrix products, arithmetic and copies ran while one was open for 2% of the time, Pallas kernels for 21%

profile of v10, /device:TPU:0, one launch (start us, length us, event | category | flops | bytes accessed | tf_op | source)
XLA Modules:
  0.0 290.2 jit_solution(454515584534693442)
XLA Ops:
  21.9 5.4 %all_gather.3 = bf16[2,40,768]{2,0,1:T(2,128)(2,1)S(1)} all-gather(bf16[2,10,768]{2,0,1:T(2,128)(2,1)S(1)} %copy.68), channel_id=1, replica_groups=mesh['blk'=8,'head'=4] {'head'}, dimensions={1}, use_global_device_ids=true | all-gather | bytes 153600 | tf_op jit(solution)/shard_map/all_gather | solution.py:1199
  29.6 4.6 %collective-permute-done.8.refs_11_.refs_7_ = bf16[96,768]{1,0:T(8,128)(2,1)S(1)} collective-permute-done((bf16[96,768]{1,0:T(8,128)(2,1)S(1)}, bf16[96,768]{1,0:T(8,128)(2,1)S(1)}, u32[]{:S(2)}, u32[]{:S(2)}) %collective-permute-start.8) | collective-permute-done | bytes 147488 | tf_op jit(solution)/shard_map/ppermute | solution.py:74
  34.1 8.9 %collective-permute-done.9.refs_6_.refs_2_ = bf16[96,3072]{1,0:T(8,128)(2,1)S(1)} collective-permute-done((bf16[96,3072]{1,0:T(8,128)(2,1)S(1)}, bf16[96,3072]{1,0:T(8,128)(2,1)S(1)}, u32[]{:S(2)}, u32[]{:S(2)}) %collective-permute-start.9) | collective-permute-done | bytes 589856 | tf_op jit(solution)/shard_map/ppermute | solution.py:74
  45.0 6.2 %shard_map.427 = (bf16[4,256,576]{2,1,0:T(8,128)(2,1)S(1)}, bf16[4,3,256,256]{3,2,1,0:T(8,128)(2,1)S(1)}, bf16[4,256,192]{2,1,0:T(8,128)(2,1)S(1)}, f32[4,64,768...) custom-call(s32[14]{0:T(128)S(1)} %pad_add_fusion.info_ref, ...), custom_call_target="tpu_custom_call" | custom-call | flops 2013265920 | bytes 8257536 | tf_op jit(solution)/shard_map/pallas_call | solution.py:308
  51.2 6.5 %collective-permute-done.11.refs_5_.refs_1_ = bf16[96,3072]{1,0:T(8,128)(2,1)S(1)} collective-permute-done((bf16[96,3072]{1,0:T(8,128)(2,1)S(1)}, bf16[96,3072]{1,0:T(8,128)(2,1)S(1)}, u32[]{:S(2)}, u32[]{:S(2)}) %collective-permute-start.11) | collective-permute-done | bytes 589856 | tf_op jit(solution)/shard_map/ppermute | solution.py:74
  61.8 13.0 %collective-permute-done.16.refs_7_.refs_3_ = bf16[96,3072]{1,0:T(8,128)(2,1)S(1)} collective-permute-done((bf16[96,3072]{1,0:T(8,128)(2,1)S(1)}, bf16[96,3072]{1,0:T(8,128)(2,1)S(1)}, u32[]{:S(2)}, u32[]{:S(2)}) %collective-permute-start.16) | collective-permute-done | bytes 589856 | tf_op jit(solution)/shard_map/ppermute | solution.py:74
  81.1 9.8 %collective-permute-done.19.refs_2_ = bf16[4,64,768]{2,1,0:T(8,128)(2,1)S(1)} collective-permute-done((bf16[4,64,768]{2,1,0:T(8,128)(2,1)S(1)}, bf16[4,64,768]{2,1,0:T(8,128)(2,1)S(1)}, u32[]{:S(2)}, u32[]{:S(2)}) %collective-permute-start.19) | collective-permute-done | bytes 393248 | tf_op jit(solution)/shard_map/ppermute | solution.py:26
  93.6 5.3 %shard_map.429 = (bf16[4,256,768]{2,1,0:T(8,128)(2,1)S(1)}, bf16[4,256,768]{2,1,0:T(8,128)(2,1)S(1)}, f32[4,64,768]{2,1,0:T(8,128)S(1)}, bf16[4,64,768]{2,1,0:T(...) custom-call(s32[14]{0:T(128)S(1)} %pad_add_fusion.info_ref, ...), custom_call_target="tpu_custom_call" | custom-call | flops 2415919104 | bytes 11796480 | tf_op jit(solution)/shard_map/pallas_call | solution.py:308
  108.7 4.5 %collective-permute-done.28.refs_4_ = bf16[96,1536]{1,0:T(8,128)(2,1)S(1)} collective-permute-done((bf16[96,1536]{1,0:T(8,128)(2,1)S(1)}, bf16[96,1536]{1,0:T(8,128)(2,1)S(1)}, u32[]{:S(2)}, u32[]{:S(2)}) %collective-permute-start.28) | collective-permute-done | bytes 294944 | tf_op jit(solution)/shard_map/ppermute | solution.py:74
  119.8 5.2 %collective-permute-done.32.refs_6_ = bf16[96,1536]{1,0:T(8,128)(2,1)S(1)} collective-permute-done((bf16[96,1536]{1,0:T(8,128)(2,1)S(1)}, bf16[96,1536]{1,0:T(8,128)(2,1)S(1)}, u32[]{:S(2)}, u32[]{:S(2)}) %collective-permute-start.32) | collective-permute-done | bytes 294944 | tf_op jit(solution)/shard_map/ppermute | solution.py:74
  125.2 3.8 %collective-permute-done.31.refs_2_.refs_9_ = bf16[5,64,768]{2,1,0:T(8,128)(2,1)S(1)} collective-permute-done((bf16[5,64,768]{2,1,0:T(8,128)(2,1)S(1)}, bf16[5,64,768]{2,1,0:T(8,128)(2,1)S(1)}, u32[]{:S(2)}, u32[]{:S(2)}) %collective-permute-start.31) | collective-permute-done | bytes 491552 | tf_op jit(solution)/shard_map/ppermute | solution.py:26
  130.8 3.4 %shard_map.433 = (bf16[4,256,384]{2,1,0:T(8,128)(2,1)S(1)}, f32[48,768]{1,0:T(8,128)}, bf16[48,768]{1,0:T(8,128)(2,1)}, bf16[48,192]{1,0:T(8,128)(2,1)S(1)}, f32[48,384]{1,0:T(8,128)S(1)}) custom-call(s32[14]{0:T(128)S(1)} %pad_add_fusion.info_ref, bf16[5,64,768]{2,1,0:T(8,128)(2,1)S(1)} %shard_map.431.refs_0_, ...), custom_call_target="tpu_custom_call" | custom-call | flops 603979776 | bytes 4476096 | tf_op jit(solution)/shard_map/pallas_call | solution.py:308
  135.6 4.3 %collective-permute-done.35.refs_1_ = f32[48,384]{1,0:T(8,128)S(1)} collective-permute-done((f32[48,384]{1,0:T(8,128)S(1)}, f32[48,384]{1,0:T(8,128)S(1)}, u32[]{:S(2)}, u32[]{:S(2)}) %collective-permute-start.35) | collective-permute-done | bytes 73760 | tf_op jit(solution)/shard_map/ppermute | solution.py:26
  141.2 4.1 %collective-permute-start.39 = (f32[48,384]{1,0:T(8,128)S(1)}, f32[48,384]{1,0:T(8,128)S(1)}, u32[]{:S(2)}, u32[]{:S(2)}) collective-permute-start(f32[48,384]{1,0:T(8,128)S(1)} %shard_map.434.refs_0_), channel_id=1, source_target_pairs={{0,24},{4,28},{8,16},{12,20},{16,8},{20,12},{24,0},{28,4},{1,25},{... | collective-permute-start | bytes 221192 | tf_op jit(solution)/shard_map/ppermute | solution.py:26
  161.3 3.4 %collective-permute-done.44.refs_5_ = bf16[48,768]{1,0:T(8,128)(2,1)S(1)} collective-permute-done((bf16[48,768]{1,0:T(8,128)(2,1)S(1)}, bf16[48,768]{1,0:T(8,128)(2,1)S(1)}, u32[]{:S(2)}, u32[]{:S(2)}) %collective-permute-start.44) | collective-permute-done | bytes 73760 | tf_op jit(solution)/shard_map/ppermute | solution.py:26
  185.8 3.6 %collective-permute-done.53.refs_1_ = f32[48,192]{1,0:T(8,128)S(1)} collective-permute-done((f32[48,192]{1,0:T(8,128)S(1)}, f32[48,192]{1,0:T(8,128)S(1)}, u32[]{:S(2)}, u32[]{:S(2)}) %collective-permute-start.53) | collective-permute-done | bytes 36896 | tf_op jit(solution)/shard_map/ppermute | solution.py:26
  190.6 5.5 %collective-permute-done.52.refs_2_.refs_7_.refs_10_ = bf16[5,64,768]{2,1,0:T(8,128)(2,1)S(1)} collective-permute-done((bf16[5,64,768]{2,1,0:T(8,128)(2,1)S(1)}, bf16[5,64,768]{2,1,0:T(8,128)(2,1)S(1)}, u32[]{:S(2)}, u32[]{:S(2)}) %collective-permute-start.52) | collective-permute-done | bytes 491552 | tf_op jit(solution)/shard_map/ppermute | solution.py:26
  198.0 3.8 %shard_map.444 = (bf16[4,256,768]{2,1,0:T(8,128)(2,1)S(1)}, f32[4,64,768]{2,1,0:T(8,128)S(1)}, bf16[4,64,768]{2,1,0:T(8,128)(2,1)S(1)}, f32[4,64,768]{2,1,0:T(8,128)S(1)}, bf16[4,64,768]{2,1,0:T(8,128)(2,1)S(1)}) custom-call(s32[14]{0:T(128)S(1)} %pad_add_fusion.info_ref, bf16[5,64,768]{2,1,0:T(8,128)(2,1)S(1)} %get-tuple-element.665.refs_0_.refs_5_, ...), custom_call_target="tpu_custom_call" | custom-call | flops 2415919104 | bytes 9830400 | tf_op jit(solution)/shard_map/pallas_call | solution.py:308
  208.0 5.0 %shard_map.446 = (f32[96,1920]{1,0:T(8,128)}, bf16[96,1920]{1,0:T(8,128)(2,1)}, bf16[96,1920]{1,0:T(8,128)(2,1)}, bf16[96,1920]{1,0:T(8,128)(2,1)}, bf16[96,1920...) custom-call(s32[14]{0:T(128)S(1)} %pad_add_fusion.info_ref, ...), custom_call_target="tpu_custom_call" | custom-call | flops 2415919104 | bytes 11182080 | tf_op jit(solution)/shard_map/pallas_call | solution.py:308
  222.8 6.1 %collective-permute-done.63.refs_0_ = bf16[96,1920]{1,0:T(8,128)(2,1)S(1)} collective-permute-done((bf16[96,1920]{1,0:T(8,128)(2,1)S(1)}, bf16[96,1920]{1,0:T(8,128)(2,1)S(1)}, u32[]{:S(2)}, u32[]{:S(2)}) %collective-permute-start.63) | collective-permute-done | bytes 368672 | tf_op jit(solution)/shard_map/ppermute | solution.py:141
  234.6 9.0 %shard_map.449 = (f32[4,64,768]{2,1,0:T(8,128)S(1)}, bf16[4,64,768]{2,1,0:T(8,128)(2,1)S(1)}, f32[4,64,768]{2,1,0:T(8,128)S(1)}, bf16[4,64,768]{2,1,0:T(8,128)(2...) custom-call(s32[14]{0:T(128)S(1)} %pad_add_fusion.info_ref, ...), custom_call_target="tpu_custom_call" | custom-call | flops 4429185024 | bytes 11559936 | tf_op jit(solution)/shard_map/pallas_call | solution.py:308
  251.6 3.4 %shard_map.453 = (f32[96,192]{1,0:T(8,128)}, f32[96,192]{1,0:T(8,128)}, f32[96,192]{1,0:T(8,128)}, f32[96,192]{1,0:T(8,128)}, f32[96,768]{1,0:T(8,128)}, /*index...) custom-call(s32[14]{0:T(128)S(1)} %pad_add_fusion.info_ref, bf16[48,768]{1,0:T(8,128)(2,1)} %get-tuple-element.748.refs_0_, ...), custom_call_target="tpu_custom_call" | custom-call | flops 70778880 | bytes 1732608 | tf_op jit(solution)/shard_map/pallas_call | solution.py:308
  255.0 3.8 %collective-permute-done.69.refs_0_.refs_2_ = bf16[96,2688]{1,0:T(8,128)(2,1)S(1)} collective-permute-done((bf16[96,2688]{1,0:T(8,128)(2,1)S(1)}, bf16[96,2688]{1,0:T(8,128)(2,1)S(1)}, u32[]{:S(2)}, u32[]{:S(2)}) %collective-permute-start.69) | collective-permute-done | bytes 516128 | tf_op jit(solution)/shard_map/ppermute | solution.py:141
  264.8 8.9 %collective-permute-done.77 = f32[5,768]{1,0:T(8,128)S(1)} collective-permute-done((f32[5,768]{1,0:T(8,128)S(1)}, f32[5,768]{1,0:T(8,128)S(1)}, u32[]{:S(2)}, u32[]{:S(2)}) %collective-permute-start.77) | collective-permute-done | bytes 15392 | tf_op jit(solution)/shard_map/ppermute | solution.py:26
  (291 shorter events, 151.1 us)
Async XLA Ops:
  11.0 16.3 %collective-permute-start.6 = (bf16[4,64,768]{2,1,0:T(8,128)(2,1)S(1)}, bf16[4,64,768]{2,1,0:T(8,128)(2,1)S(1)}, u32[]{:S(2)}, u32[]{:S(2)}) collective-permute-start(bf16[4,64,768]{2,1,0:T(8,128)(2,1)S(1)} %shard_map.426.refs_0_.refs_4_), channel_id=1, source_target_pairs={{0,1},{1,0},{2,3},{3,2},{4,5},{5,4},{6,7},{7,6},{8,9},{9,8},{10,11... | collective-permute-start | bytes 1179656 | tf_op jit(solution)/shard_map/ppermute | solution.py:26
  11.1 16.3 %collective-permute-start.7 = (bf16[4,64,768]{2,1,0:T(8,128)(2,1)S(1)}, bf16[4,64,768]{2,1,0:T(8,128)(2,1)S(1)}, u32[]{:S(2)}, u32[]{:S(2)}) collective-permute-start(bf16[4,64,768]{2,1,0:T(8,128)(2,1)S(1)} %shard_map.426.refs_0_.refs_4_), channel_id=1, source_target_pairs={{0,2},{1,3},{2,0},{3,1},{4,6},{5,7},{6,4},{7,5},{8,10},{9,11},{10,... | collective-permute-start | bytes 1179656 | tf_op jit(solution)/shard_map/ppermute | solution.py:26
  27.4 15.6 %collective-permute-start.9 = (bf16[96,3072]{1,0:T(8,128)(2,1)S(1)}, bf16[96,3072]{1,0:T(8,128)(2,1)S(1)}, u32[]{:S(2)}, u32[]{:S(2)}) collective-permute-start(bf16[96,3072]{1,0:T(8,128)(2,1)S(1)} %concatenate.15.refs_4_.refs_0_), channel_id=1, source_target_pairs={{8,0},{16,8},{24,16},{28,24},{20,28},{12,20},{4,12},{0,4},{9,1},{1... | collective-permute-start | bytes 1769480 | tf_op jit(solution)/shard_map/ppermute | solution.py:74
  43.0 14.8 %collective-permute-start.11 = (bf16[96,3072]{1,0:T(8,128)(2,1)S(1)}, bf16[96,3072]{1,0:T(8,128)(2,1)S(1)}, u32[]{:S(2)}, u32[]{:S(2)}) collective-permute-start(bf16[96,3072]{1,0:T(8,128)(2,1)S(1)} %concatenate.15.refs_4_.refs_0_), channel_id=1, source_target_pairs={{0,8},{8,16},{16,24},{24,28},{28,20},{20,12},{12,4},{4,0},{1,9},{9... | collective-permute-start | bytes 1769480 | tf_op jit(solution)/shard_map/ppermute | solution.py:74
  44.6 14.5 %collective-permute-start.12 = (bf16[96,3072]{1,0:T(8,128)(2,1)S(1)}, bf16[96,3072]{1,0:T(8,128)(2,1)S(1)}, u32[]{:S(2)}, u32[]{:S(2)}) collective-permute-start(bf16[96,3072]{1,0:T(8,128)(2,1)S(1)} %collective-permute-done.9.refs_6_.refs_2_), channel_id=1, source_target_pairs={{8,0},{16,8},{24,16},{28,24},{20,28},{12,20},{4,12},{0,4},{9,1},{1... | collective-permute-start | bytes 1769480 | tf_op jit(solution)/shard_map/ppermute | solution.py:74
  59.1 15.7 %collective-permute-start.16 = (bf16[96,3072]{1,0:T(8,128)(2,1)S(1)}, bf16[96,3072]{1,0:T(8,128)(2,1)S(1)}, u32[]{:S(2)}, u32[]{:S(2)}) collective-permute-start(bf16[96,3072]{1,0:T(8,128)(2,1)S(1)} %collective-permute-done.11.refs_5_.refs_1_), channel_id=1, source_target_pairs={{0,8},{8,16},{16,24},{24,28},{28,20},{20,12},{12,4},{4,0},{1,9},{9... | collective-permute-start | bytes 1769480 | tf_op jit(solution)/shard_map/ppermute | solution.py:74
  60.6 15.5 %collective-permute-start.17 = (bf16[96,3072]{1,0:T(8,128)(2,1)S(1)}, bf16[96,3072]{1,0:T(8,128)(2,1)S(1)}, u32[]{:S(2)}, u32[]{:S(2)}) collective-permute-start(bf16[96,3072]{1,0:T(8,128)(2,1)S(1)} %collective-permute-done.12.refs_8_.refs_4_), channel_id=1, source_target_pairs={{8,0},{16,8},{24,16},{28,24},{20,28},{12,20},{4,12},{0,4},{9,1},{1... | collective-permute-start | bytes 1769480 | tf_op jit(solution)/shard_map/ppermute | solution.py:74
  61.2 14.9 %collective-permute-start.14 = (bf16[4,64,768]{2,1,0:T(8,128)(2,1)S(1)}, bf16[4,64,768]{2,1,0:T(8,128)(2,1)S(1)}, u32[]{:S(2)}, u32[]{:S(2)}) collective-permute-start(bf16[4,64,768]{2,1,0:T(8,128)(2,1)S(1)} %add_convert_fusion.4), channel_id=1, source_target_pairs={{0,2},{1,3},{2,0},{3,1},{4,6},{5,7},{6,4},{7,5},{8,10},{9,11},{10,... | collective-permute-start | bytes 1179656 | tf_op jit(solution)/shard_map/ppermute | solution.py:26
  61.8 14.3 %collective-permute-start.15 = (bf16[4,64,768]{2,1,0:T(8,128)(2,1)S(1)}, bf16[4,64,768]{2,1,0:T(8,128)(2,1)S(1)}, u32[]{:S(2)}, u32[]{:S(2)}) collective-permute-start(bf16[4,64,768]{2,1,0:T(8,128)(2,1)S(1)} %get-tuple-element.465), channel_id=1, source_target_pairs={{0,1},{1,0},{2,3},{3,2},{4,5},{5,4},{6,7},{7,6},{8,9},{9,8},{10,11... | collective-permute-start | bytes 1179656 | tf_op jit(solution)/shard_map/ppermute | solution.py:26
  76.1 14.8 %collective-permute-start.20 = (bf16[96,3072]{1,0:T(8,128)(2,1)S(1)}, bf16[96,3072]{1,0:T(8,128)(2,1)S(1)}, u32[]{:S(2)}, u32[]{:S(2)}) collective-permute-start(bf16[96,3072]{1,0:T(8,128)(2,1)S(1)} %collective-permute-done.16.refs_7_.refs_3_), channel_id=1, source_target_pairs={{0,8},{8,16},{16,24},{24,28},{28,20},{20,12},{12,4},{4,0},{1,9},{9... | collective-permute-start | bytes 1769480 | tf_op jit(solution)/shard_map/ppermute | solution.py:74
  77.2 14.4 %collective-permute-start.21 = (bf16[96,3072]{1,0:T(8,128)(2,1)S(1)}, bf16[96,3072]{1,0:T(8,128)(2,1)S(1)}, u32[]{:S(2)}, u32[]{:S(2)}) collective-permute-start(bf16[96,3072]{1,0:T(8,128)(2,1)S(1)} %collective-permute-done.17.refs_10_.refs_6_), channel_id=1, source_target_pairs={{8,0},{16,8},{24,16},{28,24},{20,28},{12,20},{4,12},{0,4},{9,1},{1... | collective-permute-start | bytes 1769480 | tf_op jit(solution)/shard_map/ppermute | solution.py:74
  79.4 11.5 %collective-permute-start.19 = (bf16[4,64,768]{2,1,0:T(8,128)(2,1)S(1)}, bf16[4,64,768]{2,1,0:T(8,128)(2,1)S(1)}, u32[]{:S(2)}, u32[]{:S(2)}) collective-permute-start(bf16[4,64,768]{2,1,0:T(8,128)(2,1)S(1)} %get-tuple-element.497.refs_0_), channel_id=1, source_target_pairs={{0,2},{1,3},{2,0},{3,1},{4,6},{5,7},{6,4},{7,5},{8,10},{9,11},{10,... | collective-permute-start | bytes 1179656 | tf_op jit(solution)/shard_map/ppermute | solution.py:26
  115.3 13.6 %collective-permute-start.31 = (bf16[5,64,768]{2,1,0:T(8,128)(2,1)S(1)}, bf16[5,64,768]{2,1,0:T(8,128)(2,1)S(1)}, u32[]{:S(2)}, u32[]{:S(2)}) collective-permute-start(bf16[5,64,768]{2,1,0:T(8,128)(2,1)S(1)} %shard_map.431.refs_0_), channel_id=1, source_target_pairs={{0,2},{1,3},{2,0},{3,1},{4,6},{5,7},{6,4},{7,5},{8,10},{9,11},{10,... | collective-permute-start | bytes 1474568 | tf_op jit(solution)/shard_map/ppermute | solution.py:26
  129.0 11.8 %collective-permute-start.36 = (bf16[96,1536]{1,0:T(8,128)(2,1)S(1)}, bf16[96,1536]{1,0:T(8,128)(2,1)S(1)}, u32[]{:S(2)}, u32[]{:S(2)}) collective-permute-start(bf16[96,1536]{1,0:T(8,128)(2,1)S(1)} %collective-permute-done.32.refs_6_), channel_id=1, source_target_pairs={{0,8},{8,16},{16,24},{24,28},{28,20},{20,12},{12,4},{4,0},{1,9},{9... | collective-permute-start | bytes 884744 | tf_op jit(solution)/shard_map/ppermute | solution.py:74
  170.1 11.5 %collective-permute-start.47 = (bf16[4,64,768]{2,1,0:T(8,128)(2,1)S(1)}, bf16[4,64,768]{2,1,0:T(8,128)(2,1)S(1)}, u32[]{:S(2)}, u32[]{:S(2)}) collective-permute-start(bf16[4,64,768]{2,1,0:T(8,128)(2,1)S(1)} %add_convert_fusion.2), channel_id=1, source_target_pairs={{0,2},{1,3},{2,0},{3,1},{4,6},{5,7},{6,4},{7,5},{8,10},{9,11},{10,... | collective-permute-start | bytes 1179656 | tf_op jit(solution)/shard_map/ppermute | solution.py:26
  182.5 13.6 %collective-permute-start.52 = (bf16[5,64,768]{2,1,0:T(8,128)(2,1)S(1)}, bf16[5,64,768]{2,1,0:T(8,128)(2,1)S(1)}, u32[]{:S(2)}, u32[]{:S(2)}) collective-permute-start(bf16[5,64,768]{2,1,0:T(8,128)(2,1)S(1)} %get-tuple-element.665.refs_0_.refs_5_), channel_id=1, source_target_pairs={{0,2},{1,3},{2,0},{3,1},{4,6},{5,7},{6,4},{7,5},{8,10},{9,11},{10,... | collective-permute-start | bytes 1474568 | tf_op jit(solution)/shard_map/ppermute | solution.py:26
  204.2 11.5 %collective-permute-start.59 = (bf16[4,64,768]{2,1,0:T(8,128)(2,1)S(1)}, bf16[4,64,768]{2,1,0:T(8,128)(2,1)S(1)}, u32[]{:S(2)}, u32[]{:S(2)}) collective-permute-start(bf16[4,64,768]{2,1,0:T(8,128)(2,1)S(1)} %add_convert_fusion.1), channel_id=1, source_target_pairs={{0,2},{1,3},{2,0},{3,1},{4,6},{5,7},{6,4},{7,5},{8,10},{9,11},{10,... | collective-permute-start | bytes 1179656 | tf_op jit(solution)/shard_map/ppermute | solution.py:26
  217.3 12.7 %collective-permute-start.61 = (bf16[5,64,768]{2,1,0:T(8,128)(2,1)S(1)}, bf16[5,64,768]{2,1,0:T(8,128)(2,1)S(1)}, u32[]{:S(2)}, u32[]{:S(2)}) collective-permute-start(bf16[5,64,768]{2,1,0:T(8,128)(2,1)S(1)} %get-tuple-element.707.refs_0_), channel_id=1, source_target_pairs={{0,1},{1,0},{2,3},{3,2},{4,5},{5,4},{6,7},{7,6},{8,9},{9,8},{10,11... | collective-permute-start | bytes 1474568 | tf_op jit(solution)/shard_map/ppermute | solution.py:26
  217.4 13.6 %collective-permute-start.62 = (bf16[5,64,768]{2,1,0:T(8,128)(2,1)S(1)}, bf16[5,64,768]{2,1,0:T(8,128)(2,1)S(1)}, u32[]{:S(2)}, u32[]{:S(2)}) collective-permute-start(bf16[5,64,768]{2,1,0:T(8,128)(2,1)S(1)} %get-tuple-element.707.refs_0_), channel_id=1, source_target_pairs={{0,2},{1,3},{2,0},{3,1},{4,6},{5,7},{6,4},{7,5},{8,10},{9,11},{10,... | collective-permute-start | bytes 1474568 | tf_op jit(solution)/shard_map/ppermute | solution.py:26
  245.8 12.9 %collective-permute-start.69 = (bf16[96,2688]{1,0:T(8,128)(2,1)S(1)}, bf16[96,2688]{1,0:T(8,128)(2,1)S(1)}, u32[]{:S(2)}, u32[]{:S(2)}) collective-permute-start(bf16[96,2688]{1,0:T(8,128)(2,1)S(1)} %get-tuple-element.745), channel_id=1, source_target_pairs={{0,8},{8,16},{16,24},{24,28},{28,20},{20,12},{12,4},{4,0},{1,9},{9... | collective-permute-start | bytes 1548296 | tf_op jit(solution)/shard_map/ppermute | solution.py:141
  246.5 13.1 %collective-permute-start.70 = (bf16[96,2688]{1,0:T(8,128)(2,1)S(1)}, bf16[96,2688]{1,0:T(8,128)(2,1)S(1)}, u32[]{:S(2)}, u32[]{:S(2)}) collective-permute-start(bf16[96,2688]{1,0:T(8,128)(2,1)S(1)} %get-tuple-element.746), channel_id=1, source_target_pairs={{8,0},{16,8},{24,16},{28,24},{20,28},{12,20},{4,12},{0,4},{9,1},{1... | collective-permute-start | bytes 1548296 | tf_op jit(solution)/shard_map/ppermute | solution.py:141
  260.9 12.8 %collective-permute-start.75 = (bf16[96,2688]{1,0:T(8,128)(2,1)S(1)}, bf16[96,2688]{1,0:T(8,128)(2,1)S(1)}, u32[]{:S(2)}, u32[]{:S(2)}) collective-permute-start(bf16[96,2688]{1,0:T(8,128)(2,1)S(1)} %get-tuple-element.769), channel_id=1, source_target_pairs={{0,8},{8,16},{16,24},{24,28},{28,20},{20,12},{12,4},{4,0},{1,9},{9... | collective-permute-start | bytes 1548296 | tf_op jit(solution)/shard_map/ppermute | solution.py:141
  261.5 12.2 %collective-permute-start.73 = (bf16[4,64,768]{2,1,0:T(8,128)(2,1)S(1)}, bf16[4,64,768]{2,1,0:T(8,128)(2,1)S(1)}, u32[]{:S(2)}, u32[]{:S(2)}) collective-permute-start(bf16[4,64,768]{2,1,0:T(8,128)(2,1)S(1)} %add_convert_fusion), channel_id=1, source_target_pairs={{0,2},{1,3},{2,0},{3,1},{4,6},{5,7},{6,4},{7,5},{8,10},{9,11},{10,... | collective-permute-start | bytes 1179656 | tf_op jit(solution)/shard_map/ppermute | solution.py:26
  262.4 11.3 %collective-permute-start.74 = (bf16[4,64,768]{2,1,0:T(8,128)(2,1)S(1)}, bf16[4,64,768]{2,1,0:T(8,128)(2,1)S(1)}, u32[]{:S(2)}, u32[]{:S(2)}) collective-permute-start(bf16[4,64,768]{2,1,0:T(8,128)(2,1)S(1)} %get-tuple-element.760), channel_id=1, source_target_pairs={{0,1},{1,0},{2,3},{3,2},{4,5},{5,4},{6,7},{7,6},{8,9},{9,8},{10,11... | collective-permute-start | bytes 1179656 | tf_op jit(solution)/shard_map/ppermute | solution.py:26
  (98 other events, 796.3 us)
